TPU v7x, 128 devices: a whole 4x4x4 slice. The times are simulated.
128 devices in a mesh: slab: 32 (over y, x_lo, z), chan: 4 (over x_hi, core).
Axes of the slice: x: 4 (x_hi: 2, x_lo: 2; x = x_hi * 2 + x_lo), y: 4, z: 4, core: 2. Of those that a mesh axis runs over, the one named last changes fastest.
Arguments:
- features: bfloat16 [4, 128, 128, 512], P(None, 'slab', 'chan'), may hold values from -6 to 6
- neighbours: int32 [128, 27], P('slab'), may hold values from -1 to 7, as said below
- face_lists: int32 [32, 2, 2], P('slab'), may hold values from -1 to 3, as said below
- weight_first: bfloat16 [27, 128, 128], P(None, None, 'chan'), may hold values from -0.109375 to 0.109375
- bias_first: float32 [128], P('chan'), may hold values from -3 to 3
- weight_second: bfloat16 [27, 128, 128], P(None, None, 'chan'), may hold values from -0.109375 to 0.109375
- bias_second: float32 [128], P('chan'), may hold values from -3 to 3
- level_embed: float32 [4, 128], P(None, 'chan'), may hold values from -3 to 3
Outputs:
- denoised: bfloat16 [4, 128, 128, 512], P(None, 'slab', 'chan')
Inputs may be any that keep to these rules, and one draw needn't show every extreme that they name: `neighbours`: slab s holds in its used slots, in some order, the active bricks of its two brick layers at positions of a 8 x 8 grid; each layer has at most 2 active bricks. Rows of unused slots are all -1; a used slot names itself at offset 13. Offsets with dz = -1 from the bottom layer name the slab below (never for slab 0), dz = +1 from the top layer the slab above (never for the last slab). `face_lists`: entry [s, 0, c] is the slot of the active bottom-layer brick at position c, entry [s, 1, c] that of the top-layer brick; -1 where the position has no active brick. The slots of a slab's used bricks each appear once.
All inputs are finite; a program needn't handle non-finite values.
Results may differ from a plain program's by a relative error of at most 0.02.
Values may be sent and summed in bfloat16 or wider, within the bound.
No kernel may reach another device: no remote copies, remote signals or barrier semaphores. Data moves between devices by JAX's collectives and lax.ppermute only.
A program may use at most 128 MiB of HBM per device.

v0:
```python
import jax
import jax.numpy as jnp
import numpy as np
from jax import lax
from jax.sharding import PartitionSpec as P


def shifted(value, axis, steps):
    count = lax.axis_size(axis)
    first, last = (max(0, -steps), min(count, count - steps))
    return lax.ppermute(value, axis, [(source, source + steps) for source in range(first, last)])


def position_tables():
    place = np.arange(1000)
    pos_z = place // 100
    pos_y = place // 10 % 10
    pos_x = place % 10
    step_z = np.where(pos_z == 0, -1, np.where(pos_z == 9, 1, 0))
    step_y = np.where(pos_y == 0, -1, np.where(pos_y == 9, 1, 0))
    step_x = np.where(pos_x == 0, -1, np.where(pos_x == 9, 1, 0))
    vox_z = (pos_z - 1) % 8
    vox_y = (pos_y - 1) % 8
    vox_x = (pos_x - 1) % 8
    offset_k = 9 * (step_z + 1) + 3 * (step_y + 1) + (step_x + 1)
    within = 64 * vox_z + 8 * vox_y + vox_x
    flat_plane = 8 * vox_y + vox_x
    side = np.where(
        step_z < 0,
        1,
        np.where(
            step_z > 0,
            0,
            np.where(step_y < 0, 3, np.where(step_y > 0, 2, np.where(step_x < 0, 5, 4))),
        ),
    )
    side_off = np.where(
        step_z != 0, 8 * vox_y + vox_x, np.where(step_y != 0, 8 * vox_z + vox_x, 8 * vox_z + vox_y)
    )
    center_pos = (step_z == 0) & (step_y == 0) & (step_x == 0)
    return (
        offset_k.astype(np.int32),
        step_z.astype(np.int32),
        within.astype(np.int32),
        flat_plane.astype(np.int32),
        (side * 64 + side_off).astype(np.int32),
        center_pos,
    )


def fetch(bricks, listed):
    count = bricks.shape[1]
    with_blank = jnp.concatenate([bricks, jnp.zeros_like(bricks[:, :1])], axis=1)
    return jnp.take(with_blank, jnp.where(listed < 0, count, listed), axis=1)


def crop(result):
    count, outputs = (result.shape[0], result.shape[1])
    result = jnp.pad(result, ((0, 0), (0, 0), (0, 22)))
    return result.reshape(count, outputs, 8, 10, 10)[:, :, :, :8, :8].reshape(count, outputs, 512)


def shifted_products(kernel, level_rows):
    offsets = [
        100 * dz + 10 * dy + dx for dz in (-1, 0, 1) for dy in (-1, 0, 1) for dx in (-1, 0, 1)
    ]
    acc = jnp.zeros((level_rows.shape[1], kernel.shape[1], 778), jnp.float32)
    for k in range(27):
        window = level_rows[:, :, 111 + offsets[k] : 889 + offsets[k]]
        acc = acc + jnp.einsum("oc,cbq->boq", kernel[k], window, preferred_element_type=jnp.float32)
    return acc


def conv_layer(features, table, face_lists, weight, bias, shift):
    levels, count, group, voxels = features.shape
    face = face_lists.shape[2]
    offset_k, step_z, within, flat_plane, side_code, center_pos = position_tables()
    upward = fetch(features, face_lists[0, 1])
    downward = fetch(features, face_lists[0, 0])
    below = shifted(upward, "slab", 1)[:, :, :, 448:512]
    above = shifted(downward, "slab", -1)[:, :, :, 0:64]
    flat = features.transpose(0, 2, 1, 3).reshape(levels, group, count * 512)
    below_flat = below.transpose(0, 2, 1, 3).reshape(levels, group, face * 64)
    above_flat = above.transpose(0, 2, 1, 3).reshape(levels, group, face * 64)
    blank = jnp.zeros((levels, group, 1), features.dtype)
    pool = jnp.concatenate([flat, below_flat, above_flat, blank], axis=2)
    target = jnp.take(table, jnp.asarray(offset_k), axis=1)
    dz_row = jnp.asarray(step_z)[None, :]
    in_slab = (target >= 0) & (target < count)
    from_below = (dz_row < 0) & (target >= count) & (target < count + face)
    from_above = (dz_row > 0) & (target >= count + face)
    zero_at = count * 512 + 2 * face * 64
    index = jnp.where(
        in_slab,
        target * 512 + jnp.asarray(within)[None, :],
        jnp.where(
            from_below | from_above,
            count * 512 + (target - count) * 64 + jnp.asarray(flat_plane)[None, :],
            zero_at,
        ),
    )
    padded = jnp.take(pool, index.reshape(-1), axis=2).reshape(levels, group, count, 1000)

    def per_level(level_rows):
        return crop(shifted_products(weight, level_rows))

    term = lax.map(per_level, padded)
    whole = lax.psum(term.astype(jnp.bfloat16), "chan").astype(jnp.float32)
    total = lax.dynamic_slice_in_dim(whole, lax.axis_index("chan") * group, group, 2)
    mask = (table[:, 13] >= 0).astype(jnp.float32)
    act = (
        jax.nn.silu(total + bias[None, None, :, None] + shift[:, None, :, None])
        * mask[None, :, None, None]
    )
    return act.astype(jnp.bfloat16)


def shards(
    features,
    neighbours,
    face_lists,
    weight_first,
    bias_first,
    weight_second,
    bias_second,
    level_embed,
):
    hidden = conv_layer(features, neighbours, face_lists, weight_first, bias_first, level_embed)
    no_shift = jnp.zeros_like(level_embed)
    return conv_layer(hidden, neighbours, face_lists, weight_second, bias_second, no_shift)


def solution(mesh):
    placed = (
        P(None, "slab", "chan", None),
        P("slab", None),
        P("slab", None, None),
        P(None, None, "chan"),
        P("chan"),
        P(None, None, "chan"),
        P("chan"),
        P(None, "chan"),
    )
    return jax.shard_map(
        shards, mesh=mesh, in_specs=placed, out_specs=P(None, "slab", "chan", None), check_vma=False
    )
```

profile of v0, /device:TPU:25, one launch (start us, length us, event | category | flops | bytes accessed | tf_op | source)
XLA Modules:
  0.0 701.6 jit_solution(8023602212281622452)
XLA Ops:
  9.2 3.5 collective-permute-start
  13.4 5.1 collective-permute-start.1
  18.7 2.9 gather_fusion.2
  23.8 2.5 copy.67
  26.3 28.4 %gather_fusion.3 = bf16[4000,4,32]{2,1,0:T(4,128)(2,1)} fusion(bf16[4,32,2305]{1,0,2:T(4,128)(2,1)S(1)} %copy.67, s32[4096]{0:T(1024)S(1)} %pad_clamp_fusion), kind=kCustom, calls=%fused_computation.2.clone | custom fusion | bytes 2064000 | tf_op jit(solution)/shard_map/jit(_take)/gather | solution.py:102
  54.8 16.6 %broadcast_select_fusion = bf16[4000,4,32]{2,1,0:T(4,128)(2,1)} fusion(bf16[4000,4,32]{2,1,0:T(4,128)(2,1)} %gather_fusion.3, pred[4000]{0:T(1024)(128)(4,1)S(1)} %compare_and_fusion), kind=kLoop, calls=%fused_computation.245 | loop fusion | flops 512000 | bytes 2052000 | tf_op jit(solution)/shard_map/jit(_take)/select_n | solution.py:102
  71.3 6.7 copy.69
  79.6 208.5 %while.24 = (s32[]{:T(128)}, bf16[4,4,128,512]{3,2,1,0:T(8,128)(2,1)}, bf16[4,32,4,1000]{3,1,2,0:T(8,128)(2,1)}, bf16[27,128,32]{1,2,0:T(8,128)(2,1)S(1)}, s32[]{:T(128)}, /*index=5*/bf16[]{:T(256)}) while((s32[]{:T(128)}, bf16[4,4,128,512]{3,2,1,0:T(8,128)(2,1)}, bf16[4,32,4,1000]{3,1,2,0:T(8,128)(2,1)}, bf16[27,128,32]{1,2,0:T(8,128)(2,1)S(1)}, ...), condition=%wide.region_1.5_spmd, body=%wide.region_0.4_spmd.sunk | while | flops 699079680 | bytes 97006152 | solution.py:107
  85.5 1.7 fusion.447
  88.9 1.8 fusion.449
  99.2 1.7 fusion.455
  102.6 1.7 fusion.457
  106.0 1.8 fusion.459
  111.2 1.8 fusion.462
  117.9 11.7 %bitcast_add_fusion.23 = bf16[4,128,778]{1,2,0:T(8,128)(2,1)S(1)} fusion(f32[4,778,128]{2,1,0:T(8,128)S(1)} %fusion.440, f32[4,778,128]{2,1,0:T(8,128)S(1)} %fusion.441, f32[4,778,128]{2,1,0:T(8,128)S(1)} %fusion.442, f32[4,778,128]{2,1,0:T(8,128)S(1)} %fusion.443, f32[4,778,128]{2,1,0:T(8,128)S(1)} %fusion.444, f32[4,778,128]{2,1,0:T(8,128)S(1)} %fusion.445, ...), kind=kOutput, calls=%fused_computation.7.clone.1 | convolution fusion | flops 36248576 | bytes 42534912 | tf_op jit(solution)/shard_map/while/body/eval_jaxpr/oc,cbq->boq/dot_general | solution.py:70
  137.6 1.7 fusion.447
  141.0 1.8 fusion.449
  151.3 1.7 fusion.455
  158.2 1.8 fusion.459
  163.3 1.8 fusion.462
  170.0 11.7 %bitcast_add_fusion.23 = bf16[4,128,778]{1,2,0:T(8,128)(2,1)S(1)} fusion(f32[4,778,128]{2,1,0:T(8,128)S(1)} %fusion.440, f32[4,778,128]{2,1,0:T(8,128)S(1)} %fusion.441, f32[4,778,128]{2,1,0:T(8,128)S(1)} %fusion.442, f32[4,778,128]{2,1,0:T(8,128)S(1)} %fusion.443, f32[4,778,128]{2,1,0:T(8,128)S(1)} %fusion.444, f32[4,778,128]{2,1,0:T(8,128)S(1)} %fusion.445, ...), kind=kOutput, calls=%fused_computation.7.clone.1 | convolution fusion | flops 36248576 | bytes 42534912 | tf_op jit(solution)/shard_map/while/body/eval_jaxpr/oc,cbq->boq/dot_general | solution.py:70
  189.7 1.7 fusion.447
  193.1 1.8 fusion.449
  203.4 1.7 fusion.455
  210.3 1.8 fusion.459
  215.4 1.8 fusion.462
  222.2 11.7 %bitcast_add_fusion.23 = bf16[4,128,778]{1,2,0:T(8,128)(2,1)S(1)} fusion(f32[4,778,128]{2,1,0:T(8,128)S(1)} %fusion.440, f32[4,778,128]{2,1,0:T(8,128)S(1)} %fusion.441, f32[4,778,128]{2,1,0:T(8,128)S(1)} %fusion.442, f32[4,778,128]{2,1,0:T(8,128)S(1)} %fusion.443, f32[4,778,128]{2,1,0:T(8,128)S(1)} %fusion.444, f32[4,778,128]{2,1,0:T(8,128)S(1)} %fusion.445, ...), kind=kOutput, calls=%fused_computation.7.clone.1 | convolution fusion | flops 36248576 | bytes 42534912 | tf_op jit(solution)/shard_map/while/body/eval_jaxpr/oc,cbq->boq/dot_general | solution.py:70
  241.8 1.7 fusion.447
  245.2 1.8 fusion.449
  255.6 1.7 fusion.455
  262.4 1.8 fusion.459
  267.6 1.8 fusion.462
  274.3 11.7 %bitcast_add_fusion.23 = bf16[4,128,778]{1,2,0:T(8,128)(2,1)S(1)} fusion(f32[4,778,128]{2,1,0:T(8,128)S(1)} %fusion.440, f32[4,778,128]{2,1,0:T(8,128)S(1)} %fusion.441, f32[4,778,128]{2,1,0:T(8,128)S(1)} %fusion.442, f32[4,778,128]{2,1,0:T(8,128)S(1)} %fusion.443, f32[4,778,128]{2,1,0:T(8,128)S(1)} %fusion.444, f32[4,778,128]{2,1,0:T(8,128)S(1)} %fusion.445, ...), kind=kOutput, calls=%fused_computation.7.clone.1 | convolution fusion | flops 36248576 | bytes 42534912 | tf_op jit(solution)/shard_map/while/body/eval_jaxpr/oc,cbq->boq/dot_general | solution.py:70
  288.3 62.1 %all-reduce.7.cloned.1.call-done = bf16[4,4,128,512]{3,2,1,0:T(8,128)(2,1)} async-done(((bf16[4,4,128,512]{3,2,1,0:T(8,128)(2,1)}), bf16[4,4,128,512]{3,2,1,0:T(8,128)(2,1)}) %all-reduce.7.cloned.1.call-update) | async-done | bytes 2097168 | tf_op jit(solution)/shard_map/psum | solution.py:108
  353.3 3.2 collective-permute-start.2
  356.6 5.1 collective-permute-start.3
  363.3 2.5 collective-permute-done.2
  367.0 2.5 copy.74
  369.5 28.6 %gather_fusion.6 = bf16[4000,4,32]{2,1,0:T(4,128)(2,1)} fusion(bf16[4,32,2305]{1,0,2:T(4,128)(2,1)S(1)} %copy.74, s32[4096]{0:T(1024)S(1)} %pad_clamp_fusion), kind=kCustom, calls=%fused_computation.6.clone | custom fusion | bytes 2064000 | tf_op jit(solution)/shard_map/jit(_take)/gather | solution.py:102
  398.2 16.6 %broadcast_select_fusion.1 = bf16[4000,4,32]{2,1,0:T(4,128)(2,1)} fusion(bf16[4000,4,32]{2,1,0:T(4,128)(2,1)} %gather_fusion.6, pred[4000]{0:T(1024)(128)(4,1)S(1)} %compare_and_fusion), kind=kLoop, calls=%fused_computation.246 | loop fusion | flops 512000 | bytes 2052000 | tf_op jit(solution)/shard_map/jit(_take)/select_n | solution.py:102
  414.7 6.7 copy.76
  423.0 208.5 %while.25 = (s32[]{:T(128)}, bf16[4,4,128,512]{3,2,1,0:T(8,128)(2,1)}, bf16[4,32,4,1000]{3,1,2,0:T(8,128)(2,1)}, bf16[27,128,32]{1,2,0:T(8,128)(2,1)S(1)}, s32[]{:T(128)}, /*index=5*/bf16[]{:T(256)}) while((s32[]{:T(128)}, bf16[4,4,128,512]{3,2,1,0:T(8,128)(2,1)}, bf16[4,32,4,1000]{3,1,2,0:T(8,128)(2,1)}, bf16[27,128,32]{1,2,0:T(8,128)(2,1)S(1)}, ...), condition=%wide.region_4.8_spmd, body=%wide.region_3.7_spmd.sunk | while | flops 699079680 | bytes 97006152 | solution.py:107
  428.9 1.7 fusion.527
  432.3 1.8 fusion.529
  449.4 1.8 fusion.539
  454.6 1.8 fusion.542
  461.3 11.7 %bitcast_add_fusion.24 = bf16[4,128,778]{1,2,0:T(8,128)(2,1)S(1)} fusion(f32[4,778,128]{2,1,0:T(8,128)S(1)} %fusion.520, f32[4,778,128]{2,1,0:T(8,128)S(1)} %fusion.521, f32[4,778,128]{2,1,0:T(8,128)S(1)} %fusion.522, f32[4,778,128]{2,1,0:T(8,128)S(1)} %fusion.523, f32[4,778,128]{2,1,0:T(8,128)S(1)} %fusion.524, f32[4,778,128]{2,1,0:T(8,128)S(1)} %fusion.525, ...), kind=kOutput, calls=%fused_computation.126.clone.1 | convolution fusion | flops 36248576 | bytes 42534912 | tf_op jit(solution)/shard_map/while/body/eval_jaxpr/oc,cbq->boq/dot_general | solution.py:70
  481.0 1.7 fusion.527
  484.4 1.8 fusion.529
  501.5 1.8 fusion.539
  506.7 1.8 fusion.542
  513.4 11.7 %bitcast_add_fusion.24 = bf16[4,128,778]{1,2,0:T(8,128)(2,1)S(1)} fusion(f32[4,778,128]{2,1,0:T(8,128)S(1)} %fusion.520, f32[4,778,128]{2,1,0:T(8,128)S(1)} %fusion.521, f32[4,778,128]{2,1,0:T(8,128)S(1)} %fusion.522, f32[4,778,128]{2,1,0:T(8,128)S(1)} %fusion.523, f32[4,778,128]{2,1,0:T(8,128)S(1)} %fusion.524, f32[4,778,128]{2,1,0:T(8,128)S(1)} %fusion.525, ...), kind=kOutput, calls=%fused_computation.126.clone.1 | convolution fusion | flops 36248576 | bytes 42534912 | tf_op jit(solution)/shard_map/while/body/eval_jaxpr/oc,cbq->boq/dot_general | solution.py:70
  533.1 1.7 fusion.527
  536.5 1.8 fusion.529
  553.6 1.8 fusion.539
  558.8 1.8 fusion.542
  565.5 11.7 %bitcast_add_fusion.24 = bf16[4,128,778]{1,2,0:T(8,128)(2,1)S(1)} fusion(f32[4,778,128]{2,1,0:T(8,128)S(1)} %fusion.520, f32[4,778,128]{2,1,0:T(8,128)S(1)} %fusion.521, f32[4,778,128]{2,1,0:T(8,128)S(1)} %fusion.522, f32[4,778,128]{2,1,0:T(8,128)S(1)} %fusion.523, f32[4,778,128]{2,1,0:T(8,128)S(1)} %fusion.524, f32[4,778,128]{2,1,0:T(8,128)S(1)} %fusion.525, ...), kind=kOutput, calls=%fused_computation.126.clone.1 | convolution fusion | flops 36248576 | bytes 42534912 | tf_op jit(solution)/shard_map/while/body/eval_jaxpr/oc,cbq->boq/dot_general | solution.py:70
  585.2 1.7 fusion.527
  588.6 1.8 fusion.529
  605.7 1.8 fusion.539
  610.9 1.8 fusion.542
  617.7 11.7 %bitcast_add_fusion.24 = bf16[4,128,778]{1,2,0:T(8,128)(2,1)S(1)} fusion(f32[4,778,128]{2,1,0:T(8,128)S(1)} %fusion.520, f32[4,778,128]{2,1,0:T(8,128)S(1)} %fusion.521, f32[4,778,128]{2,1,0:T(8,128)S(1)} %fusion.522, f32[4,778,128]{2,1,0:T(8,128)S(1)} %fusion.523, f32[4,778,128]{2,1,0:T(8,128)S(1)} %fusion.524, f32[4,778,128]{2,1,0:T(8,128)S(1)} %fusion.525, ...), kind=kOutput, calls=%fused_computation.126.clone.1 | convolution fusion | flops 36248576 | bytes 42534912 | tf_op jit(solution)/shard_map/while/body/eval_jaxpr/oc,cbq->boq/dot_general | solution.py:70
  631.5 61.1 %all-reduce.9.cloned.1.call-done = bf16[4,4,128,512]{3,2,1,0:T(8,128)(2,1)} async-done(((bf16[4,4,128,512]{3,2,1,0:T(8,128)(2,1)}), bf16[4,4,128,512]{3,2,1,0:T(8,128)(2,1)}) %all-reduce.9.cloned.1.call-update) | async-done | bytes 2097168 | tf_op jit(solution)/shard_map/psum | solution.py:108
  692.5 2.2 multiply_convert_fusion
  (293 shorter events, 271.5 us)
Async XLA Ops:
  6.5 344.0 %all-reduce.7.cloned.1.call-start = ((), (), s32[]{:S(2)}) async-start(), calls=%async_computation | async-start | bytes 4194304 | tf_op jit(solution)/shard_map/psum | solution.py:108
  7.3 11.3 %copy-start.4 = (s32[4,27]{1,0:T(4,128)S(1)}, s32[4,27]{1,0:T(4,128)}, u32[]{:S(2)}) copy-start(s32[4,27]{1,0:T(4,128)} %param.27) | copy-start | bytes 1300
  7.3 11.4 %copy-start.5 = (s32[1000]{0:T(1024)S(1)}, s32[1000]{0:T(1024)}, u32[]{:S(2)}) copy-start(s32[1000]{0:T(1024)} %constant.145) | copy-start | bytes 12004
  8.4 13.3 %copy-start.6 = (s32[1000]{0:T(1024)S(1)}, s32[1000]{0:T(1024)}, u32[]{:S(2)}) copy-start(s32[1000]{0:T(1024)} %constant.121.clone) | copy-start | bytes 12004
  8.5 13.3 %copy-start.7 = (s32[1000]{0:T(1024)S(1)}, s32[1000]{0:T(1024)}, u32[]{:S(2)}) copy-start(s32[1000]{0:T(1024)} %constant.122.clone) | copy-start | bytes 12004
  8.5 13.3 %copy-start.9 = (pred[1000]{0:T(1024)(128)(4,1)S(1)}, pred[1000]{0:T(1024)(128)(4,1)}, u32[]{:S(2)}) copy-start(pred[1000]{0:T(1024)(128)(4,1)} %constant.134) | copy-start | bytes 3004
  8.5 13.3 %copy-start.10 = (pred[1000]{0:T(1024)(128)(4,1)S(1)}, pred[1000]{0:T(1024)(128)(4,1)}, u32[]{:S(2)}) copy-start(pred[1000]{0:T(1024)(128)(4,1)} %constant.135) | copy-start | bytes 3004
  8.5 13.5 %copy-start.2 = (bf16[4,4,32,512]{3,2,1,0:T(8,128)(2,1)S(1)}, bf16[4,4,32,512]{3,2,1,0:T(8,128)(2,1)}, u32[]{:S(2)}) copy-start(bf16[4,4,32,512]{3,2,1,0:T(8,128)(2,1)} %param.26) | copy-start | bytes 1572868
  9.2 12.9 %collective-permute-start = (bf16[4,2,32,512]{3,2,0,1:T(8,128)(2,1)S(1)}, bf16[4,2,32,512]{3,2,0,1:T(8,128)(2,1)S(1)}, u32[]{:S(2)}, u32[]{:S(2)}) collective-permute-start(bf16[4,2,32,512]{3,2,0,1:T(8,128)(2,1)S(1)} %select_bitcast_fusion.3), channel_id=1, source_target_pairs={{0,4},{4,8},{8,12},{12,16},{16,20},{20,24},{24,28},{28,32},{32,36}... | collective-permute-start | bytes 786440 | tf_op jit(solution)/shard_map/ppermute | solution.py:11
  13.4 10.1 %collective-permute-start.1 = (bf16[4,2,32,512]{3,2,0,1:T(8,128)(2,1)S(1)}, bf16[4,2,32,512]{3,2,0,1:T(8,128)(2,1)S(1)}, u32[]{:S(2)}, u32[]{:S(2)}) collective-permute-start(bf16[4,2,32,512]{3,2,0,1:T(8,128)(2,1)S(1)} %select_bitcast_fusion.2), channel_id=1, source_target_pairs={{4,0},{8,4},{12,8},{16,12},{20,16},{24,20},{28,24},{32,28},{36,32}... | collective-permute-start | bytes 786440 | tf_op jit(solution)/shard_map/ppermute | solution.py:11
  78.0 1.6 copy-start
  288.1 62.4 %copy-start.3 = (f32[4,32]{1,0:T(4,128)S(1)}, f32[4,32]{1,0:T(4,128)}, u32[]{:S(2)}) copy-start(f32[4,32]{1,0:T(4,128)} %param.33) | copy-start | bytes 1540
  288.1 62.4 %copy-start.8 = (f32[32]{0:T(128)S(1)}, f32[32]{0:T(128)}, u32[]{:S(2)}) copy-start(f32[32]{0:T(128)} %param.30) | copy-start | bytes 388
  288.1 404.4 %all-reduce.9.cloned.1.call-start = ((), (), s32[]{:S(2)}) async-start(), calls=%async_computation.1 | async-start | bytes 4194304 | tf_op jit(solution)/shard_map/psum | solution.py:108
  353.3 12.5 %collective-permute-start.2 = (bf16[4,2,32,512]{3,2,0,1:T(8,128)(2,1)S(1)}, bf16[4,2,32,512]{3,2,0,1:T(8,128)(2,1)S(1)}, u32[]{:S(2)}, u32[]{:S(2)}) collective-permute-start(bf16[4,2,32,512]{3,2,0,1:T(8,128)(2,1)S(1)} %select_bitcast_fusion.1), channel_id=1, source_target_pairs={{0,4},{4,8},{8,12},{12,16},{16,20},{20,24},{24,28},{28,32},{32,36}... | collective-permute-start | bytes 786440 | tf_op jit(solution)/shard_map/ppermute | solution.py:11
  356.6 10.1 %collective-permute-start.3 = (bf16[4,2,32,512]{3,2,0,1:T(8,128)(2,1)S(1)}, bf16[4,2,32,512]{3,2,0,1:T(8,128)(2,1)S(1)}, u32[]{:S(2)}, u32[]{:S(2)}) collective-permute-start(bf16[4,2,32,512]{3,2,0,1:T(8,128)(2,1)S(1)} %select_bitcast_fusion), channel_id=1, source_target_pairs={{4,0},{8,4},{12,8},{16,12},{20,16},{24,20},{28,24},{32,28},{36,32}... | collective-permute-start | bytes 786440 | tf_op jit(solution)/shard_map/ppermute | solution.py:11
  421.4 1.5 copy-start.1
  631.4 61.1 %copy-start.11 = (f32[32]{0:T(128)S(1)}, f32[32]{0:T(128)}, u32[]{:S(2)}) copy-start(f32[32]{0:T(128)} %param.32) | copy-start | bytes 388
Sparse Core Ops, SparseCore 0:
  288.2 62.2 all-reduce.6
  631.6 60.8 all-reduce.8
where the time goes:
time: 704 us; the launch traced here: 702 us
  matrix products  393 us (56%)
  waiting for transfers between devices  128 us (18%)
  local copies, waits for them, and re-layouts  110 us (16%)
  other arithmetic  40 us (6%)
  starting transfers between devices  17 us (2%)
  between operations  13.8 us (2%)
    dot_general x216, matrix products, shifted_products(): jnp.einsum('oc,cbq->boq', kernel[k], window, preferred_element_type=jnp.f...  393 us
    psum x2, waiting for transfers between devices, conv_layer(): whole = lax.psum(term.astype(jnp.bfloat16), 'chan').astype(jnp.float32)  123 us
    gather x2, local copies, waits for them, and re-layouts, conv_layer(): jnp.take(pool, index.reshape(-1), axis=2)  57.1 us
    select_n x3, other arithmetic, conv_layer(): jnp.take(pool, index.reshape(-1), axis=2)  33.1 us
    ppermute x4, starting transfers between devices, shifted(): lax.ppermute(value, axis, [(source, source + steps) for source in range(f...  17 us
  transfers between devices with their start and end apart: 6, of which 5 were waited for; matrix products, arithmetic and copies ran while one was open for 1% of the time, Pallas kernels for 0%

commit v1 on v0

v1 whole, which is shorter than its diff:
```python
import jax
import jax.numpy as jnp
from jax import lax
from jax.experimental import pallas as pl
from jax.experimental.pallas import tpu as pltpu
from jax.sharding import PartitionSpec as P

BF16, F32 = jnp.bfloat16, jnp.float32
NONE = 8
HBM = pl.BlockSpec(memory_space=pl.ANY)
VMEM = pl.BlockSpec(memory_space=pltpu.VMEM)
SMEM = pl.BlockSpec(memory_space=pltpu.SMEM)
SPAN = {-1: (7, 0, 1), 0: (0, 1, 8), 1: (0, 9, 1)}


def offset(dz, dy, dx):
    return 9 * (dz + 1) + 3 * (dy + 1) + (dx + 1)


def split_kernel(feat, lists, *refs):
    outs, sem = refs[:11], refs[11]
    pieces, up, down = outs[:3], outs[3:7], outs[7:11]
    me = lax.axis_index("chan")
    copies = []
    for m in range(4):
        level = me ^ m
        for c in range(2):
            top = jnp.maximum(lists[0, 1, c], 0)
            low = jnp.maximum(lists[0, 0, c], 0)
            copies.append((feat.at[level, top, :, pl.ds(384, 128)], up[m].at[c]))
            copies.append((feat.at[level, low, :, pl.ds(0, 128)], down[m].at[c]))
        if m:
            copies.append((feat.at[level], pieces[m - 1]))
    started = []
    for i, (source, target) in enumerate(copies):
        copy = pltpu.make_async_copy(source, target, sem.at[i])
        copy.start()
        started.append(copy)
    for copy in started:
        copy.wait()


def split(features, face_lists):
    piece = jax.ShapeDtypeStruct((4, 32, 512), BF16)
    side = jax.ShapeDtypeStruct((2, 32, 128), BF16)
    return pl.pallas_call(
        split_kernel,
        out_shape=[piece] * 3 + [side] * 8,
        in_specs=[HBM, SMEM],
        out_specs=[HBM] * 11,
        scratch_shapes=[pltpu.SemaphoreType.DMA((19,))],
        name="split_features",
    )(features, face_lists)


def weights_kernel(w1, w2, b1, b2, lev, out1, out2):
    me = lax.axis_index("chan")
    rows = lax.broadcasted_iota(jnp.int32, (32, 32), 0)
    eye = (rows == lax.broadcasted_iota(jnp.int32, (32, 32), 1)).astype(BF16)
    for w, out in ((w1, out1), (w2, out2)):
        for k in range(27):
            turned = lax.dot_general(eye, w[k], (((1,), (1,)), ((), ())), preferred_element_type=F32)
            out[pl.ds(32 * k, 32), :] = turned.astype(BF16)
    values = jnp.concatenate([b1[...], b2[...], lev[...], jnp.zeros((2, 32), F32)], axis=0)
    values = jnp.concatenate([values] * 4, axis=1)
    lane = lax.broadcasted_iota(jnp.int32, (8, 128), 1)
    values = jnp.where(lane // 32 == me, values, 0.0)
    high = values.astype(BF16).astype(F32)
    out1[pl.ds(864, 16), :] = jnp.concatenate([high, values - high], axis=0).astype(BF16)
    out1[pl.ds(880, 16), :] = jnp.zeros((16, 128), BF16)


def turn_weights(w1, w2, b1, b2, lev):
    return pl.pallas_call(
        weights_kernel,
        out_shape=[jax.ShapeDtypeStruct((896, 128), BF16), jax.ShapeDtypeStruct((864, 128), BF16)],
        in_specs=[VMEM] * 5,
        out_specs=[VMEM] * 2,
        compiler_params=pltpu.CompilerParams(vmem_limit_bytes=24 << 20),
        name="turn_weights",
    )(w1, w2, b1.reshape(1, 32), b2.reshape(1, 32), lev)


def silu(v):
    return v / (1.0 + jnp.exp(-v))


def gather_padded(slots, pad, lead, slot, planes):
    x = lax.broadcasted_iota(jnp.int32, (1, 8, 128), 1)
    for dz, z_from, z_to in planes:
        for dy in (-1, 0, 1):
            y_from, y_to, n = SPAN[dy]
            parts = ([], [], [])
            for w in range(2):
                mid, left, right = (
                    slots[slot(w, offset(dz, dy, dx)), z_from, y_from : y_from + n] for dx in (0, -1, 1)
                )
                parts[0].append(pltpu.roll(jnp.where(x == 7, left, mid), 1, 1))
                parts[1].append(mid)
                parts[2].append(pltpu.roll(jnp.where(x == 0, right, mid), 7, 1))
            for d in range(3):
                tile = jnp.concatenate(parts[d], axis=1).astype(BF16)
                pad[lead, z_to, y_to : y_to + n, :, 128 * d : 128 * d + 128] = tile


OWN_PLANES = [(-1, 7, 0)] + [(0, z, z + 1) for z in range(8)] + [(1, 0, 9)]


def conv_pair(pad, lead, w):
    zero = jnp.zeros((128, 128), BF16)
    total = None
    blocks = [(zin, dy) for zin in range(4) for dy in range(3)]
    for first in range(0, 12, 2):
        left, right = [], []
        for zin, dy in blocks[first : first + 2]:
            planes = [pad[lead, zin + 2 * j, dy : dy + 8].reshape(128, 384) for j in range(4)]
            left.append(jnp.concatenate(planes, axis=0))
            for dx in range(3):
                even = w[9 * zin + 3 * dy + dx] if zin < 3 else zero
                odd = w[9 * (zin - 1) + 3 * dy + dx] if zin > 0 else zero
                right.append(jnp.concatenate([even, odd], axis=1))
        part = jnp.dot(
            jnp.concatenate(left, axis=1), jnp.concatenate(right, axis=0), preferred_element_type=F32
        )
        total = part if total is None else total + part
    return total


def conv_face(pad, w):
    total = None
    blocks = [(dz, dy) for dz in range(3) for dy in range(3)]
    for group in (blocks[0:2], blocks[2:4], blocks[4:6], blocks[6:9]):
        left, right = [], []
        for dz, dy in group:
            sides = [pad[side, dz, dy : dy + 8].reshape(128, 384) for side in range(2)]
            left.append(jnp.concatenate(sides, axis=0))
            right += [w[9 * dz + 3 * dy + dx] for dx in range(3)]
        part = jnp.dot(
            jnp.concatenate(left, axis=1), jnp.concatenate(right, axis=0), preferred_element_type=F32
        )
        total = part if total is None else total + part
    return total


def conv_kernel(tab, fl, tab_b, fl_b, tab_a, fl_a, *refs):
    feat, side_b, side_a = refs[0:4], refs[4:8], refs[8:12]
    w1_in, w2_in = refs[12:16], refs[16:20]
    outs = refs[20:24]
    fs, hs, w1, w2, bias, slots, pad, pad_face, acc, shift, turned, sem = refs[24:]
    me = lax.axis_index("chan")

    f_copies, w1_copies, w2_copies = [], [], []
    for m in range(4):
        f_copies.append(pltpu.make_async_copy(feat[m], fs.at[m], sem.at[m]))
        f_copies.append(pltpu.make_async_copy(side_b[m], hs.at[0, m], sem.at[4 + m]))
        f_copies.append(pltpu.make_async_copy(side_a[m], hs.at[1, m], sem.at[8 + m]))
        g = pl.multiple_of((me ^ m) * 32, 32)
        w1_copies.append(
            pltpu.make_async_copy(
                w1_in[m].at[pl.ds(0, 27)], w1.at[:, pl.ds(32 * m, 32), :], sem.at[12 + m]
            )
        )
        w1_copies.append(
            pltpu.make_async_copy(w1_in[m].at[27, pl.ds(0, 16)], bias.at[m], sem.at[16 + m])
        )
        w2_copies.append(pltpu.make_async_copy(w2_in[m], w2.at[:, pl.ds(g, 32), :], sem.at[20 + m]))
    for copy in f_copies + w1_copies + w2_copies:
        copy.start()
    for copy in f_copies:
        copy.wait()

    slots[NONE] = jnp.zeros((8, 8, 8, 128), F32)
    for b in range(4):
        brick = jnp.concatenate([fs[m, b] for m in range(4)], axis=0)
        slots[b] = brick.T.astype(F32).reshape(8, 8, 8, 128)
    for side in range(2):
        for c in range(2):
            face = jnp.concatenate([hs[side, m, c] for m in range(4)], axis=0)
            first = 6 if side == 0 else 0
            slots[4 + 2 * side + c, first : first + 2] = face.T.astype(F32).reshape(2, 8, 8, 128)

    def own(pair):
        def slot(w, k):
            t = tab[2 * pair + w, k]
            return jnp.where(t < 0, NONE, t)

        return slot

    def below(c, k):
        t = tab_b[jnp.maximum(fl_b[0, 1, c], 0), k]
        if k < 18:
            found = jnp.where(t == fl_b[0, 1, 0], 4, jnp.where(t == fl_b[0, 1, 1], 5, NONE))
            return jnp.where(t < 0, NONE, found)
        u = fl[0, 0, jnp.clip(t - 6, 0, 1)]
        return jnp.where((t < 6) | (u < 0), NONE, u)

    def above(c, k):
        t = tab_a[jnp.maximum(fl_a[0, 0, c], 0), k]
        if k >= 9:
            found = jnp.where(t == fl_a[0, 0, 0], 6, jnp.where(t == fl_a[0, 0, 1], 7, NONE))
            return jnp.where(t < 0, NONE, found)
        u = fl[0, 1, jnp.clip(t - 4, 0, 1)]
        return jnp.where((t < 4) | (t > 5) | (u < 0), NONE, u)

    gather_padded(slots, pad_face, 0, below, [(0, 6, 0), (0, 7, 1), (1, 0, 2)])
    gather_padded(slots, pad_face, 1, above, [(-1, 7, 0), (0, 0, 1), (0, 1, 2)])
    for pair in range(2):
        gather_padded(slots, pad, pair, own(pair), OWN_PLANES)

    for copy in w1_copies:
        copy.wait()
    values = sum(bias[m].astype(F32) for m in range(4))
    shift[...] = values[0:8] + values[8:16]
    shift_second = shift[1:2, :]
    shift_first = shift[0:1, :] + shift[pl.ds(2 + me, 1), :]

    def finish(pair, moved):
        for j in range(4):
            for zo in range(2):
                tile = silu(acc[128 * j : 128 * j + 128, 128 * zo : 128 * zo + 128] + moved)
                tile = tile.reshape(8, 2, 8, 128)
                for w in range(2):
                    b = 2 * pair + w
                    slots[b, 2 * j + zo] = jnp.where(tab[b, 13] >= 0, tile[:, w], 0.0)

    for pair in range(2):
        acc[...] = conv_pair(pad, pair, w1)
        finish(pair, shift_first)
    faces = silu(conv_face(pad_face, w1) + shift_first).reshape(2, 8, 2, 8, 128)
    for c in range(2):
        slots[4 + c, 7] = faces[0, :, c]
        slots[6 + c, 0] = faces[1, :, c]

    for pair in range(2):
        gather_padded(slots, pad, pair, own(pair), OWN_PLANES)
    for copy in w2_copies:
        copy.wait()
    for pair in range(2):
        acc[...] = conv_pair(pad, pair, w2)
        finish(pair, shift_second)
    for b in range(4):
        brick = slots[b].reshape(512, 128).astype(BF16).T
        for g in range(4):
            turned[g, b] = brick[32 * g : 32 * g + 32]
    out_copies = [
        pltpu.make_async_copy(turned.at[me ^ m], outs[m], sem.at[24 + m]) for m in range(4)
    ]
    for copy in out_copies:
        copy.start()
    for copy in out_copies:
        copy.wait()


def convolve(tables, feat, side_b, side_a, w1, w2):
    piece = jax.ShapeDtypeStruct((4, 32, 512), BF16)
    return pl.pallas_call(
        conv_kernel,
        out_shape=[piece] * 4,
        in_specs=[SMEM] * 6 + [HBM] * 20,
        out_specs=[HBM] * 4,
        scratch_shapes=[
            pltpu.VMEM((4, 4, 32, 512), BF16),
            pltpu.VMEM((2, 4, 2, 32, 128), BF16),
            pltpu.VMEM((27, 128, 128), BF16),
            pltpu.VMEM((27, 128, 128), BF16),
            pltpu.VMEM((4, 16, 128), BF16),
            pltpu.VMEM((9, 8, 8, 8, 128), F32),
            pltpu.VMEM((2, 10, 10, 16, 384), BF16),
            pltpu.VMEM((2, 3, 10, 16, 384), BF16),
            pltpu.VMEM((512, 256), F32),
            pltpu.VMEM((8, 128), F32),
            pltpu.VMEM((4, 4, 32, 512), BF16),
            pltpu.SemaphoreType.DMA((28,)),
        ],
        compiler_params=pltpu.CompilerParams(vmem_limit_bytes=40 << 20),
        cost_estimate=pl.CostEstimate(flops=8 * 10**9, bytes_accessed=4 * 10**6, transcendentals=10**6),
        name="convolve",
    )(*tables, *feat, *side_b, *side_a, *w1, *w2)


def join_kernel(*refs):
    pieces, out, sem = refs[:4], refs[4], refs[5]
    me = lax.axis_index("chan")
    copies = [pltpu.make_async_copy(pieces[m], out.at[me ^ m], sem.at[m]) for m in range(4)]
    for copy in copies:
        copy.start()
    for copy in copies:
        copy.wait()


def join(pieces):
    return pl.pallas_call(
        join_kernel,
        out_shape=jax.ShapeDtypeStruct((4, 4, 32, 512), BF16),
        in_specs=[HBM] * 4,
        out_specs=HBM,
        scratch_shapes=[pltpu.SemaphoreType.DMA((4,))],
        name="join_levels",
    )(*pieces)


def swap(value, m):
    return lax.ppermute(value, "chan", [(i, i ^ m) for i in range(4)])


def to_slab(value, steps, m):
    slabs = lax.axis_size("slab")
    pairs = [
        (4 * s + g, 4 * (s + steps) + (g ^ m))
        for s in range(slabs)
        if 0 <= s + steps < slabs
        for g in range(4)
    ]
    return lax.ppermute(value, ("slab", "chan"), pairs)


def shards(features, neighbours, face_lists, w_first, b_first, w_second, b_second, level_embed):
    parts = split(features, face_lists)
    pieces, up, down = parts[:3], parts[3:7], parts[7:11]
    w1, w2 = turn_weights(w_first, w_second, b_first, b_second, level_embed)
    w1, w2 = w1.reshape(28, 32, 128), w2.reshape(27, 32, 128)

    side_b = [to_slab(up[m], 1, m) for m in range(4)]
    side_a = [to_slab(down[m], -1, m) for m in range(4)]
    tables = [neighbours, face_lists]
    tables += [to_slab(neighbours, 1, 0), to_slab(face_lists, 1, 0)]
    tables += [to_slab(neighbours, -1, 0), to_slab(face_lists, -1, 0)]

    me = lax.axis_index("chan")
    mine = lax.dynamic_index_in_dim(features, me, 0, keepdims=False)
    feat = [mine, swap(pieces[0], 1), swap(pieces[1], 2), swap(pieces[2], 3)]

    def all_shards(w):
        near, far = swap(w, 1), swap(w, 2)
        return [w, near, far, swap(far, 1)]

    outs = convolve(tables, feat, side_b, side_a, all_shards(w1), all_shards(w2))
    return join([outs[0]] + [swap(outs[m], m) for m in (1, 2, 3)])


def solution(mesh):
    placed = (
        P(None, "slab", "chan", None),
        P("slab", None),
        P("slab", None, None),
        P(None, None, "chan"),
        P("chan"),
        P(None, None, "chan"),
        P("chan"),
        P(None, "chan"),
    )
    return jax.shard_map(
        shards, mesh=mesh, in_specs=placed, out_specs=P(None, "slab", "chan", None), check_vma=False
    )
```

time: 704 us -> 143 us (0.20)
  the two profiles are of different devices: /device:TPU:25 before, /device:TPU:103 now
where the time goes in v1:
time: 143 us
  starting transfers between devices  57.6 us (40%)
  Pallas kernels  46.3 us (32%)
  waiting for transfers between devices  33.9 us (24%)
  local copies, waits for them, and re-layouts  4.73 us (3%)
    ppermute x12, starting transfers between devices, to_slab(): return lax.ppermute(value, ('slab', 'chan'), pairs)  42.5 us
    ppermute x12, waiting for transfers between devices, to_slab(): return lax.ppermute(value, ('slab', 'chan'), pairs)  21.2 us
    pallas_call x1, Pallas kernels, split(): pl.pallas_call(split_kernel, out_shape=[piece] * 3 + [side] * 8, in_specs...  17.8 us
    pallas_call x1, Pallas kernels, join(): pl.pallas_call(join_kernel, out_shape=jax.ShapeDtypeStruct((4, 4, 32, 512...  17 us
    ppermute x12, starting transfers between devices, swap(): return lax.ppermute(value, 'chan', [(i, i ^ m) for i in range(4)])  15.1 us
    ppermute x12, waiting for transfers between devices, swap(): return lax.ppermute(value, 'chan', [(i, i ^ m) for i in range(4)])  12.7 us
    pallas_call x1, Pallas kernels, convolve(): pl.pallas_call(conv_kernel, out_shape=[piece] * 4, in_specs=[SMEM] * 6 +...  10.4 us
    unnamed x24, local copies, waits for them, and re-layouts  3.81 us
  transfers between devices with their start and end apart: 24, of which 8 were waited for; matrix products, arithmetic and copies ran while one was open for 1% of the time, Pallas kernels for 12%

profile of v1, /device:TPU:103, one launch (start us, length us, event | category | flops | bytes accessed | tf_op | source)
XLA Modules:
  0.0 142.9 jit_solution(5006246859559197157)
XLA Ops:
  0.0 1.4 copy.9.w1
  1.4 0.0 copy-done.6
  1.4 0.4 copy.10.w2
  1.9 0.0 copy-start.1
  1.9 0.0 copy-start.3
  1.9 0.0 copy-start.4
  1.9 0.6 copy-done.1
  2.5 0.0 copy-done.3
  2.5 1.0 turn_weights.1
  3.6 1.2 collective-permute-start.16
  4.7 1.8 %collective-permute-start.19 = (bf16[27,32,128]{2,1,0:T(8,128)(2,1)S(1)}, bf16[27,32,128]{2,1,0:T(8,128)(2,1)S(1)}, u32[]{:S(2)}, u32[]{:S(2)}) collective-permute-start(bf16[27,32,128]{2,1,0:T(8,128)(2,1)S(1)} %bitcast.11), channel_id=1, source_target_pairs={{0,2},{1,3},{2,0},{3,1},{4,6},{5,7},{6,4},{7,5},{8,10},{9,11},{10,... | collective-permute-start | bytes 663560 | tf_op jit(solution)/shard_map/ppermute | solution.py:303
  6.6 17.8 %split_features.1 = (bf16[4,32,512]{2,1,0:T(8,128)(2,1)}, bf16[4,32,512]{2,1,0:T(8,128)(2,1)}, bf16[4,32,512]{2,1,0:T(8,128)(2,1)}, bf16[2,32,128]{2,1,0:T(8,128...) custom-call(bf16[4,4,32,512]{3,2,1,0:T(8,128)(2,1)} %feat.1, ...), custom_call_target="tpu_custom_call" | custom-call | tf_op jit(solution)/shard_map/split_features/pallas_call | solution.py:46
  24.4 0.0 copy-start.2
  24.5 1.3 collective-permute-start.4
  25.8 2.0 %collective-permute-start.3 = (s32[1,2,2]{2,1,0:T(2,128)S(1)}, s32[1,2,2]{2,1,0:T(2,128)S(1)}, u32[]{:S(2)}, u32[]{:S(2)}) collective-permute-start(s32[1,2,2]{2,1,0:T(2,128)S(1)} %copy-done.2), channel_id=1, source_target_pairs={{4,0},{5,1},{6,2},{7,3},{8,4},{9,5},{10,6},{11,7},{12,8},{13,9},{1... | collective-permute-start | bytes 56 | tf_op jit(solution)/shard_map/ppermute | solution.py:314
  27.8 6.3 %collective-permute-start = (s32[4,27]{1,0:T(4,128)S(1)}, s32[4,27]{1,0:T(4,128)S(1)}, u32[]{:S(2)}, u32[]{:S(2)}) collective-permute-start(s32[4,27]{1,0:T(4,128)S(1)} %copy-done.5), channel_id=1, source_target_pairs={{0,4},{1,5},{2,6},{3,7},{4,8},{5,9},{6,10},{7,11},{8,12},{9,13},{1... | collective-permute-start | bytes 1304 | tf_op jit(solution)/shard_map/ppermute | solution.py:314
  34.1 0.0 collective-permute-done.3.fl_a
  34.1 1.9 %collective-permute-start.1 = (s32[1,2,2]{2,1,0:T(2,128)S(1)}, s32[1,2,2]{2,1,0:T(2,128)S(1)}, u32[]{:S(2)}, u32[]{:S(2)}) collective-permute-start(s32[1,2,2]{2,1,0:T(2,128)S(1)} %copy-done.2), channel_id=1, source_target_pairs={{0,4},{1,5},{2,6},{3,7},{4,8},{5,9},{6,10},{7,11},{8,12},{9,13},{1... | collective-permute-start | bytes 56 | tf_op jit(solution)/shard_map/ppermute | solution.py:314
  36.0 2.4 %collective-permute-done.1.fl_b = s32[1,2,2]{2,1,0:T(2,128)S(1)} collective-permute-done((s32[1,2,2]{2,1,0:T(2,128)S(1)}, s32[1,2,2]{2,1,0:T(2,128)S(1)}, u32[]{:S(2)}, u32[]{:S(2)}) %collective-permute-start.1) | collective-permute-done | bytes 48 | tf_op jit(solution)/shard_map/ppermute | solution.py:314
  38.4 1.9 %collective-permute-start.2 = (s32[4,27]{1,0:T(4,128)S(1)}, s32[4,27]{1,0:T(4,128)S(1)}, u32[]{:S(2)}, u32[]{:S(2)}) collective-permute-start(s32[4,27]{1,0:T(4,128)S(1)} %copy-done.5), channel_id=1, source_target_pairs={{4,0},{5,1},{6,2},{7,3},{8,4},{9,5},{10,6},{11,7},{12,8},{13,9},{1... | collective-permute-start | bytes 1304 | tf_op jit(solution)/shard_map/ppermute | solution.py:314
  40.3 0.0 collective-permute-done.tab_b
  40.3 6.4 %collective-permute-start.7 = (bf16[2,32,128]{2,1,0:T(8,128)(2,1)}, bf16[2,32,128]{2,1,0:T(8,128)(2,1)S(1)}, u32[]{:S(2)}, u32[]{:S(2)}) collective-permute-start(bf16[2,32,128]{2,1,0:T(8,128)(2,1)} %get-tuple-element.25), channel_id=1, source_target_pairs={{0,4},{1,5},{2,6},{3,7},{4,8},{5,9},{6,10},{7,11},{8,12},{9,13},{1... | collective-permute-start | bytes 49160 | tf_op jit(solution)/shard_map/ppermute | solution.py:314
  46.7 0.0 collective-permute-done.2.tab_a
  46.7 4.4 %collective-permute-start.8 = (bf16[2,32,128]{2,1,0:T(8,128)(2,1)}, bf16[2,32,128]{2,1,0:T(8,128)(2,1)S(1)}, u32[]{:S(2)}, u32[]{:S(2)}) collective-permute-start(bf16[2,32,128]{2,1,0:T(8,128)(2,1)} %get-tuple-element.26), channel_id=1, source_target_pairs={{0,5},{1,4},{2,7},{3,6},{4,9},{5,8},{6,11},{7,10},{8,13},{9,12},{1... | collective-permute-start | bytes 49160 | tf_op jit(solution)/shard_map/ppermute | solution.py:314
  51.1 0.0 collective-permute-done.7.refs_4_
  51.1 3.2 %collective-permute-start.9 = (bf16[2,32,128]{2,1,0:T(8,128)(2,1)}, bf16[2,32,128]{2,1,0:T(8,128)(2,1)S(1)}, u32[]{:S(2)}, u32[]{:S(2)}) collective-permute-start(bf16[2,32,128]{2,1,0:T(8,128)(2,1)} %get-tuple-element.27), channel_id=1, source_target_pairs={{0,6},{1,7},{2,4},{3,5},{4,10},{5,11},{6,8},{7,9},{8,14},{9,15},{1... | collective-permute-start | bytes 49160 | tf_op jit(solution)/shard_map/ppermute | solution.py:314
  54.4 0.0 collective-permute-done.8.refs_5_
  54.4 5.5 %collective-permute-start.10 = (bf16[2,32,128]{2,1,0:T(8,128)(2,1)}, bf16[2,32,128]{2,1,0:T(8,128)(2,1)S(1)}, u32[]{:S(2)}, u32[]{:S(2)}) collective-permute-start(bf16[2,32,128]{2,1,0:T(8,128)(2,1)} %get-tuple-element.28), channel_id=1, source_target_pairs={{0,7},{1,6},{2,5},{3,4},{4,11},{5,10},{6,9},{7,8},{8,15},{9,14},{1... | collective-permute-start | bytes 49160 | tf_op jit(solution)/shard_map/ppermute | solution.py:314
  59.9 0.0 collective-permute-done.9.refs_6_
  59.9 5.2 %collective-permute-start.11 = (bf16[2,32,128]{2,1,0:T(8,128)(2,1)}, bf16[2,32,128]{2,1,0:T(8,128)(2,1)S(1)}, u32[]{:S(2)}, u32[]{:S(2)}) collective-permute-start(bf16[2,32,128]{2,1,0:T(8,128)(2,1)} %get-tuple-element.29), channel_id=1, source_target_pairs={{4,0},{5,1},{6,2},{7,3},{8,4},{9,5},{10,6},{11,7},{12,8},{13,9},{1... | collective-permute-start | bytes 49160 | tf_op jit(solution)/shard_map/ppermute | solution.py:314
  65.1 0.0 collective-permute-done.10.refs_7_
  65.1 1.9 %collective-permute-start.12 = (bf16[2,32,128]{2,1,0:T(8,128)(2,1)}, bf16[2,32,128]{2,1,0:T(8,128)(2,1)S(1)}, u32[]{:S(2)}, u32[]{:S(2)}) collective-permute-start(bf16[2,32,128]{2,1,0:T(8,128)(2,1)} %get-tuple-element.30), channel_id=1, source_target_pairs={{4,1},{5,0},{6,3},{7,2},{8,5},{9,4},{10,7},{11,6},{12,9},{13,8},{1... | collective-permute-start | bytes 49160 | tf_op jit(solution)/shard_map/ppermute | solution.py:314
  67.1 0.6 collective-permute-done.11.refs_8_
  67.6 1.8 %collective-permute-start.5 = (bf16[4,32,512]{2,1,0:T(8,128)(2,1)}, bf16[4,32,512]{2,1,0:T(8,128)(2,1)S(1)}, u32[]{:S(2)}, u32[]{:S(2)}) collective-permute-start(bf16[4,32,512]{2,1,0:T(8,128)(2,1)} %get-tuple-element.23), channel_id=1, source_target_pairs={{0,2},{1,3},{2,0},{3,1},{4,6},{5,7},{6,4},{7,5},{8,10},{9,11},{10,... | collective-permute-start | bytes 393224 | tf_op jit(solution)/shard_map/ppermute | solution.py:303
  69.4 4.0 %collective-permute-done.12.refs_9_ = bf16[2,32,128]{2,1,0:T(8,128)(2,1)S(1)} collective-permute-done((bf16[2,32,128]{2,1,0:T(8,128)(2,1)}, bf16[2,32,128]{2,1,0:T(8,128)(2,1)S(1)}, u32[]{:S(2)}, u32[]{:S(2)}) %collective-permute-start.12) | collective-permute-done | bytes 16416 | tf_op jit(solution)/shard_map/ppermute | solution.py:314
  73.4 1.9 %collective-permute-start.13 = (bf16[2,32,128]{2,1,0:T(8,128)(2,1)}, bf16[2,32,128]{2,1,0:T(8,128)(2,1)S(1)}, u32[]{:S(2)}, u32[]{:S(2)}) collective-permute-start(bf16[2,32,128]{2,1,0:T(8,128)(2,1)} %get-tuple-element.31), channel_id=1, source_target_pairs={{4,2},{5,3},{6,0},{7,1},{8,6},{9,7},{10,4},{11,5},{12,10},{13,11},... | collective-permute-start | bytes 49160 | tf_op jit(solution)/shard_map/ppermute | solution.py:314
  75.3 7.0 %collective-permute-done.13.refs_10_ = bf16[2,32,128]{2,1,0:T(8,128)(2,1)S(1)} collective-permute-done((bf16[2,32,128]{2,1,0:T(8,128)(2,1)}, bf16[2,32,128]{2,1,0:T(8,128)(2,1)S(1)}, u32[]{:S(2)}, u32[]{:S(2)}) %collective-permute-start.13) | collective-permute-done | bytes 16416 | tf_op jit(solution)/shard_map/ppermute | solution.py:314
  82.3 1.9 %collective-permute-start.14 = (bf16[2,32,128]{2,1,0:T(8,128)(2,1)S(1)}, bf16[2,32,128]{2,1,0:T(8,128)(2,1)S(1)}, u32[]{:S(2)}, u32[]{:S(2)}) collective-permute-start(bf16[2,32,128]{2,1,0:T(8,128)(2,1)S(1)} %copy-done.10), channel_id=1, source_target_pairs={{4,3},{5,2},{6,1},{7,0},{8,7},{9,6},{10,5},{11,4},{12,11},{13,10},... | collective-permute-start | bytes 49160 | tf_op jit(solution)/shard_map/ppermute | solution.py:314
  84.2 7.3 %collective-permute-done.14.refs_11_ = bf16[2,32,128]{2,1,0:T(8,128)(2,1)S(1)} collective-permute-done((bf16[2,32,128]{2,1,0:T(8,128)(2,1)S(1)}, bf16[2,32,128]{2,1,0:T(8,128)(2,1)S(1)}, u32[]{:S(2)}, u32[]{:S(2)}) %collective-permute-start.14) | collective-permute-done | bytes 16416 | tf_op jit(solution)/shard_map/ppermute | solution.py:314
  91.6 4.7 %collective-permute-start.15 = (bf16[28,32,128]{2,1,0:T(8,128)(2,1)S(1)}, bf16[28,32,128]{2,1,0:T(8,128)(2,1)S(1)}, u32[]{:S(2)}, u32[]{:S(2)}) collective-permute-start(bf16[28,32,128]{2,1,0:T(8,128)(2,1)S(1)} %bitcast.9), channel_id=1, source_target_pairs={{0,1},{1,0},{2,3},{3,2},{4,5},{5,4},{6,7},{7,6},{8,9},{9,8},{10,11... | collective-permute-start | bytes 688136 | tf_op jit(solution)/shard_map/ppermute | solution.py:303
  96.2 0.0 collective-permute-done.16.refs_14_
  96.2 0.0 collective-permute-start.17
  96.2 0.0 collective-permute-done.4.refs_1_
  96.3 0.5 collective-permute-start.18
  96.8 0.0 collective-permute-done.19.refs_18_
  96.8 0.1 collective-permute-start.20
  96.8 0.0 collective-permute-done.5.refs_2_
  96.8 0.0 collective-permute-start.6
  96.9 0.9 dynamic-slice_bitcast_fusion.refs_0_
  97.8 6.3 %collective-permute-done.6.refs_3_ = bf16[4,32,512]{2,1,0:T(8,128)(2,1)S(1)} collective-permute-done((bf16[4,32,512]{2,1,0:T(8,128)(2,1)}, bf16[4,32,512]{2,1,0:T(8,128)(2,1)S(1)}, u32[]{:S(2)}, u32[]{:S(2)}) %collective-permute-start.6) | collective-permute-done | bytes 131104 | tf_op jit(solution)/shard_map/ppermute | solution.py:303
  104.1 0.0 collective-permute-done.18.refs_17_
  104.1 0.0 collective-permute-done.15.refs_13_
  104.1 0.0 collective-permute-done.20.refs_19_
  104.1 0.0 collective-permute-done.17.refs_15_
  104.2 10.4 %convolve.1 = (bf16[4,32,512]{2,1,0:T(8,128)(2,1)S(1)}, bf16[4,32,512]{2,1,0:T(8,128)(2,1)S(1)}, bf16[4,32,512]{2,1,0:T(8,128)(2,1)S(1)}, bf16[4,32,512]{2,1,0:T(8,128)(2,1)S(1)}) custom-call(s32[4,27]{1,0:T(4,128)S(1)} %copy-done.5, s32[1,2,2]{2,1,0:T(2,128)S(1)} %copy-done.2, s32[4,27]{1,0:T(4,128)S(1)} %collective-permute-done.tab_b, ...), custom_call_target="tpu_custom_call" | custom-call | flops 8000000000 | bytes 4000000 | tf_op jit(solution)/shard_map/convolve/pallas_call | solution.py:256
  114.6 0.6 copy-done
  115.2 0.4 collective-permute-start.21
  115.6 0.0 collective-permute-start.22
  115.6 3.2 %collective-permute-start.23 = (bf16[4,32,512]{2,1,0:T(8,128)(2,1)S(1)}, bf16[4,32,512]{2,1,0:T(8,128)(2,1)S(1)}, u32[]{:S(2)}, u32[]{:S(2)}) collective-permute-start(bf16[4,32,512]{2,1,0:T(8,128)(2,1)S(1)} %get-tuple-element.38), channel_id=1, source_target_pairs={{0,3},{1,2},{2,1},{3,0},{4,7},{5,6},{6,5},{7,4},{8,11},{9,10},{10,... | collective-permute-start | bytes 393224 | tf_op jit(solution)/shard_map/ppermute | solution.py:303
  118.9 0.0 collective-permute-done.21.refs_1_
  118.9 3.3 %collective-permute-done.22.refs_2_ = bf16[4,32,512]{2,1,0:T(8,128)(2,1)S(1)} collective-permute-done((bf16[4,32,512]{2,1,0:T(8,128)(2,1)S(1)}, bf16[4,32,512]{2,1,0:T(8,128)(2,1)S(1)}, u32[]{:S(2)}, u32[]{:S(2)}) %collective-permute-start.22) | collective-permute-done | bytes 131104 | tf_op jit(solution)/shard_map/ppermute | solution.py:303
  122.2 3.0 %collective-permute-done.23.refs_3_ = bf16[4,32,512]{2,1,0:T(8,128)(2,1)S(1)} collective-permute-done((bf16[4,32,512]{2,1,0:T(8,128)(2,1)S(1)}, bf16[4,32,512]{2,1,0:T(8,128)(2,1)S(1)}, u32[]{:S(2)}, u32[]{:S(2)}) %collective-permute-start.23) | collective-permute-done | bytes 131104 | tf_op jit(solution)/shard_map/ppermute | solution.py:303
  125.2 0.7 copy-done.9
  125.9 17.0 %join_levels.1 = bf16[4,4,32,512]{3,2,1,0:T(8,128)(2,1)} custom-call(bf16[4,32,512]{2,1,0:T(8,128)(2,1)} %copy-done, bf16[4,32,512]{2,1,0:T(8,128)(2,1)} %copy-done.7, bf16[4,32,512]{2,1,0:T(8,128)(2,1)} %copy-done.8, bf16[4,32,512]{2,1,0:T(8,128)(2,1)} %copy-done.9), custom_call_target="tpu_custom_call" | custom-call | tf_op jit(solution)/shard_map/join_levels/pallas_call | solution.py:292
  (13 shorter events, 0.0 us)
Async XLA Ops:
  0.0 1.4 copy-start.6
  1.9 0.7 copy-start.1
  1.9 0.7 copy-start.3
  1.9 0.7 copy-start.4
  3.6 92.7 %collective-permute-start.16 = (bf16[28,32,128]{2,1,0:T(8,128)(2,1)S(1)}, bf16[28,32,128]{2,1,0:T(8,128)(2,1)S(1)}, u32[]{:S(2)}, u32[]{:S(2)}) collective-permute-start(bf16[28,32,128]{2,1,0:T(8,128)(2,1)S(1)} %bitcast.8), channel_id=1, source_target_pairs={{0,2},{1,3},{2,0},{3,1},{4,6},{5,7},{6,4},{7,5},{8,10},{9,11},{10,... | collective-permute-start | bytes 688136 | tf_op jit(solution)/shard_map/ppermute | solution.py:303
  4.7 23.1 %copy-start.5 = (s32[4,27]{1,0:T(4,128)S(1)}, s32[4,27]{1,0:T(4,128)}, u32[]{:S(2)}) copy-start(s32[4,27]{1,0:T(4,128)} %tab.1) | copy-start | bytes 1300
  4.7 92.0 %collective-permute-start.19 = (bf16[27,32,128]{2,1,0:T(8,128)(2,1)S(1)}, bf16[27,32,128]{2,1,0:T(8,128)(2,1)S(1)}, u32[]{:S(2)}, u32[]{:S(2)}) collective-permute-start(bf16[27,32,128]{2,1,0:T(8,128)(2,1)S(1)} %bitcast.11), channel_id=1, source_target_pairs={{0,2},{1,3},{2,0},{3,1},{4,6},{5,7},{6,4},{7,5},{8,10},{9,11},{10,... | collective-permute-start | bytes 663560 | tf_op jit(solution)/shard_map/ppermute | solution.py:303
  24.4 1.3 copy-start.2
  24.5 57.8 %copy-start.10 = (bf16[2,32,128]{2,1,0:T(8,128)(2,1)S(1)}, bf16[2,32,128]{2,1,0:T(8,128)(2,1)}, u32[]{:S(2)}) copy-start(bf16[2,32,128]{2,1,0:T(8,128)(2,1)} %get-tuple-element.32) | copy-start | bytes 49156
  24.5 71.8 %collective-permute-start.4 = (bf16[4,32,512]{2,1,0:T(8,128)(2,1)}, bf16[4,32,512]{2,1,0:T(8,128)(2,1)S(1)}, u32[]{:S(2)}, u32[]{:S(2)}) collective-permute-start(bf16[4,32,512]{2,1,0:T(8,128)(2,1)} %get-tuple-element.22), channel_id=1, source_target_pairs={{0,1},{1,0},{2,3},{3,2},{4,5},{5,4},{6,7},{7,6},{8,9},{9,8},{10,11... | collective-permute-start | bytes 393224 | tf_op jit(solution)/shard_map/ppermute | solution.py:303
  25.8 8.3 %collective-permute-start.3 = (s32[1,2,2]{2,1,0:T(2,128)S(1)}, s32[1,2,2]{2,1,0:T(2,128)S(1)}, u32[]{:S(2)}, u32[]{:S(2)}) collective-permute-start(s32[1,2,2]{2,1,0:T(2,128)S(1)} %copy-done.2), channel_id=1, source_target_pairs={{4,0},{5,1},{6,2},{7,3},{8,4},{9,5},{10,6},{11,7},{12,8},{13,9},{1... | collective-permute-start | bytes 56 | tf_op jit(solution)/shard_map/ppermute | solution.py:314
  27.8 12.5 %collective-permute-start = (s32[4,27]{1,0:T(4,128)S(1)}, s32[4,27]{1,0:T(4,128)S(1)}, u32[]{:S(2)}, u32[]{:S(2)}) collective-permute-start(s32[4,27]{1,0:T(4,128)S(1)} %copy-done.5), channel_id=1, source_target_pairs={{0,4},{1,5},{2,6},{3,7},{4,8},{5,9},{6,10},{7,11},{8,12},{9,13},{1... | collective-permute-start | bytes 1304 | tf_op jit(solution)/shard_map/ppermute | solution.py:314
  34.1 4.3 %collective-permute-start.1 = (s32[1,2,2]{2,1,0:T(2,128)S(1)}, s32[1,2,2]{2,1,0:T(2,128)S(1)}, u32[]{:S(2)}, u32[]{:S(2)}) collective-permute-start(s32[1,2,2]{2,1,0:T(2,128)S(1)} %copy-done.2), channel_id=1, source_target_pairs={{0,4},{1,5},{2,6},{3,7},{4,8},{5,9},{6,10},{7,11},{8,12},{9,13},{1... | collective-permute-start | bytes 56 | tf_op jit(solution)/shard_map/ppermute | solution.py:314
  38.4 8.3 %collective-permute-start.2 = (s32[4,27]{1,0:T(4,128)S(1)}, s32[4,27]{1,0:T(4,128)S(1)}, u32[]{:S(2)}, u32[]{:S(2)}) collective-permute-start(s32[4,27]{1,0:T(4,128)S(1)} %copy-done.5), channel_id=1, source_target_pairs={{4,0},{5,1},{6,2},{7,3},{8,4},{9,5},{10,6},{11,7},{12,8},{13,9},{1... | collective-permute-start | bytes 1304 | tf_op jit(solution)/shard_map/ppermute | solution.py:314
  40.3 10.8 %collective-permute-start.7 = (bf16[2,32,128]{2,1,0:T(8,128)(2,1)}, bf16[2,32,128]{2,1,0:T(8,128)(2,1)S(1)}, u32[]{:S(2)}, u32[]{:S(2)}) collective-permute-start(bf16[2,32,128]{2,1,0:T(8,128)(2,1)} %get-tuple-element.25), channel_id=1, source_target_pairs={{0,4},{1,5},{2,6},{3,7},{4,8},{5,9},{6,10},{7,11},{8,12},{9,13},{1... | collective-permute-start | bytes 49160 | tf_op jit(solution)/shard_map/ppermute | solution.py:314
  46.7 7.6 %collective-permute-start.8 = (bf16[2,32,128]{2,1,0:T(8,128)(2,1)}, bf16[2,32,128]{2,1,0:T(8,128)(2,1)S(1)}, u32[]{:S(2)}, u32[]{:S(2)}) collective-permute-start(bf16[2,32,128]{2,1,0:T(8,128)(2,1)} %get-tuple-element.26), channel_id=1, source_target_pairs={{0,5},{1,4},{2,7},{3,6},{4,9},{5,8},{6,11},{7,10},{8,13},{9,12},{1... | collective-permute-start | bytes 49160 | tf_op jit(solution)/shard_map/ppermute | solution.py:314
  51.1 8.8 %collective-permute-start.9 = (bf16[2,32,128]{2,1,0:T(8,128)(2,1)}, bf16[2,32,128]{2,1,0:T(8,128)(2,1)S(1)}, u32[]{:S(2)}, u32[]{:S(2)}) collective-permute-start(bf16[2,32,128]{2,1,0:T(8,128)(2,1)} %get-tuple-element.27), channel_id=1, source_target_pairs={{0,6},{1,7},{2,4},{3,5},{4,10},{5,11},{6,8},{7,9},{8,14},{9,15},{1... | collective-permute-start | bytes 49160 | tf_op jit(solution)/shard_map/ppermute | solution.py:314
  54.4 10.8 %collective-permute-start.10 = (bf16[2,32,128]{2,1,0:T(8,128)(2,1)}, bf16[2,32,128]{2,1,0:T(8,128)(2,1)S(1)}, u32[]{:S(2)}, u32[]{:S(2)}) collective-permute-start(bf16[2,32,128]{2,1,0:T(8,128)(2,1)} %get-tuple-element.28), channel_id=1, source_target_pairs={{0,7},{1,6},{2,5},{3,4},{4,11},{5,10},{6,9},{7,8},{8,15},{9,14},{1... | collective-permute-start | bytes 49160 | tf_op jit(solution)/shard_map/ppermute | solution.py:314
  59.9 7.7 %collective-permute-start.11 = (bf16[2,32,128]{2,1,0:T(8,128)(2,1)}, bf16[2,32,128]{2,1,0:T(8,128)(2,1)S(1)}, u32[]{:S(2)}, u32[]{:S(2)}) collective-permute-start(bf16[2,32,128]{2,1,0:T(8,128)(2,1)} %get-tuple-element.29), channel_id=1, source_target_pairs={{4,0},{5,1},{6,2},{7,3},{8,4},{9,5},{10,6},{11,7},{12,8},{13,9},{1... | collective-permute-start | bytes 49160 | tf_op jit(solution)/shard_map/ppermute | solution.py:314
  65.1 8.3 %collective-permute-start.12 = (bf16[2,32,128]{2,1,0:T(8,128)(2,1)}, bf16[2,32,128]{2,1,0:T(8,128)(2,1)S(1)}, u32[]{:S(2)}, u32[]{:S(2)}) collective-permute-start(bf16[2,32,128]{2,1,0:T(8,128)(2,1)} %get-tuple-element.30), channel_id=1, source_target_pairs={{4,1},{5,0},{6,3},{7,2},{8,5},{9,4},{10,7},{11,6},{12,9},{13,8},{1... | collective-permute-start | bytes 49160 | tf_op jit(solution)/shard_map/ppermute | solution.py:314
  67.6 29.2 %collective-permute-start.5 = (bf16[4,32,512]{2,1,0:T(8,128)(2,1)}, bf16[4,32,512]{2,1,0:T(8,128)(2,1)S(1)}, u32[]{:S(2)}, u32[]{:S(2)}) collective-permute-start(bf16[4,32,512]{2,1,0:T(8,128)(2,1)} %get-tuple-element.23), channel_id=1, source_target_pairs={{0,2},{1,3},{2,0},{3,1},{4,6},{5,7},{6,4},{7,5},{8,10},{9,11},{10,... | collective-permute-start | bytes 393224 | tf_op jit(solution)/shard_map/ppermute | solution.py:303
  73.4 8.9 %collective-permute-start.13 = (bf16[2,32,128]{2,1,0:T(8,128)(2,1)}, bf16[2,32,128]{2,1,0:T(8,128)(2,1)S(1)}, u32[]{:S(2)}, u32[]{:S(2)}) collective-permute-start(bf16[2,32,128]{2,1,0:T(8,128)(2,1)} %get-tuple-element.31), channel_id=1, source_target_pairs={{4,2},{5,3},{6,0},{7,1},{8,6},{9,7},{10,4},{11,5},{12,10},{13,11},... | collective-permute-start | bytes 49160 | tf_op jit(solution)/shard_map/ppermute | solution.py:314
  82.3 9.3 %collective-permute-start.14 = (bf16[2,32,128]{2,1,0:T(8,128)(2,1)S(1)}, bf16[2,32,128]{2,1,0:T(8,128)(2,1)S(1)}, u32[]{:S(2)}, u32[]{:S(2)}) collective-permute-start(bf16[2,32,128]{2,1,0:T(8,128)(2,1)S(1)} %copy-done.10), channel_id=1, source_target_pairs={{4,3},{5,2},{6,1},{7,0},{8,7},{9,6},{10,5},{11,4},{12,11},{13,10},... | collective-permute-start | bytes 49160 | tf_op jit(solution)/shard_map/ppermute | solution.py:314
  91.6 12.6 %collective-permute-start.15 = (bf16[28,32,128]{2,1,0:T(8,128)(2,1)S(1)}, bf16[28,32,128]{2,1,0:T(8,128)(2,1)S(1)}, u32[]{:S(2)}, u32[]{:S(2)}) collective-permute-start(bf16[28,32,128]{2,1,0:T(8,128)(2,1)S(1)} %bitcast.9), channel_id=1, source_target_pairs={{0,1},{1,0},{2,3},{3,2},{4,5},{5,4},{6,7},{7,6},{8,9},{9,8},{10,11... | collective-permute-start | bytes 688136 | tf_op jit(solution)/shard_map/ppermute | solution.py:303
  96.2 7.9 %collective-permute-start.17 = (bf16[28,32,128]{2,1,0:T(8,128)(2,1)S(1)}, bf16[28,32,128]{2,1,0:T(8,128)(2,1)S(1)}, u32[]{:S(2)}, u32[]{:S(2)}) collective-permute-start(bf16[28,32,128]{2,1,0:T(8,128)(2,1)S(1)} %collective-permute-done.16.refs_14_), channel_id=1, source_target_pairs={{0,1},{1,0},{2,3},{3,2},{4,5},{5,4},{6,7},{7,6},{8,9},{9,8},{10,11... | collective-permute-start | bytes 688136 | tf_op jit(solution)/shard_map/ppermute | solution.py:303
  96.3 7.9 %collective-permute-start.18 = (bf16[27,32,128]{2,1,0:T(8,128)(2,1)S(1)}, bf16[27,32,128]{2,1,0:T(8,128)(2,1)S(1)}, u32[]{:S(2)}, u32[]{:S(2)}) collective-permute-start(bf16[27,32,128]{2,1,0:T(8,128)(2,1)S(1)} %bitcast.12), channel_id=1, source_target_pairs={{0,1},{1,0},{2,3},{3,2},{4,5},{5,4},{6,7},{7,6},{8,9},{9,8},{10,11... | collective-permute-start | bytes 663560 | tf_op jit(solution)/shard_map/ppermute | solution.py:303
  96.8 7.4 %collective-permute-start.20 = (bf16[27,32,128]{2,1,0:T(8,128)(2,1)S(1)}, bf16[27,32,128]{2,1,0:T(8,128)(2,1)S(1)}, u32[]{:S(2)}, u32[]{:S(2)}) collective-permute-start(bf16[27,32,128]{2,1,0:T(8,128)(2,1)S(1)} %collective-permute-done.19.refs_18_), channel_id=1, source_target_pairs={{0,1},{1,0},{2,3},{3,2},{4,5},{5,4},{6,7},{7,6},{8,9},{9,8},{10,11... | collective-permute-start | bytes 663560 | tf_op jit(solution)/shard_map/ppermute | solution.py:303
  96.8 7.3 %collective-permute-start.6 = (bf16[4,32,512]{2,1,0:T(8,128)(2,1)}, bf16[4,32,512]{2,1,0:T(8,128)(2,1)S(1)}, u32[]{:S(2)}, u32[]{:S(2)}) collective-permute-start(bf16[4,32,512]{2,1,0:T(8,128)(2,1)} %get-tuple-element.24), channel_id=1, source_target_pairs={{0,3},{1,2},{2,1},{3,0},{4,7},{5,6},{6,5},{7,4},{8,11},{9,10},{10,... | collective-permute-start | bytes 393224 | tf_op jit(solution)/shard_map/ppermute | solution.py:303
  114.6 0.6 copy-start
  115.2 3.6 %collective-permute-start.21 = (bf16[4,32,512]{2,1,0:T(8,128)(2,1)S(1)}, bf16[4,32,512]{2,1,0:T(8,128)(2,1)S(1)}, u32[]{:S(2)}, u32[]{:S(2)}) collective-permute-start(bf16[4,32,512]{2,1,0:T(8,128)(2,1)S(1)} %get-tuple-element.36), channel_id=1, source_target_pairs={{0,1},{1,0},{2,3},{3,2},{4,5},{5,4},{6,7},{7,6},{8,9},{9,8},{10,11... | collective-permute-start | bytes 393224 | tf_op jit(solution)/shard_map/ppermute | solution.py:303
  115.6 6.6 %collective-permute-start.22 = (bf16[4,32,512]{2,1,0:T(8,128)(2,1)S(1)}, bf16[4,32,512]{2,1,0:T(8,128)(2,1)S(1)}, u32[]{:S(2)}, u32[]{:S(2)}) collective-permute-start(bf16[4,32,512]{2,1,0:T(8,128)(2,1)S(1)} %get-tuple-element.37), channel_id=1, source_target_pairs={{0,2},{1,3},{2,0},{3,1},{4,6},{5,7},{6,4},{7,5},{8,10},{9,11},{10,... | collective-permute-start | bytes 393224 | tf_op jit(solution)/shard_map/ppermute | solution.py:303
  115.6 9.6 %collective-permute-start.23 = (bf16[4,32,512]{2,1,0:T(8,128)(2,1)S(1)}, bf16[4,32,512]{2,1,0:T(8,128)(2,1)S(1)}, u32[]{:S(2)}, u32[]{:S(2)}) collective-permute-start(bf16[4,32,512]{2,1,0:T(8,128)(2,1)S(1)} %get-tuple-element.38), channel_id=1, source_target_pairs={{0,3},{1,2},{2,1},{3,0},{4,7},{5,6},{6,5},{7,4},{8,11},{9,10},{10,... | collective-permute-start | bytes 393224 | tf_op jit(solution)/shard_map/ppermute | solution.py:303
  118.9 6.3 %copy-start.7 = (bf16[4,32,512]{2,1,0:T(8,128)(2,1)}, bf16[4,32,512]{2,1,0:T(8,128)(2,1)S(1)}, u32[]{:S(2)}) copy-start(bf16[4,32,512]{2,1,0:T(8,128)(2,1)S(1)} %collective-permute-done.21.refs_1_) | copy-start | bytes 393220
  122.2 3.0 %copy-start.8 = (bf16[4,32,512]{2,1,0:T(8,128)(2,1)}, bf16[4,32,512]{2,1,0:T(8,128)(2,1)S(1)}, u32[]{:S(2)}) copy-start(bf16[4,32,512]{2,1,0:T(8,128)(2,1)S(1)} %collective-permute-done.22.refs_2_) | copy-start | bytes 393220
  125.2 0.7 copy-start.9

commit v2 on v1

v2 whole, which is shorter than its diff:
```python
import jax
import jax.numpy as jnp
from jax import lax
from jax.experimental import pallas as pl
from jax.experimental.pallas import tpu as pltpu
from jax.sharding import PartitionSpec as P

BF16, F32 = jnp.bfloat16, jnp.float32
NONE = 8
HBM = pl.BlockSpec(memory_space=pl.ANY)
VMEM = pl.BlockSpec(memory_space=pltpu.VMEM)
SMEM = pl.BlockSpec(memory_space=pltpu.SMEM)
SPAN = {-1: (7, 0, 1), 0: (0, 1, 8), 1: (0, 9, 1)}


def offset(dz, dy, dx):
    return 9 * (dz + 1) + 3 * (dy + 1) + (dx + 1)


def split_kernel(feat, near, lists_block, lists, *refs):
    pieces, sides = refs[:3], refs[3:5]
    me = lax.axis_index("chan")
    for m in range(1, 4):
        pieces[m - 1][...] = feat[me ^ m]
    for tier, lanes, out in ((1, 384, sides[0]), (0, 0, sides[1])):
        for c in range(2):
            b = jnp.maximum(lists[0, tier, c], 0)
            for level in range(4):
                out[pl.ds(64 * level + 32 * c, 32), :] = feat[level, b, :, lanes : lanes + 128]
        out[pl.ds(256, 16), :] = jnp.zeros((16, 128), BF16)
        out[pl.ds(256, 4), pl.ds(0, 27)] = near[...].astype(F32).astype(BF16)
        out[pl.ds(264, 2), pl.ds(0, 2)] = lists_block[0].astype(F32).astype(BF16)


def split(features, neighbours, face_lists):
    piece = jax.ShapeDtypeStruct((4, 32, 512), BF16)
    side = jax.ShapeDtypeStruct((272, 128), BF16)
    return pl.pallas_call(
        split_kernel,
        out_shape=[piece] * 3 + [side] * 2,
        in_specs=[VMEM, VMEM, VMEM, SMEM],
        out_specs=[VMEM] * 5,
        name="split_features",
    )(features, neighbours, face_lists, face_lists)


def sides_kernel(from_below, from_above, *refs):
    pieces, tables = refs[:4], refs[4]
    me = lax.axis_index("chan")
    for side, source in enumerate((from_below, from_above)):
        for m in range(4):
            rows = pl.ds(pl.multiple_of(64 * (me ^ m), 64), 64)
            pieces[m][pl.ds(64 * side, 64), :] = source[rows, :]
        tables[pl.ds(16 * side, 16), :] = source[pl.ds(256, 16), :].astype(F32).astype(jnp.int32)


def sort_sides(from_below, from_above):
    side = jax.ShapeDtypeStruct((128, 128), BF16)
    return pl.pallas_call(
        sides_kernel,
        out_shape=[side] * 4 + [jax.ShapeDtypeStruct((32, 128), jnp.int32)],
        in_specs=[VMEM] * 2,
        out_specs=[VMEM] * 5,
        name="sort_sides",
    )(from_below, from_above)


def weights_kernel(w1, w2, b1, b2, lev, both, cross):
    me = lax.axis_index("chan")
    odd = lax.axis_index("slab") % 2
    rows = lax.broadcasted_iota(jnp.int32, (32, 32), 0)
    eye = (rows == lax.broadcasted_iota(jnp.int32, (32, 32), 1)).astype(BF16)
    for i, w in enumerate((w1, w2)):
        for k in range(27):
            turned = lax.dot_general(eye, w[k], (((1,), (1,)), ((), ())), preferred_element_type=F32)
            both[i, k] = turned.astype(BF16)
    values = jnp.concatenate([b1[...], b2[...], lev[...], jnp.zeros((2, 32), F32)], axis=0)
    values = jnp.concatenate([values] * 4, axis=1)
    lane = lax.broadcasted_iota(jnp.int32, (8, 128), 1)
    values = jnp.where(lane // 32 == me, values, 0.0)
    high = values.astype(BF16).astype(F32)
    both[0, 27] = jnp.concatenate([high, values - high, jnp.zeros((16, 128), F32)], axis=0).astype(BF16)
    both[1, 27] = jnp.zeros((32, 128), BF16)
    cross[...] = both[odd]


def turn_weights(w1, w2, b1, b2, lev):
    shard = (28, 32, 128)
    return pl.pallas_call(
        weights_kernel,
        out_shape=[jax.ShapeDtypeStruct((2, *shard), BF16), jax.ShapeDtypeStruct(shard, BF16)],
        in_specs=[VMEM] * 5,
        out_specs=[VMEM] * 2,
        compiler_params=pltpu.CompilerParams(vmem_limit_bytes=24 << 20),
        name="turn_weights",
    )(w1, w2, b1.reshape(1, 32), b2.reshape(1, 32), lev)


def silu(v):
    return v / (1.0 + jnp.exp(-v))


def gather_padded(slots, pad, lead, slot, planes):
    x = lax.broadcasted_iota(jnp.int32, (1, 8, 128), 1)
    for dz, z_from, z_to in planes:
        for dy in (-1, 0, 1):
            y_from, y_to, n = SPAN[dy]
            parts = ([], [], [])
            for w in range(2):
                mid, left, right = (
                    slots[slot(w, offset(dz, dy, dx)), z_from, y_from : y_from + n] for dx in (0, -1, 1)
                )
                parts[0].append(pltpu.roll(jnp.where(x == 7, left, mid), 1, 1))
                parts[1].append(mid)
                parts[2].append(pltpu.roll(jnp.where(x == 0, right, mid), 7, 1))
            for d in range(3):
                tile = jnp.concatenate(parts[d], axis=1).astype(BF16)
                pad[lead, z_to, y_to : y_to + n, :, 128 * d : 128 * d + 128] = tile


OWN_PLANES = [(-1, 7, 0)] + [(0, z, z + 1) for z in range(8)] + [(1, 0, 9)]


def conv_pair(pad, lead, w):
    zero = jnp.zeros((128, 128), BF16)
    total = None
    blocks = [(zin, dy) for zin in range(4) for dy in range(3)]
    for first in range(0, 12, 2):
        left, right = [], []
        for zin, dy in blocks[first : first + 2]:
            planes = [pad[lead, zin + 2 * j, dy : dy + 8].reshape(128, 384) for j in range(4)]
            left.append(jnp.concatenate(planes, axis=0))
            for dx in range(3):
                even = w[9 * zin + 3 * dy + dx] if zin < 3 else zero
                odd = w[9 * (zin - 1) + 3 * dy + dx] if zin > 0 else zero
                right.append(jnp.concatenate([even, odd], axis=1))
        part = jnp.dot(
            jnp.concatenate(left, axis=1), jnp.concatenate(right, axis=0), preferred_element_type=F32
        )
        total = part if total is None else total + part
    return total


def conv_face(pad, w):
    total = None
    blocks = [(dz, dy) for dz in range(3) for dy in range(3)]
    for group in (blocks[0:2], blocks[2:4], blocks[4:6], blocks[6:9]):
        left, right = [], []
        for dz, dy in group:
            sides = [pad[side, dz, dy : dy + 8].reshape(128, 384) for side in range(2)]
            left.append(jnp.concatenate(sides, axis=0))
            right += [w[9 * dz + 3 * dy + dx] for dx in range(3)]
        part = jnp.dot(
            jnp.concatenate(left, axis=1), jnp.concatenate(right, axis=0), preferred_element_type=F32
        )
        total = part if total is None else total + part
    return total


def conv_kernel(tab, fl, features, *refs):
    feat, sides, tables_in = refs[0:3], refs[3:7], refs[7]
    own_w, near_w, far_w = refs[8], refs[9], refs[10:14]
    outs = refs[14:18]
    fs, hs, w1, w2, bias, tables, slots, pad, pad_face, acc, shift, turned, sem = refs[18:]
    me = lax.axis_index("chan")
    odd = lax.axis_index("slab") % 2

    f_copies = [pltpu.make_async_copy(tables_in, tables, sem.at[0])]
    for m in range(4):
        source = feat[m - 1] if m else features.at[me]
        f_copies.append(pltpu.make_async_copy(source, fs.at[m], sem.at[4 + m]))
        f_copies.append(pltpu.make_async_copy(sides[m], hs.at[m], sem.at[8 + m]))
    for copy in f_copies:
        copy.start()

    def load_shard(m, layer, source, at):
        weights = (w1, w2)[layer]
        g = 32 * m if layer == 0 else pl.multiple_of((me ^ m) * 32, 32)
        found = [pltpu.make_async_copy(source.at[pl.ds(0, 27)], weights.at[:, pl.ds(g, 32), :], sem.at[at])]
        if layer == 0:
            found.append(
                pltpu.make_async_copy(source.at[27, pl.ds(0, 16)], bias.at[m], sem.at[at + 1])
            )
        return found

    w_copies = ([], [])
    for layer in range(2):
        w_copies[layer].extend(load_shard(0, layer, own_w.at[layer], 12 + 2 * layer))
        w_copies[layer].extend(load_shard(1, layer, near_w.at[layer], 16 + 2 * layer))
    for layer in range(2):
        for copy in w_copies[layer]:
            copy.start()
    for layer in range(2):
        for m in (2, 3):
            at = 20 + 4 * (m - 2) + 2 * layer
            mine, other = far_w[m - 2], far_w[m]

            @pl.when(odd == layer)
            def _():
                for copy in load_shard(m, layer, mine, at):
                    copy.start()

            @pl.when(odd != layer)
            def _():
                for copy in load_shard(m, layer, other, at):
                    copy.start()

            w_copies[layer].extend(load_shard(m, layer, mine, at))
    w1_copies, w2_copies = w_copies
    for copy in f_copies:
        copy.wait()

    slots[NONE] = jnp.zeros((8, 8, 8, 128), F32)
    for b in range(4):
        brick = jnp.concatenate([fs[m, b] for m in range(4)], axis=0)
        slots[b] = brick.T.astype(F32).reshape(8, 8, 8, 128)
    for side in range(2):
        for c in range(2):
            face = jnp.concatenate([hs[m, pl.ds(64 * side + 32 * c, 32)] for m in range(4)], axis=0)
            first = 6 if side == 0 else 0
            slots[4 + 2 * side + c, first : first + 2] = face.T.astype(F32).reshape(2, 8, 8, 128)

    def own(pair):
        def slot(w, k):
            t = tab[2 * pair + w, k]
            return jnp.where(t < 0, NONE, t)

        return slot

    def below(c, k):
        t = tables[0 + jnp.maximum(tables[9, c], 0), k]
        if k < 18:
            found = jnp.where(t == tables[9, 0], 4, jnp.where(t == tables[9, 1], 5, NONE))
            return jnp.where(t < 0, NONE, found)
        u = fl[0, 0, jnp.clip(t - 6, 0, 1)]
        return jnp.where((t < 6) | (u < 0), NONE, u)

    def above(c, k):
        t = tables[16 + jnp.maximum(tables[24, c], 0), k]
        if k >= 9:
            found = jnp.where(t == tables[24, 0], 6, jnp.where(t == tables[24, 1], 7, NONE))
            return jnp.where(t < 0, NONE, found)
        u = fl[0, 1, jnp.clip(t - 4, 0, 1)]
        return jnp.where((t < 4) | (t > 5) | (u < 0), NONE, u)

    gather_padded(slots, pad_face, 0, below, [(0, 6, 0), (0, 7, 1), (1, 0, 2)])
    gather_padded(slots, pad_face, 1, above, [(-1, 7, 0), (0, 0, 1), (0, 1, 2)])
    for pair in range(2):
        gather_padded(slots, pad, pair, own(pair), OWN_PLANES)

    for copy in w1_copies:
        copy.wait()
    values = sum(bias[m].astype(F32) for m in range(4))
    shift[...] = values[0:8] + values[8:16]
    shift_second = shift[1:2, :]
    shift_first = shift[0:1, :] + shift[pl.ds(2 + me, 1), :]

    def finish(pair, moved):
        for j in range(4):
            for zo in range(2):
                tile = silu(acc[128 * j : 128 * j + 128, 128 * zo : 128 * zo + 128] + moved)
                tile = tile.reshape(8, 2, 8, 128)
                for w in range(2):
                    b = 2 * pair + w
                    slots[b, 2 * j + zo] = jnp.where(tab[b, 13] >= 0, tile[:, w], 0.0)

    for pair in range(2):
        acc[...] = conv_pair(pad, pair, w1)
        finish(pair, shift_first)
    faces = silu(conv_face(pad_face, w1) + shift_first).reshape(2, 8, 2, 8, 128)
    for c in range(2):
        slots[4 + c, 7] = faces[0, :, c]
        slots[6 + c, 0] = faces[1, :, c]

    for pair in range(2):
        gather_padded(slots, pad, pair, own(pair), OWN_PLANES)
    for copy in w2_copies:
        copy.wait()
    for pair in range(2):
        acc[...] = conv_pair(pad, pair, w2)
        finish(pair, shift_second)
    for b in range(4):
        brick = slots[b].reshape(512, 128).astype(BF16).T
        for g in range(4):
            turned[g, b] = brick[32 * g : 32 * g + 32]
    out_copies = [
        pltpu.make_async_copy(turned.at[me ^ m], outs[m], sem.at[28 + m]) for m in range(4)
    ]
    for copy in out_copies:
        copy.start()
    for copy in out_copies:
        copy.wait()


def convolve(neighbours, face_lists, features, feat, sides, tables, own_w, near_w, far_w):
    piece = jax.ShapeDtypeStruct((4, 32, 512), BF16)
    return pl.pallas_call(
        conv_kernel,
        out_shape=[piece] * 4,
        in_specs=[SMEM] * 2 + [HBM] * 15,
        out_specs=[HBM] * 4,
        scratch_shapes=[
            pltpu.VMEM((4, 4, 32, 512), BF16),
            pltpu.VMEM((4, 128, 128), BF16),
            pltpu.VMEM((27, 128, 128), BF16),
            pltpu.VMEM((27, 128, 128), BF16),
            pltpu.VMEM((4, 16, 128), BF16),
            pltpu.SMEM((32, 128), jnp.int32),
            pltpu.VMEM((9, 8, 8, 8, 128), F32),
            pltpu.VMEM((2, 10, 10, 16, 384), BF16),
            pltpu.VMEM((2, 3, 10, 16, 384), BF16),
            pltpu.VMEM((512, 256), F32),
            pltpu.VMEM((8, 128), F32),
            pltpu.VMEM((4, 4, 32, 512), BF16),
            pltpu.SemaphoreType.DMA((32,)),
        ],
        compiler_params=pltpu.CompilerParams(vmem_limit_bytes=40 << 20),
        cost_estimate=pl.CostEstimate(flops=8 * 10**9, bytes_accessed=4 * 10**6, transcendentals=10**6),
        name="convolve",
    )(neighbours, face_lists, features, *feat, *sides, tables, own_w, near_w, *far_w)


def join_kernel(*refs):
    pieces, out = refs[:4], refs[4]
    me = lax.axis_index("chan")
    for m in range(4):
        out[me ^ m] = pieces[m][...]


def join(pieces):
    return pl.pallas_call(
        join_kernel,
        out_shape=jax.ShapeDtypeStruct((4, 4, 32, 512), BF16),
        in_specs=[VMEM] * 4,
        out_specs=VMEM,
        name="join_levels",
    )(*pieces)


def swap(value, m):
    return lax.ppermute(value, "chan", [(i, i ^ m) for i in range(4)])


def swap_slabs(value, m):
    count = lax.axis_size("slab")
    pairs = [(4 * s + g, 4 * (s ^ 1) + (g ^ m)) for s in range(count) for g in range(4)]
    return lax.ppermute(value, ("slab", "chan"), pairs)


def to_slab(value, steps):
    count = lax.axis_size("slab")
    return lax.ppermute(value, "slab", [(s, (s + steps) % count) for s in range(count)])


def shards(features, neighbours, face_lists, w_first, b_first, w_second, b_second, level_embed):
    *pieces, up, down = split(features, neighbours, face_lists)
    from_below, from_above = to_slab(up, 1), to_slab(down, -1)
    both, cross = turn_weights(w_first, w_second, b_first, b_second, level_embed)
    fetched = swap(cross, 2)
    feat = [swap(pieces[m - 1], m) for m in (1, 2, 3)]
    near = swap(both, 1)
    far = [fetched, swap(fetched, 1), swap_slabs(fetched, 0), swap_slabs(fetched, 1)]
    *sides, tables = sort_sides(from_below, from_above)
    sides = [sides[0]] + [swap(sides[m], m) for m in (1, 2, 3)]
    outs = convolve(neighbours, face_lists, features, feat, sides, tables, both, near, far)
    return join([outs[0]] + [swap(outs[m], m) for m in (1, 2, 3)])


def solution(mesh):
    placed = (
        P(None, "slab", "chan", None),
        P("slab", None),
        P("slab", None, None),
        P(None, None, "chan"),
        P("chan"),
        P(None, None, "chan"),
        P("chan"),
        P(None, "chan"),
    )
    return jax.shard_map(
        shards, mesh=mesh, in_specs=placed, out_specs=P(None, "slab", "chan", None), check_vma=False
    )
```

time: 143 us -> 69.5 us (0.49)
  the two profiles are of different devices: /device:TPU:103 before, /device:TPU:1 now
where the time goes in v2:
time: 69.5 us; the launch traced here: 69.1 us
  starting transfers between devices  26.6 us (38%)
  waiting for transfers between devices  18.4 us (26%)
  Pallas kernels  16.8 us (24%)
  local copies, waits for them, and re-layouts  7.18 us (10%)
    ppermute x12, starting transfers between devices, swap(): return lax.ppermute(value, 'chan', [(i, i ^ m) for i in range(4)])  20.3 us
    ppermute x12, waiting for transfers between devices, swap(): return lax.ppermute(value, 'chan', [(i, i ^ m) for i in range(4)])  15.2 us
    pallas_call x1, Pallas kernels, convolve(): pl.pallas_call(conv_kernel, out_shape=[piece] * 4, in_specs=[SMEM] * 2 +...  10.4 us
    unnamed x34, local copies, waits for them, and re-layouts  7.18 us
    ppermute x2, starting transfers between devices, to_slab(): lax.ppermute(value, 'slab', [(s, (s + steps) % count) for s in range(coun...  6.31 us
    ppermute x2, waiting for transfers between devices, to_slab(): lax.ppermute(value, 'slab', [(s, (s + steps) % count) for s in range(coun...  2.99 us
    pallas_call x1, Pallas kernels, join(): pl.pallas_call(join_kernel, out_shape=jax.ShapeDtypeStruct((4, 4, 32, 512...  1.93 us
    pallas_call x1, Pallas kernels, split(): pl.pallas_call(split_kernel, out_shape=[piece] * 3 + [side] * 2, in_specs...  1.91 us
  transfers between devices with their start and end apart: 16, of which 7 were waited for; matrix products, arithmetic and copies ran while one was open for 0% of the time, Pallas kernels for 5%

profile of v2, /device:TPU:1, one launch (start us, length us, event | category | flops | bytes accessed | tf_op | source)
XLA Modules:
  0.0 69.1 jit_solution(4596945140381188317)
XLA Ops:
  0.0 0.0 copy-start.9
  0.0 1.4 %copy.9.w1 = bf16[27,128,32]{2,1,0:T(8,128)(2,1)S(1)} copy(bf16[27,128,32]{1,2,0:T(8,128)(2,1)} %param.11) | data formatting | bytes 442368 | tf_op args[3]
  1.4 0.0 copy-done.9
  1.4 0.4 copy.10.w2
  1.9 0.0 copy-start.4
  1.9 0.0 copy-start.5
  1.9 0.0 copy-start.6
  1.9 0.6 copy-done.4
  2.5 0.0 copy-done.5
  2.5 0.0 copy-done.6
  2.5 1.0 %turn_weights.1 = (bf16[2,28,32,128]{3,2,1,0:T(8,128)(2,1)S(1)}, bf16[28,32,128]{2,1,0:T(8,128)(2,1)S(1)}) custom-call(bf16[27,128,32]{2,1,0:T(8,128)(2,1)S(1)} %copy.9.w1, bf16[27,128,32]{2,1,0:T(8,128)(2,1)S(1)} %copy.10.w2, f32[1,32]{1,0:T(1,128)S(1)} %bitcast.2, f32[1,32]{1,0:T(1,128)S(1)} %bitcast.3, f32[4,32]{1,0:T(4,128)S(1)} %copy-done.4), custom_call_target="tpu_custom_call" | custom-call | tf_op jit(solution)/shard_map/turn_weights/pallas_call | solution.py:89
  3.6 0.0 copy-start
  3.6 3.7 %collective-permute-start.9 = (bf16[28,32,128]{2,1,0:T(8,128)(2,1)S(1)}, bf16[28,32,128]{2,1,0:T(8,128)(2,1)S(1)}, u32[]{:S(2)}, u32[]{:S(2)}) collective-permute-start(bf16[28,32,128]{2,1,0:T(8,128)(2,1)S(1)} %get-tuple-element.32), channel_id=1, source_target_pairs={{0,2},{1,3},{2,0},{3,1},{4,6},{5,7},{6,4},{7,5},{8,10},{9,11},{10,... | collective-permute-start | bytes 688136 | tf_op jit(solution)/shard_map/ppermute | solution.py:341
  7.2 1.0 %collective-permute-start.8 = (bf16[2,28,32,128]{3,2,1,0:T(8,128)(2,1)S(1)}, bf16[2,28,32,128]{3,2,1,0:T(8,128)(2,1)S(1)}, u32[]{:S(2)}, u32[]{:S(2)}) collective-permute-start(bf16[2,28,32,128]{3,2,1,0:T(8,128)(2,1)S(1)} %get-tuple-element.31.refs_8_), channel_id=1, source_target_pairs={{0,1},{1,0},{2,3},{3,2},{4,5},{5,4},{6,7},{7,6},{8,9},{9,8},{10,11... | collective-permute-start | bytes 1376264 | tf_op jit(solution)/shard_map/ppermute | solution.py:341
  8.2 1.9 %split_features.1 = (bf16[4,32,512]{2,1,0:T(8,128)(2,1)}, bf16[4,32,512]{2,1,0:T(8,128)(2,1)}, bf16[4,32,512]{2,1,0:T(8,128)(2,1)}, bf16[272,128]{1,0:T(8,128)(2,1)}, bf16[272,128]{1,0:T(8,128)(2,1)}) custom-call(bf16[4,4,32,512]{3,2,1,0:T(8,128)(2,1)} %features.1, s32[4,27]{1,0:T(4,128)} %tab.1, s32[1,2,2]{2,1,0:T(2,128)} %fl.1, s32[1,2,2]{2,1,0:T(2,128)} %fl.1), custom_call_target="tpu_custom_call" | custom-call | tf_op jit(solution)/shard_map/split_features/pallas_call | solution.py:38
  10.1 0.0 copy-start.15
  10.1 1.6 %collective-permute-start.3 = (bf16[272,128]{1,0:T(8,128)(2,1)}, bf16[272,128]{1,0:T(8,128)(2,1)S(1)}, u32[]{:S(2)}, u32[]{:S(2)}) collective-permute-start(bf16[272,128]{1,0:T(8,128)(2,1)} %get-tuple-element.24), channel_id=1, source_target_pairs={{0,4},{4,8},{8,12},{12,16},{16,20},{20,24},{24,28},{28,32},{32,36}... | collective-permute-start | bytes 208904 | tf_op jit(solution)/shard_map/ppermute | solution.py:352
  11.7 4.7 %collective-permute-start.4 = (bf16[272,128]{1,0:T(8,128)(2,1)}, bf16[272,128]{1,0:T(8,128)(2,1)S(1)}, u32[]{:S(2)}, u32[]{:S(2)}) collective-permute-start(bf16[272,128]{1,0:T(8,128)(2,1)} %get-tuple-element.25), channel_id=1, source_target_pairs={{0,124},{4,0},{8,4},{12,8},{16,12},{20,16},{24,20},{28,24},{32,28}... | collective-permute-start | bytes 208904 | tf_op jit(solution)/shard_map/ppermute | solution.py:352
  16.4 0.3 collective-permute-start
  16.7 3.0 %collective-permute-done.3.from_below = bf16[272,128]{1,0:T(8,128)(2,1)S(1)} collective-permute-done((bf16[272,128]{1,0:T(8,128)(2,1)}, bf16[272,128]{1,0:T(8,128)(2,1)S(1)}, u32[]{:S(2)}, u32[]{:S(2)}) %collective-permute-start.3) | collective-permute-done | bytes 69664 | tf_op jit(solution)/shard_map/ppermute | solution.py:352
  19.7 0.0 copy-start.13
  19.7 0.0 collective-permute-done.4.from_above
  19.7 0.6 copy-done.13
  20.3 0.0 copy-start.14
  20.3 0.6 copy-done.14
  20.9 1.6 %sort_sides.1 = (bf16[128,128]{1,0:T(8,128)(2,1)}, bf16[128,128]{1,0:T(8,128)(2,1)}, bf16[128,128]{1,0:T(8,128)(2,1)}, bf16[128,128]{1,0:T(8,128)(2,1)}, s32[32,128]{1,0:T(8,128)}) custom-call(bf16[272,128]{1,0:T(8,128)(2,1)} %copy-done.13, bf16[272,128]{1,0:T(8,128)(2,1)} %copy-done.14), custom_call_target="tpu_custom_call" | custom-call | tf_op jit(solution)/shard_map/sort_sides/pallas_call | solution.py:59
  22.5 1.8 %collective-permute-start.5 = (bf16[128,128]{1,0:T(8,128)(2,1)}, bf16[128,128]{1,0:T(8,128)(2,1)S(1)}, u32[]{:S(2)}, u32[]{:S(2)}) collective-permute-start(bf16[128,128]{1,0:T(8,128)(2,1)} %get-tuple-element.27), channel_id=1, source_target_pairs={{0,1},{1,0},{2,3},{3,2},{4,5},{5,4},{6,7},{7,6},{8,9},{9,8},{10,11... | collective-permute-start | bytes 98312 | tf_op jit(solution)/shard_map/ppermute | solution.py:341
  24.4 1.7 %collective-permute-start.6 = (bf16[128,128]{1,0:T(8,128)(2,1)}, bf16[128,128]{1,0:T(8,128)(2,1)S(1)}, u32[]{:S(2)}, u32[]{:S(2)}) collective-permute-start(bf16[128,128]{1,0:T(8,128)(2,1)} %get-tuple-element.28), channel_id=1, source_target_pairs={{0,2},{1,3},{2,0},{3,1},{4,6},{5,7},{6,4},{7,5},{8,10},{9,11},{10,... | collective-permute-start | bytes 98312 | tf_op jit(solution)/shard_map/ppermute | solution.py:341
  26.1 0.0 collective-permute-done.5.refs_4_
  26.1 1.2 %collective-permute-start.1 = (bf16[4,32,512]{2,1,0:T(8,128)(2,1)}, bf16[4,32,512]{2,1,0:T(8,128)(2,1)S(1)}, u32[]{:S(2)}, u32[]{:S(2)}) collective-permute-start(bf16[4,32,512]{2,1,0:T(8,128)(2,1)} %get-tuple-element.22), channel_id=1, source_target_pairs={{0,2},{1,3},{2,0},{3,1},{4,6},{5,7},{6,4},{7,5},{8,10},{9,11},{10,... | collective-permute-start | bytes 393224 | tf_op jit(solution)/shard_map/ppermute | solution.py:341
  27.3 1.5 %collective-permute-done.6.refs_5_ = bf16[128,128]{1,0:T(8,128)(2,1)S(1)} collective-permute-done((bf16[128,128]{1,0:T(8,128)(2,1)}, bf16[128,128]{1,0:T(8,128)(2,1)S(1)}, u32[]{:S(2)}, u32[]{:S(2)}) %collective-permute-start.6) | collective-permute-done | bytes 32800 | tf_op jit(solution)/shard_map/ppermute | solution.py:341
  28.8 2.8 %collective-permute-start.7 = (bf16[128,128]{1,0:T(8,128)(2,1)}, bf16[128,128]{1,0:T(8,128)(2,1)S(1)}, u32[]{:S(2)}, u32[]{:S(2)}) collective-permute-start(bf16[128,128]{1,0:T(8,128)(2,1)} %get-tuple-element.29), channel_id=1, source_target_pairs={{0,3},{1,2},{2,1},{3,0},{4,7},{5,6},{6,5},{7,4},{8,11},{9,10},{10,... | collective-permute-start | bytes 98312 | tf_op jit(solution)/shard_map/ppermute | solution.py:341
  31.6 0.0 collective-permute-done.9.refs_10_
  31.6 0.0 collective-permute-start.12
  31.6 2.3 %collective-permute-done.7.refs_6_ = bf16[128,128]{1,0:T(8,128)(2,1)S(1)} collective-permute-done((bf16[128,128]{1,0:T(8,128)(2,1)}, bf16[128,128]{1,0:T(8,128)(2,1)S(1)}, u32[]{:S(2)}, u32[]{:S(2)}) %collective-permute-start.7) | collective-permute-done | bytes 32800 | tf_op jit(solution)/shard_map/ppermute | solution.py:341
  33.9 0.0 collective-permute-start.11
  33.9 0.0 collective-permute-done.refs_0_
  33.9 1.2 %collective-permute-start.10 = (bf16[28,32,128]{2,1,0:T(8,128)(2,1)S(1)}, bf16[28,32,128]{2,1,0:T(8,128)(2,1)S(1)}, u32[]{:S(2)}, u32[]{:S(2)}) collective-permute-start(bf16[28,32,128]{2,1,0:T(8,128)(2,1)S(1)} %collective-permute-done.9.refs_10_), channel_id=1, source_target_pairs={{0,1},{1,0},{2,3},{3,2},{4,5},{5,4},{6,7},{7,6},{8,9},{9,8},{10,11... | collective-permute-start | bytes 688136 | tf_op jit(solution)/shard_map/ppermute | solution.py:341
  35.1 0.0 collective-permute-done.1.refs_1_
  35.1 0.0 copy-done.15
  35.1 1.7 %collective-permute-start.2 = (bf16[4,32,512]{2,1,0:T(8,128)(2,1)S(1)}, bf16[4,32,512]{2,1,0:T(8,128)(2,1)S(1)}, u32[]{:S(2)}, u32[]{:S(2)}) collective-permute-start(bf16[4,32,512]{2,1,0:T(8,128)(2,1)S(1)} %copy-done.15), channel_id=1, source_target_pairs={{0,3},{1,2},{2,1},{3,0},{4,7},{5,6},{6,5},{7,4},{8,11},{9,10},{10,... | collective-permute-start | bytes 393224 | tf_op jit(solution)/shard_map/ppermute | solution.py:341
  36.8 5.0 %collective-permute-done.2.refs_2_ = bf16[4,32,512]{2,1,0:T(8,128)(2,1)S(1)} collective-permute-done((bf16[4,32,512]{2,1,0:T(8,128)(2,1)S(1)}, bf16[4,32,512]{2,1,0:T(8,128)(2,1)S(1)}, u32[]{:S(2)}, u32[]{:S(2)}) %collective-permute-start.2) | collective-permute-done | bytes 131104 | tf_op jit(solution)/shard_map/ppermute | solution.py:341
  41.8 0.0 collective-permute-done.12.refs_13_
  41.8 0.2 collective-permute-done.11.refs_12_
  42.0 0.0 collective-permute-done.10.refs_11_
  42.0 0.0 collective-permute-done.8.refs_9_
  42.0 0.0 copy-done
  42.0 0.0 copy-done.3
  42.0 0.7 copy-done.2
  42.7 0.8 %copy-done.7 = bf16[128,128]{1,0:T(8,128)(2,1)S(1)} copy-done((bf16[128,128]{1,0:T(8,128)(2,1)S(1)}, bf16[128,128]{1,0:T(8,128)(2,1)}, u32[]{:S(2)}) %copy-start.7) | copy-done | bytes 32792
  43.5 0.7 %copy-done.8 = s32[32,128]{1,0:T(8,128)S(1)} copy-done((s32[32,128]{1,0:T(8,128)S(1)}, s32[32,128]{1,0:T(8,128)}, u32[]{:S(2)}) %copy-start.8) | copy-done | bytes 16408
  44.2 10.4 %convolve.1 = (bf16[4,32,512]{2,1,0:T(8,128)(2,1)S(1)}, bf16[4,32,512]{2,1,0:T(8,128)(2,1)S(1)}, bf16[4,32,512]{2,1,0:T(8,128)(2,1)S(1)}, bf16[4,32,512]{2,1,0:T(8,128)(2,1)S(1)}) custom-call(s32[4,27]{1,0:T(4,128)S(1)} %copy-done.3, s32[1,2,2]{2,1,0:T(2,128)S(1)} %copy-done.2, bf16[4,4,32,512]{3,2,1,0:T(8,128)(2,1)S(1)} %copy-done, ...), custom_call_target="tpu_custom_call" | custom-call | flops 8000000000 | bytes 4000000 | tf_op jit(solution)/shard_map/convolve/pallas_call | solution.py:297
  54.6 0.0 copy-start.1
  54.6 0.6 copy-done.1
  55.2 1.8 %collective-permute-start.13 = (bf16[4,32,512]{2,1,0:T(8,128)(2,1)S(1)}, bf16[4,32,512]{2,1,0:T(8,128)(2,1)S(1)}, u32[]{:S(2)}, u32[]{:S(2)}) collective-permute-start(bf16[4,32,512]{2,1,0:T(8,128)(2,1)S(1)} %get-tuple-element.34), channel_id=1, source_target_pairs={{0,1},{1,0},{2,3},{3,2},{4,5},{5,4},{6,7},{7,6},{8,9},{9,8},{10,11... | collective-permute-start | bytes 393224 | tf_op jit(solution)/shard_map/ppermute | solution.py:341
  57.0 1.2 %collective-permute-start.14 = (bf16[4,32,512]{2,1,0:T(8,128)(2,1)S(1)}, bf16[4,32,512]{2,1,0:T(8,128)(2,1)S(1)}, u32[]{:S(2)}, u32[]{:S(2)}) collective-permute-start(bf16[4,32,512]{2,1,0:T(8,128)(2,1)S(1)} %get-tuple-element.35), channel_id=1, source_target_pairs={{0,2},{1,3},{2,0},{3,1},{4,6},{5,7},{6,4},{7,5},{8,10},{9,11},{10,... | collective-permute-start | bytes 393224 | tf_op jit(solution)/shard_map/ppermute | solution.py:341
  58.2 1.9 %collective-permute-start.15 = (bf16[4,32,512]{2,1,0:T(8,128)(2,1)S(1)}, bf16[4,32,512]{2,1,0:T(8,128)(2,1)S(1)}, u32[]{:S(2)}, u32[]{:S(2)}) collective-permute-start(bf16[4,32,512]{2,1,0:T(8,128)(2,1)S(1)} %get-tuple-element.36), channel_id=1, source_target_pairs={{0,3},{1,2},{2,1},{3,0},{4,7},{5,6},{6,5},{7,4},{8,11},{9,10},{10,... | collective-permute-start | bytes 393224 | tf_op jit(solution)/shard_map/ppermute | solution.py:341
  60.1 0.0 collective-permute-done.13.refs_1_
  60.1 3.5 %collective-permute-done.14.refs_2_ = bf16[4,32,512]{2,1,0:T(8,128)(2,1)S(1)} collective-permute-done((bf16[4,32,512]{2,1,0:T(8,128)(2,1)S(1)}, bf16[4,32,512]{2,1,0:T(8,128)(2,1)S(1)}, u32[]{:S(2)}, u32[]{:S(2)}) %collective-permute-start.14) | collective-permute-done | bytes 131104 | tf_op jit(solution)/shard_map/ppermute | solution.py:341
  63.6 2.9 %collective-permute-done.15.refs_3_ = bf16[4,32,512]{2,1,0:T(8,128)(2,1)S(1)} collective-permute-done((bf16[4,32,512]{2,1,0:T(8,128)(2,1)S(1)}, bf16[4,32,512]{2,1,0:T(8,128)(2,1)S(1)}, u32[]{:S(2)}, u32[]{:S(2)}) %collective-permute-start.15) | collective-permute-done | bytes 131104 | tf_op jit(solution)/shard_map/ppermute | solution.py:341
  66.5 0.0 copy-done.10
  66.5 0.0 copy-done.11
  66.5 0.6 copy-done.12
  67.2 1.9 %join_levels.1 = bf16[4,4,32,512]{3,2,1,0:T(8,128)(2,1)} custom-call(bf16[4,32,512]{2,1,0:T(8,128)(2,1)} %copy-done.1, bf16[4,32,512]{2,1,0:T(8,128)(2,1)} %copy-done.10, bf16[4,32,512]{2,1,0:T(8,128)(2,1)} %copy-done.11, bf16[4,32,512]{2,1,0:T(8,128)(2,1)} %copy-done.12), custom_call_target="tpu_custom_call" | custom-call | tf_op jit(solution)/shard_map/join_levels/pallas_call | solution.py:331
  (7 shorter events, 0.0 us)
Async XLA Ops:
  0.0 1.4 %copy-start.9 = (bf16[27,128,32]{1,2,0:T(8,128)(2,1)S(1)}, bf16[27,128,32]{1,2,0:T(8,128)(2,1)}, u32[]{:S(2)}) copy-start(bf16[27,128,32]{1,2,0:T(8,128)(2,1)} %param.13) | copy-start | bytes 663556
  1.9 0.7 copy-start.4
  1.9 0.7 copy-start.5
  1.9 0.7 copy-start.6
  3.6 38.5 %copy-start = (bf16[4,4,32,512]{3,2,1,0:T(8,128)(2,1)S(1)}, bf16[4,4,32,512]{3,2,1,0:T(8,128)(2,1)}, u32[]{:S(2)}) copy-start(bf16[4,4,32,512]{3,2,1,0:T(8,128)(2,1)} %features.1) | copy-start | bytes 1572868
  3.6 28.0 %collective-permute-start.9 = (bf16[28,32,128]{2,1,0:T(8,128)(2,1)S(1)}, bf16[28,32,128]{2,1,0:T(8,128)(2,1)S(1)}, u32[]{:S(2)}, u32[]{:S(2)}) collective-permute-start(bf16[28,32,128]{2,1,0:T(8,128)(2,1)S(1)} %get-tuple-element.32), channel_id=1, source_target_pairs={{0,2},{1,3},{2,0},{3,1},{4,6},{5,7},{6,4},{7,5},{8,10},{9,11},{10,... | collective-permute-start | bytes 688136 | tf_op jit(solution)/shard_map/ppermute | solution.py:341
  7.2 34.8 %collective-permute-start.8 = (bf16[2,28,32,128]{3,2,1,0:T(8,128)(2,1)S(1)}, bf16[2,28,32,128]{3,2,1,0:T(8,128)(2,1)S(1)}, u32[]{:S(2)}, u32[]{:S(2)}) collective-permute-start(bf16[2,28,32,128]{3,2,1,0:T(8,128)(2,1)S(1)} %get-tuple-element.31.refs_8_), channel_id=1, source_target_pairs={{0,1},{1,0},{2,3},{3,2},{4,5},{5,4},{6,7},{7,6},{8,9},{9,8},{10,11... | collective-permute-start | bytes 1376264 | tf_op jit(solution)/shard_map/ppermute | solution.py:341
  10.1 25.0 %copy-start.15 = (bf16[4,32,512]{2,1,0:T(8,128)(2,1)S(1)}, bf16[4,32,512]{2,1,0:T(8,128)(2,1)}, u32[]{:S(2)}) copy-start(bf16[4,32,512]{2,1,0:T(8,128)(2,1)} %get-tuple-element.23) | copy-start | bytes 393220
  10.1 9.6 %collective-permute-start.3 = (bf16[272,128]{1,0:T(8,128)(2,1)}, bf16[272,128]{1,0:T(8,128)(2,1)S(1)}, u32[]{:S(2)}, u32[]{:S(2)}) collective-permute-start(bf16[272,128]{1,0:T(8,128)(2,1)} %get-tuple-element.24), channel_id=1, source_target_pairs={{0,4},{4,8},{8,12},{12,16},{16,20},{20,24},{24,28},{28,32},{32,36}... | collective-permute-start | bytes 208904 | tf_op jit(solution)/shard_map/ppermute | solution.py:352
  11.7 7.9 %collective-permute-start.4 = (bf16[272,128]{1,0:T(8,128)(2,1)}, bf16[272,128]{1,0:T(8,128)(2,1)S(1)}, u32[]{:S(2)}, u32[]{:S(2)}) collective-permute-start(bf16[272,128]{1,0:T(8,128)(2,1)} %get-tuple-element.25), channel_id=1, source_target_pairs={{0,124},{4,0},{8,4},{12,8},{16,12},{20,16},{24,20},{28,24},{32,28}... | collective-permute-start | bytes 208904 | tf_op jit(solution)/shard_map/ppermute | solution.py:352
  16.4 17.5 %collective-permute-start = (bf16[4,32,512]{2,1,0:T(8,128)(2,1)}, bf16[4,32,512]{2,1,0:T(8,128)(2,1)S(1)}, u32[]{:S(2)}, u32[]{:S(2)}) collective-permute-start(bf16[4,32,512]{2,1,0:T(8,128)(2,1)} %get-tuple-element.21), channel_id=1, source_target_pairs={{0,1},{1,0},{2,3},{3,2},{4,5},{5,4},{6,7},{7,6},{8,9},{9,8},{10,11... | collective-permute-start | bytes 393224 | tf_op jit(solution)/shard_map/ppermute | solution.py:341
  19.7 0.6 copy-start.13
  20.3 0.6 copy-start.14
  22.5 3.6 %collective-permute-start.5 = (bf16[128,128]{1,0:T(8,128)(2,1)}, bf16[128,128]{1,0:T(8,128)(2,1)S(1)}, u32[]{:S(2)}, u32[]{:S(2)}) collective-permute-start(bf16[128,128]{1,0:T(8,128)(2,1)} %get-tuple-element.27), channel_id=1, source_target_pairs={{0,1},{1,0},{2,3},{3,2},{4,5},{5,4},{6,7},{7,6},{8,9},{9,8},{10,11... | collective-permute-start | bytes 98312 | tf_op jit(solution)/shard_map/ppermute | solution.py:341
  24.4 4.5 %collective-permute-start.6 = (bf16[128,128]{1,0:T(8,128)(2,1)}, bf16[128,128]{1,0:T(8,128)(2,1)S(1)}, u32[]{:S(2)}, u32[]{:S(2)}) collective-permute-start(bf16[128,128]{1,0:T(8,128)(2,1)} %get-tuple-element.28), channel_id=1, source_target_pairs={{0,2},{1,3},{2,0},{3,1},{4,6},{5,7},{6,4},{7,5},{8,10},{9,11},{10,... | collective-permute-start | bytes 98312 | tf_op jit(solution)/shard_map/ppermute | solution.py:341
  26.1 9.0 %collective-permute-start.1 = (bf16[4,32,512]{2,1,0:T(8,128)(2,1)}, bf16[4,32,512]{2,1,0:T(8,128)(2,1)S(1)}, u32[]{:S(2)}, u32[]{:S(2)}) collective-permute-start(bf16[4,32,512]{2,1,0:T(8,128)(2,1)} %get-tuple-element.22), channel_id=1, source_target_pairs={{0,2},{1,3},{2,0},{3,1},{4,6},{5,7},{6,4},{7,5},{8,10},{9,11},{10,... | collective-permute-start | bytes 393224 | tf_op jit(solution)/shard_map/ppermute | solution.py:341
  28.8 5.1 %collective-permute-start.7 = (bf16[128,128]{1,0:T(8,128)(2,1)}, bf16[128,128]{1,0:T(8,128)(2,1)S(1)}, u32[]{:S(2)}, u32[]{:S(2)}) collective-permute-start(bf16[128,128]{1,0:T(8,128)(2,1)} %get-tuple-element.29), channel_id=1, source_target_pairs={{0,3},{1,2},{2,1},{3,0},{4,7},{5,6},{6,5},{7,4},{8,11},{9,10},{10,... | collective-permute-start | bytes 98312 | tf_op jit(solution)/shard_map/ppermute | solution.py:341
  31.6 10.2 %collective-permute-start.12 = (bf16[28,32,128]{2,1,0:T(8,128)(2,1)S(1)}, bf16[28,32,128]{2,1,0:T(8,128)(2,1)S(1)}, u32[]{:S(2)}, u32[]{:S(2)}) collective-permute-start(bf16[28,32,128]{2,1,0:T(8,128)(2,1)S(1)} %collective-permute-done.9.refs_10_), channel_id=1, source_target_pairs={{0,5},{1,4},{2,7},{3,6},{4,1},{5,0},{6,3},{7,2},{8,13},{9,12},{10,... | collective-permute-start | bytes 688136 | tf_op jit(solution)/shard_map/ppermute | solution.py:347
  33.9 8.1 %collective-permute-start.11 = (bf16[28,32,128]{2,1,0:T(8,128)(2,1)S(1)}, bf16[28,32,128]{2,1,0:T(8,128)(2,1)S(1)}, u32[]{:S(2)}, u32[]{:S(2)}) collective-permute-start(bf16[28,32,128]{2,1,0:T(8,128)(2,1)S(1)} %collective-permute-done.9.refs_10_), channel_id=1, source_target_pairs={{0,4},{1,5},{2,6},{3,7},{4,0},{5,1},{6,2},{7,3},{8,12},{9,13},{10,... | collective-permute-start | bytes 688136 | tf_op jit(solution)/shard_map/ppermute | solution.py:347
  33.9 8.1 %collective-permute-start.10 = (bf16[28,32,128]{2,1,0:T(8,128)(2,1)S(1)}, bf16[28,32,128]{2,1,0:T(8,128)(2,1)S(1)}, u32[]{:S(2)}, u32[]{:S(2)}) collective-permute-start(bf16[28,32,128]{2,1,0:T(8,128)(2,1)S(1)} %collective-permute-done.9.refs_10_), channel_id=1, source_target_pairs={{0,1},{1,0},{2,3},{3,2},{4,5},{5,4},{6,7},{7,6},{8,9},{9,8},{10,11... | collective-permute-start | bytes 688136 | tf_op jit(solution)/shard_map/ppermute | solution.py:341
  35.1 7.0 %copy-start.3 = (s32[4,27]{1,0:T(4,128)S(1)}, s32[4,27]{1,0:T(4,128)}, u32[]{:S(2)}) copy-start(s32[4,27]{1,0:T(4,128)} %tab.1) | copy-start | bytes 1300
  35.1 6.7 %collective-permute-start.2 = (bf16[4,32,512]{2,1,0:T(8,128)(2,1)S(1)}, bf16[4,32,512]{2,1,0:T(8,128)(2,1)S(1)}, u32[]{:S(2)}, u32[]{:S(2)}) collective-permute-start(bf16[4,32,512]{2,1,0:T(8,128)(2,1)S(1)} %copy-done.15), channel_id=1, source_target_pairs={{0,3},{1,2},{2,1},{3,0},{4,7},{5,6},{6,5},{7,4},{8,11},{9,10},{10,... | collective-permute-start | bytes 393224 | tf_op jit(solution)/shard_map/ppermute | solution.py:341
  42.0 0.7 copy-start.2
  42.7 0.8 %copy-start.7 = (bf16[128,128]{1,0:T(8,128)(2,1)S(1)}, bf16[128,128]{1,0:T(8,128)(2,1)}, u32[]{:S(2)}) copy-start(bf16[128,128]{1,0:T(8,128)(2,1)} %get-tuple-element.26.refs_3_) | copy-start | bytes 98308
  43.5 0.7 %copy-start.8 = (s32[32,128]{1,0:T(8,128)S(1)}, s32[32,128]{1,0:T(8,128)}, u32[]{:S(2)}) copy-start(s32[32,128]{1,0:T(8,128)} %get-tuple-element.30.refs_7_) | copy-start | bytes 49156
  54.6 0.6 copy-start.1
  55.2 4.9 %collective-permute-start.13 = (bf16[4,32,512]{2,1,0:T(8,128)(2,1)S(1)}, bf16[4,32,512]{2,1,0:T(8,128)(2,1)S(1)}, u32[]{:S(2)}, u32[]{:S(2)}) collective-permute-start(bf16[4,32,512]{2,1,0:T(8,128)(2,1)S(1)} %get-tuple-element.34), channel_id=1, source_target_pairs={{0,1},{1,0},{2,3},{3,2},{4,5},{5,4},{6,7},{7,6},{8,9},{9,8},{10,11... | collective-permute-start | bytes 393224 | tf_op jit(solution)/shard_map/ppermute | solution.py:341
  57.0 6.6 %collective-permute-start.14 = (bf16[4,32,512]{2,1,0:T(8,128)(2,1)S(1)}, bf16[4,32,512]{2,1,0:T(8,128)(2,1)S(1)}, u32[]{:S(2)}, u32[]{:S(2)}) collective-permute-start(bf16[4,32,512]{2,1,0:T(8,128)(2,1)S(1)} %get-tuple-element.35), channel_id=1, source_target_pairs={{0,2},{1,3},{2,0},{3,1},{4,6},{5,7},{6,4},{7,5},{8,10},{9,11},{10,... | collective-permute-start | bytes 393224 | tf_op jit(solution)/shard_map/ppermute | solution.py:341
  58.2 8.3 %collective-permute-start.15 = (bf16[4,32,512]{2,1,0:T(8,128)(2,1)S(1)}, bf16[4,32,512]{2,1,0:T(8,128)(2,1)S(1)}, u32[]{:S(2)}, u32[]{:S(2)}) collective-permute-start(bf16[4,32,512]{2,1,0:T(8,128)(2,1)S(1)} %get-tuple-element.36), channel_id=1, source_target_pairs={{0,3},{1,2},{2,1},{3,0},{4,7},{5,6},{6,5},{7,4},{8,11},{9,10},{10,... | collective-permute-start | bytes 393224 | tf_op jit(solution)/shard_map/ppermute | solution.py:341
  60.1 6.4 %copy-start.10 = (bf16[4,32,512]{2,1,0:T(8,128)(2,1)}, bf16[4,32,512]{2,1,0:T(8,128)(2,1)S(1)}, u32[]{:S(2)}) copy-start(bf16[4,32,512]{2,1,0:T(8,128)(2,1)S(1)} %collective-permute-done.13.refs_1_) | copy-start | bytes 393220
  63.6 2.9 %copy-start.11 = (bf16[4,32,512]{2,1,0:T(8,128)(2,1)}, bf16[4,32,512]{2,1,0:T(8,128)(2,1)S(1)}, u32[]{:S(2)}) copy-start(bf16[4,32,512]{2,1,0:T(8,128)(2,1)S(1)} %collective-permute-done.14.refs_2_) | copy-start | bytes 393220
  66.5 0.7 copy-start.12

commit v3 on v2

v3 whole, which is shorter than its diff:
```python
import jax
import jax.numpy as jnp
from jax import lax
from jax.experimental import pallas as pl
from jax.experimental.pallas import tpu as pltpu
from jax.sharding import PartitionSpec as P

BF16, F32 = jnp.bfloat16, jnp.float32
NONE = 8
HBM = pl.BlockSpec(memory_space=pl.ANY)
VMEM = pl.BlockSpec(memory_space=pltpu.VMEM)
SMEM = pl.BlockSpec(memory_space=pltpu.SMEM)
SPAN = {-1: (7, 0, 1), 0: (0, 1, 8), 1: (0, 9, 1)}


def offset(dz, dy, dx):
    return 9 * (dz + 1) + 3 * (dy + 1) + (dx + 1)


PIECE = 17


def split_kernel(feat, w1, w2, b1, b2, lev, *refs):
    pieces, cross, held, sem = refs[:4], refs[4], refs[5], refs[6]
    me = lax.axis_index("chan")
    odd = lax.axis_index("slab") % 2

    @pl.when(odd == 0)
    def _():
        pltpu.make_async_copy(w1, cross, sem.at[0]).start()

    @pl.when(odd == 1)
    def _():
        pltpu.make_async_copy(w2, cross, sem.at[0]).start()

    small = [
        pltpu.make_async_copy(b1, held.at[pl.ds(0, 1)], sem.at[1]),
        pltpu.make_async_copy(b2, held.at[pl.ds(1, 1)], sem.at[2]),
        pltpu.make_async_copy(lev, held.at[pl.ds(2, 4)], sem.at[3]),
    ]
    large = [
        pltpu.make_async_copy(w, pieces[1].at[pl.ds(PIECE + 27 * layer, 27)], sem.at[4 + layer])
        for layer, w in enumerate((w1, w2))
    ]
    for m in range(4):
        for v in range(4):
            run = feat.at[me ^ m, :, :, pl.ds(128 * v, 128)]
            large.append(
                pltpu.make_async_copy(run, pieces[m].at[pl.ds(4 * v, 4)], sem.at[6 + 4 * m + v])
            )
    held[pl.ds(6, 2), :] = jnp.zeros((2, 32), F32)
    for copy in small + large:
        copy.start()
    for copy in small:
        copy.wait()

    values = jnp.concatenate([held[...]] * 4, axis=1)
    lane = lax.broadcasted_iota(jnp.int32, (8, 128), 1)
    values = jnp.where(lane // 32 == me, values, 0.0)
    high = values.astype(BF16).astype(F32)
    values = jnp.concatenate([high, values - high, jnp.zeros((16, 128), F32)], axis=0).astype(BF16)
    for m in range(4):
        pieces[m][16] = values
    pltpu.make_async_copy(w1, cross, sem.at[0]).wait()
    for copy in large:
        copy.wait()


def split(features, w1, w2, b1, b2, lev):
    piece = jax.ShapeDtypeStruct((PIECE, 32, 128), BF16)
    loaded = jax.ShapeDtypeStruct((PIECE + 54, 32, 128), BF16)
    return pl.pallas_call(
        split_kernel,
        out_shape=[piece, loaded, piece, piece, jax.ShapeDtypeStruct((27, 32, 128), BF16)],
        in_specs=[pl.BlockSpec(memory_space=pltpu.HBM)] * 6,
        out_specs=[VMEM] * 5,
        scratch_shapes=[pltpu.VMEM((8, 32), F32), pltpu.SemaphoreType.DMA((22,))],
        compiler_params=pltpu.CompilerParams(vmem_limit_bytes=60 << 20),
        name="split_features",
    )(features, w1, w2, b1.reshape(1, 32), b2.reshape(1, 32), lev)


def faces_kernel(near, lists_block, lists, *refs):
    pieces, sides, sem = refs[:4], refs[4:6], refs[6]
    copies = []
    for tier, run, out in ((1, 3, sides[0]), (0, 0, sides[1])):
        for c in range(2):
            b = jnp.maximum(lists[0, tier, c], 0)
            for m in range(4):
                i = 8 * tier + 4 * c + m
                copies.append(pltpu.make_async_copy(pieces[m].at[4 * run + b], out.at[4 * c + m], sem.at[i]))
    for copy in copies:
        copy.start()
    for out in sides:
        out[8] = jnp.zeros((32, 128), BF16)
        out[8, pl.ds(0, 4), pl.ds(0, 27)] = near[...].astype(F32).astype(BF16)
        out[8, pl.ds(8, 2), pl.ds(0, 2)] = lists_block[0].astype(F32).astype(BF16)
    for copy in copies:
        copy.wait()


def faces(neighbours, face_lists, pieces):
    side = jax.ShapeDtypeStruct((9, 32, 128), BF16)
    return pl.pallas_call(
        faces_kernel,
        out_shape=[side] * 2,
        in_specs=[VMEM, VMEM, SMEM] + [HBM] * 4,
        out_specs=[VMEM] * 2,
        scratch_shapes=[pltpu.SemaphoreType.DMA((16,))],
        compiler_params=pltpu.CompilerParams(vmem_limit_bytes=4 << 20),
        name="pick_faces",
    )(neighbours, face_lists, face_lists, *pieces)


def silu(v):
    return v / (1.0 + jnp.exp(-v))


def gather_padded(slots, pad, lead, slot, planes):
    x = lax.broadcasted_iota(jnp.int32, (1, 8, 128), 1)
    for dz, z_from, z_to in planes:
        for dy in (-1, 0, 1):
            y_from, y_to, n = SPAN[dy]
            parts = ([], [], [])
            for w in range(2):
                mid, left, right = (
                    slots[slot(w, offset(dz, dy, dx)), z_from, y_from : y_from + n] for dx in (0, -1, 1)
                )
                parts[0].append(pltpu.roll(jnp.where(x == 7, left, mid), 1, 1))
                parts[1].append(mid)
                parts[2].append(pltpu.roll(jnp.where(x == 0, right, mid), 7, 1))
            for d in range(3):
                tile = jnp.concatenate(parts[d], axis=1).astype(BF16)
                pad[lead, z_to, y_to : y_to + n, :, 128 * d : 128 * d + 128] = tile


OWN_PLANES = [(-1, 7, 0)] + [(0, z, z + 1) for z in range(8)] + [(1, 0, 9)]


def conv_pair(pad, lead, w):
    zero = jnp.zeros((128, 128), BF16)
    total = None
    blocks = [(zin, dy) for zin in range(4) for dy in range(3)]
    for first in range(0, 12, 2):
        left, right = [], []
        for zin, dy in blocks[first : first + 2]:
            planes = [pad[lead, zin + 2 * j, dy : dy + 8].reshape(128, 384) for j in range(4)]
            left.append(jnp.concatenate(planes, axis=0))
            for dx in range(3):
                even = w[9 * zin + 3 * dy + dx] if zin < 3 else zero
                odd = w[9 * (zin - 1) + 3 * dy + dx] if zin > 0 else zero
                right.append(jnp.concatenate([even, odd], axis=1))
        part = jnp.dot(
            jnp.concatenate(left, axis=1), jnp.concatenate(right, axis=0), preferred_element_type=F32
        )
        total = part if total is None else total + part
    return total


def conv_face(pad, w):
    total = None
    blocks = [(dz, dy) for dz in range(3) for dy in range(3)]
    for group in (blocks[0:2], blocks[2:4], blocks[4:6], blocks[6:9]):
        left, right = [], []
        for dz, dy in group:
            sides = [pad[side, dz, dy : dy + 8].reshape(128, 384) for side in range(2)]
            left.append(jnp.concatenate(sides, axis=0))
            right += [w[9 * dz + 3 * dy + dx] for dx in range(3)]
        part = jnp.dot(
            jnp.concatenate(left, axis=1), jnp.concatenate(right, axis=0), preferred_element_type=F32
        )
        total = part if total is None else total + part
    return total


def conv_kernel(tab, fl, *refs):
    feat, sides, own_w, far_w = refs[0:4], refs[4:6], refs[6:8], refs[8:12]
    outs = refs[12:16]
    fs, hs, w1, w2, bias, sent, sent_int, tables, slots, pad, pad_face, acc, shift, turned, sem = refs[16:]
    me = lax.axis_index("chan")
    odd = lax.axis_index("slab") % 2

    f_copies, t_copies = [], []
    for side in range(2):
        t_copies.append(
            pltpu.make_async_copy(sides[side].at[8, pl.ds(0, 16)], sent.at[side], sem.at[side])
        )
        f_copies.append(pltpu.make_async_copy(sides[side].at[pl.ds(0, 8)], hs.at[side], sem.at[2 + side]))
    for m in range(4):
        f_copies.append(pltpu.make_async_copy(feat[m].at[pl.ds(0, 16)], fs.at[m], sem.at[4 + m]))
        f_copies.append(pltpu.make_async_copy(feat[m].at[16, pl.ds(0, 16)], bias.at[m], sem.at[8 + m]))
    for copy in t_copies + f_copies:
        copy.start()

    def load_shard(m, layer, source):
        g = 32 * m if layer == 0 else pl.multiple_of((me ^ m) * 32, 32)
        return pltpu.make_async_copy(source, (w1, w2)[layer].at[:, pl.ds(g, 32), :], sem.at[12 + 2 * m + layer])

    w_copies = ([], [])
    for layer in range(2):
        near = [load_shard(0, layer, own_w[layer])]
        near.append(load_shard(1, layer, feat[1].at[pl.ds(PIECE + 27 * layer, 27)]))
        for copy in near:
            copy.start()
        w_copies[layer].extend(near)
        for m in (2, 3):
            mine, other = far_w[m - 2], far_w[m]

            @pl.when(odd == layer)
            def _():
                load_shard(m, layer, mine).start()

            @pl.when(odd != layer)
            def _():
                load_shard(m, layer, other).start()

            w_copies[layer].append(load_shard(m, layer, mine))
    w1_copies, w2_copies = w_copies
    for copy in t_copies:
        copy.wait()
    sent_int[...] = sent[...].astype(F32).astype(jnp.int32).reshape(32, 128)
    to_scalars = pltpu.make_async_copy(sent_int, tables, sem.at[24])
    to_scalars.start()
    for copy in f_copies:
        copy.wait()

    slots[NONE] = jnp.zeros((8, 8, 8, 128), F32)
    for b in range(4):
        for v in range(4):
            brick = jnp.concatenate([fs[m, 4 * v + b] for m in range(4)], axis=0)
            slots[b, 2 * v : 2 * v + 2] = brick.T.astype(F32).reshape(2, 8, 8, 128)
    for side in range(2):
        for c in range(2):
            face = jnp.concatenate([hs[side, 4 * c + m] for m in range(4)], axis=0)
            first = 6 if side == 0 else 0
            slots[4 + 2 * side + c, first : first + 2] = face.T.astype(F32).reshape(2, 8, 8, 128)

    to_scalars.wait()

    def own(pair):
        def slot(w, k):
            t = tab[2 * pair + w, k]
            return jnp.where(t < 0, NONE, t)

        return slot

    def below(c, k):
        t = tables[0 + jnp.maximum(tables[9, c], 0), k]
        if k < 18:
            found = jnp.where(t == tables[9, 0], 4, jnp.where(t == tables[9, 1], 5, NONE))
            return jnp.where(t < 0, NONE, found)
        u = fl[0, 0, jnp.clip(t - 6, 0, 1)]
        return jnp.where((t < 6) | (u < 0), NONE, u)

    def above(c, k):
        t = tables[16 + jnp.maximum(tables[24, c], 0), k]
        if k >= 9:
            found = jnp.where(t == tables[24, 0], 6, jnp.where(t == tables[24, 1], 7, NONE))
            return jnp.where(t < 0, NONE, found)
        u = fl[0, 1, jnp.clip(t - 4, 0, 1)]
        return jnp.where((t < 4) | (t > 5) | (u < 0), NONE, u)

    gather_padded(slots, pad_face, 0, below, [(0, 6, 0), (0, 7, 1), (1, 0, 2)])
    gather_padded(slots, pad_face, 1, above, [(-1, 7, 0), (0, 0, 1), (0, 1, 2)])
    for pair in range(2):
        gather_padded(slots, pad, pair, own(pair), OWN_PLANES)

    for copy in w1_copies:
        copy.wait()
    values = sum(bias[m].astype(F32) for m in range(4))
    shift[...] = values[0:8] + values[8:16]
    shift_second = shift[1:2, :]
    shift_first = shift[0:1, :] + shift[pl.ds(2 + me, 1), :]

    def finish(pair, moved):
        for j in range(4):
            for zo in range(2):
                tile = silu(acc[128 * j : 128 * j + 128, 128 * zo : 128 * zo + 128] + moved)
                tile = tile.reshape(8, 2, 8, 128)
                for w in range(2):
                    b = 2 * pair + w
                    slots[b, 2 * j + zo] = jnp.where(tab[b, 13] >= 0, tile[:, w], 0.0)

    for pair in range(2):
        acc[...] = conv_pair(pad, pair, w1)
        finish(pair, shift_first)
    faces = silu(conv_face(pad_face, w1) + shift_first).reshape(2, 8, 2, 8, 128)
    for c in range(2):
        slots[4 + c, 7] = faces[0, :, c]
        slots[6 + c, 0] = faces[1, :, c]

    for pair in range(2):
        gather_padded(slots, pad, pair, own(pair), OWN_PLANES)
    for copy in w2_copies:
        copy.wait()
    for pair in range(2):
        acc[...] = conv_pair(pad, pair, w2)
        finish(pair, shift_second)
    for b in range(4):
        brick = slots[b].reshape(512, 128).astype(BF16).T
        for g in range(4):
            turned[g, b] = brick[32 * g : 32 * g + 32]
    out_copies = [
        pltpu.make_async_copy(turned.at[me ^ m], outs[m], sem.at[20 + m]) for m in range(4)
    ]
    for copy in out_copies:
        copy.start()
    for copy in out_copies:
        copy.wait()


def convolve(neighbours, face_lists, feat, sides, own_w, far_w):
    piece = jax.ShapeDtypeStruct((4, 32, 512), BF16)
    return pl.pallas_call(
        conv_kernel,
        out_shape=[piece] * 4,
        in_specs=[SMEM] * 2 + [HBM] * 12,
        out_specs=[HBM] * 4,
        scratch_shapes=[
            pltpu.VMEM((4, 16, 32, 128), BF16),
            pltpu.VMEM((2, 8, 32, 128), BF16),
            pltpu.VMEM((27, 128, 128), BF16),
            pltpu.VMEM((27, 128, 128), BF16),
            pltpu.VMEM((4, 16, 128), BF16),
            pltpu.VMEM((2, 16, 128), BF16),
            pltpu.VMEM((32, 128), jnp.int32),
            pltpu.SMEM((32, 128), jnp.int32),
            pltpu.VMEM((9, 8, 8, 8, 128), F32),
            pltpu.VMEM((2, 10, 10, 16, 384), BF16),
            pltpu.VMEM((2, 3, 10, 16, 384), BF16),
            pltpu.VMEM((512, 256), F32),
            pltpu.VMEM((8, 128), F32),
            pltpu.VMEM((4, 4, 32, 512), BF16),
            pltpu.SemaphoreType.DMA((32,)),
        ],
        compiler_params=pltpu.CompilerParams(vmem_limit_bytes=40 << 20),
        cost_estimate=pl.CostEstimate(flops=8 * 10**9, bytes_accessed=4 * 10**6, transcendentals=10**6),
        name="convolve",
    )(neighbours, face_lists, *feat, *sides, *own_w, *far_w)


def join_kernel(*refs):
    pieces, out, sem = refs[:4], refs[4], refs[5]
    me = lax.axis_index("chan")
    copies = [pltpu.make_async_copy(pieces[m], out.at[me ^ m], sem.at[m]) for m in range(4)]
    for copy in copies:
        copy.start()
    for copy in copies:
        copy.wait()


def join(pieces):
    return pl.pallas_call(
        join_kernel,
        out_shape=jax.ShapeDtypeStruct((4, 4, 32, 512), BF16),
        in_specs=[HBM] * 4,
        out_specs=HBM,
        scratch_shapes=[pltpu.SemaphoreType.DMA((4,))],
        compiler_params=pltpu.CompilerParams(vmem_limit_bytes=8 << 20),
        name="join_levels",
    )(*pieces)


def swap(value, m):
    return lax.ppermute(value, "chan", [(i, i ^ m) for i in range(4)])


def swap_slabs(value, m):
    count = lax.axis_size("slab")
    pairs = [(4 * s + g, 4 * (s ^ 1) + (g ^ m)) for s in range(count) for g in range(4)]
    return lax.ppermute(value, ("slab", "chan"), pairs)


def to_slab(value, steps):
    count = lax.axis_size("slab")
    return lax.ppermute(value, "slab", [(s, (s + steps) % count) for s in range(count)])


def shards(features, neighbours, face_lists, w_first, b_first, w_second, b_second, level_embed):
    w1, w2 = w_first.transpose(0, 2, 1), w_second.transpose(0, 2, 1)
    own, one, two, three, cross = split(features, w1, w2, b_first, b_second, level_embed)
    fetched, two, three = lax.optimization_barrier((swap(cross, 2), swap(two, 2), swap(three, 3)))
    pieces = [own, swap(one, 1), two, three]
    up, down = faces(neighbours, face_lists, pieces)
    sides = [to_slab(up, 1), to_slab(down, -1)]
    far = [fetched, swap(fetched, 1), swap_slabs(fetched, 0), swap_slabs(fetched, 1)]
    outs = convolve(neighbours, face_lists, pieces, sides, (w1, w2), far)
    return join([outs[0]] + [swap(outs[m], m) for m in (1, 2, 3)])


def solution(mesh):
    placed = (
        P(None, "slab", "chan", None),
        P("slab", None),
        P("slab", None, None),
        P(None, None, "chan"),
        P("chan"),
        P(None, None, "chan"),
        P("chan"),
        P(None, "chan"),
    )
    return jax.shard_map(
        shards, mesh=mesh, in_specs=placed, out_specs=P(None, "slab", "chan", None), check_vma=False
    )
```

time: 69.5 us -> 55.2 us (0.79)
  the two profiles are of different devices: /device:TPU:1 before, /device:TPU:25 now
where the time goes in v3:
time: 55.2 us; the launch traced here: 54.2 us
  waiting for transfers between devices  19.7 us (36%)
  starting transfers between devices  18.2 us (33%)
  Pallas kernels  15.3 us (28%)
  local copies, waits for them, and re-layouts  0.92 us (2%)
    ppermute x8, waiting for transfers between devices, swap(): return lax.ppermute(value, 'chan', [(i, i ^ m) for i in range(4)])  15.1 us
    ppermute x8, starting transfers between devices, swap(): return lax.ppermute(value, 'chan', [(i, i ^ m) for i in range(4)])  11.5 us
    pallas_call x1, Pallas kernels, convolve(): pl.pallas_call(conv_kernel, out_shape=[piece] * 4, in_specs=[SMEM] * 2 +...  11.1 us
    ppermute x2, starting transfers between devices, to_slab(): lax.ppermute(value, 'slab', [(s, (s + steps) % count) for s in range(coun...  4.99 us
    ppermute x2, waiting for transfers between devices, swap_slabs(): return lax.ppermute(value, ('slab', 'chan'), pairs)  3.05 us
    pallas_call x1, Pallas kernels, split(): pl.pallas_call(split_kernel, out_shape=[piece, loaded, piece, piece, jax....  2.5 us
    ppermute x2, starting transfers between devices, swap_slabs(): return lax.ppermute(value, ('slab', 'chan'), pairs)  1.74 us
    ppermute x2, waiting for transfers between devices, to_slab(): lax.ppermute(value, 'slab', [(s, (s + steps) % count) for s in range(coun...  1.58 us
  transfers between devices with their start and end apart: 12, of which 7 were waited for; matrix products, arithmetic and copies ran while one was open for 0% of the time, Pallas kernels for 2%

profile of v3, /device:TPU:25, one launch (start us, length us, event | category | flops | bytes accessed | tf_op | source)
XLA Modules:
  0.0 54.2 jit_solution(7509989449912537249)
XLA Ops:
  0.0 2.5 %split_features.1 = (bf16[17,32,128]{2,1,0:T(8,128)(2,1)}, bf16[71,32,128]{2,1,0:T(8,128)(2,1)}, bf16[17,32,128]{2,1,0:T(8,128)(2,1)}, bf16[17,32,128]{2,1,0:T(8,128)(2,1)}, bf16[27,32,128]{2,1,0:T(8,128)(2,1)}) custom-call(bf16[4,4,32,512]{3,2,1,0:T(8,128)(2,1)} %feat.1, bf16[27,32,128]{2,1,0:T(8,128)(2,1)} %bitcast.4, bf16[27,32,128]{2,1,0:T(8,128)(2,1)} %bitcast.6, ...), custom_call_target="tpu_custom_call" | custom-call | tf_op jit(solution)/shard_map/split_features/pallas_call | solution.py:72
  2.5 0.8 %collective-permute-start = (bf16[71,32,128]{2,1,0:T(8,128)(2,1)}, bf16[71,32,128]{2,1,0:T(8,128)(2,1)S(1)}, u32[]{:S(2)}, u32[]{:S(2)}) collective-permute-start(bf16[71,32,128]{2,1,0:T(8,128)(2,1)} %get-tuple-element.20), channel_id=1, source_target_pairs={{0,1},{1,0},{2,3},{3,2},{4,5},{5,4},{6,7},{7,6},{8,9},{9,8},{10,11... | collective-permute-start | bytes 1744904 | tf_op jit(solution)/shard_map/ppermute | solution.py:365
  3.3 2.8 %collective-permute-start.1 = (bf16[27,32,128]{2,1,0:T(8,128)(2,1)}, bf16[27,32,128]{2,1,0:T(8,128)(2,1)S(1)}, u32[]{:S(2)}, u32[]{:S(2)}) collective-permute-start(bf16[27,32,128]{2,1,0:T(8,128)(2,1)} %get-tuple-element.21), channel_id=1, source_target_pairs={{0,2},{1,3},{2,0},{3,1},{4,6},{5,7},{6,4},{7,5},{8,10},{9,11},{10,... | collective-permute-start | bytes 663560 | tf_op jit(solution)/shard_map/ppermute | solution.py:365
  6.0 0.0 copy-start.5
  6.0 0.2 collective-permute-start.2
  6.3 0.0 copy-start.4
  6.3 3.3 %collective-permute-start.3 = (bf16[17,32,128]{2,1,0:T(8,128)(2,1)}, bf16[17,32,128]{2,1,0:T(8,128)(2,1)S(1)}, u32[]{:S(2)}, u32[]{:S(2)}) collective-permute-start(bf16[17,32,128]{2,1,0:T(8,128)(2,1)} %get-tuple-element.23), channel_id=1, source_target_pairs={{0,3},{1,2},{2,1},{3,0},{4,7},{5,6},{6,5},{7,4},{8,11},{9,10},{10,... | collective-permute-start | bytes 417800 | tf_op jit(solution)/shard_map/ppermute | solution.py:365
  9.5 5.4 %collective-permute-done.2.refs_2_ = bf16[17,32,128]{2,1,0:T(8,128)(2,1)S(1)} collective-permute-done((bf16[17,32,128]{2,1,0:T(8,128)(2,1)}, bf16[17,32,128]{2,1,0:T(8,128)(2,1)S(1)}, u32[]{:S(2)}, u32[]{:S(2)}) %collective-permute-start.2) | collective-permute-done | bytes 139296 | tf_op jit(solution)/shard_map/ppermute | solution.py:365
  14.9 3.2 %collective-permute-done.3.refs_3_ = bf16[17,32,128]{2,1,0:T(8,128)(2,1)S(1)} collective-permute-done((bf16[17,32,128]{2,1,0:T(8,128)(2,1)}, bf16[17,32,128]{2,1,0:T(8,128)(2,1)S(1)}, u32[]{:S(2)}, u32[]{:S(2)}) %collective-permute-start.3) | collective-permute-done | bytes 139296 | tf_op jit(solution)/shard_map/ppermute | solution.py:365
  18.1 0.0 collective-permute-done.1.refs_8_
  18.1 1.7 %collective-permute-start.8 = (bf16[27,32,128]{2,1,0:T(8,128)(2,1)S(1)}, bf16[27,32,128]{2,1,0:T(8,128)(2,1)S(1)}, u32[]{:S(2)}, u32[]{:S(2)}) collective-permute-start(bf16[27,32,128]{2,1,0:T(8,128)(2,1)S(1)} %collective-permute-done.1.refs_8_), channel_id=1, source_target_pairs={{0,5},{1,4},{2,7},{3,6},{4,1},{5,0},{6,3},{7,2},{8,13},{9,12},{10,... | collective-permute-start | bytes 663560 | tf_op jit(solution)/shard_map/ppermute | solution.py:371
  19.9 0.0 collective-permute-start.7
  19.9 0.4 collective-permute-start.6
  20.3 0.0 collective-permute-done.refs_1_
  20.3 0.0 copy-done.5
  20.3 0.0 copy-done.4
  20.3 0.0 copy-start.2
  20.3 0.9 %copy-done.2 = bf16[17,32,128]{2,1,0:T(8,128)(2,1)S(1)} copy-done((bf16[17,32,128]{2,1,0:T(8,128)(2,1)S(1)}, bf16[17,32,128]{2,1,0:T(8,128)(2,1)}, u32[]{:S(2)}) %copy-start.2) | copy-done | bytes 139288
  21.2 0.0 copy-start
  21.2 0.0 copy-start.1
  21.2 0.0 copy-start.3
  21.2 0.9 %pick_faces.1 = (bf16[9,32,128]{2,1,0:T(8,128)(2,1)S(1)}, bf16[9,32,128]{2,1,0:T(8,128)(2,1)S(1)}) custom-call(s32[4,27]{1,0:T(4,128)S(1)} %copy-done.5, s32[1,2,2]{2,1,0:T(2,128)S(1)} %copy-done.4, s32[1,2,2]{2,1,0:T(2,128)S(1)} %copy-done.4, bf16[17,32,128]{2,1,0:T(8,128)(2,1)S(1)} %copy-done.2, bf16[71,32,128]{2,1,0:T(8,128)(2,1)S(1)} %collective-permute-done.refs_1_, ...), custom_call_target="tpu_custom_call" | custom-call | tf_op jit(solution)/shard_map/pick_faces/pallas_call | solution.py:104
  22.1 1.7 %collective-permute-start.4 = (bf16[9,32,128]{2,1,0:T(8,128)(2,1)S(1)}, bf16[9,32,128]{2,1,0:T(8,128)(2,1)S(1)}, u32[]{:S(2)}, u32[]{:S(2)}) collective-permute-start(bf16[9,32,128]{2,1,0:T(8,128)(2,1)S(1)} %get-tuple-element.26), channel_id=1, source_target_pairs={{0,4},{4,8},{8,12},{12,16},{16,20},{20,24},{24,28},{28,32},{32,36}... | collective-permute-start | bytes 221192 | tf_op jit(solution)/shard_map/ppermute | solution.py:376
  23.8 3.3 %collective-permute-start.5 = (bf16[9,32,128]{2,1,0:T(8,128)(2,1)S(1)}, bf16[9,32,128]{2,1,0:T(8,128)(2,1)S(1)}, u32[]{:S(2)}, u32[]{:S(2)}) collective-permute-start(bf16[9,32,128]{2,1,0:T(8,128)(2,1)S(1)} %get-tuple-element.27), channel_id=1, source_target_pairs={{0,124},{4,0},{8,4},{12,8},{16,12},{20,16},{24,20},{28,24},{32,28}... | collective-permute-start | bytes 221192 | tf_op jit(solution)/shard_map/ppermute | solution.py:376
  27.1 0.0 collective-permute-done.8.refs_11_
  27.1 3.0 %collective-permute-done.7.refs_10_ = bf16[27,32,128]{2,1,0:T(8,128)(2,1)S(1)} collective-permute-done((bf16[27,32,128]{2,1,0:T(8,128)(2,1)S(1)}, bf16[27,32,128]{2,1,0:T(8,128)(2,1)S(1)}, u32[]{:S(2)}, u32[]{:S(2)}) %collective-permute-start.7) | collective-permute-done | bytes 221216 | tf_op jit(solution)/shard_map/ppermute | solution.py:371
  30.2 0.0 collective-permute-done.6.refs_9_
  30.2 0.8 %collective-permute-done.4.refs_4_ = bf16[9,32,128]{2,1,0:T(8,128)(2,1)S(1)} collective-permute-done((bf16[9,32,128]{2,1,0:T(8,128)(2,1)S(1)}, bf16[9,32,128]{2,1,0:T(8,128)(2,1)S(1)}, u32[]{:S(2)}, u32[]{:S(2)}) %collective-permute-start.4) | collective-permute-done | bytes 73760 | tf_op jit(solution)/shard_map/ppermute | solution.py:376
  31.0 0.7 %collective-permute-done.5.refs_5_ = bf16[9,32,128]{2,1,0:T(8,128)(2,1)S(1)} collective-permute-done((bf16[9,32,128]{2,1,0:T(8,128)(2,1)S(1)}, bf16[9,32,128]{2,1,0:T(8,128)(2,1)S(1)}, u32[]{:S(2)}, u32[]{:S(2)}) %collective-permute-start.5) | collective-permute-done | bytes 73760 | tf_op jit(solution)/shard_map/ppermute | solution.py:376
  31.8 0.0 copy-done
  31.8 0.0 copy-done.1
  31.8 0.0 copy-done.3
  31.8 11.1 %convolve.1 = (bf16[4,32,512]{2,1,0:T(8,128)(2,1)S(1)}, bf16[4,32,512]{2,1,0:T(8,128)(2,1)S(1)}, bf16[4,32,512]{2,1,0:T(8,128)(2,1)S(1)}, bf16[4,32,512]{2,1,0:T(8,128)(2,1)S(1)}) custom-call(s32[4,27]{1,0:T(4,128)S(1)} %copy-done.5, s32[1,2,2]{2,1,0:T(2,128)S(1)} %copy-done.4, bf16[17,32,128]{2,1,0:T(8,128)(2,1)S(1)} %copy-done.3, ...), custom_call_target="tpu_custom_call" | custom-call | flops 8000000000 | bytes 4000000 | tf_op jit(solution)/shard_map/convolve/pallas_call | solution.py:314
  42.8 0.8 %collective-permute-start.9 = (bf16[4,32,512]{2,1,0:T(8,128)(2,1)S(1)}, bf16[4,32,512]{2,1,0:T(8,128)(2,1)S(1)}, u32[]{:S(2)}, u32[]{:S(2)}) collective-permute-start(bf16[4,32,512]{2,1,0:T(8,128)(2,1)S(1)} %get-tuple-element.30), channel_id=1, source_target_pairs={{0,1},{1,0},{2,3},{3,2},{4,5},{5,4},{6,7},{7,6},{8,9},{9,8},{10,11... | collective-permute-start | bytes 393224 | tf_op jit(solution)/shard_map/ppermute | solution.py:365
  43.6 2.8 %collective-permute-start.10 = (bf16[4,32,512]{2,1,0:T(8,128)(2,1)S(1)}, bf16[4,32,512]{2,1,0:T(8,128)(2,1)S(1)}, u32[]{:S(2)}, u32[]{:S(2)}) collective-permute-start(bf16[4,32,512]{2,1,0:T(8,128)(2,1)S(1)} %get-tuple-element.31), channel_id=1, source_target_pairs={{0,2},{1,3},{2,0},{3,1},{4,6},{5,7},{6,4},{7,5},{8,10},{9,11},{10,... | collective-permute-start | bytes 393224 | tf_op jit(solution)/shard_map/ppermute | solution.py:365
  46.4 0.5 collective-permute-start.11
  46.9 0.0 collective-permute-done.9.refs_1_
  46.9 3.3 %collective-permute-done.10.refs_2_ = bf16[4,32,512]{2,1,0:T(8,128)(2,1)S(1)} collective-permute-done((bf16[4,32,512]{2,1,0:T(8,128)(2,1)S(1)}, bf16[4,32,512]{2,1,0:T(8,128)(2,1)S(1)}, u32[]{:S(2)}, u32[]{:S(2)}) %collective-permute-start.10) | collective-permute-done | bytes 131104 | tf_op jit(solution)/shard_map/ppermute | solution.py:365
  50.2 3.2 %collective-permute-done.11.refs_3_ = bf16[4,32,512]{2,1,0:T(8,128)(2,1)S(1)} collective-permute-done((bf16[4,32,512]{2,1,0:T(8,128)(2,1)S(1)}, bf16[4,32,512]{2,1,0:T(8,128)(2,1)S(1)}, u32[]{:S(2)}, u32[]{:S(2)}) %collective-permute-start.11) | collective-permute-done | bytes 131104 | tf_op jit(solution)/shard_map/ppermute | solution.py:365
  53.4 0.8 %join_levels.1 = bf16[4,4,32,512]{3,2,1,0:T(8,128)(2,1)} custom-call(bf16[4,32,512]{2,1,0:T(8,128)(2,1)S(1)} %get-tuple-element.29.refs_0_, bf16[4,32,512]{2,1,0:T(8,128)(2,1)S(1)} %collective-permute-done.9.refs_1_, bf16[4,32,512]{2,1,0:T(8,128)(2,1)S(1)} %collective-permute-done.10.refs_2_, bf16[4,32,512]{2,1,0:T(8,128)(2,1)S(1)} %collective-permute-done.11.refs_3_), custom_call_target="tpu_custom_call" | custom-call | tf_op jit(solution)/shard_map/join_levels/pallas_call | solution.py:353
Async XLA Ops:
  2.5 17.8 %collective-permute-start = (bf16[71,32,128]{2,1,0:T(8,128)(2,1)}, bf16[71,32,128]{2,1,0:T(8,128)(2,1)S(1)}, u32[]{:S(2)}, u32[]{:S(2)}) collective-permute-start(bf16[71,32,128]{2,1,0:T(8,128)(2,1)} %get-tuple-element.20), channel_id=1, source_target_pairs={{0,1},{1,0},{2,3},{3,2},{4,5},{5,4},{6,7},{7,6},{8,9},{9,8},{10,11... | collective-permute-start | bytes 1744904 | tf_op jit(solution)/shard_map/ppermute | solution.py:365
  3.3 14.9 %collective-permute-start.1 = (bf16[27,32,128]{2,1,0:T(8,128)(2,1)}, bf16[27,32,128]{2,1,0:T(8,128)(2,1)S(1)}, u32[]{:S(2)}, u32[]{:S(2)}) collective-permute-start(bf16[27,32,128]{2,1,0:T(8,128)(2,1)} %get-tuple-element.21), channel_id=1, source_target_pairs={{0,2},{1,3},{2,0},{3,1},{4,6},{5,7},{6,4},{7,5},{8,10},{9,11},{10,... | collective-permute-start | bytes 663560 | tf_op jit(solution)/shard_map/ppermute | solution.py:365
  6.0 14.3 %copy-start.5 = (s32[4,27]{1,0:T(4,128)S(1)}, s32[4,27]{1,0:T(4,128)}, u32[]{:S(2)}) copy-start(s32[4,27]{1,0:T(4,128)} %tab.1) | copy-start | bytes 1300
  6.0 8.9 %collective-permute-start.2 = (bf16[17,32,128]{2,1,0:T(8,128)(2,1)}, bf16[17,32,128]{2,1,0:T(8,128)(2,1)S(1)}, u32[]{:S(2)}, u32[]{:S(2)}) collective-permute-start(bf16[17,32,128]{2,1,0:T(8,128)(2,1)} %get-tuple-element.22), channel_id=1, source_target_pairs={{0,2},{1,3},{2,0},{3,1},{4,6},{5,7},{6,4},{7,5},{8,10},{9,11},{10,... | collective-permute-start | bytes 417800 | tf_op jit(solution)/shard_map/ppermute | solution.py:365
  6.3 14.0 %copy-start.4 = (s32[1,2,2]{2,1,0:T(2,128)S(1)}, s32[1,2,2]{2,1,0:T(2,128)}, u32[]{:S(2)}) copy-start(s32[1,2,2]{2,1,0:T(2,128)} %fl.1) | copy-start | bytes 52
  6.3 11.9 %collective-permute-start.3 = (bf16[17,32,128]{2,1,0:T(8,128)(2,1)}, bf16[17,32,128]{2,1,0:T(8,128)(2,1)S(1)}, u32[]{:S(2)}, u32[]{:S(2)}) collective-permute-start(bf16[17,32,128]{2,1,0:T(8,128)(2,1)} %get-tuple-element.23), channel_id=1, source_target_pairs={{0,3},{1,2},{2,1},{3,0},{4,7},{5,6},{6,5},{7,4},{8,11},{9,10},{10,... | collective-permute-start | bytes 417800 | tf_op jit(solution)/shard_map/ppermute | solution.py:365
  18.1 9.0 %collective-permute-start.8 = (bf16[27,32,128]{2,1,0:T(8,128)(2,1)S(1)}, bf16[27,32,128]{2,1,0:T(8,128)(2,1)S(1)}, u32[]{:S(2)}, u32[]{:S(2)}) collective-permute-start(bf16[27,32,128]{2,1,0:T(8,128)(2,1)S(1)} %collective-permute-done.1.refs_8_), channel_id=1, source_target_pairs={{0,5},{1,4},{2,7},{3,6},{4,1},{5,0},{6,3},{7,2},{8,13},{9,12},{10,... | collective-permute-start | bytes 663560 | tf_op jit(solution)/shard_map/ppermute | solution.py:371
  19.9 10.3 %collective-permute-start.7 = (bf16[27,32,128]{2,1,0:T(8,128)(2,1)S(1)}, bf16[27,32,128]{2,1,0:T(8,128)(2,1)S(1)}, u32[]{:S(2)}, u32[]{:S(2)}) collective-permute-start(bf16[27,32,128]{2,1,0:T(8,128)(2,1)S(1)} %collective-permute-done.1.refs_8_), channel_id=1, source_target_pairs={{0,4},{1,5},{2,6},{3,7},{4,0},{5,1},{6,2},{7,3},{8,12},{9,13},{10,... | collective-permute-start | bytes 663560 | tf_op jit(solution)/shard_map/ppermute | solution.py:371
  19.9 10.3 %collective-permute-start.6 = (bf16[27,32,128]{2,1,0:T(8,128)(2,1)S(1)}, bf16[27,32,128]{2,1,0:T(8,128)(2,1)S(1)}, u32[]{:S(2)}, u32[]{:S(2)}) collective-permute-start(bf16[27,32,128]{2,1,0:T(8,128)(2,1)S(1)} %collective-permute-done.1.refs_8_), channel_id=1, source_target_pairs={{0,1},{1,0},{2,3},{3,2},{4,5},{5,4},{6,7},{7,6},{8,9},{9,8},{10,11... | collective-permute-start | bytes 663560 | tf_op jit(solution)/shard_map/ppermute | solution.py:365
  20.3 0.9 %copy-start.2 = (bf16[17,32,128]{2,1,0:T(8,128)(2,1)S(1)}, bf16[17,32,128]{2,1,0:T(8,128)(2,1)}, u32[]{:S(2)}) copy-start(bf16[17,32,128]{2,1,0:T(8,128)(2,1)} %get-tuple-element.19.refs_0_) | copy-start | bytes 417796
  21.2 10.5 %copy-start = (bf16[27,128,32]{1,2,0:T(8,128)(2,1)S(1)}, bf16[27,128,32]{1,2,0:T(8,128)(2,1)}, u32[]{:S(2)}) copy-start(bf16[27,128,32]{1,2,0:T(8,128)(2,1)} %param.11) | copy-start | bytes 663556
  21.2 10.6 %copy-start.1 = (bf16[27,128,32]{1,2,0:T(8,128)(2,1)S(1)}, bf16[27,128,32]{1,2,0:T(8,128)(2,1)}, u32[]{:S(2)}) copy-start(bf16[27,128,32]{1,2,0:T(8,128)(2,1)} %param.13) | copy-start | bytes 663556
  21.2 10.6 %copy-start.3 = (bf16[17,32,128]{2,1,0:T(8,128)(2,1)S(1)}, bf16[17,32,128]{2,1,0:T(8,128)(2,1)}, u32[]{:S(2)}) copy-start(bf16[17,32,128]{2,1,0:T(8,128)(2,1)} %get-tuple-element.19.refs_0_) | copy-start | bytes 417796
  22.1 8.9 %collective-permute-start.4 = (bf16[9,32,128]{2,1,0:T(8,128)(2,1)S(1)}, bf16[9,32,128]{2,1,0:T(8,128)(2,1)S(1)}, u32[]{:S(2)}, u32[]{:S(2)}) collective-permute-start(bf16[9,32,128]{2,1,0:T(8,128)(2,1)S(1)} %get-tuple-element.26), channel_id=1, source_target_pairs={{0,4},{4,8},{8,12},{12,16},{16,20},{20,24},{24,28},{28,32},{32,36}... | collective-permute-start | bytes 221192 | tf_op jit(solution)/shard_map/ppermute | solution.py:376
  23.8 7.9 %collective-permute-start.5 = (bf16[9,32,128]{2,1,0:T(8,128)(2,1)S(1)}, bf16[9,32,128]{2,1,0:T(8,128)(2,1)S(1)}, u32[]{:S(2)}, u32[]{:S(2)}) collective-permute-start(bf16[9,32,128]{2,1,0:T(8,128)(2,1)S(1)} %get-tuple-element.27), channel_id=1, source_target_pairs={{0,124},{4,0},{8,4},{12,8},{16,12},{20,16},{24,20},{28,24},{32,28}... | collective-permute-start | bytes 221192 | tf_op jit(solution)/shard_map/ppermute | solution.py:376
  42.8 4.0 %collective-permute-start.9 = (bf16[4,32,512]{2,1,0:T(8,128)(2,1)S(1)}, bf16[4,32,512]{2,1,0:T(8,128)(2,1)S(1)}, u32[]{:S(2)}, u32[]{:S(2)}) collective-permute-start(bf16[4,32,512]{2,1,0:T(8,128)(2,1)S(1)} %get-tuple-element.30), channel_id=1, source_target_pairs={{0,1},{1,0},{2,3},{3,2},{4,5},{5,4},{6,7},{7,6},{8,9},{9,8},{10,11... | collective-permute-start | bytes 393224 | tf_op jit(solution)/shard_map/ppermute | solution.py:365
  43.6 6.6 %collective-permute-start.10 = (bf16[4,32,512]{2,1,0:T(8,128)(2,1)S(1)}, bf16[4,32,512]{2,1,0:T(8,128)(2,1)S(1)}, u32[]{:S(2)}, u32[]{:S(2)}) collective-permute-start(bf16[4,32,512]{2,1,0:T(8,128)(2,1)S(1)} %get-tuple-element.31), channel_id=1, source_target_pairs={{0,2},{1,3},{2,0},{3,1},{4,6},{5,7},{6,4},{7,5},{8,10},{9,11},{10,... | collective-permute-start | bytes 393224 | tf_op jit(solution)/shard_map/ppermute | solution.py:365
  46.4 7.0 %collective-permute-start.11 = (bf16[4,32,512]{2,1,0:T(8,128)(2,1)S(1)}, bf16[4,32,512]{2,1,0:T(8,128)(2,1)S(1)}, u32[]{:S(2)}, u32[]{:S(2)}) collective-permute-start(bf16[4,32,512]{2,1,0:T(8,128)(2,1)S(1)} %get-tuple-element.32), channel_id=1, source_target_pairs={{0,3},{1,2},{2,1},{3,0},{4,7},{5,6},{6,5},{7,4},{8,11},{9,10},{10,... | collective-permute-start | bytes 393224 | tf_op jit(solution)/shard_map/ppermute | solution.py:365

commit v4 on v3

--- a/solution.py
+++ b/solution.py
@@ -23,7 +23,7 @@
 def split_kernel(feat, w1, w2, b1, b2, lev, *refs):
     pieces, cross, held, sem = refs[:4], refs[4], refs[5], refs[6]
     me = lax.axis_index("chan")
-    odd = lax.axis_index("slab") % 2
+    odd = layer_of_slab()
 
     @pl.when(odd == 0)
     def _():
@@ -178,7 +178,7 @@
     outs = refs[12:16]
     fs, hs, w1, w2, bias, sent, sent_int, tables, slots, pad, pad_face, acc, shift, turned, sem = refs[16:]
     me = lax.axis_index("chan")
-    odd = lax.axis_index("slab") % 2
+    odd = layer_of_slab()
 
     f_copies, t_copies = [], []
     for side in range(2):
@@ -365,9 +365,14 @@
     return lax.ppermute(value, "chan", [(i, i ^ m) for i in range(4)])
 
 
-def swap_slabs(value, m):
+def layer_of_slab():
+    slab = lax.axis_index("slab")
+    return (slab + slab // 8) % 2
+
+
+def swap_slabs(value, step, m):
     count = lax.axis_size("slab")
-    pairs = [(4 * s + g, 4 * (s ^ 1) + (g ^ m)) for s in range(count) for g in range(4)]
+    pairs = [(4 * s + g, 4 * (s ^ step) + (g ^ m)) for s in range(count) for g in range(4)]
     return lax.ppermute(value, ("slab", "chan"), pairs)
 
 
@@ -383,7 +388,7 @@
     pieces = [own, swap(one, 1), two, three]
     up, down = faces(neighbours, face_lists, pieces)
     sides = [to_slab(up, 1), to_slab(down, -1)]
-    far = [fetched, swap(fetched, 1), swap_slabs(fetched, 0), swap_slabs(fetched, 1)]
+    far = [fetched, swap(fetched, 1), swap_slabs(fetched, 1, 0), swap_slabs(fetched, 8, 1)]
     outs = convolve(neighbours, face_lists, pieces, sides, (w1, w2), far)
     return join([outs[0]] + [swap(outs[m], m) for m in (1, 2, 3)])
 

time: 55.2 us -> 55.3 us (level)
  the two profiles are of different devices: /device:TPU:25 before, /device:TPU:1 now
where the time goes in v4:
time: 55.3 us; the launch traced here: 55.1 us
  starting transfers between devices  21.4 us (39%)
  waiting for transfers between devices  17.4 us (31%)
  Pallas kernels  15.3 us (28%)
  local copies, waits for them, and re-layouts  0.92 us (2%)
    ppermute x8, waiting for transfers between devices, swap(): return lax.ppermute(value, 'chan', [(i, i ^ m) for i in range(4)])  15 us
    ppermute x8, starting transfers between devices, swap(): return lax.ppermute(value, 'chan', [(i, i ^ m) for i in range(4)])  12.5 us
    pallas_call x1, Pallas kernels, convolve(): pl.pallas_call(conv_kernel, out_shape=[piece] * 4, in_specs=[SMEM] * 2 +...  11.1 us
    ppermute x2, starting transfers between devices, to_slab(): lax.ppermute(value, 'slab', [(s, (s + steps) % count) for s in range(coun...  5.75 us
    ppermute x2, starting transfers between devices, swap_slabs(): return lax.ppermute(value, ('slab', 'chan'), pairs)  3.12 us
    pallas_call x1, Pallas kernels, split(): pl.pallas_call(split_kernel, out_shape=[piece, loaded, piece, piece, jax....  2.5 us
    ppermute x2, waiting for transfers between devices, to_slab(): lax.ppermute(value, 'slab', [(s, (s + steps) % count) for s in range(coun...  2.42 us
  transfers between devices with their start and end apart: 12, of which 5 were waited for; matrix products, arithmetic and copies ran while one was open for 0% of the time, Pallas kernels for 2%

profile of v4, /device:TPU:1, one launch (start us, length us, event | category | flops | bytes accessed | tf_op | source)
XLA Modules:
  0.0 55.1 jit_solution(13967227595694734672)
XLA Ops:
  0.0 2.5 %split_features.1 = (bf16[17,32,128]{2,1,0:T(8,128)(2,1)}, bf16[71,32,128]{2,1,0:T(8,128)(2,1)}, bf16[17,32,128]{2,1,0:T(8,128)(2,1)}, bf16[17,32,128]{2,1,0:T(8,128)(2,1)}, bf16[27,32,128]{2,1,0:T(8,128)(2,1)}) custom-call(bf16[4,4,32,512]{3,2,1,0:T(8,128)(2,1)} %feat.1, bf16[27,32,128]{2,1,0:T(8,128)(2,1)} %bitcast.4, bf16[27,32,128]{2,1,0:T(8,128)(2,1)} %bitcast.6, ...), custom_call_target="tpu_custom_call" | custom-call | tf_op jit(solution)/shard_map/split_features/pallas_call | solution.py:72
  2.5 1.5 %collective-permute-start = (bf16[71,32,128]{2,1,0:T(8,128)(2,1)}, bf16[71,32,128]{2,1,0:T(8,128)(2,1)S(1)}, u32[]{:S(2)}, u32[]{:S(2)}) collective-permute-start(bf16[71,32,128]{2,1,0:T(8,128)(2,1)} %get-tuple-element.20), channel_id=1, source_target_pairs={{0,1},{1,0},{2,3},{3,2},{4,5},{5,4},{6,7},{7,6},{8,9},{9,8},{10,11... | collective-permute-start | bytes 1744904 | tf_op jit(solution)/shard_map/ppermute | solution.py:365
  4.0 2.8 %collective-permute-start.1 = (bf16[27,32,128]{2,1,0:T(8,128)(2,1)}, bf16[27,32,128]{2,1,0:T(8,128)(2,1)S(1)}, u32[]{:S(2)}, u32[]{:S(2)}) collective-permute-start(bf16[27,32,128]{2,1,0:T(8,128)(2,1)} %get-tuple-element.21), channel_id=1, source_target_pairs={{0,2},{1,3},{2,0},{3,1},{4,6},{5,7},{6,4},{7,5},{8,10},{9,11},{10,... | collective-permute-start | bytes 663560 | tf_op jit(solution)/shard_map/ppermute | solution.py:365
  6.9 0.0 copy-start.5
  6.9 0.1 collective-permute-start.2
  7.0 0.0 copy-start.4
  7.0 3.4 %collective-permute-start.3 = (bf16[17,32,128]{2,1,0:T(8,128)(2,1)}, bf16[17,32,128]{2,1,0:T(8,128)(2,1)S(1)}, u32[]{:S(2)}, u32[]{:S(2)}) collective-permute-start(bf16[17,32,128]{2,1,0:T(8,128)(2,1)} %get-tuple-element.23), channel_id=1, source_target_pairs={{0,3},{1,2},{2,1},{3,0},{4,7},{5,6},{6,5},{7,4},{8,11},{9,10},{10,... | collective-permute-start | bytes 417800 | tf_op jit(solution)/shard_map/ppermute | solution.py:365
  10.4 5.3 %collective-permute-done.2.refs_2_ = bf16[17,32,128]{2,1,0:T(8,128)(2,1)S(1)} collective-permute-done((bf16[17,32,128]{2,1,0:T(8,128)(2,1)}, bf16[17,32,128]{2,1,0:T(8,128)(2,1)S(1)}, u32[]{:S(2)}, u32[]{:S(2)}) %collective-permute-start.2) | collective-permute-done | bytes 139296 | tf_op jit(solution)/shard_map/ppermute | solution.py:365
  15.7 3.2 %collective-permute-done.3.refs_3_ = bf16[17,32,128]{2,1,0:T(8,128)(2,1)S(1)} collective-permute-done((bf16[17,32,128]{2,1,0:T(8,128)(2,1)}, bf16[17,32,128]{2,1,0:T(8,128)(2,1)S(1)}, u32[]{:S(2)}, u32[]{:S(2)}) %collective-permute-start.3) | collective-permute-done | bytes 139296 | tf_op jit(solution)/shard_map/ppermute | solution.py:365
  18.9 0.0 collective-permute-done.1.refs_8_
  18.9 1.5 %collective-permute-start.8 = (bf16[27,32,128]{2,1,0:T(8,128)(2,1)S(1)}, bf16[27,32,128]{2,1,0:T(8,128)(2,1)S(1)}, u32[]{:S(2)}, u32[]{:S(2)}) collective-permute-start(bf16[27,32,128]{2,1,0:T(8,128)(2,1)S(1)} %collective-permute-done.1.refs_8_), channel_id=1, source_target_pairs={{0,33},{1,32},{2,35},{3,34},{4,37},{5,36},{6,39},{7,38},{8,41},{9,... | collective-permute-start | bytes 663560 | tf_op jit(solution)/shard_map/ppermute | solution.py:376
  20.3 1.6 %collective-permute-start.7 = (bf16[27,32,128]{2,1,0:T(8,128)(2,1)S(1)}, bf16[27,32,128]{2,1,0:T(8,128)(2,1)S(1)}, u32[]{:S(2)}, u32[]{:S(2)}) collective-permute-start(bf16[27,32,128]{2,1,0:T(8,128)(2,1)S(1)} %collective-permute-done.1.refs_8_), channel_id=1, source_target_pairs={{0,4},{1,5},{2,6},{3,7},{4,0},{5,1},{6,2},{7,3},{8,12},{9,13},{10,... | collective-permute-start | bytes 663560 | tf_op jit(solution)/shard_map/ppermute | solution.py:376
  22.0 0.6 %collective-permute-start.6 = (bf16[27,32,128]{2,1,0:T(8,128)(2,1)S(1)}, bf16[27,32,128]{2,1,0:T(8,128)(2,1)S(1)}, u32[]{:S(2)}, u32[]{:S(2)}) collective-permute-start(bf16[27,32,128]{2,1,0:T(8,128)(2,1)S(1)} %collective-permute-done.1.refs_8_), channel_id=1, source_target_pairs={{0,1},{1,0},{2,3},{3,2},{4,5},{5,4},{6,7},{7,6},{8,9},{9,8},{10,11... | collective-permute-start | bytes 663560 | tf_op jit(solution)/shard_map/ppermute | solution.py:365
  22.6 0.0 collective-permute-done.refs_1_
  22.6 0.0 copy-done.5
  22.6 0.0 copy-done.4
  22.6 0.0 copy-start.2
  22.6 0.9 %copy-done.2 = bf16[17,32,128]{2,1,0:T(8,128)(2,1)S(1)} copy-done((bf16[17,32,128]{2,1,0:T(8,128)(2,1)S(1)}, bf16[17,32,128]{2,1,0:T(8,128)(2,1)}, u32[]{:S(2)}) %copy-start.2) | copy-done | bytes 139288
  23.5 0.0 copy-start
  23.5 0.0 copy-start.1
  23.5 0.0 copy-start.3
  23.5 0.9 %pick_faces.1 = (bf16[9,32,128]{2,1,0:T(8,128)(2,1)S(1)}, bf16[9,32,128]{2,1,0:T(8,128)(2,1)S(1)}) custom-call(s32[4,27]{1,0:T(4,128)S(1)} %copy-done.5, s32[1,2,2]{2,1,0:T(2,128)S(1)} %copy-done.4, s32[1,2,2]{2,1,0:T(2,128)S(1)} %copy-done.4, bf16[17,32,128]{2,1,0:T(8,128)(2,1)S(1)} %copy-done.2, bf16[71,32,128]{2,1,0:T(8,128)(2,1)S(1)} %collective-permute-done.refs_1_, ...), custom_call_target="tpu_custom_call" | custom-call | tf_op jit(solution)/shard_map/pick_faces/pallas_call | solution.py:104
  24.4 0.1 collective-permute-start.4
  24.5 5.7 %collective-permute-start.5 = (bf16[9,32,128]{2,1,0:T(8,128)(2,1)S(1)}, bf16[9,32,128]{2,1,0:T(8,128)(2,1)S(1)}, u32[]{:S(2)}, u32[]{:S(2)}) collective-permute-start(bf16[9,32,128]{2,1,0:T(8,128)(2,1)S(1)} %get-tuple-element.27), channel_id=1, source_target_pairs={{0,124},{4,0},{8,4},{12,8},{16,12},{20,16},{24,20},{28,24},{32,28}... | collective-permute-start | bytes 221192 | tf_op jit(solution)/shard_map/ppermute | solution.py:381
  30.2 0.0 collective-permute-done.8.refs_11_
  30.2 0.0 collective-permute-done.7.refs_10_
  30.2 0.0 collective-permute-done.6.refs_9_
  30.2 2.4 %collective-permute-done.4.refs_4_ = bf16[9,32,128]{2,1,0:T(8,128)(2,1)S(1)} collective-permute-done((bf16[9,32,128]{2,1,0:T(8,128)(2,1)S(1)}, bf16[9,32,128]{2,1,0:T(8,128)(2,1)S(1)}, u32[]{:S(2)}, u32[]{:S(2)}) %collective-permute-start.4) | collective-permute-done | bytes 73760 | tf_op jit(solution)/shard_map/ppermute | solution.py:381
  32.6 0.0 collective-permute-done.5.refs_5_
  32.6 0.0 copy-done
  32.6 0.0 copy-done.1
  32.6 0.0 copy-done.3
  32.6 11.1 %convolve.1 = (bf16[4,32,512]{2,1,0:T(8,128)(2,1)S(1)}, bf16[4,32,512]{2,1,0:T(8,128)(2,1)S(1)}, bf16[4,32,512]{2,1,0:T(8,128)(2,1)S(1)}, bf16[4,32,512]{2,1,0:T(8,128)(2,1)S(1)}) custom-call(s32[4,27]{1,0:T(4,128)S(1)} %copy-done.5, s32[1,2,2]{2,1,0:T(2,128)S(1)} %copy-done.4, bf16[17,32,128]{2,1,0:T(8,128)(2,1)S(1)} %copy-done.3, ...), custom_call_target="tpu_custom_call" | custom-call | flops 8000000000 | bytes 4000000 | tf_op jit(solution)/shard_map/convolve/pallas_call | solution.py:314
  43.7 0.9 %collective-permute-start.9 = (bf16[4,32,512]{2,1,0:T(8,128)(2,1)S(1)}, bf16[4,32,512]{2,1,0:T(8,128)(2,1)S(1)}, u32[]{:S(2)}, u32[]{:S(2)}) collective-permute-start(bf16[4,32,512]{2,1,0:T(8,128)(2,1)S(1)} %get-tuple-element.30), channel_id=1, source_target_pairs={{0,1},{1,0},{2,3},{3,2},{4,5},{5,4},{6,7},{7,6},{8,9},{9,8},{10,11... | collective-permute-start | bytes 393224 | tf_op jit(solution)/shard_map/ppermute | solution.py:365
  44.6 2.8 %collective-permute-start.10 = (bf16[4,32,512]{2,1,0:T(8,128)(2,1)S(1)}, bf16[4,32,512]{2,1,0:T(8,128)(2,1)S(1)}, u32[]{:S(2)}, u32[]{:S(2)}) collective-permute-start(bf16[4,32,512]{2,1,0:T(8,128)(2,1)S(1)} %get-tuple-element.31), channel_id=1, source_target_pairs={{0,2},{1,3},{2,0},{3,1},{4,6},{5,7},{6,4},{7,5},{8,10},{9,11},{10,... | collective-permute-start | bytes 393224 | tf_op jit(solution)/shard_map/ppermute | solution.py:365
  47.3 0.5 collective-permute-start.11
  47.8 0.0 collective-permute-done.9.refs_1_
  47.8 3.3 %collective-permute-done.10.refs_2_ = bf16[4,32,512]{2,1,0:T(8,128)(2,1)S(1)} collective-permute-done((bf16[4,32,512]{2,1,0:T(8,128)(2,1)S(1)}, bf16[4,32,512]{2,1,0:T(8,128)(2,1)S(1)}, u32[]{:S(2)}, u32[]{:S(2)}) %collective-permute-start.10) | collective-permute-done | bytes 131104 | tf_op jit(solution)/shard_map/ppermute | solution.py:365
  51.1 3.2 %collective-permute-done.11.refs_3_ = bf16[4,32,512]{2,1,0:T(8,128)(2,1)S(1)} collective-permute-done((bf16[4,32,512]{2,1,0:T(8,128)(2,1)S(1)}, bf16[4,32,512]{2,1,0:T(8,128)(2,1)S(1)}, u32[]{:S(2)}, u32[]{:S(2)}) %collective-permute-start.11) | collective-permute-done | bytes 131104 | tf_op jit(solution)/shard_map/ppermute | solution.py:365
  54.3 0.8 %join_levels.1 = bf16[4,4,32,512]{3,2,1,0:T(8,128)(2,1)} custom-call(bf16[4,32,512]{2,1,0:T(8,128)(2,1)S(1)} %get-tuple-element.29.refs_0_, bf16[4,32,512]{2,1,0:T(8,128)(2,1)S(1)} %collective-permute-done.9.refs_1_, bf16[4,32,512]{2,1,0:T(8,128)(2,1)S(1)} %collective-permute-done.10.refs_2_, bf16[4,32,512]{2,1,0:T(8,128)(2,1)S(1)} %collective-permute-done.11.refs_3_), custom_call_target="tpu_custom_call" | custom-call | tf_op jit(solution)/shard_map/join_levels/pallas_call | solution.py:353
Async XLA Ops:
  2.5 20.1 %collective-permute-start = (bf16[71,32,128]{2,1,0:T(8,128)(2,1)}, bf16[71,32,128]{2,1,0:T(8,128)(2,1)S(1)}, u32[]{:S(2)}, u32[]{:S(2)}) collective-permute-start(bf16[71,32,128]{2,1,0:T(8,128)(2,1)} %get-tuple-element.20), channel_id=1, source_target_pairs={{0,1},{1,0},{2,3},{3,2},{4,5},{5,4},{6,7},{7,6},{8,9},{9,8},{10,11... | collective-permute-start | bytes 1744904 | tf_op jit(solution)/shard_map/ppermute | solution.py:365
  4.0 14.9 %collective-permute-start.1 = (bf16[27,32,128]{2,1,0:T(8,128)(2,1)}, bf16[27,32,128]{2,1,0:T(8,128)(2,1)S(1)}, u32[]{:S(2)}, u32[]{:S(2)}) collective-permute-start(bf16[27,32,128]{2,1,0:T(8,128)(2,1)} %get-tuple-element.21), channel_id=1, source_target_pairs={{0,2},{1,3},{2,0},{3,1},{4,6},{5,7},{6,4},{7,5},{8,10},{9,11},{10,... | collective-permute-start | bytes 663560 | tf_op jit(solution)/shard_map/ppermute | solution.py:365
  6.9 15.7 %copy-start.5 = (s32[4,27]{1,0:T(4,128)S(1)}, s32[4,27]{1,0:T(4,128)}, u32[]{:S(2)}) copy-start(s32[4,27]{1,0:T(4,128)} %tab.1) | copy-start | bytes 1300
  6.9 8.8 %collective-permute-start.2 = (bf16[17,32,128]{2,1,0:T(8,128)(2,1)}, bf16[17,32,128]{2,1,0:T(8,128)(2,1)S(1)}, u32[]{:S(2)}, u32[]{:S(2)}) collective-permute-start(bf16[17,32,128]{2,1,0:T(8,128)(2,1)} %get-tuple-element.22), channel_id=1, source_target_pairs={{0,2},{1,3},{2,0},{3,1},{4,6},{5,7},{6,4},{7,5},{8,10},{9,11},{10,... | collective-permute-start | bytes 417800 | tf_op jit(solution)/shard_map/ppermute | solution.py:365
  7.0 15.6 %copy-start.4 = (s32[1,2,2]{2,1,0:T(2,128)S(1)}, s32[1,2,2]{2,1,0:T(2,128)}, u32[]{:S(2)}) copy-start(s32[1,2,2]{2,1,0:T(2,128)} %fl.1) | copy-start | bytes 52
  7.0 11.9 %collective-permute-start.3 = (bf16[17,32,128]{2,1,0:T(8,128)(2,1)}, bf16[17,32,128]{2,1,0:T(8,128)(2,1)S(1)}, u32[]{:S(2)}, u32[]{:S(2)}) collective-permute-start(bf16[17,32,128]{2,1,0:T(8,128)(2,1)} %get-tuple-element.23), channel_id=1, source_target_pairs={{0,3},{1,2},{2,1},{3,0},{4,7},{5,6},{6,5},{7,4},{8,11},{9,10},{10,... | collective-permute-start | bytes 417800 | tf_op jit(solution)/shard_map/ppermute | solution.py:365
  18.9 11.3 %collective-permute-start.8 = (bf16[27,32,128]{2,1,0:T(8,128)(2,1)S(1)}, bf16[27,32,128]{2,1,0:T(8,128)(2,1)S(1)}, u32[]{:S(2)}, u32[]{:S(2)}) collective-permute-start(bf16[27,32,128]{2,1,0:T(8,128)(2,1)S(1)} %collective-permute-done.1.refs_8_), channel_id=1, source_target_pairs={{0,33},{1,32},{2,35},{3,34},{4,37},{5,36},{6,39},{7,38},{8,41},{9,... | collective-permute-start | bytes 663560 | tf_op jit(solution)/shard_map/ppermute | solution.py:376
  20.3 9.8 %collective-permute-start.7 = (bf16[27,32,128]{2,1,0:T(8,128)(2,1)S(1)}, bf16[27,32,128]{2,1,0:T(8,128)(2,1)S(1)}, u32[]{:S(2)}, u32[]{:S(2)}) collective-permute-start(bf16[27,32,128]{2,1,0:T(8,128)(2,1)S(1)} %collective-permute-done.1.refs_8_), channel_id=1, source_target_pairs={{0,4},{1,5},{2,6},{3,7},{4,0},{5,1},{6,2},{7,3},{8,12},{9,13},{10,... | collective-permute-start | bytes 663560 | tf_op jit(solution)/shard_map/ppermute | solution.py:376
  22.0 8.2 %collective-permute-start.6 = (bf16[27,32,128]{2,1,0:T(8,128)(2,1)S(1)}, bf16[27,32,128]{2,1,0:T(8,128)(2,1)S(1)}, u32[]{:S(2)}, u32[]{:S(2)}) collective-permute-start(bf16[27,32,128]{2,1,0:T(8,128)(2,1)S(1)} %collective-permute-done.1.refs_8_), channel_id=1, source_target_pairs={{0,1},{1,0},{2,3},{3,2},{4,5},{5,4},{6,7},{7,6},{8,9},{9,8},{10,11... | collective-permute-start | bytes 663560 | tf_op jit(solution)/shard_map/ppermute | solution.py:365
  22.6 0.9 %copy-start.2 = (bf16[17,32,128]{2,1,0:T(8,128)(2,1)S(1)}, bf16[17,32,128]{2,1,0:T(8,128)(2,1)}, u32[]{:S(2)}) copy-start(bf16[17,32,128]{2,1,0:T(8,128)(2,1)} %get-tuple-element.19.refs_0_) | copy-start | bytes 417796
  23.5 9.1 %copy-start = (bf16[27,128,32]{1,2,0:T(8,128)(2,1)S(1)}, bf16[27,128,32]{1,2,0:T(8,128)(2,1)}, u32[]{:S(2)}) copy-start(bf16[27,128,32]{1,2,0:T(8,128)(2,1)} %param.11) | copy-start | bytes 663556
  23.5 9.1 %copy-start.1 = (bf16[27,128,32]{1,2,0:T(8,128)(2,1)S(1)}, bf16[27,128,32]{1,2,0:T(8,128)(2,1)}, u32[]{:S(2)}) copy-start(bf16[27,128,32]{1,2,0:T(8,128)(2,1)} %param.13) | copy-start | bytes 663556
  23.5 9.1 %copy-start.3 = (bf16[17,32,128]{2,1,0:T(8,128)(2,1)S(1)}, bf16[17,32,128]{2,1,0:T(8,128)(2,1)}, u32[]{:S(2)}) copy-start(bf16[17,32,128]{2,1,0:T(8,128)(2,1)} %get-tuple-element.19.refs_0_) | copy-start | bytes 417796
  24.4 8.2 %collective-permute-start.4 = (bf16[9,32,128]{2,1,0:T(8,128)(2,1)S(1)}, bf16[9,32,128]{2,1,0:T(8,128)(2,1)S(1)}, u32[]{:S(2)}, u32[]{:S(2)}) collective-permute-start(bf16[9,32,128]{2,1,0:T(8,128)(2,1)S(1)} %get-tuple-element.26), channel_id=1, source_target_pairs={{0,4},{4,8},{8,12},{12,16},{16,20},{20,24},{24,28},{28,32},{32,36}... | collective-permute-start | bytes 221192 | tf_op jit(solution)/shard_map/ppermute | solution.py:381
  24.5 8.1 %collective-permute-start.5 = (bf16[9,32,128]{2,1,0:T(8,128)(2,1)S(1)}, bf16[9,32,128]{2,1,0:T(8,128)(2,1)S(1)}, u32[]{:S(2)}, u32[]{:S(2)}) collective-permute-start(bf16[9,32,128]{2,1,0:T(8,128)(2,1)S(1)} %get-tuple-element.27), channel_id=1, source_target_pairs={{0,124},{4,0},{8,4},{12,8},{16,12},{20,16},{24,20},{28,24},{32,28}... | collective-permute-start | bytes 221192 | tf_op jit(solution)/shard_map/ppermute | solution.py:381
  43.7 4.1 %collective-permute-start.9 = (bf16[4,32,512]{2,1,0:T(8,128)(2,1)S(1)}, bf16[4,32,512]{2,1,0:T(8,128)(2,1)S(1)}, u32[]{:S(2)}, u32[]{:S(2)}) collective-permute-start(bf16[4,32,512]{2,1,0:T(8,128)(2,1)S(1)} %get-tuple-element.30), channel_id=1, source_target_pairs={{0,1},{1,0},{2,3},{3,2},{4,5},{5,4},{6,7},{7,6},{8,9},{9,8},{10,11... | collective-permute-start | bytes 393224 | tf_op jit(solution)/shard_map/ppermute | solution.py:365
  44.6 6.6 %collective-permute-start.10 = (bf16[4,32,512]{2,1,0:T(8,128)(2,1)S(1)}, bf16[4,32,512]{2,1,0:T(8,128)(2,1)S(1)}, u32[]{:S(2)}, u32[]{:S(2)}) collective-permute-start(bf16[4,32,512]{2,1,0:T(8,128)(2,1)S(1)} %get-tuple-element.31), channel_id=1, source_target_pairs={{0,2},{1,3},{2,0},{3,1},{4,6},{5,7},{6,4},{7,5},{8,10},{9,11},{10,... | collective-permute-start | bytes 393224 | tf_op jit(solution)/shard_map/ppermute | solution.py:365
  47.3 7.0 %collective-permute-start.11 = (bf16[4,32,512]{2,1,0:T(8,128)(2,1)S(1)}, bf16[4,32,512]{2,1,0:T(8,128)(2,1)S(1)}, u32[]{:S(2)}, u32[]{:S(2)}) collective-permute-start(bf16[4,32,512]{2,1,0:T(8,128)(2,1)S(1)} %get-tuple-element.32), channel_id=1, source_target_pairs={{0,3},{1,2},{2,1},{3,0},{4,7},{5,6},{6,5},{7,4},{8,11},{9,10},{10,... | collective-permute-start | bytes 393224 | tf_op jit(solution)/shard_map/ppermute | solution.py:365

commit v5 on v4

--- a/solution.py
+++ b/solution.py
@@ -82,13 +82,15 @@
 
 def faces_kernel(near, lists_block, lists, *refs):
     pieces, sides, sem = refs[:4], refs[4:6], refs[6]
+    odd = lax.axis_index("slab") % 2
     copies = []
-    for tier, run, out in ((1, 3, sides[0]), (0, 0, sides[1])):
+    for i, out in enumerate(sides):
+        tier = (odd + 1 + i) % 2
         for c in range(2):
             b = jnp.maximum(lists[0, tier, c], 0)
             for m in range(4):
-                i = 8 * tier + 4 * c + m
-                copies.append(pltpu.make_async_copy(pieces[m].at[4 * run + b], out.at[4 * c + m], sem.at[i]))
+                source = pieces[m].at[12 * tier + b]
+                copies.append(pltpu.make_async_copy(source, out.at[4 * c + m], sem.at[8 * i + 4 * c + m]))
     for copy in copies:
         copy.start()
     for out in sides:
@@ -181,11 +183,10 @@
     odd = layer_of_slab()
 
     f_copies, t_copies = [], []
-    for side in range(2):
-        t_copies.append(
-            pltpu.make_async_copy(sides[side].at[8, pl.ds(0, 16)], sent.at[side], sem.at[side])
-        )
-        f_copies.append(pltpu.make_async_copy(sides[side].at[pl.ds(0, 8)], hs.at[side], sem.at[2 + side]))
+    for i in range(2):
+        side = (lax.axis_index("slab") + 1 + i) % 2
+        t_copies.append(pltpu.make_async_copy(sides[i].at[8, pl.ds(0, 16)], sent.at[side], sem.at[i]))
+        f_copies.append(pltpu.make_async_copy(sides[i].at[pl.ds(0, 8)], hs.at[side], sem.at[2 + i]))
     for m in range(4):
         f_copies.append(pltpu.make_async_copy(feat[m].at[pl.ds(0, 16)], fs.at[m], sem.at[4 + m]))
         f_copies.append(pltpu.make_async_copy(feat[m].at[16, pl.ds(0, 16)], bias.at[m], sem.at[8 + m]))
@@ -376,9 +377,9 @@
     return lax.ppermute(value, ("slab", "chan"), pairs)
 
 
-def to_slab(value, steps):
+def swap_faces(value, first):
     count = lax.axis_size("slab")
-    return lax.ppermute(value, "slab", [(s, (s + steps) % count) for s in range(count)])
+    return lax.ppermute(value, "slab", [(s, (((s + first) ^ 1) - first) % count) for s in range(count)])
 
 
 def shards(features, neighbours, face_lists, w_first, b_first, w_second, b_second, level_embed):
@@ -386,8 +387,8 @@
     own, one, two, three, cross = split(features, w1, w2, b_first, b_second, level_embed)
     fetched, two, three = lax.optimization_barrier((swap(cross, 2), swap(two, 2), swap(three, 3)))
     pieces = [own, swap(one, 1), two, three]
-    up, down = faces(neighbours, face_lists, pieces)
-    sides = [to_slab(up, 1), to_slab(down, -1)]
+    sides = faces(neighbours, face_lists, pieces)
+    sides = [swap_faces(sides[i], i) for i in range(2)]
     far = [fetched, swap(fetched, 1), swap_slabs(fetched, 1, 0), swap_slabs(fetched, 8, 1)]
     outs = convolve(neighbours, face_lists, pieces, sides, (w1, w2), far)
     return join([outs[0]] + [swap(outs[m], m) for m in (1, 2, 3)])

time: 55.3 us -> 55.6 us (level)
  no operation moved by 1% of the time
where the time goes in v5:
time: 55.6 us; the launch traced here: 55.5 us
  starting transfers between devices  21.8 us (39%)
  waiting for transfers between devices  17.3 us (31%)
  Pallas kernels  15.3 us (28%)
  local copies, waits for them, and re-layouts  0.92 us (2%)
    ppermute x8, waiting for transfers between devices, swap(): return lax.ppermute(value, 'chan', [(i, i ^ m) for i in range(4)])  14.9 us
    ppermute x8, starting transfers between devices, swap(): return lax.ppermute(value, 'chan', [(i, i ^ m) for i in range(4)])  12.5 us
    pallas_call x1, Pallas kernels, convolve(): pl.pallas_call(conv_kernel, out_shape=[piece] * 4, in_specs=[SMEM] * 2 +...  11.1 us
    ppermute x2, starting transfers between devices, swap_faces(): lax.ppermute(value, 'slab', [(s, ((s + first ^ 1) - first) % count) for s...  6.2 us
    ppermute x2, starting transfers between devices, swap_slabs(): return lax.ppermute(value, ('slab', 'chan'), pairs)  3.12 us
    pallas_call x1, Pallas kernels, split(): pl.pallas_call(split_kernel, out_shape=[piece, loaded, piece, piece, jax....  2.5 us
    ppermute x2, waiting for transfers between devices, swap_faces(): lax.ppermute(value, 'slab', [(s, ((s + first ^ 1) - first) % count) for s...  2.41 us
  transfers between devices with their start and end apart: 12, of which 5 were waited for; matrix products, arithmetic and copies ran while one was open for 0% of the time, Pallas kernels for 2%

profile of v5, /device:TPU:1, one launch (start us, length us, event | category | flops | bytes accessed | tf_op | source)
XLA Modules:
  0.0 55.5 jit_solution(11022199597264473813)
XLA Ops:
  0.0 2.5 %split_features.1 = (bf16[17,32,128]{2,1,0:T(8,128)(2,1)}, bf16[71,32,128]{2,1,0:T(8,128)(2,1)}, bf16[17,32,128]{2,1,0:T(8,128)(2,1)}, bf16[17,32,128]{2,1,0:T(8,128)(2,1)}, bf16[27,32,128]{2,1,0:T(8,128)(2,1)}) custom-call(bf16[4,4,32,512]{3,2,1,0:T(8,128)(2,1)} %feat.1, bf16[27,32,128]{2,1,0:T(8,128)(2,1)} %bitcast.4, bf16[27,32,128]{2,1,0:T(8,128)(2,1)} %bitcast.6, ...), custom_call_target="tpu_custom_call" | custom-call | tf_op jit(solution)/shard_map/split_features/pallas_call | solution.py:72
  2.5 1.5 %collective-permute-start = (bf16[71,32,128]{2,1,0:T(8,128)(2,1)}, bf16[71,32,128]{2,1,0:T(8,128)(2,1)S(1)}, u32[]{:S(2)}, u32[]{:S(2)}) collective-permute-start(bf16[71,32,128]{2,1,0:T(8,128)(2,1)} %get-tuple-element.20), channel_id=1, source_target_pairs={{0,1},{1,0},{2,3},{3,2},{4,5},{5,4},{6,7},{7,6},{8,9},{9,8},{10,11... | collective-permute-start | bytes 1744904 | tf_op jit(solution)/shard_map/ppermute | solution.py:366
  4.0 2.8 %collective-permute-start.1 = (bf16[27,32,128]{2,1,0:T(8,128)(2,1)}, bf16[27,32,128]{2,1,0:T(8,128)(2,1)S(1)}, u32[]{:S(2)}, u32[]{:S(2)}) collective-permute-start(bf16[27,32,128]{2,1,0:T(8,128)(2,1)} %get-tuple-element.21), channel_id=1, source_target_pairs={{0,2},{1,3},{2,0},{3,1},{4,6},{5,7},{6,4},{7,5},{8,10},{9,11},{10,... | collective-permute-start | bytes 663560 | tf_op jit(solution)/shard_map/ppermute | solution.py:366
  6.9 0.0 copy-start.5
  6.9 0.1 collective-permute-start.2
  7.0 0.0 copy-start.4
  7.0 3.4 %collective-permute-start.3 = (bf16[17,32,128]{2,1,0:T(8,128)(2,1)}, bf16[17,32,128]{2,1,0:T(8,128)(2,1)S(1)}, u32[]{:S(2)}, u32[]{:S(2)}) collective-permute-start(bf16[17,32,128]{2,1,0:T(8,128)(2,1)} %get-tuple-element.23), channel_id=1, source_target_pairs={{0,3},{1,2},{2,1},{3,0},{4,7},{5,6},{6,5},{7,4},{8,11},{9,10},{10,... | collective-permute-start | bytes 417800 | tf_op jit(solution)/shard_map/ppermute | solution.py:366
  10.4 5.3 %collective-permute-done.2.refs_2_ = bf16[17,32,128]{2,1,0:T(8,128)(2,1)S(1)} collective-permute-done((bf16[17,32,128]{2,1,0:T(8,128)(2,1)}, bf16[17,32,128]{2,1,0:T(8,128)(2,1)S(1)}, u32[]{:S(2)}, u32[]{:S(2)}) %collective-permute-start.2) | collective-permute-done | bytes 139296 | tf_op jit(solution)/shard_map/ppermute | solution.py:366
  15.7 3.2 %collective-permute-done.3.refs_3_ = bf16[17,32,128]{2,1,0:T(8,128)(2,1)S(1)} collective-permute-done((bf16[17,32,128]{2,1,0:T(8,128)(2,1)}, bf16[17,32,128]{2,1,0:T(8,128)(2,1)S(1)}, u32[]{:S(2)}, u32[]{:S(2)}) %collective-permute-start.3) | collective-permute-done | bytes 139296 | tf_op jit(solution)/shard_map/ppermute | solution.py:366
  18.9 0.0 collective-permute-done.1.refs_8_
  18.9 1.5 %collective-permute-start.8 = (bf16[27,32,128]{2,1,0:T(8,128)(2,1)S(1)}, bf16[27,32,128]{2,1,0:T(8,128)(2,1)S(1)}, u32[]{:S(2)}, u32[]{:S(2)}) collective-permute-start(bf16[27,32,128]{2,1,0:T(8,128)(2,1)S(1)} %collective-permute-done.1.refs_8_), channel_id=1, source_target_pairs={{0,33},{1,32},{2,35},{3,34},{4,37},{5,36},{6,39},{7,38},{8,41},{9,... | collective-permute-start | bytes 663560 | tf_op jit(solution)/shard_map/ppermute | solution.py:377
  20.3 1.6 %collective-permute-start.7 = (bf16[27,32,128]{2,1,0:T(8,128)(2,1)S(1)}, bf16[27,32,128]{2,1,0:T(8,128)(2,1)S(1)}, u32[]{:S(2)}, u32[]{:S(2)}) collective-permute-start(bf16[27,32,128]{2,1,0:T(8,128)(2,1)S(1)} %collective-permute-done.1.refs_8_), channel_id=1, source_target_pairs={{0,4},{1,5},{2,6},{3,7},{4,0},{5,1},{6,2},{7,3},{8,12},{9,13},{10,... | collective-permute-start | bytes 663560 | tf_op jit(solution)/shard_map/ppermute | solution.py:377
  22.0 0.6 %collective-permute-start.6 = (bf16[27,32,128]{2,1,0:T(8,128)(2,1)S(1)}, bf16[27,32,128]{2,1,0:T(8,128)(2,1)S(1)}, u32[]{:S(2)}, u32[]{:S(2)}) collective-permute-start(bf16[27,32,128]{2,1,0:T(8,128)(2,1)S(1)} %collective-permute-done.1.refs_8_), channel_id=1, source_target_pairs={{0,1},{1,0},{2,3},{3,2},{4,5},{5,4},{6,7},{7,6},{8,9},{9,8},{10,11... | collective-permute-start | bytes 663560 | tf_op jit(solution)/shard_map/ppermute | solution.py:366
  22.6 0.0 collective-permute-done.refs_1_
  22.6 0.0 copy-done.5
  22.6 0.0 copy-done.4
  22.6 0.0 copy-start.2
  22.6 0.9 %copy-done.2 = bf16[17,32,128]{2,1,0:T(8,128)(2,1)S(1)} copy-done((bf16[17,32,128]{2,1,0:T(8,128)(2,1)S(1)}, bf16[17,32,128]{2,1,0:T(8,128)(2,1)}, u32[]{:S(2)}) %copy-start.2) | copy-done | bytes 139288
  23.5 0.0 copy-start
  23.5 0.0 copy-start.1
  23.5 0.0 copy-start.3
  23.5 0.9 %pick_faces.1 = (bf16[9,32,128]{2,1,0:T(8,128)(2,1)S(1)}, bf16[9,32,128]{2,1,0:T(8,128)(2,1)S(1)}) custom-call(s32[4,27]{1,0:T(4,128)S(1)} %copy-done.5, s32[1,2,2]{2,1,0:T(2,128)S(1)} %copy-done.4, s32[1,2,2]{2,1,0:T(2,128)S(1)} %copy-done.4, bf16[17,32,128]{2,1,0:T(8,128)(2,1)S(1)} %copy-done.2, bf16[71,32,128]{2,1,0:T(8,128)(2,1)S(1)} %collective-permute-done.refs_1_, ...), custom_call_target="tpu_custom_call" | custom-call | tf_op jit(solution)/shard_map/pick_faces/pallas_call | solution.py:106
  24.4 0.1 collective-permute-start.4
  24.5 6.1 %collective-permute-start.5 = (bf16[9,32,128]{2,1,0:T(8,128)(2,1)S(1)}, bf16[9,32,128]{2,1,0:T(8,128)(2,1)S(1)}, u32[]{:S(2)}, u32[]{:S(2)}) collective-permute-start(bf16[9,32,128]{2,1,0:T(8,128)(2,1)S(1)} %get-tuple-element.27), channel_id=1, source_target_pairs={{0,124},{4,8},{8,4},{12,16},{16,12},{20,24},{24,20},{28,32},{32,28... | collective-permute-start | bytes 221192 | tf_op jit(solution)/shard_map/ppermute | solution.py:382
  30.6 0.0 collective-permute-done.8.refs_11_
  30.6 0.0 collective-permute-done.7.refs_10_
  30.6 0.0 collective-permute-done.6.refs_9_
  30.6 0.0 collective-permute-done.4.refs_4_
  30.6 2.4 %collective-permute-done.5.refs_5_ = bf16[9,32,128]{2,1,0:T(8,128)(2,1)S(1)} collective-permute-done((bf16[9,32,128]{2,1,0:T(8,128)(2,1)S(1)}, bf16[9,32,128]{2,1,0:T(8,128)(2,1)S(1)}, u32[]{:S(2)}, u32[]{:S(2)}) %collective-permute-start.5) | collective-permute-done | bytes 73760 | tf_op jit(solution)/shard_map/ppermute | solution.py:382
  33.1 0.0 copy-done
  33.1 0.0 copy-done.1
  33.1 0.0 copy-done.3
  33.1 11.1 %convolve.1 = (bf16[4,32,512]{2,1,0:T(8,128)(2,1)S(1)}, bf16[4,32,512]{2,1,0:T(8,128)(2,1)S(1)}, bf16[4,32,512]{2,1,0:T(8,128)(2,1)S(1)}, bf16[4,32,512]{2,1,0:T(8,128)(2,1)S(1)}) custom-call(s32[4,27]{1,0:T(4,128)S(1)} %copy-done.5, s32[1,2,2]{2,1,0:T(2,128)S(1)} %copy-done.4, bf16[17,32,128]{2,1,0:T(8,128)(2,1)S(1)} %copy-done.3, ...), custom_call_target="tpu_custom_call" | custom-call | flops 8000000000 | bytes 4000000 | tf_op jit(solution)/shard_map/convolve/pallas_call | solution.py:315
  44.2 0.9 %collective-permute-start.9 = (bf16[4,32,512]{2,1,0:T(8,128)(2,1)S(1)}, bf16[4,32,512]{2,1,0:T(8,128)(2,1)S(1)}, u32[]{:S(2)}, u32[]{:S(2)}) collective-permute-start(bf16[4,32,512]{2,1,0:T(8,128)(2,1)S(1)} %get-tuple-element.30), channel_id=1, source_target_pairs={{0,1},{1,0},{2,3},{3,2},{4,5},{5,4},{6,7},{7,6},{8,9},{9,8},{10,11... | collective-permute-start | bytes 393224 | tf_op jit(solution)/shard_map/ppermute | solution.py:366
  45.0 2.5 %collective-permute-start.10 = (bf16[4,32,512]{2,1,0:T(8,128)(2,1)S(1)}, bf16[4,32,512]{2,1,0:T(8,128)(2,1)S(1)}, u32[]{:S(2)}, u32[]{:S(2)}) collective-permute-start(bf16[4,32,512]{2,1,0:T(8,128)(2,1)S(1)} %get-tuple-element.31), channel_id=1, source_target_pairs={{0,2},{1,3},{2,0},{3,1},{4,6},{5,7},{6,4},{7,5},{8,10},{9,11},{10,... | collective-permute-start | bytes 393224 | tf_op jit(solution)/shard_map/ppermute | solution.py:366
  47.5 0.8 %collective-permute-start.11 = (bf16[4,32,512]{2,1,0:T(8,128)(2,1)S(1)}, bf16[4,32,512]{2,1,0:T(8,128)(2,1)S(1)}, u32[]{:S(2)}, u32[]{:S(2)}) collective-permute-start(bf16[4,32,512]{2,1,0:T(8,128)(2,1)S(1)} %get-tuple-element.32), channel_id=1, source_target_pairs={{0,3},{1,2},{2,1},{3,0},{4,7},{5,6},{6,5},{7,4},{8,11},{9,10},{10,... | collective-permute-start | bytes 393224 | tf_op jit(solution)/shard_map/ppermute | solution.py:366
  48.3 0.0 collective-permute-done.9.refs_1_
  48.3 3.3 %collective-permute-done.10.refs_2_ = bf16[4,32,512]{2,1,0:T(8,128)(2,1)S(1)} collective-permute-done((bf16[4,32,512]{2,1,0:T(8,128)(2,1)S(1)}, bf16[4,32,512]{2,1,0:T(8,128)(2,1)S(1)}, u32[]{:S(2)}, u32[]{:S(2)}) %collective-permute-start.10) | collective-permute-done | bytes 131104 | tf_op jit(solution)/shard_map/ppermute | solution.py:366
  51.6 3.1 %collective-permute-done.11.refs_3_ = bf16[4,32,512]{2,1,0:T(8,128)(2,1)S(1)} collective-permute-done((bf16[4,32,512]{2,1,0:T(8,128)(2,1)S(1)}, bf16[4,32,512]{2,1,0:T(8,128)(2,1)S(1)}, u32[]{:S(2)}, u32[]{:S(2)}) %collective-permute-start.11) | collective-permute-done | bytes 131104 | tf_op jit(solution)/shard_map/ppermute | solution.py:366
  54.7 0.8 %join_levels.1 = bf16[4,4,32,512]{3,2,1,0:T(8,128)(2,1)} custom-call(bf16[4,32,512]{2,1,0:T(8,128)(2,1)S(1)} %get-tuple-element.29.refs_0_, bf16[4,32,512]{2,1,0:T(8,128)(2,1)S(1)} %collective-permute-done.9.refs_1_, bf16[4,32,512]{2,1,0:T(8,128)(2,1)S(1)} %collective-permute-done.10.refs_2_, bf16[4,32,512]{2,1,0:T(8,128)(2,1)S(1)} %collective-permute-done.11.refs_3_), custom_call_target="tpu_custom_call" | custom-call | tf_op jit(solution)/shard_map/join_levels/pallas_call | solution.py:354
Async XLA Ops:
  2.5 20.1 %collective-permute-start = (bf16[71,32,128]{2,1,0:T(8,128)(2,1)}, bf16[71,32,128]{2,1,0:T(8,128)(2,1)S(1)}, u32[]{:S(2)}, u32[]{:S(2)}) collective-permute-start(bf16[71,32,128]{2,1,0:T(8,128)(2,1)} %get-tuple-element.20), channel_id=1, source_target_pairs={{0,1},{1,0},{2,3},{3,2},{4,5},{5,4},{6,7},{7,6},{8,9},{9,8},{10,11... | collective-permute-start | bytes 1744904 | tf_op jit(solution)/shard_map/ppermute | solution.py:366
  4.0 14.9 %collective-permute-start.1 = (bf16[27,32,128]{2,1,0:T(8,128)(2,1)}, bf16[27,32,128]{2,1,0:T(8,128)(2,1)S(1)}, u32[]{:S(2)}, u32[]{:S(2)}) collective-permute-start(bf16[27,32,128]{2,1,0:T(8,128)(2,1)} %get-tuple-element.21), channel_id=1, source_target_pairs={{0,2},{1,3},{2,0},{3,1},{4,6},{5,7},{6,4},{7,5},{8,10},{9,11},{10,... | collective-permute-start | bytes 663560 | tf_op jit(solution)/shard_map/ppermute | solution.py:366
  6.9 15.7 %copy-start.5 = (s32[4,27]{1,0:T(4,128)S(1)}, s32[4,27]{1,0:T(4,128)}, u32[]{:S(2)}) copy-start(s32[4,27]{1,0:T(4,128)} %tab.1) | copy-start | bytes 1300
  6.9 8.8 %collective-permute-start.2 = (bf16[17,32,128]{2,1,0:T(8,128)(2,1)}, bf16[17,32,128]{2,1,0:T(8,128)(2,1)S(1)}, u32[]{:S(2)}, u32[]{:S(2)}) collective-permute-start(bf16[17,32,128]{2,1,0:T(8,128)(2,1)} %get-tuple-element.22), channel_id=1, source_target_pairs={{0,2},{1,3},{2,0},{3,1},{4,6},{5,7},{6,4},{7,5},{8,10},{9,11},{10,... | collective-permute-start | bytes 417800 | tf_op jit(solution)/shard_map/ppermute | solution.py:366
  7.0 15.6 %copy-start.4 = (s32[1,2,2]{2,1,0:T(2,128)S(1)}, s32[1,2,2]{2,1,0:T(2,128)}, u32[]{:S(2)}) copy-start(s32[1,2,2]{2,1,0:T(2,128)} %fl.1) | copy-start | bytes 52
  7.0 11.9 %collective-permute-start.3 = (bf16[17,32,128]{2,1,0:T(8,128)(2,1)}, bf16[17,32,128]{2,1,0:T(8,128)(2,1)S(1)}, u32[]{:S(2)}, u32[]{:S(2)}) collective-permute-start(bf16[17,32,128]{2,1,0:T(8,128)(2,1)} %get-tuple-element.23), channel_id=1, source_target_pairs={{0,3},{1,2},{2,1},{3,0},{4,7},{5,6},{6,5},{7,4},{8,11},{9,10},{10,... | collective-permute-start | bytes 417800 | tf_op jit(solution)/shard_map/ppermute | solution.py:366
  18.9 11.8 %collective-permute-start.8 = (bf16[27,32,128]{2,1,0:T(8,128)(2,1)S(1)}, bf16[27,32,128]{2,1,0:T(8,128)(2,1)S(1)}, u32[]{:S(2)}, u32[]{:S(2)}) collective-permute-start(bf16[27,32,128]{2,1,0:T(8,128)(2,1)S(1)} %collective-permute-done.1.refs_8_), channel_id=1, source_target_pairs={{0,33},{1,32},{2,35},{3,34},{4,37},{5,36},{6,39},{7,38},{8,41},{9,... | collective-permute-start | bytes 663560 | tf_op jit(solution)/shard_map/ppermute | solution.py:377
  20.3 10.3 %collective-permute-start.7 = (bf16[27,32,128]{2,1,0:T(8,128)(2,1)S(1)}, bf16[27,32,128]{2,1,0:T(8,128)(2,1)S(1)}, u32[]{:S(2)}, u32[]{:S(2)}) collective-permute-start(bf16[27,32,128]{2,1,0:T(8,128)(2,1)S(1)} %collective-permute-done.1.refs_8_), channel_id=1, source_target_pairs={{0,4},{1,5},{2,6},{3,7},{4,0},{5,1},{6,2},{7,3},{8,12},{9,13},{10,... | collective-permute-start | bytes 663560 | tf_op jit(solution)/shard_map/ppermute | solution.py:377
  22.0 8.7 %collective-permute-start.6 = (bf16[27,32,128]{2,1,0:T(8,128)(2,1)S(1)}, bf16[27,32,128]{2,1,0:T(8,128)(2,1)S(1)}, u32[]{:S(2)}, u32[]{:S(2)}) collective-permute-start(bf16[27,32,128]{2,1,0:T(8,128)(2,1)S(1)} %collective-permute-done.1.refs_8_), channel_id=1, source_target_pairs={{0,1},{1,0},{2,3},{3,2},{4,5},{5,4},{6,7},{7,6},{8,9},{9,8},{10,11... | collective-permute-start | bytes 663560 | tf_op jit(solution)/shard_map/ppermute | solution.py:366
  22.6 0.9 %copy-start.2 = (bf16[17,32,128]{2,1,0:T(8,128)(2,1)S(1)}, bf16[17,32,128]{2,1,0:T(8,128)(2,1)}, u32[]{:S(2)}) copy-start(bf16[17,32,128]{2,1,0:T(8,128)(2,1)} %get-tuple-element.19.refs_0_) | copy-start | bytes 417796
  23.5 9.6 %copy-start = (bf16[27,128,32]{1,2,0:T(8,128)(2,1)S(1)}, bf16[27,128,32]{1,2,0:T(8,128)(2,1)}, u32[]{:S(2)}) copy-start(bf16[27,128,32]{1,2,0:T(8,128)(2,1)} %param.11) | copy-start | bytes 663556
  23.5 9.6 %copy-start.1 = (bf16[27,128,32]{1,2,0:T(8,128)(2,1)S(1)}, bf16[27,128,32]{1,2,0:T(8,128)(2,1)}, u32[]{:S(2)}) copy-start(bf16[27,128,32]{1,2,0:T(8,128)(2,1)} %param.13) | copy-start | bytes 663556
  23.5 9.6 %copy-start.3 = (bf16[17,32,128]{2,1,0:T(8,128)(2,1)S(1)}, bf16[17,32,128]{2,1,0:T(8,128)(2,1)}, u32[]{:S(2)}) copy-start(bf16[17,32,128]{2,1,0:T(8,128)(2,1)} %get-tuple-element.19.refs_0_) | copy-start | bytes 417796
  24.4 6.2 %collective-permute-start.4 = (bf16[9,32,128]{2,1,0:T(8,128)(2,1)S(1)}, bf16[9,32,128]{2,1,0:T(8,128)(2,1)S(1)}, u32[]{:S(2)}, u32[]{:S(2)}) collective-permute-start(bf16[9,32,128]{2,1,0:T(8,128)(2,1)S(1)} %get-tuple-element.26), channel_id=1, source_target_pairs={{0,4},{4,0},{8,12},{12,8},{16,20},{20,16},{24,28},{28,24},{32,36},... | collective-permute-start | bytes 221192 | tf_op jit(solution)/shard_map/ppermute | solution.py:382
  24.5 8.5 %collective-permute-start.5 = (bf16[9,32,128]{2,1,0:T(8,128)(2,1)S(1)}, bf16[9,32,128]{2,1,0:T(8,128)(2,1)S(1)}, u32[]{:S(2)}, u32[]{:S(2)}) collective-permute-start(bf16[9,32,128]{2,1,0:T(8,128)(2,1)S(1)} %get-tuple-element.27), channel_id=1, source_target_pairs={{0,124},{4,8},{8,4},{12,16},{16,12},{20,24},{24,20},{28,32},{32,28... | collective-permute-start | bytes 221192 | tf_op jit(solution)/shard_map/ppermute | solution.py:382
  44.2 4.1 %collective-permute-start.9 = (bf16[4,32,512]{2,1,0:T(8,128)(2,1)S(1)}, bf16[4,32,512]{2,1,0:T(8,128)(2,1)S(1)}, u32[]{:S(2)}, u32[]{:S(2)}) collective-permute-start(bf16[4,32,512]{2,1,0:T(8,128)(2,1)S(1)} %get-tuple-element.30), channel_id=1, source_target_pairs={{0,1},{1,0},{2,3},{3,2},{4,5},{5,4},{6,7},{7,6},{8,9},{9,8},{10,11... | collective-permute-start | bytes 393224 | tf_op jit(solution)/shard_map/ppermute | solution.py:366
  45.0 6.6 %collective-permute-start.10 = (bf16[4,32,512]{2,1,0:T(8,128)(2,1)S(1)}, bf16[4,32,512]{2,1,0:T(8,128)(2,1)S(1)}, u32[]{:S(2)}, u32[]{:S(2)}) collective-permute-start(bf16[4,32,512]{2,1,0:T(8,128)(2,1)S(1)} %get-tuple-element.31), channel_id=1, source_target_pairs={{0,2},{1,3},{2,0},{3,1},{4,6},{5,7},{6,4},{7,5},{8,10},{9,11},{10,... | collective-permute-start | bytes 393224 | tf_op jit(solution)/shard_map/ppermute | solution.py:366
  47.5 7.2 %collective-permute-start.11 = (bf16[4,32,512]{2,1,0:T(8,128)(2,1)S(1)}, bf16[4,32,512]{2,1,0:T(8,128)(2,1)S(1)}, u32[]{:S(2)}, u32[]{:S(2)}) collective-permute-start(bf16[4,32,512]{2,1,0:T(8,128)(2,1)S(1)} %get-tuple-element.32), channel_id=1, source_target_pairs={{0,3},{1,2},{2,1},{3,0},{4,7},{5,6},{6,5},{7,4},{8,11},{9,10},{10,... | collective-permute-start | bytes 393224 | tf_op jit(solution)/shard_map/ppermute | solution.py:366

commit v6 on v5

v6 whole, which is shorter than its diff:
```python
import jax
import jax.numpy as jnp
from jax import lax
from jax.experimental import pallas as pl
from jax.experimental.pallas import tpu as pltpu
from jax.sharding import PartitionSpec as P

BF16, F32 = jnp.bfloat16, jnp.float32
NONE = 8
HBM = pl.BlockSpec(memory_space=pl.ANY)
VMEM = pl.BlockSpec(memory_space=pltpu.VMEM)
SMEM = pl.BlockSpec(memory_space=pltpu.SMEM)
SPAN = {-1: (7, 0, 1), 0: (0, 1, 8), 1: (0, 9, 1)}


def offset(dz, dy, dx):
    return 9 * (dz + 1) + 3 * (dy + 1) + (dx + 1)


PIECE = 17


def split_kernel(feat, near, lists, b1, b2, lev, *refs):
    pieces, tables = refs[:4], refs[4]
    me = lax.axis_index("chan")
    values = jnp.concatenate([b1[...], b2[...], lev[...], jnp.zeros((2, 32), F32)], axis=0)
    values = jnp.concatenate([values] * 4, axis=1)
    lane = lax.broadcasted_iota(jnp.int32, (8, 128), 1)
    values = jnp.where(lane // 32 == me, values, 0.0)
    high = values.astype(BF16).astype(F32)
    values = jnp.concatenate([high, values - high, jnp.zeros((16, 128), F32)], axis=0).astype(BF16)
    for m in range(4):
        for b in range(4):
            for v in range(4):
                pieces[m][4 * v + b] = feat[me ^ m, b, :, 128 * v : 128 * v + 128]
        pieces[m][16] = values
    tables[...] = jnp.zeros((8, 128), jnp.int32)
    tables[pl.ds(0, 4), pl.ds(0, 27)] = near[...]
    tables[pl.ds(4, 2), pl.ds(0, 2)] = lists[0]
    sent = tables[...].astype(F32)
    pieces[0][17] = jnp.concatenate([sent, jnp.zeros((24, 128), F32)], axis=0).astype(BF16)


def split(features, neighbours, face_lists, b1, b2, lev):
    piece = jax.ShapeDtypeStruct((PIECE, 32, 128), BF16)
    kept = jax.ShapeDtypeStruct((PIECE + 1, 32, 128), BF16)
    return pl.pallas_call(
        split_kernel,
        out_shape=[kept, piece, piece, piece, jax.ShapeDtypeStruct((8, 128), jnp.int32)],
        in_specs=[VMEM] * 6,
        out_specs=[VMEM] * 5,
        compiler_params=pltpu.CompilerParams(vmem_limit_bytes=8 << 20),
        name="split_features",
    )(features, neighbours, face_lists, b1.reshape(1, 32), b2.reshape(1, 32), lev)


def faces_kernel(tables, *refs):
    pieces, sides, sem = refs[:4], refs[4:6], refs[6]
    odd = lax.axis_index("slab") % 2
    copies = []
    for i, out in enumerate(sides):
        tier = (odd + 1 + i) % 2
        for c in range(2):
            b = jnp.maximum(tables[4 + tier, c], 0)
            for m in range(4):
                source = pieces[m].at[12 * tier + b]
                copies.append(pltpu.make_async_copy(source, out.at[4 * c + m], sem.at[8 * i + 4 * c + m]))
        copies.append(pltpu.make_async_copy(pieces[0].at[17], out.at[8], sem.at[16 + i]))
    for copy in copies:
        copy.start()
    for copy in copies:
        copy.wait()


def faces(tables, pieces):
    side = jax.ShapeDtypeStruct((9, 32, 128), BF16)
    return pl.pallas_call(
        faces_kernel,
        out_shape=[side] * 2,
        in_specs=[SMEM] + [HBM] * 4,
        out_specs=[VMEM] * 2,
        scratch_shapes=[pltpu.SemaphoreType.DMA((18,))],
        compiler_params=pltpu.CompilerParams(vmem_limit_bytes=4 << 20),
        name="pick_faces",
    )(tables, *pieces)


def silu(v):
    return v / (1.0 + jnp.exp(-v))


def gather_padded(slots, pad, lead, slot, planes):
    x = lax.broadcasted_iota(jnp.int32, (1, 8, 128), 1)
    for dz, z_from, z_to in planes:
        for dy in (-1, 0, 1):
            y_from, y_to, n = SPAN[dy]
            parts = ([], [], [])
            for w in range(2):
                mid, left, right = (
                    slots[slot(w, offset(dz, dy, dx)), z_from, y_from : y_from + n] for dx in (0, -1, 1)
                )
                parts[0].append(pltpu.roll(jnp.where(x == 7, left, mid), 1, 1))
                parts[1].append(mid)
                parts[2].append(pltpu.roll(jnp.where(x == 0, right, mid), 7, 1))
            for d in range(3):
                tile = jnp.concatenate(parts[d], axis=1).astype(BF16)
                pad[lead, z_to, y_to : y_to + n, :, 128 * d : 128 * d + 128] = tile


OWN_PLANES = [(-1, 7, 0)] + [(0, z, z + 1) for z in range(8)] + [(1, 0, 9)]


def conv_pair(pad, lead, w):
    zero = jnp.zeros((128, 128), BF16)
    total = None
    blocks = [(zin, dy) for zin in range(4) for dy in range(3)]
    for first in range(0, 12, 2):
        left, right = [], []
        for zin, dy in blocks[first : first + 2]:
            planes = [pad[lead, zin + 2 * j, dy : dy + 8].reshape(128, 384) for j in range(4)]
            left.append(jnp.concatenate(planes, axis=0))
            for dx in range(3):
                even = w[9 * zin + 3 * dy + dx] if zin < 3 else zero
                odd = w[9 * (zin - 1) + 3 * dy + dx] if zin > 0 else zero
                right.append(jnp.concatenate([even, odd], axis=1))
        part = jnp.dot(
            jnp.concatenate(left, axis=1), jnp.concatenate(right, axis=0), preferred_element_type=F32
        )
        total = part if total is None else total + part
    return total


def conv_face(pad, w):
    total = None
    blocks = [(dz, dy) for dz in range(3) for dy in range(3)]
    for group in (blocks[0:2], blocks[2:4], blocks[4:6], blocks[6:9]):
        left, right = [], []
        for dz, dy in group:
            sides = [pad[side, dz, dy : dy + 8].reshape(128, 384) for side in range(2)]
            left.append(jnp.concatenate(sides, axis=0))
            right += [w[9 * dz + 3 * dy + dx] for dx in range(3)]
        part = jnp.dot(
            jnp.concatenate(left, axis=1), jnp.concatenate(right, axis=0), preferred_element_type=F32
        )
        total = part if total is None else total + part
    return total


def load_shards(sources, weights, order, sem):
    return [
        pltpu.make_async_copy(
            source, weights.at[:, pl.ds(pl.multiple_of(32 * order[m], 32), 32), :], sem.at[m]
        )
        for m, source in enumerate(sources)
    ]


def finish(acc, moved, tab, pair, slots):
    for j in range(4):
        for zo in range(2):
            tile = silu(acc[pair, 128 * j : 128 * j + 128, 128 * zo : 128 * zo + 128] + moved)
            tile = tile.reshape(8, 2, 8, 128)
            for w in range(2):
                b = 2 * pair + w
                slots[b, 2 * j + zo] = jnp.where(tab[b, 13] >= 0, tile[:, w], 0.0)


def first_kernel(tab, *refs):
    feat, sides, shards = refs[0:4], refs[4:6], refs[6:10]
    pad_out, shift = refs[10:12]
    fs, hs, w1, bias, sent, sent_int, tables, slots, pad, pad_face, acc, sem = refs[12:]
    me = lax.axis_index("chan")

    f_copies, t_copies = [], []
    for i in range(2):
        side = (lax.axis_index("slab") + 1 + i) % 2
        t_copies.append(pltpu.make_async_copy(sides[i].at[8, pl.ds(0, 16)], sent.at[side], sem.at[i]))
        f_copies.append(pltpu.make_async_copy(sides[i].at[pl.ds(0, 8)], hs.at[side], sem.at[2 + i]))
    for m in range(4):
        f_copies.append(pltpu.make_async_copy(feat[m].at[pl.ds(0, 16)], fs.at[m], sem.at[4 + m]))
        f_copies.append(pltpu.make_async_copy(feat[m].at[16, pl.ds(0, 16)], bias.at[m], sem.at[8 + m]))
    w_copies = [
        pltpu.make_async_copy(shards[m], w1.at[:, pl.ds(32 * m, 32), :], sem.at[12 + m]) for m in range(4)
    ]
    for copy in t_copies + f_copies + w_copies:
        copy.start()
    for copy in t_copies:
        copy.wait()
    sent_int[...] = sent[...].astype(F32).astype(jnp.int32).reshape(32, 128)
    to_scalars = pltpu.make_async_copy(sent_int, tables, sem.at[16])
    to_scalars.start()
    for copy in f_copies:
        copy.wait()

    slots[NONE] = jnp.zeros((8, 8, 8, 128), F32)
    for b in range(4):
        for v in range(4):
            brick = jnp.concatenate([fs[m, 4 * v + b] for m in range(4)], axis=0)
            slots[b, 2 * v : 2 * v + 2] = brick.T.astype(F32).reshape(2, 8, 8, 128)
    for side in range(2):
        for c in range(2):
            face = jnp.concatenate([hs[side, 4 * c + m] for m in range(4)], axis=0)
            first = 6 if side == 0 else 0
            slots[4 + 2 * side + c, first : first + 2] = face.T.astype(F32).reshape(2, 8, 8, 128)

    to_scalars.wait()

    def own(pair):
        def slot(w, k):
            t = tab[2 * pair + w, k]
            return jnp.where(t < 0, NONE, t)

        return slot

    def below(c, k):
        t = tables[0 + jnp.maximum(tables[5, c], 0), k]
        if k < 18:
            found = jnp.where(t == tables[5, 0], 4, jnp.where(t == tables[5, 1], 5, NONE))
            return jnp.where(t < 0, NONE, found)
        u = tab[4, jnp.clip(t - 6, 0, 1)]
        return jnp.where((t < 6) | (u < 0), NONE, u)

    def above(c, k):
        t = tables[16 + jnp.maximum(tables[20, c], 0), k]
        if k >= 9:
            found = jnp.where(t == tables[20, 0], 6, jnp.where(t == tables[20, 1], 7, NONE))
            return jnp.where(t < 0, NONE, found)
        u = tab[5, jnp.clip(t - 4, 0, 1)]
        return jnp.where((t < 4) | (t > 5) | (u < 0), NONE, u)

    gather_padded(slots, pad_face, 0, below, [(0, 6, 0), (0, 7, 1), (1, 0, 2)])
    gather_padded(slots, pad_face, 1, above, [(-1, 7, 0), (0, 0, 1), (0, 1, 2)])
    for pair in range(2):
        gather_padded(slots, pad, pair, own(pair), OWN_PLANES)

    values = sum(bias[m].astype(F32) for m in range(4))
    shift[...] = values[0:8] + values[8:16]
    moved = shift[0:1, :] + shift[pl.ds(2 + me, 1), :]
    for copy in w_copies:
        copy.wait()

    for pair in range(2):
        acc[pair] = conv_pair(pad, pair, w1)
        finish(acc, moved, tab, pair, slots)
    sides_out = silu(conv_face(pad_face, w1) + moved).reshape(2, 8, 2, 8, 128)
    for c in range(2):
        slots[4 + c, 7] = sides_out[0, :, c]
        slots[6 + c, 0] = sides_out[1, :, c]
    for pair in range(2):
        gather_padded(slots, pad_out, pair, own(pair), OWN_PLANES)


def convolve_first(tables, feat, sides, shards):
    return pl.pallas_call(
        first_kernel,
        out_shape=[jax.ShapeDtypeStruct((2, 10, 10, 16, 384), BF16), jax.ShapeDtypeStruct((8, 128), F32)],
        in_specs=[SMEM] + [HBM] * 10,
        out_specs=[VMEM] * 2,
        scratch_shapes=[
            pltpu.VMEM((4, 16, 32, 128), BF16),
            pltpu.VMEM((2, 8, 32, 128), BF16),
            pltpu.VMEM((27, 128, 128), BF16),
            pltpu.VMEM((4, 16, 128), BF16),
            pltpu.VMEM((2, 16, 128), BF16),
            pltpu.VMEM((32, 128), jnp.int32),
            pltpu.SMEM((32, 128), jnp.int32),
            pltpu.VMEM((9, 8, 8, 8, 128), F32),
            pltpu.VMEM((2, 10, 10, 16, 384), BF16),
            pltpu.VMEM((2, 3, 10, 16, 384), BF16),
            pltpu.VMEM((2, 512, 256), F32),
            pltpu.SemaphoreType.DMA((17,)),
        ],
        compiler_params=pltpu.CompilerParams(vmem_limit_bytes=24 << 20),
        cost_estimate=pl.CostEstimate(flops=5 * 10**9, bytes_accessed=4 * 10**6, transcendentals=10**6),
        name="convolve_first",
    )(tables, *feat, *sides, *shards)


def second_kernel(tab, pad, shift, *refs):
    shards, outs = refs[0:4], refs[4:8]
    w2, slots, acc, turned, sem = refs[8:]
    me = lax.axis_index("chan")
    w_copies = load_shards(shards, w2, [me ^ m for m in range(4)], sem)
    for copy in w_copies:
        copy.start()
    for copy in w_copies:
        copy.wait()
    for pair in range(2):
        acc[pair] = conv_pair(pad, pair, w2)
        finish(acc, shift[1:2, :], tab, pair, slots)
    for b in range(4):
        brick = slots[b].reshape(512, 128).astype(BF16).T
        for g in range(4):
            turned[g, b] = brick[32 * g : 32 * g + 32]
    for m in range(4):
        outs[m][...] = turned[me ^ m]


def convolve_second(tables, pad, shift, shards):
    piece = jax.ShapeDtypeStruct((4, 32, 512), BF16)
    return pl.pallas_call(
        second_kernel,
        out_shape=[piece] * 4,
        in_specs=[SMEM, VMEM, VMEM] + [HBM] * 4,
        out_specs=[VMEM] * 4,
        scratch_shapes=[
            pltpu.VMEM((27, 128, 128), BF16),
            pltpu.VMEM((4, 8, 8, 8, 128), F32),
            pltpu.VMEM((2, 512, 256), F32),
            pltpu.VMEM((4, 4, 32, 512), BF16),
            pltpu.SemaphoreType.DMA((4,)),
        ],
        compiler_params=pltpu.CompilerParams(vmem_limit_bytes=24 << 20),
        cost_estimate=pl.CostEstimate(flops=4 * 10**9, bytes_accessed=4 * 10**6, transcendentals=10**6),
        name="convolve_second",
    )(tables, pad, shift, *shards)


def join_kernel(*refs):
    pieces, out, sem = refs[:4], refs[4], refs[5]
    me = lax.axis_index("chan")
    copies = [pltpu.make_async_copy(pieces[m], out.at[me ^ m], sem.at[m]) for m in range(4)]
    for copy in copies:
        copy.start()
    for copy in copies:
        copy.wait()


def join(pieces):
    return pl.pallas_call(
        join_kernel,
        out_shape=jax.ShapeDtypeStruct((4, 4, 32, 512), BF16),
        in_specs=[HBM] * 4,
        out_specs=HBM,
        scratch_shapes=[pltpu.SemaphoreType.DMA((4,))],
        compiler_params=pltpu.CompilerParams(vmem_limit_bytes=8 << 20),
        name="join_levels",
    )(*pieces)


def swap(value, m):
    return lax.ppermute(value, "chan", [(i, i ^ m) for i in range(4)])


def swap_faces(value, first):
    count = lax.axis_size("slab")
    return lax.ppermute(value, "slab", [(s, (((s + first) ^ 1) - first) % count) for s in range(count)])


def shards(features, neighbours, face_lists, w_first, b_first, w_second, b_second, level_embed):
    w1, w2 = w_first.transpose(0, 2, 1), w_second.transpose(0, 2, 1)
    far = swap(w1, 2)
    own, one, two, three, tables = split(
        features, neighbours, face_lists, b_first, b_second, level_embed
    )
    far, two, three, later = lax.optimization_barrier((far, swap(two, 2), swap(three, 3), w2))
    pieces = [own, swap(one, 1), two, three]
    first = [w1, swap(w1, 1), far, swap(far, 1)]
    sides = faces(tables, pieces)
    sides = [swap_faces(sides[i], i) for i in range(2)]
    second = [w2] + [swap(later, m) for m in (1, 2, 3)]
    pad, shift = convolve_first(tables, pieces, sides, first)
    outs = convolve_second(tables, pad, shift, second)
    return join([outs[0]] + [swap(outs[m], m) for m in (1, 2, 3)])


def solution(mesh):
    placed = (
        P(None, "slab", "chan", None),
        P("slab", None),
        P("slab", None, None),
        P(None, None, "chan"),
        P("chan"),
        P(None, None, "chan"),
        P("chan"),
        P(None, "chan"),
    )
    return jax.shard_map(
        shards, mesh=mesh, in_specs=placed, out_specs=P(None, "slab", "chan", None), check_vma=False
    )
```

time: 55.6 us -> 56.7 us (1.020)
  local copies, waits for them, and re-layouts: 0.92 us -> 5.33 us
  Pallas kernels: 15.3 us -> 12.8 us
  waiting for transfers between devices: 17.3 us -> 15.9 us
    unnamed x12 -> x16, local copies, waits for them, and re-layouts: 0.92 us -> 5.33 us
    ppermute x8 -> x12, starting transfers between devices: 12.5 us -> 15.8 us  [swap(): return lax.ppermute(value, 'chan', [(i, i ^ m) for i in range(4)])]
    ppermute x2 -> x0, starting transfers between devices: 3.12 us -> none  [swap_slabs(): return lax.ppermute(value, ('slab', 'chan'), pairs)]
    pallas_call x3 -> x4, Pallas kernels: 14.5 us -> 12 us  [the longest x1 7.17 us: convolve_first(): pl.pallas_call(first_kernel, out_shape=[jax.ShapeDtypeStruct((2, 10, 10,...]
    ppermute x2, waiting for transfers between devices: 2.41 us -> 0.01 us  [swap_faces(): lax.ppermute(value, 'slab', [(s, ((s + first ^ 1) - first) % count) for s...]
    ppermute x8 -> x12, waiting for transfers between devices: 14.9 us -> 15.9 us  [swap(): return lax.ppermute(value, 'chan', [(i, i ^ m) for i in range(4)])]
  transfers between devices with their start and end apart: 12 -> 14, of which waited for: 5 -> 6; matrix products, arithmetic and copies ran while one was open for 0% -> 0% of each run, Pallas kernels for 2% -> 15%
where the time goes in v6:
time: 56.7 us; the launch traced here: 56.4 us
  starting transfers between devices  22.3 us (39%)
  waiting for transfers between devices  15.9 us (28%)
  Pallas kernels  12.8 us (23%)
  local copies, waits for them, and re-layouts  5.33 us (9%)
    ppermute x12, waiting for transfers between devices, swap(): return lax.ppermute(value, 'chan', [(i, i ^ m) for i in range(4)])  15.9 us
    ppermute x12, starting transfers between devices, swap(): return lax.ppermute(value, 'chan', [(i, i ^ m) for i in range(4)])  15.8 us
    pallas_call x1, Pallas kernels, convolve_first(): pl.pallas_call(first_kernel, out_shape=[jax.ShapeDtypeStruct((2, 10, 10,...  7.17 us
    ppermute x2, starting transfers between devices, swap_faces(): lax.ppermute(value, 'slab', [(s, ((s + first ^ 1) - first) % count) for s...  6.44 us
    unnamed x16, local copies, waits for them, and re-layouts  5.33 us
    pallas_call x1, Pallas kernels, convolve_second(): pl.pallas_call(second_kernel, out_shape=[piece] * 4, in_specs=[SMEM, VMEM...  3.69 us
  transfers between devices with their start and end apart: 14, of which 6 were waited for; matrix products, arithmetic and copies ran while one was open for 0% of the time, Pallas kernels for 15%

profile of v6, /device:TPU:1, one launch (start us, length us, event | category | flops | bytes accessed | tf_op | source)
XLA Modules:
  0.0 56.4 jit_solution(3176221021571159419)
XLA Ops:
  0.0 3.6 %collective-permute-start.1 = (bf16[27,32,128]{2,1,0:T(8,128)(2,1)}, bf16[27,32,128]{2,1,0:T(8,128)(2,1)S(1)}, u32[]{:S(2)}, u32[]{:S(2)}) collective-permute-start(bf16[27,32,128]{2,1,0:T(8,128)(2,1)} %bitcast.6), channel_id=1, source_target_pairs={{0,2},{1,3},{2,0},{3,1},{4,6},{5,7},{6,4},{7,5},{8,10},{9,11},{10,... | collective-permute-start | bytes 663560 | tf_op jit(solution)/shard_map/ppermute | solution.py:342
  3.6 0.0 copy-start
  3.6 1.0 %copy-done = bf16[4,4,32,512]{3,2,1,0:T(8,128)(2,1)S(1)} copy-done((bf16[4,4,32,512]{3,2,1,0:T(8,128)(2,1)S(1)}, bf16[4,4,32,512]{3,2,1,0:T(8,128)(2,1)}, u32[]{:S(2)}) %copy-start) | copy-done | bytes 524312
  4.6 0.0 copy-start.1
  4.6 0.7 %copy-done.1 = s32[4,27]{1,0:T(4,128)S(1)} copy-done((s32[4,27]{1,0:T(4,128)S(1)}, s32[4,27]{1,0:T(4,128)}, u32[]{:S(2)}) %copy-start.1) | copy-done | bytes 456
  5.3 0.0 copy-start.2
  5.3 0.7 %copy-done.2 = f32[4,32]{1,0:T(4,128)S(1)} copy-done((f32[4,32]{1,0:T(4,128)S(1)}, f32[4,32]{1,0:T(4,128)}, u32[]{:S(2)}) %copy-start.2) | copy-done | bytes 536
  6.0 0.0 copy-start.3
  6.0 0.7 %copy-done.3 = s32[1,2,2]{2,1,0:T(2,128)S(1)} copy-done((s32[1,2,2]{2,1,0:T(2,128)S(1)}, s32[1,2,2]{2,1,0:T(2,128)}, u32[]{:S(2)}) %copy-start.3) | copy-done | bytes 40
  6.7 0.0 copy-start.4
  6.7 0.7 %copy-done.4 = f32[32]{0:T(128)S(1)} copy-done((f32[32]{0:T(128)S(1)}, f32[32]{0:T(128)}, u32[]{:S(2)}) %copy-start.4) | copy-done | bytes 152
  7.3 0.0 copy-start.5
  7.3 0.7 %copy-done.5 = f32[32]{0:T(128)S(1)} copy-done((f32[32]{0:T(128)S(1)}, f32[32]{0:T(128)}, u32[]{:S(2)}) %copy-start.5) | copy-done | bytes 152
  8.0 0.1 split_features.1
  8.1 0.1 collective-permute-start.2
  8.2 4.1 %collective-permute-start.3 = (bf16[17,32,128]{2,1,0:T(8,128)(2,1)S(1)}, bf16[17,32,128]{2,1,0:T(8,128)(2,1)S(1)}, u32[]{:S(2)}, u32[]{:S(2)}) collective-permute-start(bf16[17,32,128]{2,1,0:T(8,128)(2,1)S(1)} %get-tuple-element.26), channel_id=1, source_target_pairs={{0,3},{1,2},{2,1},{3,0},{4,7},{5,6},{6,5},{7,4},{8,11},{9,10},{10,... | collective-permute-start | bytes 417800 | tf_op jit(solution)/shard_map/ppermute | solution.py:342
  12.2 0.0 collective-permute-start.6
  12.3 1.6 %collective-permute-done.2.refs_2_ = bf16[17,32,128]{2,1,0:T(8,128)(2,1)S(1)} collective-permute-done((bf16[17,32,128]{2,1,0:T(8,128)(2,1)S(1)}, bf16[17,32,128]{2,1,0:T(8,128)(2,1)S(1)}, u32[]{:S(2)}, u32[]{:S(2)}) %collective-permute-start.2) | collective-permute-done | bytes 139296 | tf_op jit(solution)/shard_map/ppermute | solution.py:342
  13.9 4.2 %collective-permute-done.3.refs_3_ = bf16[17,32,128]{2,1,0:T(8,128)(2,1)S(1)} collective-permute-done((bf16[17,32,128]{2,1,0:T(8,128)(2,1)S(1)}, bf16[17,32,128]{2,1,0:T(8,128)(2,1)S(1)}, u32[]{:S(2)}, u32[]{:S(2)}) %collective-permute-start.3) | collective-permute-done | bytes 139296 | tf_op jit(solution)/shard_map/ppermute | solution.py:342
  18.0 0.0 collective-permute-done.1.refs_8_
  18.0 0.0 collective-permute-start.7
  18.1 0.5 collective-permute-start
  18.6 1.2 %collective-permute-done.refs_1_ = bf16[17,32,128]{2,1,0:T(8,128)(2,1)S(1)} collective-permute-done((bf16[17,32,128]{2,1,0:T(8,128)(2,1)S(1)}, bf16[17,32,128]{2,1,0:T(8,128)(2,1)S(1)}, u32[]{:S(2)}, u32[]{:S(2)}) %collective-permute-start) | collective-permute-done | bytes 139296 | tf_op jit(solution)/shard_map/ppermute | solution.py:342
  19.7 0.0 copy-start.7
  19.7 1.0 %pick_faces.1 = (bf16[9,32,128]{2,1,0:T(8,128)(2,1)S(1)}, bf16[9,32,128]{2,1,0:T(8,128)(2,1)S(1)}) custom-call(s32[8,128]{1,0:T(8,128)S(1)} %get-tuple-element.22.tables.tab, bf16[18,32,128]{2,1,0:T(8,128)(2,1)S(1)} %get-tuple-element.23.refs_0_, bf16[17,32,128]{2,1,0:T(8,128)(2,1)S(1)} %collective-permute-done.refs_1_, ...), custom_call_target="tpu_custom_call" | custom-call | tf_op jit(solution)/shard_map/pick_faces/pallas_call | solution.py:77
  20.7 1.7 %collective-permute-start.4 = (bf16[9,32,128]{2,1,0:T(8,128)(2,1)S(1)}, bf16[9,32,128]{2,1,0:T(8,128)(2,1)S(1)}, u32[]{:S(2)}, u32[]{:S(2)}) collective-permute-start(bf16[9,32,128]{2,1,0:T(8,128)(2,1)S(1)} %get-tuple-element.29), channel_id=1, source_target_pairs={{0,4},{4,0},{8,12},{12,8},{16,20},{20,16},{24,28},{28,24},{32,36},... | collective-permute-start | bytes 221192 | tf_op jit(solution)/shard_map/ppermute | solution.py:347
  22.5 4.7 %collective-permute-start.5 = (bf16[9,32,128]{2,1,0:T(8,128)(2,1)S(1)}, bf16[9,32,128]{2,1,0:T(8,128)(2,1)S(1)}, u32[]{:S(2)}, u32[]{:S(2)}) collective-permute-start(bf16[9,32,128]{2,1,0:T(8,128)(2,1)S(1)} %get-tuple-element.30), channel_id=1, source_target_pairs={{0,124},{4,8},{8,4},{12,16},{16,12},{20,24},{24,20},{28,32},{32,28... | collective-permute-start | bytes 221192 | tf_op jit(solution)/shard_map/ppermute | solution.py:347
  27.2 2.9 %collective-permute-start.10 = (bf16[27,32,128]{2,1,0:T(8,128)(2,1)}, bf16[27,32,128]{2,1,0:T(8,128)(2,1)S(1)}, u32[]{:S(2)}, u32[]{:S(2)}) collective-permute-start(bf16[27,32,128]{2,1,0:T(8,128)(2,1)} %bitcast.9), channel_id=1, source_target_pairs={{0,3},{1,2},{2,1},{3,0},{4,7},{5,6},{6,5},{7,4},{8,11},{9,10},{10,... | collective-permute-start | bytes 663560 | tf_op jit(solution)/shard_map/ppermute | solution.py:342
  30.1 0.0 collective-permute-done.6.refs_7_
  30.1 0.0 collective-permute-start.8
  30.1 0.0 collective-permute-done.4.refs_4_
  30.1 0.8 %collective-permute-start.9 = (bf16[27,32,128]{2,1,0:T(8,128)(2,1)}, bf16[27,32,128]{2,1,0:T(8,128)(2,1)S(1)}, u32[]{:S(2)}, u32[]{:S(2)}) collective-permute-start(bf16[27,32,128]{2,1,0:T(8,128)(2,1)} %bitcast.11), channel_id=1, source_target_pairs={{0,2},{1,3},{2,0},{3,1},{4,6},{5,7},{6,4},{7,5},{8,10},{9,11},{10,... | collective-permute-start | bytes 663560 | tf_op jit(solution)/shard_map/ppermute | solution.py:342
  30.9 0.0 collective-permute-done.5.refs_5_
  30.9 0.0 collective-permute-done.7.refs_9_
  30.9 0.0 copy-start.6
  30.9 0.9 %copy-done.6 = bf16[27,128,32]{1,2,0:T(8,128)(2,1)S(1)} copy-done((bf16[27,128,32]{1,2,0:T(8,128)(2,1)S(1)}, bf16[27,128,32]{1,2,0:T(8,128)(2,1)}, u32[]{:S(2)}) %copy-start.6) | copy-done | bytes 221208
  31.8 7.2 %convolve_first.1 = (bf16[2,10,10,16,384]{4,3,2,1,0:T(8,128)(2,1)S(1)}, f32[8,128]{1,0:T(8,128)S(1)}) custom-call(s32[8,128]{1,0:T(8,128)S(1)} %get-tuple-element.22.tables.tab, bf16[18,32,128]{2,1,0:T(8,128)(2,1)S(1)} %get-tuple-element.23.refs_0_, bf16[17,32,128]{2,1,0:T(8,128)(2,1)S(1)} %collective-permute-done.refs_1_, ...), custom_call_target="tpu_custom_call" | custom-call | flops 5000000000 | bytes 4000000 | tf_op jit(solution)/shard_map/convolve_first/pallas_call | solution.py:254
  39.0 0.0 collective-permute-done.10.refs_3_
  39.0 0.0 collective-permute-done.8.refs_1_
  39.0 2.6 %collective-permute-done.9.refs_2_ = bf16[27,32,128]{2,1,0:T(8,128)(2,1)S(1)} collective-permute-done((bf16[27,32,128]{2,1,0:T(8,128)(2,1)}, bf16[27,32,128]{2,1,0:T(8,128)(2,1)S(1)}, u32[]{:S(2)}, u32[]{:S(2)}) %collective-permute-start.9) | collective-permute-done | bytes 221216 | tf_op jit(solution)/shard_map/ppermute | solution.py:342
  41.7 0.0 copy-done.7
  41.7 3.7 %convolve_second.1 = (bf16[4,32,512]{2,1,0:T(8,128)(2,1)S(1)}, bf16[4,32,512]{2,1,0:T(8,128)(2,1)S(1)}, bf16[4,32,512]{2,1,0:T(8,128)(2,1)S(1)}, bf16[4,32,512]{2,1,0:T(8,128)(2,1)S(1)}) custom-call(s32[8,128]{1,0:T(8,128)S(1)} %get-tuple-element.22.tables.tab, bf16[2,10,10,16,384]{4,3,2,1,0:T(8,128)(2,1)S(1)} %get-tuple-element.32.pad, ...), custom_call_target="tpu_custom_call" | custom-call | flops 4000000000 | bytes 4000000 | tf_op jit(solution)/shard_map/convolve_second/pallas_call | solution.py:301
  45.4 0.7 %collective-permute-start.11 = (bf16[4,32,512]{2,1,0:T(8,128)(2,1)S(1)}, bf16[4,32,512]{2,1,0:T(8,128)(2,1)S(1)}, u32[]{:S(2)}, u32[]{:S(2)}) collective-permute-start(bf16[4,32,512]{2,1,0:T(8,128)(2,1)S(1)} %get-tuple-element.36), channel_id=1, source_target_pairs={{0,1},{1,0},{2,3},{3,2},{4,5},{5,4},{6,7},{7,6},{8,9},{9,8},{10,11... | collective-permute-start | bytes 393224 | tf_op jit(solution)/shard_map/ppermute | solution.py:342
  46.0 1.7 %collective-permute-start.12 = (bf16[4,32,512]{2,1,0:T(8,128)(2,1)S(1)}, bf16[4,32,512]{2,1,0:T(8,128)(2,1)S(1)}, u32[]{:S(2)}, u32[]{:S(2)}) collective-permute-start(bf16[4,32,512]{2,1,0:T(8,128)(2,1)S(1)} %get-tuple-element.37), channel_id=1, source_target_pairs={{0,2},{1,3},{2,0},{3,1},{4,6},{5,7},{6,4},{7,5},{8,10},{9,11},{10,... | collective-permute-start | bytes 393224 | tf_op jit(solution)/shard_map/ppermute | solution.py:342
  47.8 1.5 %collective-permute-start.13 = (bf16[4,32,512]{2,1,0:T(8,128)(2,1)S(1)}, bf16[4,32,512]{2,1,0:T(8,128)(2,1)S(1)}, u32[]{:S(2)}, u32[]{:S(2)}) collective-permute-start(bf16[4,32,512]{2,1,0:T(8,128)(2,1)S(1)} %get-tuple-element.38), channel_id=1, source_target_pairs={{0,3},{1,2},{2,1},{3,0},{4,7},{5,6},{6,5},{7,4},{8,11},{9,10},{10,... | collective-permute-start | bytes 393224 | tf_op jit(solution)/shard_map/ppermute | solution.py:342
  49.3 0.0 collective-permute-done.11.refs_1_
  49.3 3.3 %collective-permute-done.12.refs_2_ = bf16[4,32,512]{2,1,0:T(8,128)(2,1)S(1)} collective-permute-done((bf16[4,32,512]{2,1,0:T(8,128)(2,1)S(1)}, bf16[4,32,512]{2,1,0:T(8,128)(2,1)S(1)}, u32[]{:S(2)}, u32[]{:S(2)}) %collective-permute-start.12) | collective-permute-done | bytes 131104 | tf_op jit(solution)/shard_map/ppermute | solution.py:342
  52.6 3.0 %collective-permute-done.13.refs_3_ = bf16[4,32,512]{2,1,0:T(8,128)(2,1)S(1)} collective-permute-done((bf16[4,32,512]{2,1,0:T(8,128)(2,1)S(1)}, bf16[4,32,512]{2,1,0:T(8,128)(2,1)S(1)}, u32[]{:S(2)}, u32[]{:S(2)}) %collective-permute-start.13) | collective-permute-done | bytes 131104 | tf_op jit(solution)/shard_map/ppermute | solution.py:342
  55.6 0.8 %join_levels.1 = bf16[4,4,32,512]{3,2,1,0:T(8,128)(2,1)} custom-call(bf16[4,32,512]{2,1,0:T(8,128)(2,1)S(1)} %get-tuple-element.35.refs_0_, bf16[4,32,512]{2,1,0:T(8,128)(2,1)S(1)} %collective-permute-done.11.refs_1_, bf16[4,32,512]{2,1,0:T(8,128)(2,1)S(1)} %collective-permute-done.12.refs_2_, bf16[4,32,512]{2,1,0:T(8,128)(2,1)S(1)} %collective-permute-done.13.refs_3_), custom_call_target="tpu_custom_call" | custom-call | tf_op jit(solution)/shard_map/join_levels/pallas_call | solution.py:330
Async XLA Ops:
  0.0 18.0 %collective-permute-start.1 = (bf16[27,32,128]{2,1,0:T(8,128)(2,1)}, bf16[27,32,128]{2,1,0:T(8,128)(2,1)S(1)}, u32[]{:S(2)}, u32[]{:S(2)}) collective-permute-start(bf16[27,32,128]{2,1,0:T(8,128)(2,1)} %bitcast.6), channel_id=1, source_target_pairs={{0,2},{1,3},{2,0},{3,1},{4,6},{5,7},{6,4},{7,5},{8,10},{9,11},{10,... | collective-permute-start | bytes 663560 | tf_op jit(solution)/shard_map/ppermute | solution.py:342
  3.6 1.0 %copy-start = (bf16[4,4,32,512]{3,2,1,0:T(8,128)(2,1)S(1)}, bf16[4,4,32,512]{3,2,1,0:T(8,128)(2,1)}, u32[]{:S(2)}) copy-start(bf16[4,4,32,512]{3,2,1,0:T(8,128)(2,1)} %feat.1) | copy-start | bytes 1572868
  4.6 0.7 %copy-start.1 = (s32[4,27]{1,0:T(4,128)S(1)}, s32[4,27]{1,0:T(4,128)}, u32[]{:S(2)}) copy-start(s32[4,27]{1,0:T(4,128)} %near.1) | copy-start | bytes 1300
  5.3 0.7 %copy-start.2 = (f32[4,32]{1,0:T(4,128)S(1)}, f32[4,32]{1,0:T(4,128)}, u32[]{:S(2)}) copy-start(f32[4,32]{1,0:T(4,128)} %lev.1) | copy-start | bytes 1540
  6.0 0.7 %copy-start.3 = (s32[1,2,2]{2,1,0:T(2,128)S(1)}, s32[1,2,2]{2,1,0:T(2,128)}, u32[]{:S(2)}) copy-start(s32[1,2,2]{2,1,0:T(2,128)} %lists.1) | copy-start | bytes 52
  6.7 0.7 %copy-start.4 = (f32[32]{0:T(128)S(1)}, f32[32]{0:T(128)}, u32[]{:S(2)}) copy-start(f32[32]{0:T(128)} %param.12) | copy-start | bytes 388
  7.3 0.7 %copy-start.5 = (f32[32]{0:T(128)S(1)}, f32[32]{0:T(128)}, u32[]{:S(2)}) copy-start(f32[32]{0:T(128)} %param.14) | copy-start | bytes 388
  8.1 5.8 %collective-permute-start.2 = (bf16[17,32,128]{2,1,0:T(8,128)(2,1)S(1)}, bf16[17,32,128]{2,1,0:T(8,128)(2,1)S(1)}, u32[]{:S(2)}, u32[]{:S(2)}) collective-permute-start(bf16[17,32,128]{2,1,0:T(8,128)(2,1)S(1)} %get-tuple-element.25), channel_id=1, source_target_pairs={{0,2},{1,3},{2,0},{3,1},{4,6},{5,7},{6,4},{7,5},{8,10},{9,11},{10,... | collective-permute-start | bytes 417800 | tf_op jit(solution)/shard_map/ppermute | solution.py:342
  8.2 9.9 %collective-permute-start.3 = (bf16[17,32,128]{2,1,0:T(8,128)(2,1)S(1)}, bf16[17,32,128]{2,1,0:T(8,128)(2,1)S(1)}, u32[]{:S(2)}, u32[]{:S(2)}) collective-permute-start(bf16[17,32,128]{2,1,0:T(8,128)(2,1)S(1)} %get-tuple-element.26), channel_id=1, source_target_pairs={{0,3},{1,2},{2,1},{3,0},{4,7},{5,6},{6,5},{7,4},{8,11},{9,10},{10,... | collective-permute-start | bytes 417800 | tf_op jit(solution)/shard_map/ppermute | solution.py:342
  12.2 17.8 %collective-permute-start.6 = (bf16[27,32,128]{2,1,0:T(8,128)(2,1)}, bf16[27,32,128]{2,1,0:T(8,128)(2,1)S(1)}, u32[]{:S(2)}, u32[]{:S(2)}) collective-permute-start(bf16[27,32,128]{2,1,0:T(8,128)(2,1)} %bitcast.7), channel_id=1, source_target_pairs={{0,1},{1,0},{2,3},{3,2},{4,5},{5,4},{6,7},{7,6},{8,9},{9,8},{10,11... | collective-permute-start | bytes 663560 | tf_op jit(solution)/shard_map/ppermute | solution.py:342
  18.0 12.8 %collective-permute-start.7 = (bf16[27,32,128]{2,1,0:T(8,128)(2,1)S(1)}, bf16[27,32,128]{2,1,0:T(8,128)(2,1)S(1)}, u32[]{:S(2)}, u32[]{:S(2)}) collective-permute-start(bf16[27,32,128]{2,1,0:T(8,128)(2,1)S(1)} %collective-permute-done.1.refs_8_), channel_id=1, source_target_pairs={{0,1},{1,0},{2,3},{3,2},{4,5},{5,4},{6,7},{7,6},{8,9},{9,8},{10,11... | collective-permute-start | bytes 663560 | tf_op jit(solution)/shard_map/ppermute | solution.py:342
  18.1 1.7 %collective-permute-start = (bf16[17,32,128]{2,1,0:T(8,128)(2,1)S(1)}, bf16[17,32,128]{2,1,0:T(8,128)(2,1)S(1)}, u32[]{:S(2)}, u32[]{:S(2)}) collective-permute-start(bf16[17,32,128]{2,1,0:T(8,128)(2,1)S(1)} %get-tuple-element.24), channel_id=1, source_target_pairs={{0,1},{1,0},{2,3},{3,2},{4,5},{5,4},{6,7},{7,6},{8,9},{9,8},{10,11... | collective-permute-start | bytes 417800 | tf_op jit(solution)/shard_map/ppermute | solution.py:342
  19.7 22.0 %copy-start.7 = (bf16[27,128,32]{1,2,0:T(8,128)(2,1)S(1)}, bf16[27,128,32]{1,2,0:T(8,128)(2,1)}, u32[]{:S(2)}) copy-start(bf16[27,128,32]{1,2,0:T(8,128)(2,1)} %param.13) | copy-start | bytes 663556
  20.7 9.3 %collective-permute-start.4 = (bf16[9,32,128]{2,1,0:T(8,128)(2,1)S(1)}, bf16[9,32,128]{2,1,0:T(8,128)(2,1)S(1)}, u32[]{:S(2)}, u32[]{:S(2)}) collective-permute-start(bf16[9,32,128]{2,1,0:T(8,128)(2,1)S(1)} %get-tuple-element.29), channel_id=1, source_target_pairs={{0,4},{4,0},{8,12},{12,8},{16,20},{20,16},{24,28},{28,24},{32,36},... | collective-permute-start | bytes 221192 | tf_op jit(solution)/shard_map/ppermute | solution.py:347
  22.5 8.4 %collective-permute-start.5 = (bf16[9,32,128]{2,1,0:T(8,128)(2,1)S(1)}, bf16[9,32,128]{2,1,0:T(8,128)(2,1)S(1)}, u32[]{:S(2)}, u32[]{:S(2)}) collective-permute-start(bf16[9,32,128]{2,1,0:T(8,128)(2,1)S(1)} %get-tuple-element.30), channel_id=1, source_target_pairs={{0,124},{4,8},{8,4},{12,16},{16,12},{20,24},{24,20},{28,32},{32,28... | collective-permute-start | bytes 221192 | tf_op jit(solution)/shard_map/ppermute | solution.py:347
  27.2 11.8 %collective-permute-start.10 = (bf16[27,32,128]{2,1,0:T(8,128)(2,1)}, bf16[27,32,128]{2,1,0:T(8,128)(2,1)S(1)}, u32[]{:S(2)}, u32[]{:S(2)}) collective-permute-start(bf16[27,32,128]{2,1,0:T(8,128)(2,1)} %bitcast.9), channel_id=1, source_target_pairs={{0,3},{1,2},{2,1},{3,0},{4,7},{5,6},{6,5},{7,4},{8,11},{9,10},{10,... | collective-permute-start | bytes 663560 | tf_op jit(solution)/shard_map/ppermute | solution.py:342
  30.1 9.0 %collective-permute-start.8 = (bf16[27,32,128]{2,1,0:T(8,128)(2,1)}, bf16[27,32,128]{2,1,0:T(8,128)(2,1)S(1)}, u32[]{:S(2)}, u32[]{:S(2)}) collective-permute-start(bf16[27,32,128]{2,1,0:T(8,128)(2,1)} %bitcast.10), channel_id=1, source_target_pairs={{0,1},{1,0},{2,3},{3,2},{4,5},{5,4},{6,7},{7,6},{8,9},{9,8},{10,11... | collective-permute-start | bytes 663560 | tf_op jit(solution)/shard_map/ppermute | solution.py:342
  30.1 11.6 %collective-permute-start.9 = (bf16[27,32,128]{2,1,0:T(8,128)(2,1)}, bf16[27,32,128]{2,1,0:T(8,128)(2,1)S(1)}, u32[]{:S(2)}, u32[]{:S(2)}) collective-permute-start(bf16[27,32,128]{2,1,0:T(8,128)(2,1)} %bitcast.11), channel_id=1, source_target_pairs={{0,2},{1,3},{2,0},{3,1},{4,6},{5,7},{6,4},{7,5},{8,10},{9,11},{10,... | collective-permute-start | bytes 663560 | tf_op jit(solution)/shard_map/ppermute | solution.py:342
  30.9 0.9 %copy-start.6 = (bf16[27,128,32]{1,2,0:T(8,128)(2,1)S(1)}, bf16[27,128,32]{1,2,0:T(8,128)(2,1)}, u32[]{:S(2)}) copy-start(bf16[27,128,32]{1,2,0:T(8,128)(2,1)} %param.11) | copy-start | bytes 663556
  45.4 3.9 %collective-permute-start.11 = (bf16[4,32,512]{2,1,0:T(8,128)(2,1)S(1)}, bf16[4,32,512]{2,1,0:T(8,128)(2,1)S(1)}, u32[]{:S(2)}, u32[]{:S(2)}) collective-permute-start(bf16[4,32,512]{2,1,0:T(8,128)(2,1)S(1)} %get-tuple-element.36), channel_id=1, source_target_pairs={{0,1},{1,0},{2,3},{3,2},{4,5},{5,4},{6,7},{7,6},{8,9},{9,8},{10,11... | collective-permute-start | bytes 393224 | tf_op jit(solution)/shard_map/ppermute | solution.py:342
  46.0 6.6 %collective-permute-start.12 = (bf16[4,32,512]{2,1,0:T(8,128)(2,1)S(1)}, bf16[4,32,512]{2,1,0:T(8,128)(2,1)S(1)}, u32[]{:S(2)}, u32[]{:S(2)}) collective-permute-start(bf16[4,32,512]{2,1,0:T(8,128)(2,1)S(1)} %get-tuple-element.37), channel_id=1, source_target_pairs={{0,2},{1,3},{2,0},{3,1},{4,6},{5,7},{6,4},{7,5},{8,10},{9,11},{10,... | collective-permute-start | bytes 393224 | tf_op jit(solution)/shard_map/ppermute | solution.py:342
  47.8 7.8 %collective-permute-start.13 = (bf16[4,32,512]{2,1,0:T(8,128)(2,1)S(1)}, bf16[4,32,512]{2,1,0:T(8,128)(2,1)S(1)}, u32[]{:S(2)}, u32[]{:S(2)}) collective-permute-start(bf16[4,32,512]{2,1,0:T(8,128)(2,1)S(1)} %get-tuple-element.38), channel_id=1, source_target_pairs={{0,3},{1,2},{2,1},{3,0},{4,7},{5,6},{6,5},{7,4},{8,11},{9,10},{10,... | collective-permute-start | bytes 393224 | tf_op jit(solution)/shard_map/ppermute | solution.py:342

commit v7 on v6

--- a/solution.py
+++ b/solution.py
@@ -271,7 +271,7 @@
             pltpu.SemaphoreType.DMA((17,)),
         ],
         compiler_params=pltpu.CompilerParams(vmem_limit_bytes=24 << 20),
-        cost_estimate=pl.CostEstimate(flops=5 * 10**9, bytes_accessed=4 * 10**6, transcendentals=10**6),
+        cost_estimate=pl.CostEstimate(flops=10**6, bytes_accessed=10**4, transcendentals=0),
         name="convolve_first",
     )(tables, *feat, *sides, *shards)
 
@@ -353,12 +353,14 @@
     own, one, two, three, tables = split(
         features, neighbours, face_lists, b_first, b_second, level_embed
     )
-    far, two, three, later = lax.optimization_barrier((far, swap(two, 2), swap(three, 3), w2))
-    pieces = [own, swap(one, 1), two, three]
+    far, one, two, three, later, near = lax.optimization_barrier(
+        (far, swap(one, 1), swap(two, 2), swap(three, 3), w2, swap(w2, 1))
+    )
+    pieces = [own, one, two, three]
     first = [w1, swap(w1, 1), far, swap(far, 1)]
     sides = faces(tables, pieces)
     sides = [swap_faces(sides[i], i) for i in range(2)]
-    second = [w2] + [swap(later, m) for m in (1, 2, 3)]
+    second = [w2, near, swap(later, 2), swap(later, 3)]
     pad, shift = convolve_first(tables, pieces, sides, first)
     outs = convolve_second(tables, pad, shift, second)
     return join([outs[0]] + [swap(outs[m], m) for m in (1, 2, 3)])

time: 56.7 us -> 62.4 us (1.10)
  waiting for transfers between devices: 15.9 us -> 21.9 us
    ppermute x2, waiting for transfers between devices: 0.01 us -> 9.13 us  [swap_faces(): lax.ppermute(value, 'slab', [(s, ((s + first ^ 1) - first) % count) for s...]
    ppermute x12, waiting for transfers between devices: 15.9 us -> 12.7 us  [swap(): return lax.ppermute(value, 'chan', [(i, i ^ m) for i in range(4)])]
  transfers between devices with their start and end apart: 14 -> 14, of which waited for: 6 -> 5; matrix products, arithmetic and copies ran while one was open for 0% -> 0% of each run, Pallas kernels for 15% -> 13%
where the time goes in v7:
time: 62.4 us; the launch traced here: 62.2 us
  starting transfers between devices  22.1 us (35%)
  waiting for transfers between devices  21.9 us (35%)
  Pallas kernels  12.8 us (21%)
  local copies, waits for them, and re-layouts  5.33 us (9%)
    ppermute x12, starting transfers between devices, swap(): return lax.ppermute(value, 'chan', [(i, i ^ m) for i in range(4)])  15.6 us
    ppermute x12, waiting for transfers between devices, swap(): return lax.ppermute(value, 'chan', [(i, i ^ m) for i in range(4)])  12.7 us
    ppermute x2, waiting for transfers between devices, swap_faces(): lax.ppermute(value, 'slab', [(s, ((s + first ^ 1) - first) % count) for s...  9.13 us
    pallas_call x1, Pallas kernels, convolve_first(): pl.pallas_call(first_kernel, out_shape=[jax.ShapeDtypeStruct((2, 10, 10,...  7.17 us
    ppermute x2, starting transfers between devices, swap_faces(): lax.ppermute(value, 'slab', [(s, ((s + first ^ 1) - first) % count) for s...  6.44 us
    unnamed x16, local copies, waits for them, and re-layouts  5.33 us
    pallas_call x1, Pallas kernels, convolve_second(): pl.pallas_call(second_kernel, out_shape=[piece] * 4, in_specs=[SMEM, VMEM...  3.7 us
  transfers between devices with their start and end apart: 14, of which 5 were waited for; matrix products, arithmetic and copies ran while one was open for 0% of the time, Pallas kernels for 13%

profile of v7, /device:TPU:1, one launch (start us, length us, event | category | flops | bytes accessed | tf_op | source)
XLA Modules:
  0.0 62.2 jit_solution(1098896239825277136)
XLA Ops:
  0.0 3.6 %collective-permute-start = (bf16[27,32,128]{2,1,0:T(8,128)(2,1)}, bf16[27,32,128]{2,1,0:T(8,128)(2,1)S(1)}, u32[]{:S(2)}, u32[]{:S(2)}) collective-permute-start(bf16[27,32,128]{2,1,0:T(8,128)(2,1)} %bitcast.4), channel_id=1, source_target_pairs={{0,2},{1,3},{2,0},{3,1},{4,6},{5,7},{6,4},{7,5},{8,10},{9,11},{10,... | collective-permute-start | bytes 663560 | tf_op jit(solution)/shard_map/ppermute | solution.py:342
  3.6 1.0 %collective-permute-start.4 = (bf16[27,32,128]{2,1,0:T(8,128)(2,1)}, bf16[27,32,128]{2,1,0:T(8,128)(2,1)S(1)}, u32[]{:S(2)}, u32[]{:S(2)}) collective-permute-start(bf16[27,32,128]{2,1,0:T(8,128)(2,1)} %bitcast.9), channel_id=1, source_target_pairs={{0,1},{1,0},{2,3},{3,2},{4,5},{5,4},{6,7},{7,6},{8,9},{9,8},{10,11... | collective-permute-start | bytes 663560 | tf_op jit(solution)/shard_map/ppermute | solution.py:342
  4.5 0.0 copy-start
  4.5 1.0 %copy-done = bf16[4,4,32,512]{3,2,1,0:T(8,128)(2,1)S(1)} copy-done((bf16[4,4,32,512]{3,2,1,0:T(8,128)(2,1)S(1)}, bf16[4,4,32,512]{3,2,1,0:T(8,128)(2,1)}, u32[]{:S(2)}) %copy-start) | copy-done | bytes 524312
  5.6 0.0 copy-start.2
  5.6 0.7 %copy-done.2 = s32[4,27]{1,0:T(4,128)S(1)} copy-done((s32[4,27]{1,0:T(4,128)S(1)}, s32[4,27]{1,0:T(4,128)}, u32[]{:S(2)}) %copy-start.2) | copy-done | bytes 456
  6.3 0.0 copy-start.3
  6.3 0.7 %copy-done.3 = f32[4,32]{1,0:T(4,128)S(1)} copy-done((f32[4,32]{1,0:T(4,128)S(1)}, f32[4,32]{1,0:T(4,128)}, u32[]{:S(2)}) %copy-start.3) | copy-done | bytes 536
  6.9 0.0 copy-start.4
  6.9 0.7 %copy-done.4 = s32[1,2,2]{2,1,0:T(2,128)S(1)} copy-done((s32[1,2,2]{2,1,0:T(2,128)S(1)}, s32[1,2,2]{2,1,0:T(2,128)}, u32[]{:S(2)}) %copy-start.4) | copy-done | bytes 40
  7.6 0.0 copy-start.5
  7.6 0.7 %copy-done.5 = f32[32]{0:T(128)S(1)} copy-done((f32[32]{0:T(128)S(1)}, f32[32]{0:T(128)}, u32[]{:S(2)}) %copy-start.5) | copy-done | bytes 152
  8.3 0.0 copy-start.6
  8.3 0.7 %copy-done.6 = f32[32]{0:T(128)S(1)} copy-done((f32[32]{0:T(128)S(1)}, f32[32]{0:T(128)}, u32[]{:S(2)}) %copy-start.6) | copy-done | bytes 152
  8.9 0.0 copy-start.7
  8.9 0.1 split_features.1
  9.0 0.1 collective-permute-start.1
  9.1 0.2 collective-permute-start.2
  9.4 3.4 %collective-permute-start.3 = (bf16[17,32,128]{2,1,0:T(8,128)(2,1)S(1)}, bf16[17,32,128]{2,1,0:T(8,128)(2,1)S(1)}, u32[]{:S(2)}, u32[]{:S(2)}) collective-permute-start(bf16[17,32,128]{2,1,0:T(8,128)(2,1)S(1)} %get-tuple-element.28), channel_id=1, source_target_pairs={{0,3},{1,2},{2,1},{3,0},{4,7},{5,6},{6,5},{7,4},{8,11},{9,10},{10,... | collective-permute-start | bytes 417800 | tf_op jit(solution)/shard_map/ppermute | solution.py:342
  12.8 0.0 collective-permute-done.1.refs_1_
  12.8 0.0 collective-permute-start.7
  12.8 2.8 %collective-permute-done.2.refs_2_ = bf16[17,32,128]{2,1,0:T(8,128)(2,1)S(1)} collective-permute-done((bf16[17,32,128]{2,1,0:T(8,128)(2,1)S(1)}, bf16[17,32,128]{2,1,0:T(8,128)(2,1)S(1)}, u32[]{:S(2)}, u32[]{:S(2)}) %collective-permute-start.2) | collective-permute-done | bytes 139296 | tf_op jit(solution)/shard_map/ppermute | solution.py:342
  15.6 3.5 %collective-permute-done.3.refs_3_ = bf16[17,32,128]{2,1,0:T(8,128)(2,1)S(1)} collective-permute-done((bf16[17,32,128]{2,1,0:T(8,128)(2,1)S(1)}, bf16[17,32,128]{2,1,0:T(8,128)(2,1)S(1)}, u32[]{:S(2)}, u32[]{:S(2)}) %collective-permute-start.3) | collective-permute-done | bytes 139296 | tf_op jit(solution)/shard_map/ppermute | solution.py:342
  19.1 0.0 collective-permute-done.refs_8_
  19.1 0.0 collective-permute-done.4.refs_1_
  19.1 0.0 collective-permute-start.8
  19.1 1.2 %collective-permute-start.10 = (bf16[27,32,128]{2,1,0:T(8,128)(2,1)}, bf16[27,32,128]{2,1,0:T(8,128)(2,1)S(1)}, u32[]{:S(2)}, u32[]{:S(2)}) collective-permute-start(bf16[27,32,128]{2,1,0:T(8,128)(2,1)} %bitcast.10), channel_id=1, source_target_pairs={{0,3},{1,2},{2,1},{3,0},{4,7},{5,6},{6,5},{7,4},{8,11},{9,10},{10,... | collective-permute-start | bytes 663560 | tf_op jit(solution)/shard_map/ppermute | solution.py:342
  20.3 2.1 %collective-permute-start.9 = (bf16[27,32,128]{2,1,0:T(8,128)(2,1)}, bf16[27,32,128]{2,1,0:T(8,128)(2,1)S(1)}, u32[]{:S(2)}, u32[]{:S(2)}) collective-permute-start(bf16[27,32,128]{2,1,0:T(8,128)(2,1)} %bitcast.11), channel_id=1, source_target_pairs={{0,2},{1,3},{2,0},{3,1},{4,6},{5,7},{6,4},{7,5},{8,10},{9,11},{10,... | collective-permute-start | bytes 663560 | tf_op jit(solution)/shard_map/ppermute | solution.py:342
  22.5 1.0 %pick_faces.1 = (bf16[9,32,128]{2,1,0:T(8,128)(2,1)S(1)}, bf16[9,32,128]{2,1,0:T(8,128)(2,1)S(1)}) custom-call(s32[8,128]{1,0:T(8,128)S(1)} %get-tuple-element.24.tables.tab, bf16[18,32,128]{2,1,0:T(8,128)(2,1)S(1)} %get-tuple-element.25.refs_0_, bf16[17,32,128]{2,1,0:T(8,128)(2,1)S(1)} %collective-permute-done.1.refs_1_, ...), custom_call_target="tpu_custom_call" | custom-call | tf_op jit(solution)/shard_map/pick_faces/pallas_call | solution.py:77
  23.5 1.7 %collective-permute-start.5 = (bf16[9,32,128]{2,1,0:T(8,128)(2,1)S(1)}, bf16[9,32,128]{2,1,0:T(8,128)(2,1)S(1)}, u32[]{:S(2)}, u32[]{:S(2)}) collective-permute-start(bf16[9,32,128]{2,1,0:T(8,128)(2,1)S(1)} %get-tuple-element.32), channel_id=1, source_target_pairs={{0,4},{4,0},{8,12},{12,8},{16,20},{20,16},{24,28},{28,24},{32,36},... | collective-permute-start | bytes 221192 | tf_op jit(solution)/shard_map/ppermute | solution.py:347
  25.2 0.0 collective-permute-done.7.refs_7_
  25.2 4.7 %collective-permute-start.6 = (bf16[9,32,128]{2,1,0:T(8,128)(2,1)S(1)}, bf16[9,32,128]{2,1,0:T(8,128)(2,1)S(1)}, u32[]{:S(2)}, u32[]{:S(2)}) collective-permute-start(bf16[9,32,128]{2,1,0:T(8,128)(2,1)S(1)} %get-tuple-element.33), channel_id=1, source_target_pairs={{0,124},{4,8},{8,4},{12,16},{16,12},{20,24},{24,20},{28,32},{32,28... | collective-permute-start | bytes 221192 | tf_op jit(solution)/shard_map/ppermute | solution.py:347
  30.0 0.0 collective-permute-done.5.refs_4_
  30.0 9.1 %collective-permute-done.6.refs_5_ = bf16[9,32,128]{2,1,0:T(8,128)(2,1)S(1)} collective-permute-done((bf16[9,32,128]{2,1,0:T(8,128)(2,1)S(1)}, bf16[9,32,128]{2,1,0:T(8,128)(2,1)S(1)}, u32[]{:S(2)}, u32[]{:S(2)}) %collective-permute-start.6) | collective-permute-done | bytes 73760 | tf_op jit(solution)/shard_map/ppermute | solution.py:347
  39.1 0.0 collective-permute-done.8.refs_9_
  39.1 0.0 copy-start.1
  39.1 0.9 %copy-done.1 = bf16[27,128,32]{1,2,0:T(8,128)(2,1)S(1)} copy-done((bf16[27,128,32]{1,2,0:T(8,128)(2,1)S(1)}, bf16[27,128,32]{1,2,0:T(8,128)(2,1)}, u32[]{:S(2)}) %copy-start.1) | copy-done | bytes 221208
  40.0 7.2 %convolve_first.1 = (bf16[2,10,10,16,384]{4,3,2,1,0:T(8,128)(2,1)S(1)}, f32[8,128]{1,0:T(8,128)S(1)}) custom-call(s32[8,128]{1,0:T(8,128)S(1)} %get-tuple-element.24.tables.tab, bf16[18,32,128]{2,1,0:T(8,128)(2,1)S(1)} %get-tuple-element.25.refs_0_, bf16[17,32,128]{2,1,0:T(8,128)(2,1)S(1)} %collective-permute-done.1.refs_1_, ...), custom_call_target="tpu_custom_call" | custom-call | flops 1000000 | bytes 10000 | tf_op jit(solution)/shard_map/convolve_first/pallas_call | solution.py:254
  47.2 0.0 collective-permute-done.10.refs_3_
  47.2 0.0 collective-permute-done.9.refs_2_
  47.2 0.0 copy-done.7
  47.2 3.7 %convolve_second.1 = (bf16[4,32,512]{2,1,0:T(8,128)(2,1)S(1)}, bf16[4,32,512]{2,1,0:T(8,128)(2,1)S(1)}, bf16[4,32,512]{2,1,0:T(8,128)(2,1)S(1)}, bf16[4,32,512]{2,1,0:T(8,128)(2,1)S(1)}) custom-call(s32[8,128]{1,0:T(8,128)S(1)} %get-tuple-element.24.tables.tab, bf16[2,10,10,16,384]{4,3,2,1,0:T(8,128)(2,1)S(1)} %get-tuple-element.35.pad, ...), custom_call_target="tpu_custom_call" | custom-call | flops 4000000000 | bytes 4000000 | tf_op jit(solution)/shard_map/convolve_second/pallas_call | solution.py:301
  50.9 0.8 %collective-permute-start.11 = (bf16[4,32,512]{2,1,0:T(8,128)(2,1)S(1)}, bf16[4,32,512]{2,1,0:T(8,128)(2,1)S(1)}, u32[]{:S(2)}, u32[]{:S(2)}) collective-permute-start(bf16[4,32,512]{2,1,0:T(8,128)(2,1)S(1)} %get-tuple-element.40), channel_id=1, source_target_pairs={{0,1},{1,0},{2,3},{3,2},{4,5},{5,4},{6,7},{7,6},{8,9},{9,8},{10,11... | collective-permute-start | bytes 393224 | tf_op jit(solution)/shard_map/ppermute | solution.py:342
  51.7 2.5 %collective-permute-start.12 = (bf16[4,32,512]{2,1,0:T(8,128)(2,1)S(1)}, bf16[4,32,512]{2,1,0:T(8,128)(2,1)S(1)}, u32[]{:S(2)}, u32[]{:S(2)}) collective-permute-start(bf16[4,32,512]{2,1,0:T(8,128)(2,1)S(1)} %get-tuple-element.41), channel_id=1, source_target_pairs={{0,2},{1,3},{2,0},{3,1},{4,6},{5,7},{6,4},{7,5},{8,10},{9,11},{10,... | collective-permute-start | bytes 393224 | tf_op jit(solution)/shard_map/ppermute | solution.py:342
  54.2 0.8 %collective-permute-start.13 = (bf16[4,32,512]{2,1,0:T(8,128)(2,1)S(1)}, bf16[4,32,512]{2,1,0:T(8,128)(2,1)S(1)}, u32[]{:S(2)}, u32[]{:S(2)}) collective-permute-start(bf16[4,32,512]{2,1,0:T(8,128)(2,1)S(1)} %get-tuple-element.42), channel_id=1, source_target_pairs={{0,3},{1,2},{2,1},{3,0},{4,7},{5,6},{6,5},{7,4},{8,11},{9,10},{10,... | collective-permute-start | bytes 393224 | tf_op jit(solution)/shard_map/ppermute | solution.py:342
  54.9 0.0 collective-permute-done.11.refs_1_
  54.9 3.3 %collective-permute-done.12.refs_2_ = bf16[4,32,512]{2,1,0:T(8,128)(2,1)S(1)} collective-permute-done((bf16[4,32,512]{2,1,0:T(8,128)(2,1)S(1)}, bf16[4,32,512]{2,1,0:T(8,128)(2,1)S(1)}, u32[]{:S(2)}, u32[]{:S(2)}) %collective-permute-start.12) | collective-permute-done | bytes 131104 | tf_op jit(solution)/shard_map/ppermute | solution.py:342
  58.3 3.1 %collective-permute-done.13.refs_3_ = bf16[4,32,512]{2,1,0:T(8,128)(2,1)S(1)} collective-permute-done((bf16[4,32,512]{2,1,0:T(8,128)(2,1)S(1)}, bf16[4,32,512]{2,1,0:T(8,128)(2,1)S(1)}, u32[]{:S(2)}, u32[]{:S(2)}) %collective-permute-start.13) | collective-permute-done | bytes 131104 | tf_op jit(solution)/shard_map/ppermute | solution.py:342
  61.3 0.8 %join_levels.1 = bf16[4,4,32,512]{3,2,1,0:T(8,128)(2,1)} custom-call(bf16[4,32,512]{2,1,0:T(8,128)(2,1)S(1)} %get-tuple-element.39.refs_0_, bf16[4,32,512]{2,1,0:T(8,128)(2,1)S(1)} %collective-permute-done.11.refs_1_, bf16[4,32,512]{2,1,0:T(8,128)(2,1)S(1)} %collective-permute-done.12.refs_2_, bf16[4,32,512]{2,1,0:T(8,128)(2,1)S(1)} %collective-permute-done.13.refs_3_), custom_call_target="tpu_custom_call" | custom-call | tf_op jit(solution)/shard_map/join_levels/pallas_call | solution.py:330
Async XLA Ops:
  0.0 19.1 %collective-permute-start = (bf16[27,32,128]{2,1,0:T(8,128)(2,1)}, bf16[27,32,128]{2,1,0:T(8,128)(2,1)S(1)}, u32[]{:S(2)}, u32[]{:S(2)}) collective-permute-start(bf16[27,32,128]{2,1,0:T(8,128)(2,1)} %bitcast.4), channel_id=1, source_target_pairs={{0,2},{1,3},{2,0},{3,1},{4,6},{5,7},{6,4},{7,5},{8,10},{9,11},{10,... | collective-permute-start | bytes 663560 | tf_op jit(solution)/shard_map/ppermute | solution.py:342
  3.6 15.5 %collective-permute-start.4 = (bf16[27,32,128]{2,1,0:T(8,128)(2,1)}, bf16[27,32,128]{2,1,0:T(8,128)(2,1)S(1)}, u32[]{:S(2)}, u32[]{:S(2)}) collective-permute-start(bf16[27,32,128]{2,1,0:T(8,128)(2,1)} %bitcast.9), channel_id=1, source_target_pairs={{0,1},{1,0},{2,3},{3,2},{4,5},{5,4},{6,7},{7,6},{8,9},{9,8},{10,11... | collective-permute-start | bytes 663560 | tf_op jit(solution)/shard_map/ppermute | solution.py:342
  4.5 1.0 %copy-start = (bf16[4,4,32,512]{3,2,1,0:T(8,128)(2,1)S(1)}, bf16[4,4,32,512]{3,2,1,0:T(8,128)(2,1)}, u32[]{:S(2)}) copy-start(bf16[4,4,32,512]{3,2,1,0:T(8,128)(2,1)} %feat.1) | copy-start | bytes 1572868
  5.6 0.7 %copy-start.2 = (s32[4,27]{1,0:T(4,128)S(1)}, s32[4,27]{1,0:T(4,128)}, u32[]{:S(2)}) copy-start(s32[4,27]{1,0:T(4,128)} %near.1) | copy-start | bytes 1300
  6.3 0.7 %copy-start.3 = (f32[4,32]{1,0:T(4,128)S(1)}, f32[4,32]{1,0:T(4,128)}, u32[]{:S(2)}) copy-start(f32[4,32]{1,0:T(4,128)} %lev.1) | copy-start | bytes 1540
  6.9 0.7 %copy-start.4 = (s32[1,2,2]{2,1,0:T(2,128)S(1)}, s32[1,2,2]{2,1,0:T(2,128)}, u32[]{:S(2)}) copy-start(s32[1,2,2]{2,1,0:T(2,128)} %lists.1) | copy-start | bytes 52
  7.6 0.7 %copy-start.5 = (f32[32]{0:T(128)S(1)}, f32[32]{0:T(128)}, u32[]{:S(2)}) copy-start(f32[32]{0:T(128)} %param.12) | copy-start | bytes 388
  8.3 0.7 %copy-start.6 = (f32[32]{0:T(128)S(1)}, f32[32]{0:T(128)}, u32[]{:S(2)}) copy-start(f32[32]{0:T(128)} %param.14) | copy-start | bytes 388
  8.9 38.3 %copy-start.7 = (bf16[27,128,32]{1,2,0:T(8,128)(2,1)S(1)}, bf16[27,128,32]{1,2,0:T(8,128)(2,1)}, u32[]{:S(2)}) copy-start(bf16[27,128,32]{1,2,0:T(8,128)(2,1)} %param.13) | copy-start | bytes 663556
  9.0 3.7 %collective-permute-start.1 = (bf16[17,32,128]{2,1,0:T(8,128)(2,1)S(1)}, bf16[17,32,128]{2,1,0:T(8,128)(2,1)S(1)}, u32[]{:S(2)}, u32[]{:S(2)}) collective-permute-start(bf16[17,32,128]{2,1,0:T(8,128)(2,1)S(1)} %get-tuple-element.26), channel_id=1, source_target_pairs={{0,1},{1,0},{2,3},{3,2},{4,5},{5,4},{6,7},{7,6},{8,9},{9,8},{10,11... | collective-permute-start | bytes 417800 | tf_op jit(solution)/shard_map/ppermute | solution.py:342
  9.1 6.4 %collective-permute-start.2 = (bf16[17,32,128]{2,1,0:T(8,128)(2,1)S(1)}, bf16[17,32,128]{2,1,0:T(8,128)(2,1)S(1)}, u32[]{:S(2)}, u32[]{:S(2)}) collective-permute-start(bf16[17,32,128]{2,1,0:T(8,128)(2,1)S(1)} %get-tuple-element.27), channel_id=1, source_target_pairs={{0,2},{1,3},{2,0},{3,1},{4,6},{5,7},{6,4},{7,5},{8,10},{9,11},{10,... | collective-permute-start | bytes 417800 | tf_op jit(solution)/shard_map/ppermute | solution.py:342
  9.4 9.7 %collective-permute-start.3 = (bf16[17,32,128]{2,1,0:T(8,128)(2,1)S(1)}, bf16[17,32,128]{2,1,0:T(8,128)(2,1)S(1)}, u32[]{:S(2)}, u32[]{:S(2)}) collective-permute-start(bf16[17,32,128]{2,1,0:T(8,128)(2,1)S(1)} %get-tuple-element.28), channel_id=1, source_target_pairs={{0,3},{1,2},{2,1},{3,0},{4,7},{5,6},{6,5},{7,4},{8,11},{9,10},{10,... | collective-permute-start | bytes 417800 | tf_op jit(solution)/shard_map/ppermute | solution.py:342
  12.8 12.5 %collective-permute-start.7 = (bf16[27,32,128]{2,1,0:T(8,128)(2,1)}, bf16[27,32,128]{2,1,0:T(8,128)(2,1)S(1)}, u32[]{:S(2)}, u32[]{:S(2)}) collective-permute-start(bf16[27,32,128]{2,1,0:T(8,128)(2,1)} %bitcast.5), channel_id=1, source_target_pairs={{0,1},{1,0},{2,3},{3,2},{4,5},{5,4},{6,7},{7,6},{8,9},{9,8},{10,11... | collective-permute-start | bytes 663560 | tf_op jit(solution)/shard_map/ppermute | solution.py:342
  19.1 20.0 %collective-permute-start.8 = (bf16[27,32,128]{2,1,0:T(8,128)(2,1)S(1)}, bf16[27,32,128]{2,1,0:T(8,128)(2,1)S(1)}, u32[]{:S(2)}, u32[]{:S(2)}) collective-permute-start(bf16[27,32,128]{2,1,0:T(8,128)(2,1)S(1)} %collective-permute-done.refs_8_), channel_id=1, source_target_pairs={{0,1},{1,0},{2,3},{3,2},{4,5},{5,4},{6,7},{7,6},{8,9},{9,8},{10,11... | collective-permute-start | bytes 663560 | tf_op jit(solution)/shard_map/ppermute | solution.py:342
  19.1 28.1 %collective-permute-start.10 = (bf16[27,32,128]{2,1,0:T(8,128)(2,1)}, bf16[27,32,128]{2,1,0:T(8,128)(2,1)S(1)}, u32[]{:S(2)}, u32[]{:S(2)}) collective-permute-start(bf16[27,32,128]{2,1,0:T(8,128)(2,1)} %bitcast.10), channel_id=1, source_target_pairs={{0,3},{1,2},{2,1},{3,0},{4,7},{5,6},{6,5},{7,4},{8,11},{9,10},{10,... | collective-permute-start | bytes 663560 | tf_op jit(solution)/shard_map/ppermute | solution.py:342
  20.3 26.9 %collective-permute-start.9 = (bf16[27,32,128]{2,1,0:T(8,128)(2,1)}, bf16[27,32,128]{2,1,0:T(8,128)(2,1)S(1)}, u32[]{:S(2)}, u32[]{:S(2)}) collective-permute-start(bf16[27,32,128]{2,1,0:T(8,128)(2,1)} %bitcast.11), channel_id=1, source_target_pairs={{0,2},{1,3},{2,0},{3,1},{4,6},{5,7},{6,4},{7,5},{8,10},{9,11},{10,... | collective-permute-start | bytes 663560 | tf_op jit(solution)/shard_map/ppermute | solution.py:342
  23.5 6.4 %collective-permute-start.5 = (bf16[9,32,128]{2,1,0:T(8,128)(2,1)S(1)}, bf16[9,32,128]{2,1,0:T(8,128)(2,1)S(1)}, u32[]{:S(2)}, u32[]{:S(2)}) collective-permute-start(bf16[9,32,128]{2,1,0:T(8,128)(2,1)S(1)} %get-tuple-element.32), channel_id=1, source_target_pairs={{0,4},{4,0},{8,12},{12,8},{16,20},{20,16},{24,28},{28,24},{32,36},... | collective-permute-start | bytes 221192 | tf_op jit(solution)/shard_map/ppermute | solution.py:347
  25.2 13.9 %collective-permute-start.6 = (bf16[9,32,128]{2,1,0:T(8,128)(2,1)S(1)}, bf16[9,32,128]{2,1,0:T(8,128)(2,1)S(1)}, u32[]{:S(2)}, u32[]{:S(2)}) collective-permute-start(bf16[9,32,128]{2,1,0:T(8,128)(2,1)S(1)} %get-tuple-element.33), channel_id=1, source_target_pairs={{0,124},{4,8},{8,4},{12,16},{16,12},{20,24},{24,20},{28,32},{32,28... | collective-permute-start | bytes 221192 | tf_op jit(solution)/shard_map/ppermute | solution.py:347
  39.1 0.9 %copy-start.1 = (bf16[27,128,32]{1,2,0:T(8,128)(2,1)S(1)}, bf16[27,128,32]{1,2,0:T(8,128)(2,1)}, u32[]{:S(2)}) copy-start(bf16[27,128,32]{1,2,0:T(8,128)(2,1)} %param.11) | copy-start | bytes 663556
  50.9 4.0 %collective-permute-start.11 = (bf16[4,32,512]{2,1,0:T(8,128)(2,1)S(1)}, bf16[4,32,512]{2,1,0:T(8,128)(2,1)S(1)}, u32[]{:S(2)}, u32[]{:S(2)}) collective-permute-start(bf16[4,32,512]{2,1,0:T(8,128)(2,1)S(1)} %get-tuple-element.40), channel_id=1, source_target_pairs={{0,1},{1,0},{2,3},{3,2},{4,5},{5,4},{6,7},{7,6},{8,9},{9,8},{10,11... | collective-permute-start | bytes 393224 | tf_op jit(solution)/shard_map/ppermute | solution.py:342
  51.7 6.6 %collective-permute-start.12 = (bf16[4,32,512]{2,1,0:T(8,128)(2,1)S(1)}, bf16[4,32,512]{2,1,0:T(8,128)(2,1)S(1)}, u32[]{:S(2)}, u32[]{:S(2)}) collective-permute-start(bf16[4,32,512]{2,1,0:T(8,128)(2,1)S(1)} %get-tuple-element.41), channel_id=1, source_target_pairs={{0,2},{1,3},{2,0},{3,1},{4,6},{5,7},{6,4},{7,5},{8,10},{9,11},{10,... | collective-permute-start | bytes 393224 | tf_op jit(solution)/shard_map/ppermute | solution.py:342
  54.2 7.2 %collective-permute-start.13 = (bf16[4,32,512]{2,1,0:T(8,128)(2,1)S(1)}, bf16[4,32,512]{2,1,0:T(8,128)(2,1)S(1)}, u32[]{:S(2)}, u32[]{:S(2)}) collective-permute-start(bf16[4,32,512]{2,1,0:T(8,128)(2,1)S(1)} %get-tuple-element.42), channel_id=1, source_target_pairs={{0,3},{1,2},{2,1},{3,0},{4,7},{5,6},{6,5},{7,4},{8,11},{9,10},{10,... | collective-permute-start | bytes 393224 | tf_op jit(solution)/shard_map/ppermute | solution.py:342

commit v8 on v6

--- a/solution.py
+++ b/solution.py
@@ -344,7 +344,8 @@
 
 def swap_faces(value, first):
     count = lax.axis_size("slab")
-    return lax.ppermute(value, "slab", [(s, (((s + first) ^ 1) - first) % count) for s in range(count)])
+    partner = [((s + first) ^ 1) - first for s in range(count)]
+    return lax.ppermute(value, "slab", [(s, p if 0 <= p < count else s) for s, p in enumerate(partner)])
 
 
 def shards(features, neighbours, face_lists, w_first, b_first, w_second, b_second, level_embed):
@@ -353,8 +354,10 @@
     own, one, two, three, tables = split(
         features, neighbours, face_lists, b_first, b_second, level_embed
     )
-    far, two, three, later = lax.optimization_barrier((far, swap(two, 2), swap(three, 3), w2))
-    pieces = [own, swap(one, 1), two, three]
+    far, one, two, three, later = lax.optimization_barrier(
+        (far, swap(one, 1), swap(two, 2), swap(three, 3), w2)
+    )
+    pieces = [own, one, two, three]
     first = [w1, swap(w1, 1), far, swap(far, 1)]
     sides = faces(tables, pieces)
     sides = [swap_faces(sides[i], i) for i in range(2)]

time: 56.7 us -> 54.7 us (0.965)
  the two profiles are of different devices: /device:TPU:1 before, /device:TPU:25 now
where the time goes in v8:
time: 54.7 us; the launch traced here: 54.5 us
  starting transfers between devices  21 us (38%)
  waiting for transfers between devices  15.2 us (28%)
  Pallas kernels  12.8 us (23%)
  local copies, waits for them, and re-layouts  5.33 us (10%)
    ppermute x12, waiting for transfers between devices, swap(): return lax.ppermute(value, 'chan', [(i, i ^ m) for i in range(4)])  15.2 us
    ppermute x12, starting transfers between devices, swap(): return lax.ppermute(value, 'chan', [(i, i ^ m) for i in range(4)])  15 us
    pallas_call x1, Pallas kernels, convolve_first(): pl.pallas_call(first_kernel, out_shape=[jax.ShapeDtypeStruct((2, 10, 10,...  7.17 us
    ppermute x2, starting transfers between devices, swap_faces(): lax.ppermute(value, 'slab', [(s, p if 0 <= p < count else s) for s, p in...  6.06 us
    unnamed x16, local copies, waits for them, and re-layouts  5.33 us
    pallas_call x1, Pallas kernels, convolve_second(): pl.pallas_call(second_kernel, out_shape=[piece] * 4, in_specs=[SMEM, VMEM...  3.69 us
  transfers between devices with their start and end apart: 14, of which 5 were waited for; matrix products, arithmetic and copies ran while one was open for 0% of the time, Pallas kernels for 15%

profile of v8, /device:TPU:25, one launch (start us, length us, event | category | flops | bytes accessed | tf_op | source)
XLA Modules:
  0.0 54.5 jit_solution(4059235716486954128)
XLA Ops:
  0.0 2.7 %collective-permute-start = (bf16[27,32,128]{2,1,0:T(8,128)(2,1)}, bf16[27,32,128]{2,1,0:T(8,128)(2,1)S(1)}, u32[]{:S(2)}, u32[]{:S(2)}) collective-permute-start(bf16[27,32,128]{2,1,0:T(8,128)(2,1)} %bitcast.6), channel_id=1, source_target_pairs={{0,2},{1,3},{2,0},{3,1},{4,6},{5,7},{6,4},{7,5},{8,10},{9,11},{10,... | collective-permute-start | bytes 663560 | tf_op jit(solution)/shard_map/ppermute | solution.py:342
  2.7 0.0 copy-start
  2.7 1.0 %copy-done = bf16[4,4,32,512]{3,2,1,0:T(8,128)(2,1)S(1)} copy-done((bf16[4,4,32,512]{3,2,1,0:T(8,128)(2,1)S(1)}, bf16[4,4,32,512]{3,2,1,0:T(8,128)(2,1)}, u32[]{:S(2)}) %copy-start) | copy-done | bytes 524312
  3.8 0.0 copy-start.1
  3.8 0.7 %copy-done.1 = s32[4,27]{1,0:T(4,128)S(1)} copy-done((s32[4,27]{1,0:T(4,128)S(1)}, s32[4,27]{1,0:T(4,128)}, u32[]{:S(2)}) %copy-start.1) | copy-done | bytes 456
  4.5 0.0 copy-start.2
  4.5 0.7 %copy-done.2 = f32[4,32]{1,0:T(4,128)S(1)} copy-done((f32[4,32]{1,0:T(4,128)S(1)}, f32[4,32]{1,0:T(4,128)}, u32[]{:S(2)}) %copy-start.2) | copy-done | bytes 536
  5.2 0.0 copy-start.3
  5.2 0.7 %copy-done.3 = s32[1,2,2]{2,1,0:T(2,128)S(1)} copy-done((s32[1,2,2]{2,1,0:T(2,128)S(1)}, s32[1,2,2]{2,1,0:T(2,128)}, u32[]{:S(2)}) %copy-start.3) | copy-done | bytes 40
  5.8 0.0 copy-start.4
  5.8 0.7 %copy-done.4 = f32[32]{0:T(128)S(1)} copy-done((f32[32]{0:T(128)S(1)}, f32[32]{0:T(128)}, u32[]{:S(2)}) %copy-start.4) | copy-done | bytes 152
  6.5 0.0 copy-start.5
  6.5 0.7 %copy-done.5 = f32[32]{0:T(128)S(1)} copy-done((f32[32]{0:T(128)S(1)}, f32[32]{0:T(128)}, u32[]{:S(2)}) %copy-start.5) | copy-done | bytes 152
  7.1 0.1 split_features.1
  7.2 1.0 %collective-permute-start.1 = (bf16[17,32,128]{2,1,0:T(8,128)(2,1)S(1)}, bf16[17,32,128]{2,1,0:T(8,128)(2,1)S(1)}, u32[]{:S(2)}, u32[]{:S(2)}) collective-permute-start(bf16[17,32,128]{2,1,0:T(8,128)(2,1)S(1)} %get-tuple-element.25), channel_id=1, source_target_pairs={{0,1},{1,0},{2,3},{3,2},{4,5},{5,4},{6,7},{7,6},{8,9},{9,8},{10,11... | collective-permute-start | bytes 417800 | tf_op jit(solution)/shard_map/ppermute | solution.py:342
  8.3 0.2 collective-permute-start.2
  8.5 3.0 %collective-permute-start.3 = (bf16[17,32,128]{2,1,0:T(8,128)(2,1)S(1)}, bf16[17,32,128]{2,1,0:T(8,128)(2,1)S(1)}, u32[]{:S(2)}, u32[]{:S(2)}) collective-permute-start(bf16[17,32,128]{2,1,0:T(8,128)(2,1)S(1)} %get-tuple-element.27), channel_id=1, source_target_pairs={{0,3},{1,2},{2,1},{3,0},{4,7},{5,6},{6,5},{7,4},{8,11},{9,10},{10,... | collective-permute-start | bytes 417800 | tf_op jit(solution)/shard_map/ppermute | solution.py:342
  11.5 0.2 collective-permute-start.6
  11.7 0.0 collective-permute-done.1.refs_1_
  11.7 3.4 %collective-permute-done.2.refs_2_ = bf16[17,32,128]{2,1,0:T(8,128)(2,1)S(1)} collective-permute-done((bf16[17,32,128]{2,1,0:T(8,128)(2,1)S(1)}, bf16[17,32,128]{2,1,0:T(8,128)(2,1)S(1)}, u32[]{:S(2)}, u32[]{:S(2)}) %collective-permute-start.2) | collective-permute-done | bytes 139296 | tf_op jit(solution)/shard_map/ppermute | solution.py:342
  15.0 3.2 %collective-permute-done.3.refs_3_ = bf16[17,32,128]{2,1,0:T(8,128)(2,1)S(1)} collective-permute-done((bf16[17,32,128]{2,1,0:T(8,128)(2,1)S(1)}, bf16[17,32,128]{2,1,0:T(8,128)(2,1)S(1)}, u32[]{:S(2)}, u32[]{:S(2)}) %collective-permute-start.3) | collective-permute-done | bytes 139296 | tf_op jit(solution)/shard_map/ppermute | solution.py:342
  18.2 0.0 collective-permute-done.refs_8_
  18.2 0.2 collective-permute-start.7
  18.4 0.0 copy-start.7
  18.4 1.0 %pick_faces.1 = (bf16[9,32,128]{2,1,0:T(8,128)(2,1)S(1)}, bf16[9,32,128]{2,1,0:T(8,128)(2,1)S(1)}) custom-call(s32[8,128]{1,0:T(8,128)S(1)} %get-tuple-element.23.tables.tab, bf16[18,32,128]{2,1,0:T(8,128)(2,1)S(1)} %get-tuple-element.24.refs_0_, bf16[17,32,128]{2,1,0:T(8,128)(2,1)S(1)} %collective-permute-done.1.refs_1_, ...), custom_call_target="tpu_custom_call" | custom-call | tf_op jit(solution)/shard_map/pick_faces/pallas_call | solution.py:77
  19.4 1.7 %collective-permute-start.4 = (bf16[9,32,128]{2,1,0:T(8,128)(2,1)S(1)}, bf16[9,32,128]{2,1,0:T(8,128)(2,1)S(1)}, u32[]{:S(2)}, u32[]{:S(2)}) collective-permute-start(bf16[9,32,128]{2,1,0:T(8,128)(2,1)S(1)} %get-tuple-element.31), channel_id=1, source_target_pairs={{0,4},{4,0},{8,12},{12,8},{16,20},{20,16},{24,28},{28,24},{32,36},... | collective-permute-start | bytes 221192 | tf_op jit(solution)/shard_map/ppermute | solution.py:348
  21.1 4.3 %collective-permute-start.5 = (bf16[9,32,128]{2,1,0:T(8,128)(2,1)S(1)}, bf16[9,32,128]{2,1,0:T(8,128)(2,1)S(1)}, u32[]{:S(2)}, u32[]{:S(2)}) collective-permute-start(bf16[9,32,128]{2,1,0:T(8,128)(2,1)S(1)} %get-tuple-element.32), channel_id=1, source_target_pairs={{0,0},{4,8},{8,4},{12,16},{16,12},{20,24},{24,20},{28,32},{32,28},... | collective-permute-start | bytes 221192 | tf_op jit(solution)/shard_map/ppermute | solution.py:348
  25.5 2.6 %collective-permute-start.10 = (bf16[27,32,128]{2,1,0:T(8,128)(2,1)}, bf16[27,32,128]{2,1,0:T(8,128)(2,1)S(1)}, u32[]{:S(2)}, u32[]{:S(2)}) collective-permute-start(bf16[27,32,128]{2,1,0:T(8,128)(2,1)} %bitcast.9), channel_id=1, source_target_pairs={{0,3},{1,2},{2,1},{3,0},{4,7},{5,6},{6,5},{7,4},{8,11},{9,10},{10,... | collective-permute-start | bytes 663560 | tf_op jit(solution)/shard_map/ppermute | solution.py:342
  28.1 0.0 collective-permute-done.6.refs_7_
  28.1 0.0 collective-permute-start.8
  28.1 0.0 collective-permute-done.4.refs_4_
  28.1 1.3 %collective-permute-start.9 = (bf16[27,32,128]{2,1,0:T(8,128)(2,1)}, bf16[27,32,128]{2,1,0:T(8,128)(2,1)S(1)}, u32[]{:S(2)}, u32[]{:S(2)}) collective-permute-start(bf16[27,32,128]{2,1,0:T(8,128)(2,1)} %bitcast.11), channel_id=1, source_target_pairs={{0,2},{1,3},{2,0},{3,1},{4,6},{5,7},{6,4},{7,5},{8,10},{9,11},{10,... | collective-permute-start | bytes 663560 | tf_op jit(solution)/shard_map/ppermute | solution.py:342
  29.4 0.0 collective-permute-done.5.refs_5_
  29.4 0.0 collective-permute-done.7.refs_9_
  29.4 0.0 copy-start.6
  29.4 0.9 %copy-done.6 = bf16[27,128,32]{1,2,0:T(8,128)(2,1)S(1)} copy-done((bf16[27,128,32]{1,2,0:T(8,128)(2,1)S(1)}, bf16[27,128,32]{1,2,0:T(8,128)(2,1)}, u32[]{:S(2)}) %copy-start.6) | copy-done | bytes 221208
  30.3 7.2 %convolve_first.1 = (bf16[2,10,10,16,384]{4,3,2,1,0:T(8,128)(2,1)S(1)}, f32[8,128]{1,0:T(8,128)S(1)}) custom-call(s32[8,128]{1,0:T(8,128)S(1)} %get-tuple-element.23.tables.tab, bf16[18,32,128]{2,1,0:T(8,128)(2,1)S(1)} %get-tuple-element.24.refs_0_, bf16[17,32,128]{2,1,0:T(8,128)(2,1)S(1)} %collective-permute-done.1.refs_1_, ...), custom_call_target="tpu_custom_call" | custom-call | flops 5000000000 | bytes 4000000 | tf_op jit(solution)/shard_map/convolve_first/pallas_call | solution.py:254
  37.5 0.0 collective-permute-done.10.refs_3_
  37.5 0.0 collective-permute-done.8.refs_1_
  37.5 2.4 %collective-permute-done.9.refs_2_ = bf16[27,32,128]{2,1,0:T(8,128)(2,1)S(1)} collective-permute-done((bf16[27,32,128]{2,1,0:T(8,128)(2,1)}, bf16[27,32,128]{2,1,0:T(8,128)(2,1)S(1)}, u32[]{:S(2)}, u32[]{:S(2)}) %collective-permute-start.9) | collective-permute-done | bytes 221216 | tf_op jit(solution)/shard_map/ppermute | solution.py:342
  39.9 0.0 copy-done.7
  39.9 3.7 %convolve_second.1 = (bf16[4,32,512]{2,1,0:T(8,128)(2,1)S(1)}, bf16[4,32,512]{2,1,0:T(8,128)(2,1)S(1)}, bf16[4,32,512]{2,1,0:T(8,128)(2,1)S(1)}, bf16[4,32,512]{2,1,0:T(8,128)(2,1)S(1)}) custom-call(s32[8,128]{1,0:T(8,128)S(1)} %get-tuple-element.23.tables.tab, bf16[2,10,10,16,384]{4,3,2,1,0:T(8,128)(2,1)S(1)} %get-tuple-element.34.pad, ...), custom_call_target="tpu_custom_call" | custom-call | flops 4000000000 | bytes 4000000 | tf_op jit(solution)/shard_map/convolve_second/pallas_call | solution.py:301
  43.6 0.5 collective-permute-start.11
  44.1 1.7 %collective-permute-start.12 = (bf16[4,32,512]{2,1,0:T(8,128)(2,1)S(1)}, bf16[4,32,512]{2,1,0:T(8,128)(2,1)S(1)}, u32[]{:S(2)}, u32[]{:S(2)}) collective-permute-start(bf16[4,32,512]{2,1,0:T(8,128)(2,1)S(1)} %get-tuple-element.39), channel_id=1, source_target_pairs={{0,2},{1,3},{2,0},{3,1},{4,6},{5,7},{6,4},{7,5},{8,10},{9,11},{10,... | collective-permute-start | bytes 393224 | tf_op jit(solution)/shard_map/ppermute | solution.py:342
  45.8 1.5 %collective-permute-start.13 = (bf16[4,32,512]{2,1,0:T(8,128)(2,1)S(1)}, bf16[4,32,512]{2,1,0:T(8,128)(2,1)S(1)}, u32[]{:S(2)}, u32[]{:S(2)}) collective-permute-start(bf16[4,32,512]{2,1,0:T(8,128)(2,1)S(1)} %get-tuple-element.40), channel_id=1, source_target_pairs={{0,3},{1,2},{2,1},{3,0},{4,7},{5,6},{6,5},{7,4},{8,11},{9,10},{10,... | collective-permute-start | bytes 393224 | tf_op jit(solution)/shard_map/ppermute | solution.py:342
  47.3 0.0 collective-permute-done.11.refs_1_
  47.3 3.3 %collective-permute-done.12.refs_2_ = bf16[4,32,512]{2,1,0:T(8,128)(2,1)S(1)} collective-permute-done((bf16[4,32,512]{2,1,0:T(8,128)(2,1)S(1)}, bf16[4,32,512]{2,1,0:T(8,128)(2,1)S(1)}, u32[]{:S(2)}, u32[]{:S(2)}) %collective-permute-start.12) | collective-permute-done | bytes 131104 | tf_op jit(solution)/shard_map/ppermute | solution.py:342
  50.6 3.0 %collective-permute-done.13.refs_3_ = bf16[4,32,512]{2,1,0:T(8,128)(2,1)S(1)} collective-permute-done((bf16[4,32,512]{2,1,0:T(8,128)(2,1)S(1)}, bf16[4,32,512]{2,1,0:T(8,128)(2,1)S(1)}, u32[]{:S(2)}, u32[]{:S(2)}) %collective-permute-start.13) | collective-permute-done | bytes 131104 | tf_op jit(solution)/shard_map/ppermute | solution.py:342
  53.6 0.8 %join_levels.1 = bf16[4,4,32,512]{3,2,1,0:T(8,128)(2,1)} custom-call(bf16[4,32,512]{2,1,0:T(8,128)(2,1)S(1)} %get-tuple-element.37.refs_0_, bf16[4,32,512]{2,1,0:T(8,128)(2,1)S(1)} %collective-permute-done.11.refs_1_, bf16[4,32,512]{2,1,0:T(8,128)(2,1)S(1)} %collective-permute-done.12.refs_2_, bf16[4,32,512]{2,1,0:T(8,128)(2,1)S(1)} %collective-permute-done.13.refs_3_), custom_call_target="tpu_custom_call" | custom-call | tf_op jit(solution)/shard_map/join_levels/pallas_call | solution.py:330
Async XLA Ops:
  0.0 18.2 %collective-permute-start = (bf16[27,32,128]{2,1,0:T(8,128)(2,1)}, bf16[27,32,128]{2,1,0:T(8,128)(2,1)S(1)}, u32[]{:S(2)}, u32[]{:S(2)}) collective-permute-start(bf16[27,32,128]{2,1,0:T(8,128)(2,1)} %bitcast.6), channel_id=1, source_target_pairs={{0,2},{1,3},{2,0},{3,1},{4,6},{5,7},{6,4},{7,5},{8,10},{9,11},{10,... | collective-permute-start | bytes 663560 | tf_op jit(solution)/shard_map/ppermute | solution.py:342
  2.7 1.0 %copy-start = (bf16[4,4,32,512]{3,2,1,0:T(8,128)(2,1)S(1)}, bf16[4,4,32,512]{3,2,1,0:T(8,128)(2,1)}, u32[]{:S(2)}) copy-start(bf16[4,4,32,512]{3,2,1,0:T(8,128)(2,1)} %feat.1) | copy-start | bytes 1572868
  3.8 0.7 %copy-start.1 = (s32[4,27]{1,0:T(4,128)S(1)}, s32[4,27]{1,0:T(4,128)}, u32[]{:S(2)}) copy-start(s32[4,27]{1,0:T(4,128)} %near.1) | copy-start | bytes 1300
  4.5 0.7 %copy-start.2 = (f32[4,32]{1,0:T(4,128)S(1)}, f32[4,32]{1,0:T(4,128)}, u32[]{:S(2)}) copy-start(f32[4,32]{1,0:T(4,128)} %lev.1) | copy-start | bytes 1540
  5.2 0.7 %copy-start.3 = (s32[1,2,2]{2,1,0:T(2,128)S(1)}, s32[1,2,2]{2,1,0:T(2,128)}, u32[]{:S(2)}) copy-start(s32[1,2,2]{2,1,0:T(2,128)} %lists.1) | copy-start | bytes 52
  5.8 0.7 %copy-start.4 = (f32[32]{0:T(128)S(1)}, f32[32]{0:T(128)}, u32[]{:S(2)}) copy-start(f32[32]{0:T(128)} %param.12) | copy-start | bytes 388
  6.5 0.7 %copy-start.5 = (f32[32]{0:T(128)S(1)}, f32[32]{0:T(128)}, u32[]{:S(2)}) copy-start(f32[32]{0:T(128)} %param.14) | copy-start | bytes 388
  7.2 4.4 %collective-permute-start.1 = (bf16[17,32,128]{2,1,0:T(8,128)(2,1)S(1)}, bf16[17,32,128]{2,1,0:T(8,128)(2,1)S(1)}, u32[]{:S(2)}, u32[]{:S(2)}) collective-permute-start(bf16[17,32,128]{2,1,0:T(8,128)(2,1)S(1)} %get-tuple-element.25), channel_id=1, source_target_pairs={{0,1},{1,0},{2,3},{3,2},{4,5},{5,4},{6,7},{7,6},{8,9},{9,8},{10,11... | collective-permute-start | bytes 417800 | tf_op jit(solution)/shard_map/ppermute | solution.py:342
  8.3 6.7 %collective-permute-start.2 = (bf16[17,32,128]{2,1,0:T(8,128)(2,1)S(1)}, bf16[17,32,128]{2,1,0:T(8,128)(2,1)S(1)}, u32[]{:S(2)}, u32[]{:S(2)}) collective-permute-start(bf16[17,32,128]{2,1,0:T(8,128)(2,1)S(1)} %get-tuple-element.26), channel_id=1, source_target_pairs={{0,2},{1,3},{2,0},{3,1},{4,6},{5,7},{6,4},{7,5},{8,10},{9,11},{10,... | collective-permute-start | bytes 417800 | tf_op jit(solution)/shard_map/ppermute | solution.py:342
  8.5 9.7 %collective-permute-start.3 = (bf16[17,32,128]{2,1,0:T(8,128)(2,1)S(1)}, bf16[17,32,128]{2,1,0:T(8,128)(2,1)S(1)}, u32[]{:S(2)}, u32[]{:S(2)}) collective-permute-start(bf16[17,32,128]{2,1,0:T(8,128)(2,1)S(1)} %get-tuple-element.27), channel_id=1, source_target_pairs={{0,3},{1,2},{2,1},{3,0},{4,7},{5,6},{6,5},{7,4},{8,11},{9,10},{10,... | collective-permute-start | bytes 417800 | tf_op jit(solution)/shard_map/ppermute | solution.py:342
  11.5 16.5 %collective-permute-start.6 = (bf16[27,32,128]{2,1,0:T(8,128)(2,1)}, bf16[27,32,128]{2,1,0:T(8,128)(2,1)S(1)}, u32[]{:S(2)}, u32[]{:S(2)}) collective-permute-start(bf16[27,32,128]{2,1,0:T(8,128)(2,1)} %bitcast.7), channel_id=1, source_target_pairs={{0,1},{1,0},{2,3},{3,2},{4,5},{5,4},{6,7},{7,6},{8,9},{9,8},{10,11... | collective-permute-start | bytes 663560 | tf_op jit(solution)/shard_map/ppermute | solution.py:342
  18.2 11.2 %collective-permute-start.7 = (bf16[27,32,128]{2,1,0:T(8,128)(2,1)S(1)}, bf16[27,32,128]{2,1,0:T(8,128)(2,1)S(1)}, u32[]{:S(2)}, u32[]{:S(2)}) collective-permute-start(bf16[27,32,128]{2,1,0:T(8,128)(2,1)S(1)} %collective-permute-done.refs_8_), channel_id=1, source_target_pairs={{0,1},{1,0},{2,3},{3,2},{4,5},{5,4},{6,7},{7,6},{8,9},{9,8},{10,11... | collective-permute-start | bytes 663560 | tf_op jit(solution)/shard_map/ppermute | solution.py:342
  18.4 21.5 %copy-start.7 = (bf16[27,128,32]{1,2,0:T(8,128)(2,1)S(1)}, bf16[27,128,32]{1,2,0:T(8,128)(2,1)}, u32[]{:S(2)}) copy-start(bf16[27,128,32]{1,2,0:T(8,128)(2,1)} %param.13) | copy-start | bytes 663556
  19.4 8.6 %collective-permute-start.4 = (bf16[9,32,128]{2,1,0:T(8,128)(2,1)S(1)}, bf16[9,32,128]{2,1,0:T(8,128)(2,1)S(1)}, u32[]{:S(2)}, u32[]{:S(2)}) collective-permute-start(bf16[9,32,128]{2,1,0:T(8,128)(2,1)S(1)} %get-tuple-element.31), channel_id=1, source_target_pairs={{0,4},{4,0},{8,12},{12,8},{16,20},{20,16},{24,28},{28,24},{32,36},... | collective-permute-start | bytes 221192 | tf_op jit(solution)/shard_map/ppermute | solution.py:348
  21.1 8.2 %collective-permute-start.5 = (bf16[9,32,128]{2,1,0:T(8,128)(2,1)S(1)}, bf16[9,32,128]{2,1,0:T(8,128)(2,1)S(1)}, u32[]{:S(2)}, u32[]{:S(2)}) collective-permute-start(bf16[9,32,128]{2,1,0:T(8,128)(2,1)S(1)} %get-tuple-element.32), channel_id=1, source_target_pairs={{0,0},{4,8},{8,4},{12,16},{16,12},{20,24},{24,20},{28,32},{32,28},... | collective-permute-start | bytes 221192 | tf_op jit(solution)/shard_map/ppermute | solution.py:348
  25.5 12.0 %collective-permute-start.10 = (bf16[27,32,128]{2,1,0:T(8,128)(2,1)}, bf16[27,32,128]{2,1,0:T(8,128)(2,1)S(1)}, u32[]{:S(2)}, u32[]{:S(2)}) collective-permute-start(bf16[27,32,128]{2,1,0:T(8,128)(2,1)} %bitcast.9), channel_id=1, source_target_pairs={{0,3},{1,2},{2,1},{3,0},{4,7},{5,6},{6,5},{7,4},{8,11},{9,10},{10,... | collective-permute-start | bytes 663560 | tf_op jit(solution)/shard_map/ppermute | solution.py:342
  28.1 9.5 %collective-permute-start.8 = (bf16[27,32,128]{2,1,0:T(8,128)(2,1)}, bf16[27,32,128]{2,1,0:T(8,128)(2,1)S(1)}, u32[]{:S(2)}, u32[]{:S(2)}) collective-permute-start(bf16[27,32,128]{2,1,0:T(8,128)(2,1)} %bitcast.10), channel_id=1, source_target_pairs={{0,1},{1,0},{2,3},{3,2},{4,5},{5,4},{6,7},{7,6},{8,9},{9,8},{10,11... | collective-permute-start | bytes 663560 | tf_op jit(solution)/shard_map/ppermute | solution.py:342
  28.1 11.8 %collective-permute-start.9 = (bf16[27,32,128]{2,1,0:T(8,128)(2,1)}, bf16[27,32,128]{2,1,0:T(8,128)(2,1)S(1)}, u32[]{:S(2)}, u32[]{:S(2)}) collective-permute-start(bf16[27,32,128]{2,1,0:T(8,128)(2,1)} %bitcast.11), channel_id=1, source_target_pairs={{0,2},{1,3},{2,0},{3,1},{4,6},{5,7},{6,4},{7,5},{8,10},{9,11},{10,... | collective-permute-start | bytes 663560 | tf_op jit(solution)/shard_map/ppermute | solution.py:342
  29.4 0.9 %copy-start.6 = (bf16[27,128,32]{1,2,0:T(8,128)(2,1)S(1)}, bf16[27,128,32]{1,2,0:T(8,128)(2,1)}, u32[]{:S(2)}) copy-start(bf16[27,128,32]{1,2,0:T(8,128)(2,1)} %param.11) | copy-start | bytes 663556
  43.6 3.7 %collective-permute-start.11 = (bf16[4,32,512]{2,1,0:T(8,128)(2,1)S(1)}, bf16[4,32,512]{2,1,0:T(8,128)(2,1)S(1)}, u32[]{:S(2)}, u32[]{:S(2)}) collective-permute-start(bf16[4,32,512]{2,1,0:T(8,128)(2,1)S(1)} %get-tuple-element.38), channel_id=1, source_target_pairs={{0,1},{1,0},{2,3},{3,2},{4,5},{5,4},{6,7},{7,6},{8,9},{9,8},{10,11... | collective-permute-start | bytes 393224 | tf_op jit(solution)/shard_map/ppermute | solution.py:342
  44.1 6.6 %collective-permute-start.12 = (bf16[4,32,512]{2,1,0:T(8,128)(2,1)S(1)}, bf16[4,32,512]{2,1,0:T(8,128)(2,1)S(1)}, u32[]{:S(2)}, u32[]{:S(2)}) collective-permute-start(bf16[4,32,512]{2,1,0:T(8,128)(2,1)S(1)} %get-tuple-element.39), channel_id=1, source_target_pairs={{0,2},{1,3},{2,0},{3,1},{4,6},{5,7},{6,4},{7,5},{8,10},{9,11},{10,... | collective-permute-start | bytes 393224 | tf_op jit(solution)/shard_map/ppermute | solution.py:342
  45.8 7.8 %collective-permute-start.13 = (bf16[4,32,512]{2,1,0:T(8,128)(2,1)S(1)}, bf16[4,32,512]{2,1,0:T(8,128)(2,1)S(1)}, u32[]{:S(2)}, u32[]{:S(2)}) collective-permute-start(bf16[4,32,512]{2,1,0:T(8,128)(2,1)S(1)} %get-tuple-element.40), channel_id=1, source_target_pairs={{0,3},{1,2},{2,1},{3,0},{4,7},{5,6},{6,5},{7,4},{8,11},{9,10},{10,... | collective-permute-start | bytes 393224 | tf_op jit(solution)/shard_map/ppermute | solution.py:342

commit v9 on v8

--- a/solution.py
+++ b/solution.py
@@ -89,7 +89,7 @@
     return v / (1.0 + jnp.exp(-v))
 
 
-def gather_padded(slots, pad, lead, slot, planes):
+def gather_padded(slots, pad, slot, planes):
     x = lax.broadcasted_iota(jnp.int32, (1, 8, 128), 1)
     for dz, z_from, z_to in planes:
         for dy in (-1, 0, 1):
@@ -104,20 +104,20 @@
                 parts[2].append(pltpu.roll(jnp.where(x == 0, right, mid), 7, 1))
             for d in range(3):
                 tile = jnp.concatenate(parts[d], axis=1).astype(BF16)
-                pad[lead, z_to, y_to : y_to + n, :, 128 * d : 128 * d + 128] = tile
+                pad[z_to, y_to : y_to + n, :, 128 * d : 128 * d + 128] = tile
 
 
 OWN_PLANES = [(-1, 7, 0)] + [(0, z, z + 1) for z in range(8)] + [(1, 0, 9)]
 
 
-def conv_pair(pad, lead, w):
+def conv_pair(pad, w):
     zero = jnp.zeros((128, 128), BF16)
     total = None
     blocks = [(zin, dy) for zin in range(4) for dy in range(3)]
     for first in range(0, 12, 2):
         left, right = [], []
         for zin, dy in blocks[first : first + 2]:
-            planes = [pad[lead, zin + 2 * j, dy : dy + 8].reshape(128, 384) for j in range(4)]
+            planes = [pad[zin + 2 * j, dy : dy + 8].reshape(128, 384) for j in range(4)]
             left.append(jnp.concatenate(planes, axis=0))
             for dx in range(3):
                 even = w[9 * zin + 3 * dy + dx] if zin < 3 else zero
@@ -146,30 +146,32 @@
     return total
 
 
-def load_shards(sources, weights, order, sem):
-    return [
-        pltpu.make_async_copy(
-            source, weights.at[:, pl.ds(pl.multiple_of(32 * order[m], 32), 32), :], sem.at[m]
-        )
-        for m, source in enumerate(sources)
-    ]
-
-
-def finish(acc, moved, tab, pair, slots):
+def finish(acc, moved, active, slots, first):
     for j in range(4):
         for zo in range(2):
-            tile = silu(acc[pair, 128 * j : 128 * j + 128, 128 * zo : 128 * zo + 128] + moved)
+            tile = silu(acc[128 * j : 128 * j + 128, 128 * zo : 128 * zo + 128] + moved)
             tile = tile.reshape(8, 2, 8, 128)
             for w in range(2):
-                b = 2 * pair + w
-                slots[b, 2 * j + zo] = jnp.where(tab[b, 13] >= 0, tile[:, w], 0.0)
-
-
-def first_kernel(tab, *refs):
-    feat, sides, shards = refs[0:4], refs[4:6], refs[6:10]
-    pad_out, shift = refs[10:12]
-    fs, hs, w1, bias, sent, sent_int, tables, slots, pad, pad_face, acc, sem = refs[12:]
+                slots[first + w, 2 * j + zo] = jnp.where(active[w], tile[:, w], 0.0)
+
+
+def give_out(slots, turned, outs):
     me = lax.axis_index("chan")
+    for b in range(2):
+        brick = slots[b].reshape(512, 128).astype(BF16).T
+        for g in range(4):
+            turned[g, b] = brick[32 * g : 32 * g + 32]
+    for m in range(4):
+        outs[m][...] = turned[me ^ m]
+
+
+def conv_kernel(tab, *refs):
+    feat, sides, own_w, near_w, far_w = refs[0:4], refs[4:6], refs[6:8], refs[8:10], refs[10:14]
+    outs, pad_rest, w2, shift = refs[14:18], refs[18], refs[19], refs[20]
+    fs, hs, w1, bias, sent, sent_int, tables, slots, pad, pad_face, acc, turned, sem = refs[21:]
+    pads = (pad, pad_rest)
+    me = lax.axis_index("chan")
+    odd = layer_of_slab()
 
     f_copies, t_copies = [], []
     for i in range(2):
@@ -179,15 +181,37 @@
     for m in range(4):
         f_copies.append(pltpu.make_async_copy(feat[m].at[pl.ds(0, 16)], fs.at[m], sem.at[4 + m]))
         f_copies.append(pltpu.make_async_copy(feat[m].at[16, pl.ds(0, 16)], bias.at[m], sem.at[8 + m]))
-    w_copies = [
-        pltpu.make_async_copy(shards[m], w1.at[:, pl.ds(32 * m, 32), :], sem.at[12 + m]) for m in range(4)
-    ]
-    for copy in t_copies + f_copies + w_copies:
+    for copy in t_copies + f_copies:
         copy.start()
+
+    def load_shard(m, layer, source):
+        g = 32 * m if layer == 0 else pl.multiple_of((me ^ m) * 32, 32)
+        return pltpu.make_async_copy(source, (w1, w2)[layer].at[:, pl.ds(g, 32), :], sem.at[12 + 2 * m + layer])
+
+    w_copies = ([], [])
+    for layer in range(2):
+        near = [load_shard(0, layer, own_w[layer])]
+        near.append(load_shard(1, layer, near_w[layer]))
+        for copy in near:
+            copy.start()
+        w_copies[layer].extend(near)
+        for m in (2, 3):
+            mine, other = far_w[m - 2], far_w[m]
+
+            @pl.when(odd == layer)
+            def _():
+                load_shard(m, layer, mine).start()
+
+            @pl.when(odd != layer)
+            def _():
+                load_shard(m, layer, other).start()
+
+            w_copies[layer].append(load_shard(m, layer, mine))
+    w1_copies, w2_copies = w_copies
     for copy in t_copies:
         copy.wait()
     sent_int[...] = sent[...].astype(F32).astype(jnp.int32).reshape(32, 128)
-    to_scalars = pltpu.make_async_copy(sent_int, tables, sem.at[16])
+    to_scalars = pltpu.make_async_copy(sent_int, tables, sem.at[24])
     to_scalars.start()
     for copy in f_copies:
         copy.wait()
@@ -228,34 +252,59 @@
         u = tab[5, jnp.clip(t - 4, 0, 1)]
         return jnp.where((t < 4) | (t > 5) | (u < 0), NONE, u)
 
-    gather_padded(slots, pad_face, 0, below, [(0, 6, 0), (0, 7, 1), (1, 0, 2)])
-    gather_padded(slots, pad_face, 1, above, [(-1, 7, 0), (0, 0, 1), (0, 1, 2)])
+    gather_padded(slots, pad_face.at[0], below, [(0, 6, 0), (0, 7, 1), (1, 0, 2)])
+    gather_padded(slots, pad_face.at[1], above, [(-1, 7, 0), (0, 0, 1), (0, 1, 2)])
     for pair in range(2):
-        gather_padded(slots, pad, pair, own(pair), OWN_PLANES)
-
+        gather_padded(slots, pads[pair], own(pair), OWN_PLANES)
+
+    for copy in w1_copies:
+        copy.wait()
     values = sum(bias[m].astype(F32) for m in range(4))
-    shift[...] = values[0:8] + values[8:16]
-    moved = shift[0:1, :] + shift[pl.ds(2 + me, 1), :]
-    for copy in w_copies:
-        copy.wait()
+    shift[0:8, :] = values[0:8] + values[8:16]
+    for w in range(2):
+        shift[8 + w : 9 + w, :] = jnp.full((1, 128), jnp.where(tab[2 + w, 13] >= 0, 1.0, 0.0), F32)
+    shift[10:16, :] = jnp.zeros((6, 128), F32)
+    shift_second = shift[1:2, :]
+    shift_first = shift[0:1, :] + shift[pl.ds(2 + me, 1), :]
 
     for pair in range(2):
-        acc[pair] = conv_pair(pad, pair, w1)
-        finish(acc, moved, tab, pair, slots)
-    sides_out = silu(conv_face(pad_face, w1) + moved).reshape(2, 8, 2, 8, 128)
+        acc[...] = conv_pair(pads[pair], w1)
+        finish(acc, shift_first, [tab[2 * pair + w, 13] >= 0 for w in range(2)], slots, 2 * pair)
+    faces = silu(conv_face(pad_face, w1) + shift_first).reshape(2, 8, 2, 8, 128)
     for c in range(2):
-        slots[4 + c, 7] = sides_out[0, :, c]
-        slots[6 + c, 0] = sides_out[1, :, c]
+        slots[4 + c, 7] = faces[0, :, c]
+        slots[6 + c, 0] = faces[1, :, c]
+
     for pair in range(2):
-        gather_padded(slots, pad_out, pair, own(pair), OWN_PLANES)
-
-
-def convolve_first(tables, feat, sides, shards):
-    return pl.pallas_call(
-        first_kernel,
-        out_shape=[jax.ShapeDtypeStruct((2, 10, 10, 16, 384), BF16), jax.ShapeDtypeStruct((8, 128), F32)],
-        in_specs=[SMEM] + [HBM] * 10,
-        out_specs=[VMEM] * 2,
+        gather_padded(slots, pads[pair], own(pair), OWN_PLANES)
+    for copy in w2_copies:
+        copy.wait()
+    acc[...] = conv_pair(pads[0], w2)
+    finish(acc, shift_second, [tab[w, 13] >= 0 for w in range(2)], slots, 0)
+    give_out(slots, turned, outs)
+
+
+def rest_kernel(pad, w2, shift, *refs):
+    outs, slots, acc, turned = refs[:4], refs[4], refs[5], refs[6]
+    acc[...] = conv_pair(pad, w2)
+    finish(acc, shift[1:2, :], [shift[8 + w : 9 + w, :] > 0 for w in range(2)], slots, 0)
+    give_out(slots, turned, outs)
+
+
+HALF = jax.ShapeDtypeStruct((2, 32, 512), BF16)
+
+
+def convolve(tables, feat, sides, own_w, near_w, far_w):
+    *outs, pad, w2, shift = pl.pallas_call(
+        conv_kernel,
+        out_shape=[HALF] * 4
+        + [
+            jax.ShapeDtypeStruct((10, 10, 16, 384), BF16),
+            jax.ShapeDtypeStruct((27, 128, 128), BF16),
+            jax.ShapeDtypeStruct((16, 128), F32),
+        ],
+        in_specs=[SMEM] + [HBM] * 14,
+        out_specs=[VMEM] * 7,
         scratch_shapes=[
             pltpu.VMEM((4, 16, 32, 128), BF16),
             pltpu.VMEM((2, 8, 32, 128), BF16),
@@ -265,61 +314,43 @@
             pltpu.VMEM((32, 128), jnp.int32),
             pltpu.SMEM((32, 128), jnp.int32),
             pltpu.VMEM((9, 8, 8, 8, 128), F32),
-            pltpu.VMEM((2, 10, 10, 16, 384), BF16),
+            pltpu.VMEM((10, 10, 16, 384), BF16),
             pltpu.VMEM((2, 3, 10, 16, 384), BF16),
-            pltpu.VMEM((2, 512, 256), F32),
-            pltpu.SemaphoreType.DMA((17,)),
+            pltpu.VMEM((512, 256), F32),
+            pltpu.VMEM((4, 2, 32, 512), BF16),
+            pltpu.SemaphoreType.DMA((32,)),
+        ],
+        compiler_params=pltpu.CompilerParams(vmem_limit_bytes=40 << 20),
+        cost_estimate=pl.CostEstimate(flops=6 * 10**9, bytes_accessed=4 * 10**6, transcendentals=10**6),
+        name="convolve",
+    )(tables, *feat, *sides, *own_w, *near_w, *far_w)
+    return outs, pad, w2, shift
+
+
+def convolve_rest(pad, w2, shift):
+    return pl.pallas_call(
+        rest_kernel,
+        out_shape=[HALF] * 4,
+        in_specs=[VMEM] * 3,
+        out_specs=[VMEM] * 4,
+        scratch_shapes=[
+            pltpu.VMEM((2, 8, 8, 8, 128), F32),
+            pltpu.VMEM((512, 256), F32),
+            pltpu.VMEM((4, 2, 32, 512), BF16),
         ],
         compiler_params=pltpu.CompilerParams(vmem_limit_bytes=24 << 20),
-        cost_estimate=pl.CostEstimate(flops=5 * 10**9, bytes_accessed=4 * 10**6, transcendentals=10**6),
-        name="convolve_first",
-    )(tables, *feat, *sides, *shards)
-
-
-def second_kernel(tab, pad, shift, *refs):
-    shards, outs = refs[0:4], refs[4:8]
-    w2, slots, acc, turned, sem = refs[8:]
+        cost_estimate=pl.CostEstimate(flops=2 * 10**9, bytes_accessed=4 * 10**6, transcendentals=10**6),
+        name="convolve_rest",
+    )(pad, w2, shift)
+
+
+def join_kernel(*refs):
+    pieces, out, sem = refs[:8], refs[8], refs[9]
     me = lax.axis_index("chan")
-    w_copies = load_shards(shards, w2, [me ^ m for m in range(4)], sem)
-    for copy in w_copies:
-        copy.start()
-    for copy in w_copies:
-        copy.wait()
-    for pair in range(2):
-        acc[pair] = conv_pair(pad, pair, w2)
-        finish(acc, shift[1:2, :], tab, pair, slots)
-    for b in range(4):
-        brick = slots[b].reshape(512, 128).astype(BF16).T
-        for g in range(4):
-            turned[g, b] = brick[32 * g : 32 * g + 32]
-    for m in range(4):
-        outs[m][...] = turned[me ^ m]
-
-
-def convolve_second(tables, pad, shift, shards):
-    piece = jax.ShapeDtypeStruct((4, 32, 512), BF16)
-    return pl.pallas_call(
-        second_kernel,
-        out_shape=[piece] * 4,
-        in_specs=[SMEM, VMEM, VMEM] + [HBM] * 4,
-        out_specs=[VMEM] * 4,
-        scratch_shapes=[
-            pltpu.VMEM((27, 128, 128), BF16),
-            pltpu.VMEM((4, 8, 8, 8, 128), F32),
-            pltpu.VMEM((2, 512, 256), F32),
-            pltpu.VMEM((4, 4, 32, 512), BF16),
-            pltpu.SemaphoreType.DMA((4,)),
-        ],
-        compiler_params=pltpu.CompilerParams(vmem_limit_bytes=24 << 20),
-        cost_estimate=pl.CostEstimate(flops=4 * 10**9, bytes_accessed=4 * 10**6, transcendentals=10**6),
-        name="convolve_second",
-    )(tables, pad, shift, *shards)
-
-
-def join_kernel(*refs):
-    pieces, out, sem = refs[:4], refs[4], refs[5]
-    me = lax.axis_index("chan")
-    copies = [pltpu.make_async_copy(pieces[m], out.at[me ^ m], sem.at[m]) for m in range(4)]
+    copies = [
+        pltpu.make_async_copy(pieces[i], out.at[me ^ (i % 4), pl.ds(2 * (i // 4), 2)], sem.at[i])
+        for i in range(8)
+    ]
     for copy in copies:
         copy.start()
     for copy in copies:
@@ -330,9 +361,9 @@
     return pl.pallas_call(
         join_kernel,
         out_shape=jax.ShapeDtypeStruct((4, 4, 32, 512), BF16),
-        in_specs=[HBM] * 4,
+        in_specs=[HBM] * 8,
         out_specs=HBM,
-        scratch_shapes=[pltpu.SemaphoreType.DMA((4,))],
+        scratch_shapes=[pltpu.SemaphoreType.DMA((8,))],
         compiler_params=pltpu.CompilerParams(vmem_limit_bytes=8 << 20),
         name="join_levels",
     )(*pieces)
@@ -340,6 +371,17 @@
 
 def swap(value, m):
     return lax.ppermute(value, "chan", [(i, i ^ m) for i in range(4)])
+
+
+def layer_of_slab():
+    slab = lax.axis_index("slab")
+    return (slab + slab // 8) % 2
+
+
+def swap_slabs(value, step, m):
+    count = lax.axis_size("slab")
+    pairs = [(4 * s + g, 4 * (s ^ step) + (g ^ m)) for s in range(count) for g in range(4)]
+    return lax.ppermute(value, ("slab", "chan"), pairs)
 
 
 def swap_faces(value, first):
@@ -350,21 +392,22 @@
 
 def shards(features, neighbours, face_lists, w_first, b_first, w_second, b_second, level_embed):
     w1, w2 = w_first.transpose(0, 2, 1), w_second.transpose(0, 2, 1)
-    far = swap(w1, 2)
+    fetched = swap(jnp.where(layer_of_slab() == 0, w1, w2), 2)
     own, one, two, three, tables = split(
         features, neighbours, face_lists, b_first, b_second, level_embed
     )
-    far, one, two, three, later = lax.optimization_barrier(
-        (far, swap(one, 1), swap(two, 2), swap(three, 3), w2)
+    fetched, one, two, three = lax.optimization_barrier(
+        (fetched, swap(one, 1), swap(two, 2), swap(three, 3))
     )
     pieces = [own, one, two, three]
-    first = [w1, swap(w1, 1), far, swap(far, 1)]
+    near = [swap(w1, 1), swap(w2, 1)]
+    far = [fetched, swap(fetched, 1), swap_slabs(fetched, 1, 0), swap_slabs(fetched, 8, 1)]
     sides = faces(tables, pieces)
     sides = [swap_faces(sides[i], i) for i in range(2)]
-    second = [w2] + [swap(later, m) for m in (1, 2, 3)]
-    pad, shift = convolve_first(tables, pieces, sides, first)
-    outs = convolve_second(tables, pad, shift, second)
-    return join([outs[0]] + [swap(outs[m], m) for m in (1, 2, 3)])
+    early, *state = convolve(tables, pieces, sides, (w1, w2), near, far)
+    early = [early[0]] + [swap(early[m], m) for m in (1, 2, 3)]
+    late = convolve_rest(*state)
+    return join(early + [late[0]] + [swap(late[m], m) for m in (1, 2, 3)])
 
 
 def solution(mesh):

time: 54.7 us -> 58.2 us (1.064)
  starting transfers between devices: 21 us -> 24.7 us
  waiting for transfers between devices: 15.2 us -> 12.7 us
  Pallas kernels: 12.8 us -> 14.9 us
  other arithmetic: 0 us -> 1.12 us
  local copies, waits for them, and re-layouts: 5.33 us -> 4.4 us
    ppermute x12 -> x13, waiting for transfers between devices: 15.2 us -> 10.3 us  [swap(): return lax.ppermute(value, 'chan', [(i, i ^ m) for i in range(4)])]
    ppermute x2, waiting for transfers between devices: 0.01 us -> 2.37 us  [swap_faces(): lax.ppermute(value, 'slab', [(s, p if 0 <= p < count else s) for s, p in...]
    ppermute x0 -> x2, starting transfers between devices: none -> 2.2 us  [swap_slabs(): return lax.ppermute(value, ('slab', 'chan'), pairs)]
    pallas_call x2, Pallas kernels: 10.9 us -> 12.9 us  [the longest x1 11.4 us: convolve(): pl.pallas_call(conv_kernel, out_shape=[HALF] * 4 + [jax.ShapeDtypeStruct(...]
    ppermute x12 -> x13, starting transfers between devices: 15 us -> 16.2 us  [swap(): return lax.ppermute(value, 'chan', [(i, i ^ m) for i in range(4)])]
    select_n x0 -> x1, other arithmetic: none -> 1.12 us  [shards(): fetched = swap(jnp.where(layer_of_slab() == 0, w1, w2), 2)]
    unnamed x16, local copies, waits for them, and re-layouts: 5.33 us -> 4.4 us
  transfers between devices with their start and end apart: 14 -> 17, of which waited for: 5 -> 5; matrix products, arithmetic and copies ran while one was open for 0% -> 0% of each run, Pallas kernels for 15% -> 5%
where the time goes in v9:
time: 58.2 us; the launch traced here: 57.9 us
  starting transfers between devices  24.7 us (42%)
  Pallas kernels  14.9 us (26%)
  waiting for transfers between devices  12.7 us (22%)
  local copies, waits for them, and re-layouts  4.4 us (8%)
  other arithmetic  1.12 us (2%)
    ppermute x13, starting transfers between devices, swap(): return lax.ppermute(value, 'chan', [(i, i ^ m) for i in range(4)])  16.2 us
    pallas_call x1, Pallas kernels, convolve(): pl.pallas_call(conv_kernel, out_shape=[HALF] * 4 + [jax.ShapeDtypeStruct(...  11.4 us
    ppermute x13, waiting for transfers between devices, swap(): return lax.ppermute(value, 'chan', [(i, i ^ m) for i in range(4)])  10.3 us
    ppermute x2, starting transfers between devices, swap_faces(): lax.ppermute(value, 'slab', [(s, p if 0 <= p < count else s) for s, p in...  6.3 us
    unnamed x16, local copies, waits for them, and re-layouts  4.4 us
    ppermute x2, waiting for transfers between devices, swap_faces(): lax.ppermute(value, 'slab', [(s, p if 0 <= p < count else s) for s, p in...  2.37 us
    ppermute x2, starting transfers between devices, swap_slabs(): return lax.ppermute(value, ('slab', 'chan'), pairs)  2.2 us
    pallas_call x1, Pallas kernels, convolve_rest(): pl.pallas_call(rest_kernel, out_shape=[HALF] * 4, in_specs=[VMEM] * 3, ou...  1.51 us
  transfers between devices with their start and end apart: 17, of which 5 were waited for; matrix products, arithmetic and copies ran while one was open for 0% of the time, Pallas kernels for 5%

profile of v9, /device:TPU:25, one launch (start us, length us, event | category | flops | bytes accessed | tf_op | source)
XLA Modules:
  0.0 57.9 jit_solution(888906822989692327)
XLA Ops:
  0.0 0.0 copy-start.2
  0.0 0.0 copy-start.1
  0.0 1.1 %broadcast_select_fusion = bf16[27,32,128]{2,1,0:T(8,128)(2,1)S(1)} fusion(pred[]{:T(512)S(6)} %eq.5, bf16[27,128,32]{1,2,0:T(8,128)(2,1)} %param.13, bf16[27,128,32]{1,2,0:T(8,128)(2,1)} %param.11), kind=kLoop, calls=%fused_computation | loop fusion | flops 110592 | bytes 663553 | tf_op jit(solution)/shard_map/jit(_where)/select_n | solution.py:395
  1.1 2.8 %collective-permute-start = (bf16[27,32,128]{2,1,0:T(8,128)(2,1)S(1)}, bf16[27,32,128]{2,1,0:T(8,128)(2,1)S(1)}, u32[]{:S(2)}, u32[]{:S(2)}) collective-permute-start(bf16[27,32,128]{2,1,0:T(8,128)(2,1)S(1)} %broadcast_select_fusion), channel_id=1, source_target_pairs={{0,2},{1,3},{2,0},{3,1},{4,6},{5,7},{6,4},{7,5},{8,10},{9,11},{10,... | collective-permute-start | bytes 663560 | tf_op jit(solution)/shard_map/ppermute | solution.py:373
  4.0 0.0 copy-start
  4.0 1.0 %copy-done = bf16[4,4,32,512]{3,2,1,0:T(8,128)(2,1)S(1)} copy-done((bf16[4,4,32,512]{3,2,1,0:T(8,128)(2,1)S(1)}, bf16[4,4,32,512]{3,2,1,0:T(8,128)(2,1)}, u32[]{:S(2)}) %copy-start) | copy-done | bytes 524312
  5.0 0.0 copy-start.3
  5.0 0.7 %copy-done.3 = s32[4,27]{1,0:T(4,128)S(1)} copy-done((s32[4,27]{1,0:T(4,128)S(1)}, s32[4,27]{1,0:T(4,128)}, u32[]{:S(2)}) %copy-start.3) | copy-done | bytes 456
  5.7 0.0 copy-start.4
  5.7 0.7 %copy-done.4 = f32[4,32]{1,0:T(4,128)S(1)} copy-done((f32[4,32]{1,0:T(4,128)S(1)}, f32[4,32]{1,0:T(4,128)}, u32[]{:S(2)}) %copy-start.4) | copy-done | bytes 536
  6.4 0.0 copy-start.5
  6.4 0.7 %copy-done.5 = s32[1,2,2]{2,1,0:T(2,128)S(1)} copy-done((s32[1,2,2]{2,1,0:T(2,128)S(1)}, s32[1,2,2]{2,1,0:T(2,128)}, u32[]{:S(2)}) %copy-start.5) | copy-done | bytes 40
  7.0 0.0 copy-start.6
  7.0 0.7 %copy-done.6 = f32[32]{0:T(128)S(1)} copy-done((f32[32]{0:T(128)S(1)}, f32[32]{0:T(128)}, u32[]{:S(2)}) %copy-start.6) | copy-done | bytes 152
  7.7 0.0 copy-start.7
  7.7 0.7 %copy-done.7 = f32[32]{0:T(128)S(1)} copy-done((f32[32]{0:T(128)S(1)}, f32[32]{0:T(128)}, u32[]{:S(2)}) %copy-start.7) | copy-done | bytes 152
  8.3 0.1 split_features.1
  8.5 1.0 %collective-permute-start.1 = (bf16[17,32,128]{2,1,0:T(8,128)(2,1)S(1)}, bf16[17,32,128]{2,1,0:T(8,128)(2,1)S(1)}, u32[]{:S(2)}, u32[]{:S(2)}) collective-permute-start(bf16[17,32,128]{2,1,0:T(8,128)(2,1)S(1)} %get-tuple-element.29), channel_id=1, source_target_pairs={{0,1},{1,0},{2,3},{3,2},{4,5},{5,4},{6,7},{7,6},{8,9},{9,8},{10,11... | collective-permute-start | bytes 417800 | tf_op jit(solution)/shard_map/ppermute | solution.py:373
  9.5 0.2 collective-permute-start.2
  9.7 3.0 %collective-permute-start.3 = (bf16[17,32,128]{2,1,0:T(8,128)(2,1)S(1)}, bf16[17,32,128]{2,1,0:T(8,128)(2,1)S(1)}, u32[]{:S(2)}, u32[]{:S(2)}) collective-permute-start(bf16[17,32,128]{2,1,0:T(8,128)(2,1)S(1)} %get-tuple-element.31), channel_id=1, source_target_pairs={{0,3},{1,2},{2,1},{3,0},{4,7},{5,6},{6,5},{7,4},{8,11},{9,10},{10,... | collective-permute-start | bytes 417800 | tf_op jit(solution)/shard_map/ppermute | solution.py:373
  12.7 0.0 copy-done.1
  12.7 0.2 collective-permute-start.6
  12.9 0.0 collective-permute-done.1.refs_1_
  12.9 0.0 copy-done.2
  12.9 0.4 collective-permute-start.7
  13.2 3.0 %collective-permute-done.2.refs_2_ = bf16[17,32,128]{2,1,0:T(8,128)(2,1)S(1)} collective-permute-done((bf16[17,32,128]{2,1,0:T(8,128)(2,1)S(1)}, bf16[17,32,128]{2,1,0:T(8,128)(2,1)S(1)}, u32[]{:S(2)}, u32[]{:S(2)}) %collective-permute-start.2) | collective-permute-done | bytes 139296 | tf_op jit(solution)/shard_map/ppermute | solution.py:373
  16.2 3.2 %collective-permute-done.3.refs_3_ = bf16[17,32,128]{2,1,0:T(8,128)(2,1)S(1)} collective-permute-done((bf16[17,32,128]{2,1,0:T(8,128)(2,1)S(1)}, bf16[17,32,128]{2,1,0:T(8,128)(2,1)S(1)}, u32[]{:S(2)}, u32[]{:S(2)}) %collective-permute-start.3) | collective-permute-done | bytes 139296 | tf_op jit(solution)/shard_map/ppermute | solution.py:373
  19.4 0.0 collective-permute-done.refs_10_
  19.4 0.6 collective-permute-start.10
  20.0 1.6 %collective-permute-start.9 = (bf16[27,32,128]{2,1,0:T(8,128)(2,1)S(1)}, bf16[27,32,128]{2,1,0:T(8,128)(2,1)S(1)}, u32[]{:S(2)}, u32[]{:S(2)}) collective-permute-start(bf16[27,32,128]{2,1,0:T(8,128)(2,1)S(1)} %collective-permute-done.refs_10_), channel_id=1, source_target_pairs={{0,4},{1,5},{2,6},{3,7},{4,0},{5,1},{6,2},{7,3},{8,12},{9,13},{10,... | collective-permute-start | bytes 663560 | tf_op jit(solution)/shard_map/ppermute | solution.py:384
  21.6 0.6 collective-permute-start.8
  22.2 1.0 %pick_faces.1 = (bf16[9,32,128]{2,1,0:T(8,128)(2,1)S(1)}, bf16[9,32,128]{2,1,0:T(8,128)(2,1)S(1)}) custom-call(s32[8,128]{1,0:T(8,128)S(1)} %get-tuple-element.27.tables.tab, bf16[18,32,128]{2,1,0:T(8,128)(2,1)S(1)} %get-tuple-element.28.refs_0_, bf16[17,32,128]{2,1,0:T(8,128)(2,1)S(1)} %collective-permute-done.1.refs_1_, ...), custom_call_target="tpu_custom_call" | custom-call | tf_op jit(solution)/shard_map/pick_faces/pallas_call | solution.py:77
  23.2 0.0 collective-permute-done.6.refs_8_
  23.2 0.1 collective-permute-start.4
  23.3 0.0 collective-permute-done.7.refs_9_
  23.3 6.2 %collective-permute-start.5 = (bf16[9,32,128]{2,1,0:T(8,128)(2,1)S(1)}, bf16[9,32,128]{2,1,0:T(8,128)(2,1)S(1)}, u32[]{:S(2)}, u32[]{:S(2)}) collective-permute-start(bf16[9,32,128]{2,1,0:T(8,128)(2,1)S(1)} %get-tuple-element.36), channel_id=1, source_target_pairs={{0,0},{4,8},{8,4},{12,16},{16,12},{20,24},{24,20},{28,32},{32,28},... | collective-permute-start | bytes 221192 | tf_op jit(solution)/shard_map/ppermute | solution.py:390
  29.5 0.0 collective-permute-done.4.refs_4_
  29.5 2.4 %collective-permute-done.5.refs_5_ = bf16[9,32,128]{2,1,0:T(8,128)(2,1)S(1)} collective-permute-done((bf16[9,32,128]{2,1,0:T(8,128)(2,1)S(1)}, bf16[9,32,128]{2,1,0:T(8,128)(2,1)S(1)}, u32[]{:S(2)}, u32[]{:S(2)}) %collective-permute-start.5) | collective-permute-done | bytes 73760 | tf_op jit(solution)/shard_map/ppermute | solution.py:390
  31.9 0.0 collective-permute-done.10.refs_13_
  31.9 0.0 collective-permute-done.9.refs_12_
  31.9 0.0 collective-permute-done.8.refs_11_
  31.9 11.4 %convolve.1 = (bf16[2,32,512]{2,1,0:T(8,128)(2,1)S(1)}, bf16[2,32,512]{2,1,0:T(8,128)(2,1)S(1)}, bf16[2,32,512]{2,1,0:T(8,128)(2,1)S(1)}, bf16[2,32,512]{2,1,0:T...) custom-call(s32[8,128]{1,0:T(8,128)S(1)} %get-tuple-element.27.table, ...), custom_call_target="tpu_custom_call" | custom-call | flops 6000000000 | bytes 4000000 | tf_op jit(solution)/shard_map/convolve/pallas_call | solution.py:298
  43.3 1.1 %collective-permute-start.11 = (bf16[2,32,512]{2,1,0:T(8,128)(2,1)S(1)}, bf16[2,32,512]{2,1,0:T(8,128)(2,1)S(1)}, u32[]{:S(2)}, u32[]{:S(2)}) collective-permute-start(bf16[2,32,512]{2,1,0:T(8,128)(2,1)S(1)} %get-tuple-element.39), channel_id=1, source_target_pairs={{0,1},{1,0},{2,3},{3,2},{4,5},{5,4},{6,7},{7,6},{8,9},{9,8},{10,11... | collective-permute-start | bytes 196616 | tf_op jit(solution)/shard_map/ppermute | solution.py:373
  44.4 1.6 %collective-permute-start.12 = (bf16[2,32,512]{2,1,0:T(8,128)(2,1)S(1)}, bf16[2,32,512]{2,1,0:T(8,128)(2,1)S(1)}, u32[]{:S(2)}, u32[]{:S(2)}) collective-permute-start(bf16[2,32,512]{2,1,0:T(8,128)(2,1)S(1)} %get-tuple-element.40), channel_id=1, source_target_pairs={{0,2},{1,3},{2,0},{3,1},{4,6},{5,7},{6,4},{7,5},{8,10},{9,11},{10,... | collective-permute-start | bytes 196616 | tf_op jit(solution)/shard_map/ppermute | solution.py:373
  46.0 1.6 %collective-permute-start.13 = (bf16[2,32,512]{2,1,0:T(8,128)(2,1)S(1)}, bf16[2,32,512]{2,1,0:T(8,128)(2,1)S(1)}, u32[]{:S(2)}, u32[]{:S(2)}) collective-permute-start(bf16[2,32,512]{2,1,0:T(8,128)(2,1)S(1)} %get-tuple-element.41), channel_id=1, source_target_pairs={{0,3},{1,2},{2,1},{3,0},{4,7},{5,6},{6,5},{7,4},{8,11},{9,10},{10,... | collective-permute-start | bytes 196616 | tf_op jit(solution)/shard_map/ppermute | solution.py:373
  47.6 1.5 %convolve_rest.1 = (bf16[2,32,512]{2,1,0:T(8,128)(2,1)S(1)}, bf16[2,32,512]{2,1,0:T(8,128)(2,1)S(1)}, bf16[2,32,512]{2,1,0:T(8,128)(2,1)S(1)}, bf16[2,32,512]{2,1,0:T(8,128)(2,1)S(1)}) custom-call(bf16[10,10,16,384]{3,2,1,0:T(8,128)(2,1)S(1)} %get-tuple-element.42.pad, bf16[27,128,128]{2,1,0:T(8,128)(2,1)S(1)} %get-tuple-element.43.w2, ...), custom_call_target="tpu_custom_call" | custom-call | flops 2000000000 | bytes 4000000 | tf_op jit(solution)/shard_map/convolve_rest/pallas_call | solution.py:331
  49.1 0.2 collective-permute-start.14
  49.4 1.6 %collective-permute-start.15 = (bf16[2,32,512]{2,1,0:T(8,128)(2,1)S(1)}, bf16[2,32,512]{2,1,0:T(8,128)(2,1)S(1)}, u32[]{:S(2)}, u32[]{:S(2)}) collective-permute-start(bf16[2,32,512]{2,1,0:T(8,128)(2,1)S(1)} %get-tuple-element.47), channel_id=1, source_target_pairs={{0,2},{1,3},{2,0},{3,1},{4,6},{5,7},{6,4},{7,5},{8,10},{9,11},{10,... | collective-permute-start | bytes 196616 | tf_op jit(solution)/shard_map/ppermute | solution.py:373
  50.9 0.0 collective-permute-done.11.refs_1_
  50.9 1.9 %collective-permute-start.16 = (bf16[2,32,512]{2,1,0:T(8,128)(2,1)S(1)}, bf16[2,32,512]{2,1,0:T(8,128)(2,1)S(1)}, u32[]{:S(2)}, u32[]{:S(2)}) collective-permute-start(bf16[2,32,512]{2,1,0:T(8,128)(2,1)S(1)} %get-tuple-element.48), channel_id=1, source_target_pairs={{0,3},{1,2},{2,1},{3,0},{4,7},{5,6},{6,5},{7,4},{8,11},{9,10},{10,... | collective-permute-start | bytes 196616 | tf_op jit(solution)/shard_map/ppermute | solution.py:373
  52.9 0.0 collective-permute-done.12.refs_2_
  52.9 0.0 collective-permute-done.13.refs_3_
  52.9 0.0 collective-permute-done.14.refs_5_
  52.9 1.1 %collective-permute-done.15.refs_6_ = bf16[2,32,512]{2,1,0:T(8,128)(2,1)S(1)} collective-permute-done((bf16[2,32,512]{2,1,0:T(8,128)(2,1)S(1)}, bf16[2,32,512]{2,1,0:T(8,128)(2,1)S(1)}, u32[]{:S(2)}, u32[]{:S(2)}) %collective-permute-start.15) | collective-permute-done | bytes 65568 | tf_op jit(solution)/shard_map/ppermute | solution.py:373
  54.0 3.1 %collective-permute-done.16.refs_7_ = bf16[2,32,512]{2,1,0:T(8,128)(2,1)S(1)} collective-permute-done((bf16[2,32,512]{2,1,0:T(8,128)(2,1)S(1)}, bf16[2,32,512]{2,1,0:T(8,128)(2,1)S(1)}, u32[]{:S(2)}, u32[]{:S(2)}) %collective-permute-start.16) | collective-permute-done | bytes 65568 | tf_op jit(solution)/shard_map/ppermute | solution.py:373
  57.0 0.8 %join_levels.1 = bf16[4,4,32,512]{3,2,1,0:T(8,128)(2,1)} custom-call(bf16[2,32,512]{2,1,0:T(8,128)(2,1)S(1)} %get-tuple-element.38.refs_0_, bf16[2,32,512]{2,1,0:T(8,128)(2,1)S(1)} %collective-permute-done.11.refs_1_, bf16[2,32,512]{2,1,0:T(8,128)(2,1)S(1)} %collective-permute-done.12.refs_2_, bf16[2,32,512]{2,1,0:T(8,128)(2,1)S(1)} %collective-permute-done.13.refs_3_, ...), custom_call_target="tpu_custom_call" | custom-call | tf_op jit(solution)/shard_map/join_levels/pallas_call | solution.py:361
Async XLA Ops:
  0.0 12.9 %copy-start.2 = (bf16[27,128,32]{1,2,0:T(8,128)(2,1)S(1)}, bf16[27,128,32]{1,2,0:T(8,128)(2,1)}, u32[]{:S(2)}) copy-start(bf16[27,128,32]{1,2,0:T(8,128)(2,1)} %param.13) | copy-start | bytes 663556
  0.0 12.7 %copy-start.1 = (bf16[27,128,32]{1,2,0:T(8,128)(2,1)S(1)}, bf16[27,128,32]{1,2,0:T(8,128)(2,1)}, u32[]{:S(2)}) copy-start(bf16[27,128,32]{1,2,0:T(8,128)(2,1)} %param.11) | copy-start | bytes 663556
  1.1 18.3 %collective-permute-start = (bf16[27,32,128]{2,1,0:T(8,128)(2,1)S(1)}, bf16[27,32,128]{2,1,0:T(8,128)(2,1)S(1)}, u32[]{:S(2)}, u32[]{:S(2)}) collective-permute-start(bf16[27,32,128]{2,1,0:T(8,128)(2,1)S(1)} %broadcast_select_fusion), channel_id=1, source_target_pairs={{0,2},{1,3},{2,0},{3,1},{4,6},{5,7},{6,4},{7,5},{8,10},{9,11},{10,... | collective-permute-start | bytes 663560 | tf_op jit(solution)/shard_map/ppermute | solution.py:373
  4.0 1.0 %copy-start = (bf16[4,4,32,512]{3,2,1,0:T(8,128)(2,1)S(1)}, bf16[4,4,32,512]{3,2,1,0:T(8,128)(2,1)}, u32[]{:S(2)}) copy-start(bf16[4,4,32,512]{3,2,1,0:T(8,128)(2,1)} %feat.1) | copy-start | bytes 1572868
  5.0 0.7 %copy-start.3 = (s32[4,27]{1,0:T(4,128)S(1)}, s32[4,27]{1,0:T(4,128)}, u32[]{:S(2)}) copy-start(s32[4,27]{1,0:T(4,128)} %near.1) | copy-start | bytes 1300
  5.7 0.7 %copy-start.4 = (f32[4,32]{1,0:T(4,128)S(1)}, f32[4,32]{1,0:T(4,128)}, u32[]{:S(2)}) copy-start(f32[4,32]{1,0:T(4,128)} %lev.1) | copy-start | bytes 1540
  6.4 0.7 %copy-start.5 = (s32[1,2,2]{2,1,0:T(2,128)S(1)}, s32[1,2,2]{2,1,0:T(2,128)}, u32[]{:S(2)}) copy-start(s32[1,2,2]{2,1,0:T(2,128)} %lists.1) | copy-start | bytes 52
  7.0 0.7 %copy-start.6 = (f32[32]{0:T(128)S(1)}, f32[32]{0:T(128)}, u32[]{:S(2)}) copy-start(f32[32]{0:T(128)} %param.12) | copy-start | bytes 388
  7.7 0.7 %copy-start.7 = (f32[32]{0:T(128)S(1)}, f32[32]{0:T(128)}, u32[]{:S(2)}) copy-start(f32[32]{0:T(128)} %param.14) | copy-start | bytes 388
  8.5 4.4 %collective-permute-start.1 = (bf16[17,32,128]{2,1,0:T(8,128)(2,1)S(1)}, bf16[17,32,128]{2,1,0:T(8,128)(2,1)S(1)}, u32[]{:S(2)}, u32[]{:S(2)}) collective-permute-start(bf16[17,32,128]{2,1,0:T(8,128)(2,1)S(1)} %get-tuple-element.29), channel_id=1, source_target_pairs={{0,1},{1,0},{2,3},{3,2},{4,5},{5,4},{6,7},{7,6},{8,9},{9,8},{10,11... | collective-permute-start | bytes 417800 | tf_op jit(solution)/shard_map/ppermute | solution.py:373
  9.5 6.7 %collective-permute-start.2 = (bf16[17,32,128]{2,1,0:T(8,128)(2,1)S(1)}, bf16[17,32,128]{2,1,0:T(8,128)(2,1)S(1)}, u32[]{:S(2)}, u32[]{:S(2)}) collective-permute-start(bf16[17,32,128]{2,1,0:T(8,128)(2,1)S(1)} %get-tuple-element.30), channel_id=1, source_target_pairs={{0,2},{1,3},{2,0},{3,1},{4,6},{5,7},{6,4},{7,5},{8,10},{9,11},{10,... | collective-permute-start | bytes 417800 | tf_op jit(solution)/shard_map/ppermute | solution.py:373
  9.7 9.7 %collective-permute-start.3 = (bf16[17,32,128]{2,1,0:T(8,128)(2,1)S(1)}, bf16[17,32,128]{2,1,0:T(8,128)(2,1)S(1)}, u32[]{:S(2)}, u32[]{:S(2)}) collective-permute-start(bf16[17,32,128]{2,1,0:T(8,128)(2,1)S(1)} %get-tuple-element.31), channel_id=1, source_target_pairs={{0,3},{1,2},{2,1},{3,0},{4,7},{5,6},{6,5},{7,4},{8,11},{9,10},{10,... | collective-permute-start | bytes 417800 | tf_op jit(solution)/shard_map/ppermute | solution.py:373
  12.7 10.5 %collective-permute-start.6 = (bf16[27,32,128]{2,1,0:T(8,128)(2,1)S(1)}, bf16[27,32,128]{2,1,0:T(8,128)(2,1)S(1)}, u32[]{:S(2)}, u32[]{:S(2)}) collective-permute-start(bf16[27,32,128]{2,1,0:T(8,128)(2,1)S(1)} %bitcast.6), channel_id=1, source_target_pairs={{0,1},{1,0},{2,3},{3,2},{4,5},{5,4},{6,7},{7,6},{8,9},{9,8},{10,11... | collective-permute-start | bytes 663560 | tf_op jit(solution)/shard_map/ppermute | solution.py:373
  12.9 10.4 %collective-permute-start.7 = (bf16[27,32,128]{2,1,0:T(8,128)(2,1)S(1)}, bf16[27,32,128]{2,1,0:T(8,128)(2,1)S(1)}, u32[]{:S(2)}, u32[]{:S(2)}) collective-permute-start(bf16[27,32,128]{2,1,0:T(8,128)(2,1)S(1)} %bitcast.8), channel_id=1, source_target_pairs={{0,1},{1,0},{2,3},{3,2},{4,5},{5,4},{6,7},{7,6},{8,9},{9,8},{10,11... | collective-permute-start | bytes 663560 | tf_op jit(solution)/shard_map/ppermute | solution.py:373
  19.4 12.5 %collective-permute-start.10 = (bf16[27,32,128]{2,1,0:T(8,128)(2,1)S(1)}, bf16[27,32,128]{2,1,0:T(8,128)(2,1)S(1)}, u32[]{:S(2)}, u32[]{:S(2)}) collective-permute-start(bf16[27,32,128]{2,1,0:T(8,128)(2,1)S(1)} %collective-permute-done.refs_10_), channel_id=1, source_target_pairs={{0,33},{1,32},{2,35},{3,34},{4,37},{5,36},{6,39},{7,38},{8,41},{9,... | collective-permute-start | bytes 663560 | tf_op jit(solution)/shard_map/ppermute | solution.py:384
  20.0 12.0 %collective-permute-start.9 = (bf16[27,32,128]{2,1,0:T(8,128)(2,1)S(1)}, bf16[27,32,128]{2,1,0:T(8,128)(2,1)S(1)}, u32[]{:S(2)}, u32[]{:S(2)}) collective-permute-start(bf16[27,32,128]{2,1,0:T(8,128)(2,1)S(1)} %collective-permute-done.refs_10_), channel_id=1, source_target_pairs={{0,4},{1,5},{2,6},{3,7},{4,0},{5,1},{6,2},{7,3},{8,12},{9,13},{10,... | collective-permute-start | bytes 663560 | tf_op jit(solution)/shard_map/ppermute | solution.py:384
  21.6 10.3 %collective-permute-start.8 = (bf16[27,32,128]{2,1,0:T(8,128)(2,1)S(1)}, bf16[27,32,128]{2,1,0:T(8,128)(2,1)S(1)}, u32[]{:S(2)}, u32[]{:S(2)}) collective-permute-start(bf16[27,32,128]{2,1,0:T(8,128)(2,1)S(1)} %collective-permute-done.refs_10_), channel_id=1, source_target_pairs={{0,1},{1,0},{2,3},{3,2},{4,5},{5,4},{6,7},{7,6},{8,9},{9,8},{10,11... | collective-permute-start | bytes 663560 | tf_op jit(solution)/shard_map/ppermute | solution.py:373
  23.2 6.3 %collective-permute-start.4 = (bf16[9,32,128]{2,1,0:T(8,128)(2,1)S(1)}, bf16[9,32,128]{2,1,0:T(8,128)(2,1)S(1)}, u32[]{:S(2)}, u32[]{:S(2)}) collective-permute-start(bf16[9,32,128]{2,1,0:T(8,128)(2,1)S(1)} %get-tuple-element.35), channel_id=1, source_target_pairs={{0,4},{4,0},{8,12},{12,8},{16,20},{20,16},{24,28},{28,24},{32,36},... | collective-permute-start | bytes 221192 | tf_op jit(solution)/shard_map/ppermute | solution.py:390
  23.3 8.6 %collective-permute-start.5 = (bf16[9,32,128]{2,1,0:T(8,128)(2,1)S(1)}, bf16[9,32,128]{2,1,0:T(8,128)(2,1)S(1)}, u32[]{:S(2)}, u32[]{:S(2)}) collective-permute-start(bf16[9,32,128]{2,1,0:T(8,128)(2,1)S(1)} %get-tuple-element.36), channel_id=1, source_target_pairs={{0,0},{4,8},{8,4},{12,16},{16,12},{20,24},{24,20},{28,32},{32,28},... | collective-permute-start | bytes 221192 | tf_op jit(solution)/shard_map/ppermute | solution.py:390
  43.3 7.6 %collective-permute-start.11 = (bf16[2,32,512]{2,1,0:T(8,128)(2,1)S(1)}, bf16[2,32,512]{2,1,0:T(8,128)(2,1)S(1)}, u32[]{:S(2)}, u32[]{:S(2)}) collective-permute-start(bf16[2,32,512]{2,1,0:T(8,128)(2,1)S(1)} %get-tuple-element.39), channel_id=1, source_target_pairs={{0,1},{1,0},{2,3},{3,2},{4,5},{5,4},{6,7},{7,6},{8,9},{9,8},{10,11... | collective-permute-start | bytes 196616 | tf_op jit(solution)/shard_map/ppermute | solution.py:373
  44.4 8.5 %collective-permute-start.12 = (bf16[2,32,512]{2,1,0:T(8,128)(2,1)S(1)}, bf16[2,32,512]{2,1,0:T(8,128)(2,1)S(1)}, u32[]{:S(2)}, u32[]{:S(2)}) collective-permute-start(bf16[2,32,512]{2,1,0:T(8,128)(2,1)S(1)} %get-tuple-element.40), channel_id=1, source_target_pairs={{0,2},{1,3},{2,0},{3,1},{4,6},{5,7},{6,4},{7,5},{8,10},{9,11},{10,... | collective-permute-start | bytes 196616 | tf_op jit(solution)/shard_map/ppermute | solution.py:373
  46.0 6.9 %collective-permute-start.13 = (bf16[2,32,512]{2,1,0:T(8,128)(2,1)S(1)}, bf16[2,32,512]{2,1,0:T(8,128)(2,1)S(1)}, u32[]{:S(2)}, u32[]{:S(2)}) collective-permute-start(bf16[2,32,512]{2,1,0:T(8,128)(2,1)S(1)} %get-tuple-element.41), channel_id=1, source_target_pairs={{0,3},{1,2},{2,1},{3,0},{4,7},{5,6},{6,5},{7,4},{8,11},{9,10},{10,... | collective-permute-start | bytes 196616 | tf_op jit(solution)/shard_map/ppermute | solution.py:373
  49.1 3.7 %collective-permute-start.14 = (bf16[2,32,512]{2,1,0:T(8,128)(2,1)S(1)}, bf16[2,32,512]{2,1,0:T(8,128)(2,1)S(1)}, u32[]{:S(2)}, u32[]{:S(2)}) collective-permute-start(bf16[2,32,512]{2,1,0:T(8,128)(2,1)S(1)} %get-tuple-element.46), channel_id=1, source_target_pairs={{0,1},{1,0},{2,3},{3,2},{4,5},{5,4},{6,7},{7,6},{8,9},{9,8},{10,11... | collective-permute-start | bytes 196616 | tf_op jit(solution)/shard_map/ppermute | solution.py:373
  49.4 4.6 %collective-permute-start.15 = (bf16[2,32,512]{2,1,0:T(8,128)(2,1)S(1)}, bf16[2,32,512]{2,1,0:T(8,128)(2,1)S(1)}, u32[]{:S(2)}, u32[]{:S(2)}) collective-permute-start(bf16[2,32,512]{2,1,0:T(8,128)(2,1)S(1)} %get-tuple-element.47), channel_id=1, source_target_pairs={{0,2},{1,3},{2,0},{3,1},{4,6},{5,7},{6,4},{7,5},{8,10},{9,11},{10,... | collective-permute-start | bytes 196616 | tf_op jit(solution)/shard_map/ppermute | solution.py:373
  50.9 6.1 %collective-permute-start.16 = (bf16[2,32,512]{2,1,0:T(8,128)(2,1)S(1)}, bf16[2,32,512]{2,1,0:T(8,128)(2,1)S(1)}, u32[]{:S(2)}, u32[]{:S(2)}) collective-permute-start(bf16[2,32,512]{2,1,0:T(8,128)(2,1)S(1)} %get-tuple-element.48), channel_id=1, source_target_pairs={{0,3},{1,2},{2,1},{3,0},{4,7},{5,6},{6,5},{7,4},{8,11},{9,10},{10,... | collective-permute-start | bytes 196616 | tf_op jit(solution)/shard_map/ppermute | solution.py:373

commit v10 on v8

--- a/solution.py
+++ b/solution.py
@@ -146,13 +146,30 @@
     return total
 
 
-def load_shards(sources, weights, order, sem):
-    return [
-        pltpu.make_async_copy(
-            source, weights.at[:, pl.ds(pl.multiple_of(32 * order[m], 32), 32), :], sem.at[m]
-        )
-        for m, source in enumerate(sources)
-    ]
+def layer_of_slab():
+    slab = lax.axis_index("slab")
+    return (slab + slab // 8) % 2
+
+
+def load_shards(layer, near, far, weights, order, sem):
+    copies = []
+    for m in range(4):
+        rows = weights.at[:, pl.ds(pl.multiple_of(32 * order[m], 32), 32), :]
+        if m < 2:
+            copies.append(pltpu.make_async_copy(near[m], rows, sem.at[m]))
+            copies[m].start()
+            continue
+
+        @pl.when(layer_of_slab() == layer)
+        def _():
+            pltpu.make_async_copy(far[m - 2], rows, sem.at[m]).start()
+
+        @pl.when(layer_of_slab() != layer)
+        def _():
+            pltpu.make_async_copy(far[m], rows, sem.at[m]).start()
+
+        copies.append(pltpu.make_async_copy(far[m], rows, sem.at[m]))
+    return copies
 
 
 def finish(acc, moved, tab, pair, slots):
@@ -166,9 +183,9 @@
 
 
 def first_kernel(tab, *refs):
-    feat, sides, shards = refs[0:4], refs[4:6], refs[6:10]
-    pad_out, shift = refs[10:12]
-    fs, hs, w1, bias, sent, sent_int, tables, slots, pad, pad_face, acc, sem = refs[12:]
+    feat, sides, near, far = refs[0:4], refs[4:6], refs[6:8], refs[8:12]
+    pad_out, shift = refs[12:14]
+    fs, hs, w1, bias, sent, sent_int, tables, slots, pad, pad_face, acc, sem, w_sem = refs[14:]
     me = lax.axis_index("chan")
 
     f_copies, t_copies = [], []
@@ -179,11 +196,9 @@
     for m in range(4):
         f_copies.append(pltpu.make_async_copy(feat[m].at[pl.ds(0, 16)], fs.at[m], sem.at[4 + m]))
         f_copies.append(pltpu.make_async_copy(feat[m].at[16, pl.ds(0, 16)], bias.at[m], sem.at[8 + m]))
-    w_copies = [
-        pltpu.make_async_copy(shards[m], w1.at[:, pl.ds(32 * m, 32), :], sem.at[12 + m]) for m in range(4)
-    ]
-    for copy in t_copies + f_copies + w_copies:
+    for copy in t_copies + f_copies:
         copy.start()
+    w_copies = load_shards(0, near, far, w1, range(4), w_sem)
     for copy in t_copies:
         copy.wait()
     sent_int[...] = sent[...].astype(F32).astype(jnp.int32).reshape(32, 128)
@@ -250,11 +265,11 @@
         gather_padded(slots, pad_out, pair, own(pair), OWN_PLANES)
 
 
-def convolve_first(tables, feat, sides, shards):
+def convolve_first(tables, feat, sides, near, far):
     return pl.pallas_call(
         first_kernel,
         out_shape=[jax.ShapeDtypeStruct((2, 10, 10, 16, 384), BF16), jax.ShapeDtypeStruct((8, 128), F32)],
-        in_specs=[SMEM] + [HBM] * 10,
+        in_specs=[SMEM] + [HBM] * 12,
         out_specs=[VMEM] * 2,
         scratch_shapes=[
             pltpu.VMEM((4, 16, 32, 128), BF16),
@@ -269,21 +284,19 @@
             pltpu.VMEM((2, 3, 10, 16, 384), BF16),
             pltpu.VMEM((2, 512, 256), F32),
             pltpu.SemaphoreType.DMA((17,)),
+            pltpu.SemaphoreType.DMA((4,)),
         ],
         compiler_params=pltpu.CompilerParams(vmem_limit_bytes=24 << 20),
         cost_estimate=pl.CostEstimate(flops=5 * 10**9, bytes_accessed=4 * 10**6, transcendentals=10**6),
         name="convolve_first",
-    )(tables, *feat, *sides, *shards)
+    )(tables, *feat, *sides, *near, *far)
 
 
 def second_kernel(tab, pad, shift, *refs):
-    shards, outs = refs[0:4], refs[4:8]
-    w2, slots, acc, turned, sem = refs[8:]
+    near, far, outs = refs[0:2], refs[2:6], refs[6:10]
+    w2, slots, acc, turned, sem = refs[10:]
     me = lax.axis_index("chan")
-    w_copies = load_shards(shards, w2, [me ^ m for m in range(4)], sem)
-    for copy in w_copies:
-        copy.start()
-    for copy in w_copies:
+    for copy in load_shards(1, near, far, w2, [me ^ m for m in range(4)], sem):
         copy.wait()
     for pair in range(2):
         acc[pair] = conv_pair(pad, pair, w2)
@@ -296,12 +309,12 @@
         outs[m][...] = turned[me ^ m]
 
 
-def convolve_second(tables, pad, shift, shards):
+def convolve_second(tables, pad, shift, near, far):
     piece = jax.ShapeDtypeStruct((4, 32, 512), BF16)
     return pl.pallas_call(
         second_kernel,
         out_shape=[piece] * 4,
-        in_specs=[SMEM, VMEM, VMEM] + [HBM] * 4,
+        in_specs=[SMEM, VMEM, VMEM] + [HBM] * 6,
         out_specs=[VMEM] * 4,
         scratch_shapes=[
             pltpu.VMEM((27, 128, 128), BF16),
@@ -313,7 +326,7 @@
         compiler_params=pltpu.CompilerParams(vmem_limit_bytes=24 << 20),
         cost_estimate=pl.CostEstimate(flops=4 * 10**9, bytes_accessed=4 * 10**6, transcendentals=10**6),
         name="convolve_second",
-    )(tables, pad, shift, *shards)
+    )(tables, pad, shift, *near, *far)
 
 
 def join_kernel(*refs):
@@ -342,6 +355,12 @@
     return lax.ppermute(value, "chan", [(i, i ^ m) for i in range(4)])
 
 
+def swap_slabs(value, step, m):
+    count = lax.axis_size("slab")
+    pairs = [(4 * s + g, 4 * (s ^ step) + (g ^ m)) for s in range(count) for g in range(4)]
+    return lax.ppermute(value, ("slab", "chan"), pairs)
+
+
 def swap_faces(value, first):
     count = lax.axis_size("slab")
     partner = [((s + first) ^ 1) - first for s in range(count)]
@@ -350,20 +369,19 @@
 
 def shards(features, neighbours, face_lists, w_first, b_first, w_second, b_second, level_embed):
     w1, w2 = w_first.transpose(0, 2, 1), w_second.transpose(0, 2, 1)
-    far = swap(w1, 2)
+    fetched = swap(jnp.where(layer_of_slab() == 0, w1, w2), 2)
     own, one, two, three, tables = split(
         features, neighbours, face_lists, b_first, b_second, level_embed
     )
-    far, one, two, three, later = lax.optimization_barrier(
-        (far, swap(one, 1), swap(two, 2), swap(three, 3), w2)
+    fetched, one, two, three = lax.optimization_barrier(
+        (fetched, swap(one, 1), swap(two, 2), swap(three, 3))
     )
     pieces = [own, one, two, three]
-    first = [w1, swap(w1, 1), far, swap(far, 1)]
+    far = [fetched, swap(fetched, 1), swap_slabs(fetched, 1, 0), swap_slabs(fetched, 8, 1)]
     sides = faces(tables, pieces)
     sides = [swap_faces(sides[i], i) for i in range(2)]
-    second = [w2] + [swap(later, m) for m in (1, 2, 3)]
-    pad, shift = convolve_first(tables, pieces, sides, first)
-    outs = convolve_second(tables, pad, shift, second)
+    pad, shift = convolve_first(tables, pieces, sides, (w1, swap(w1, 1)), far)
+    outs = convolve_second(tables, pad, shift, (w2, swap(w2, 1)), far)
     return join([outs[0]] + [swap(outs[m], m) for m in (1, 2, 3)])
 
 

time: 54.7 us -> 56 us (1.024)
  other arithmetic: 0 us -> 1.07 us
    ppermute x12 -> x10, starting transfers between devices: 15 us -> 12.4 us  [swap(): return lax.ppermute(value, 'chan', [(i, i ^ m) for i in range(4)])]
    ppermute x0 -> x2, starting transfers between devices: none -> 2.56 us  [swap_slabs(): return lax.ppermute(value, ('slab', 'chan'), pairs)]
    ppermute x12 -> x10, waiting for transfers between devices: 15.2 us -> 12.8 us  [swap(): return lax.ppermute(value, 'chan', [(i, i ^ m) for i in range(4)])]
    ppermute x2, waiting for transfers between devices: 0.01 us -> 1.84 us  [swap_faces(): lax.ppermute(value, 'slab', [(s, p if 0 <= p < count else s) for s, p in...]
    select_n x0 -> x1, other arithmetic: none -> 1.07 us  [shards(): fetched = swap(jnp.where(layer_of_slab() == 0, w1, w2), 2)]
where the time goes in v10:
time: 56 us; the launch traced here: 55.3 us
  starting transfers between devices  21.2 us (38%)
  waiting for transfers between devices  14.7 us (26%)
  Pallas kernels  12.9 us (23%)
  local copies, waits for them, and re-layouts  5.33 us (10%)
  other arithmetic  1.07 us (2%)
    ppermute x10, waiting for transfers between devices, swap(): return lax.ppermute(value, 'chan', [(i, i ^ m) for i in range(4)])  12.8 us
    ppermute x10, starting transfers between devices, swap(): return lax.ppermute(value, 'chan', [(i, i ^ m) for i in range(4)])  12.4 us
    pallas_call x1, Pallas kernels, convolve_first(): pl.pallas_call(first_kernel, out_shape=[jax.ShapeDtypeStruct((2, 10, 10,...  7.21 us
    ppermute x2, starting transfers between devices, swap_faces(): lax.ppermute(value, 'slab', [(s, p if 0 <= p < count else s) for s, p in...  6.3 us
    unnamed x16, local copies, waits for them, and re-layouts  5.33 us
    pallas_call x1, Pallas kernels, convolve_second(): pl.pallas_call(second_kernel, out_shape=[piece] * 4, in_specs=[SMEM, VMEM...  3.7 us
    ppermute x2, starting transfers between devices, swap_slabs(): return lax.ppermute(value, ('slab', 'chan'), pairs)  2.56 us
    ppermute x2, waiting for transfers between devices, swap_faces(): lax.ppermute(value, 'slab', [(s, p if 0 <= p < count else s) for s, p in...  1.84 us
  transfers between devices with their start and end apart: 14, of which 5 were waited for; matrix products, arithmetic and copies ran while one was open for 0% of the time, Pallas kernels for 15%

profile of v10, /device:TPU:25, one launch (start us, length us, event | category | flops | bytes accessed | tf_op | source)
XLA Modules:
  0.0 55.3 jit_solution(15398596021835441598)
XLA Ops:
  0.0 1.1 %broadcast_select_fusion = bf16[27,32,128]{2,1,0:T(8,128)(2,1)S(1)} fusion(pred[]{:T(512)S(6)} %eq.5, bf16[27,128,32]{1,2,0:T(8,128)(2,1)} %param.13, bf16[27,128,32]{1,2,0:T(8,128)(2,1)} %param.11), kind=kLoop, calls=%fused_computation | loop fusion | flops 110592 | bytes 663553 | tf_op jit(solution)/shard_map/jit(_where)/select_n | solution.py:372
  1.1 2.8 %collective-permute-start = (bf16[27,32,128]{2,1,0:T(8,128)(2,1)S(1)}, bf16[27,32,128]{2,1,0:T(8,128)(2,1)S(1)}, u32[]{:S(2)}, u32[]{:S(2)}) collective-permute-start(bf16[27,32,128]{2,1,0:T(8,128)(2,1)S(1)} %broadcast_select_fusion), channel_id=1, source_target_pairs={{0,2},{1,3},{2,0},{3,1},{4,6},{5,7},{6,4},{7,5},{8,10},{9,11},{10,... | collective-permute-start | bytes 663560 | tf_op jit(solution)/shard_map/ppermute | solution.py:355
  3.9 0.0 copy-start
  3.9 1.0 %copy-done = bf16[4,4,32,512]{3,2,1,0:T(8,128)(2,1)S(1)} copy-done((bf16[4,4,32,512]{3,2,1,0:T(8,128)(2,1)S(1)}, bf16[4,4,32,512]{3,2,1,0:T(8,128)(2,1)}, u32[]{:S(2)}) %copy-start) | copy-done | bytes 524312
  4.9 0.0 copy-start.3
  4.9 0.7 %copy-done.3 = s32[4,27]{1,0:T(4,128)S(1)} copy-done((s32[4,27]{1,0:T(4,128)S(1)}, s32[4,27]{1,0:T(4,128)}, u32[]{:S(2)}) %copy-start.3) | copy-done | bytes 456
  5.6 0.0 copy-start.4
  5.6 0.7 %copy-done.4 = f32[4,32]{1,0:T(4,128)S(1)} copy-done((f32[4,32]{1,0:T(4,128)S(1)}, f32[4,32]{1,0:T(4,128)}, u32[]{:S(2)}) %copy-start.4) | copy-done | bytes 536
  6.3 0.0 copy-start.5
  6.3 0.7 %copy-done.5 = s32[1,2,2]{2,1,0:T(2,128)S(1)} copy-done((s32[1,2,2]{2,1,0:T(2,128)S(1)}, s32[1,2,2]{2,1,0:T(2,128)}, u32[]{:S(2)}) %copy-start.5) | copy-done | bytes 40
  7.0 0.0 copy-start.6
  7.0 0.7 %copy-done.6 = f32[32]{0:T(128)S(1)} copy-done((f32[32]{0:T(128)S(1)}, f32[32]{0:T(128)}, u32[]{:S(2)}) %copy-start.6) | copy-done | bytes 152
  7.6 0.0 copy-start.7
  7.6 0.7 %copy-done.7 = f32[32]{0:T(128)S(1)} copy-done((f32[32]{0:T(128)S(1)}, f32[32]{0:T(128)}, u32[]{:S(2)}) %copy-start.7) | copy-done | bytes 152
  8.3 0.1 split_features.1
  8.4 1.0 %collective-permute-start.1 = (bf16[17,32,128]{2,1,0:T(8,128)(2,1)S(1)}, bf16[17,32,128]{2,1,0:T(8,128)(2,1)S(1)}, u32[]{:S(2)}, u32[]{:S(2)}) collective-permute-start(bf16[17,32,128]{2,1,0:T(8,128)(2,1)S(1)} %get-tuple-element.24), channel_id=1, source_target_pairs={{0,1},{1,0},{2,3},{3,2},{4,5},{5,4},{6,7},{7,6},{8,9},{9,8},{10,11... | collective-permute-start | bytes 417800 | tf_op jit(solution)/shard_map/ppermute | solution.py:355
  9.4 0.2 collective-permute-start.2
  9.7 3.0 %collective-permute-start.3 = (bf16[17,32,128]{2,1,0:T(8,128)(2,1)S(1)}, bf16[17,32,128]{2,1,0:T(8,128)(2,1)S(1)}, u32[]{:S(2)}, u32[]{:S(2)}) collective-permute-start(bf16[17,32,128]{2,1,0:T(8,128)(2,1)S(1)} %get-tuple-element.26), channel_id=1, source_target_pairs={{0,3},{1,2},{2,1},{3,0},{4,7},{5,6},{6,5},{7,4},{8,11},{9,10},{10,... | collective-permute-start | bytes 417800 | tf_op jit(solution)/shard_map/ppermute | solution.py:355
  12.7 0.2 collective-permute-start.6
  12.8 0.0 collective-permute-done.1.refs_1_
  12.8 3.4 %collective-permute-done.2.refs_2_ = bf16[17,32,128]{2,1,0:T(8,128)(2,1)S(1)} collective-permute-done((bf16[17,32,128]{2,1,0:T(8,128)(2,1)S(1)}, bf16[17,32,128]{2,1,0:T(8,128)(2,1)S(1)}, u32[]{:S(2)}, u32[]{:S(2)}) %collective-permute-start.2) | collective-permute-done | bytes 139296 | tf_op jit(solution)/shard_map/ppermute | solution.py:355
  16.2 3.2 %collective-permute-done.3.refs_3_ = bf16[17,32,128]{2,1,0:T(8,128)(2,1)S(1)} collective-permute-done((bf16[17,32,128]{2,1,0:T(8,128)(2,1)S(1)}, bf16[17,32,128]{2,1,0:T(8,128)(2,1)S(1)}, u32[]{:S(2)}, u32[]{:S(2)}) %collective-permute-start.3) | collective-permute-done | bytes 139296 | tf_op jit(solution)/shard_map/ppermute | solution.py:355
  19.3 0.0 collective-permute-done.refs_8_.refs_2_
  19.3 0.2 collective-permute-start.7
  19.6 1.6 %collective-permute-start.8 = (bf16[27,32,128]{2,1,0:T(8,128)(2,1)S(1)}, bf16[27,32,128]{2,1,0:T(8,128)(2,1)S(1)}, u32[]{:S(2)}, u32[]{:S(2)}) collective-permute-start(bf16[27,32,128]{2,1,0:T(8,128)(2,1)S(1)} %collective-permute-done.refs_8_.refs_2_), channel_id=1, source_target_pairs={{0,4},{1,5},{2,6},{3,7},{4,0},{5,1},{6,2},{7,3},{8,12},{9,13},{10,... | collective-permute-start | bytes 663560 | tf_op jit(solution)/shard_map/ppermute | solution.py:361
  21.2 0.9 %collective-permute-start.9 = (bf16[27,32,128]{2,1,0:T(8,128)(2,1)S(1)}, bf16[27,32,128]{2,1,0:T(8,128)(2,1)S(1)}, u32[]{:S(2)}, u32[]{:S(2)}) collective-permute-start(bf16[27,32,128]{2,1,0:T(8,128)(2,1)S(1)} %collective-permute-done.refs_8_.refs_2_), channel_id=1, source_target_pairs={{0,33},{1,32},{2,35},{3,34},{4,37},{5,36},{6,39},{7,38},{8,41},{9,... | collective-permute-start | bytes 663560 | tf_op jit(solution)/shard_map/ppermute | solution.py:361
  22.1 1.0 %pick_faces.1 = (bf16[9,32,128]{2,1,0:T(8,128)(2,1)S(1)}, bf16[9,32,128]{2,1,0:T(8,128)(2,1)S(1)}) custom-call(s32[8,128]{1,0:T(8,128)S(1)} %get-tuple-element.22.tables.tab, bf16[18,32,128]{2,1,0:T(8,128)(2,1)S(1)} %get-tuple-element.23.refs_0_, bf16[17,32,128]{2,1,0:T(8,128)(2,1)S(1)} %collective-permute-done.1.refs_1_, ...), custom_call_target="tpu_custom_call" | custom-call | tf_op jit(solution)/shard_map/pick_faces/pallas_call | solution.py:77
  23.1 0.1 collective-permute-start.4
  23.2 0.0 collective-permute-done.6.refs_7_
  23.2 6.2 %collective-permute-start.5 = (bf16[9,32,128]{2,1,0:T(8,128)(2,1)S(1)}, bf16[9,32,128]{2,1,0:T(8,128)(2,1)S(1)}, u32[]{:S(2)}, u32[]{:S(2)}) collective-permute-start(bf16[9,32,128]{2,1,0:T(8,128)(2,1)S(1)} %get-tuple-element.31), channel_id=1, source_target_pairs={{0,0},{4,8},{8,4},{12,16},{16,12},{20,24},{24,20},{28,32},{32,28},... | collective-permute-start | bytes 221192 | tf_op jit(solution)/shard_map/ppermute | solution.py:367
  29.5 0.0 collective-permute-done.4.refs_4_
  29.5 0.6 %collective-permute-start.10 = (bf16[27,32,128]{2,1,0:T(8,128)(2,1)}, bf16[27,32,128]{2,1,0:T(8,128)(2,1)S(1)}, u32[]{:S(2)}, u32[]{:S(2)}) collective-permute-start(bf16[27,32,128]{2,1,0:T(8,128)(2,1)} %bitcast.8), channel_id=1, source_target_pairs={{0,1},{1,0},{2,3},{3,2},{4,5},{5,4},{6,7},{7,6},{8,9},{9,8},{10,11... | collective-permute-start | bytes 663560 | tf_op jit(solution)/shard_map/ppermute | solution.py:355
  30.0 1.8 %collective-permute-done.5.refs_5_ = bf16[9,32,128]{2,1,0:T(8,128)(2,1)S(1)} collective-permute-done((bf16[9,32,128]{2,1,0:T(8,128)(2,1)S(1)}, bf16[9,32,128]{2,1,0:T(8,128)(2,1)S(1)}, u32[]{:S(2)}, u32[]{:S(2)}) %collective-permute-start.5) | collective-permute-done | bytes 73760 | tf_op jit(solution)/shard_map/ppermute | solution.py:367
  31.9 0.0 collective-permute-done.7.refs_9_.refs_3_
  31.9 0.0 collective-permute-done.8.refs_10_.refs_4_
  31.9 0.0 collective-permute-done.9.refs_11_.refs_5_
  31.9 0.0 copy-start.1
  31.9 0.9 %copy-done.1 = bf16[27,128,32]{1,2,0:T(8,128)(2,1)S(1)} copy-done((bf16[27,128,32]{1,2,0:T(8,128)(2,1)S(1)}, bf16[27,128,32]{1,2,0:T(8,128)(2,1)}, u32[]{:S(2)}) %copy-start.1) | copy-done | bytes 221208
  32.8 0.0 copy-start.2
  32.8 7.2 %convolve_first.1 = (bf16[2,10,10,16,384]{4,3,2,1,0:T(8,128)(2,1)S(1)}, f32[8,128]{1,0:T(8,128)S(1)}) custom-call(s32[8,128]{1,0:T(8,128)S(1)} %get-tuple-element.22.tables.tab, bf16[18,32,128]{2,1,0:T(8,128)(2,1)S(1)} %get-tuple-element.23.refs_0_, bf16[17,32,128]{2,1,0:T(8,128)(2,1)S(1)} %collective-permute-done.1.refs_1_, ...), custom_call_target="tpu_custom_call" | custom-call | flops 5000000000 | bytes 4000000 | tf_op jit(solution)/shard_map/convolve_first/pallas_call | solution.py:269
  40.1 0.0 collective-permute-done.10.refs_1_
  40.1 0.0 copy-done.2
  40.1 3.7 %convolve_second.1 = (bf16[4,32,512]{2,1,0:T(8,128)(2,1)S(1)}, bf16[4,32,512]{2,1,0:T(8,128)(2,1)S(1)}, bf16[4,32,512]{2,1,0:T(8,128)(2,1)S(1)}, bf16[4,32,512]{2,1,0:T(8,128)(2,1)S(1)}) custom-call(s32[8,128]{1,0:T(8,128)S(1)} %get-tuple-element.22.tables.tab, bf16[2,10,10,16,384]{4,3,2,1,0:T(8,128)(2,1)S(1)} %get-tuple-element.33.pad, ...), custom_call_target="tpu_custom_call" | custom-call | flops 4000000000 | bytes 4000000 | tf_op jit(solution)/shard_map/convolve_second/pallas_call | solution.py:314
  43.8 1.1 %collective-permute-start.11 = (bf16[4,32,512]{2,1,0:T(8,128)(2,1)S(1)}, bf16[4,32,512]{2,1,0:T(8,128)(2,1)S(1)}, u32[]{:S(2)}, u32[]{:S(2)}) collective-permute-start(bf16[4,32,512]{2,1,0:T(8,128)(2,1)S(1)} %get-tuple-element.36), channel_id=1, source_target_pairs={{0,1},{1,0},{2,3},{3,2},{4,5},{5,4},{6,7},{7,6},{8,9},{9,8},{10,11... | collective-permute-start | bytes 393224 | tf_op jit(solution)/shard_map/ppermute | solution.py:355
  44.9 1.5 %collective-permute-start.12 = (bf16[4,32,512]{2,1,0:T(8,128)(2,1)S(1)}, bf16[4,32,512]{2,1,0:T(8,128)(2,1)S(1)}, u32[]{:S(2)}, u32[]{:S(2)}) collective-permute-start(bf16[4,32,512]{2,1,0:T(8,128)(2,1)S(1)} %get-tuple-element.37), channel_id=1, source_target_pairs={{0,2},{1,3},{2,0},{3,1},{4,6},{5,7},{6,4},{7,5},{8,10},{9,11},{10,... | collective-permute-start | bytes 393224 | tf_op jit(solution)/shard_map/ppermute | solution.py:355
  46.4 1.7 %collective-permute-start.13 = (bf16[4,32,512]{2,1,0:T(8,128)(2,1)S(1)}, bf16[4,32,512]{2,1,0:T(8,128)(2,1)S(1)}, u32[]{:S(2)}, u32[]{:S(2)}) collective-permute-start(bf16[4,32,512]{2,1,0:T(8,128)(2,1)S(1)} %get-tuple-element.38), channel_id=1, source_target_pairs={{0,3},{1,2},{2,1},{3,0},{4,7},{5,6},{6,5},{7,4},{8,11},{9,10},{10,... | collective-permute-start | bytes 393224 | tf_op jit(solution)/shard_map/ppermute | solution.py:355
  48.1 0.0 collective-permute-done.11.refs_1_
  48.1 3.3 %collective-permute-done.12.refs_2_ = bf16[4,32,512]{2,1,0:T(8,128)(2,1)S(1)} collective-permute-done((bf16[4,32,512]{2,1,0:T(8,128)(2,1)S(1)}, bf16[4,32,512]{2,1,0:T(8,128)(2,1)S(1)}, u32[]{:S(2)}, u32[]{:S(2)}) %collective-permute-start.12) | collective-permute-done | bytes 131104 | tf_op jit(solution)/shard_map/ppermute | solution.py:355
  51.5 3.0 %collective-permute-done.13.refs_3_ = bf16[4,32,512]{2,1,0:T(8,128)(2,1)S(1)} collective-permute-done((bf16[4,32,512]{2,1,0:T(8,128)(2,1)S(1)}, bf16[4,32,512]{2,1,0:T(8,128)(2,1)S(1)}, u32[]{:S(2)}, u32[]{:S(2)}) %collective-permute-start.13) | collective-permute-done | bytes 131104 | tf_op jit(solution)/shard_map/ppermute | solution.py:355
  54.5 0.8 %join_levels.1 = bf16[4,4,32,512]{3,2,1,0:T(8,128)(2,1)} custom-call(bf16[4,32,512]{2,1,0:T(8,128)(2,1)S(1)} %get-tuple-element.35.refs_0_, bf16[4,32,512]{2,1,0:T(8,128)(2,1)S(1)} %collective-permute-done.11.refs_1_, bf16[4,32,512]{2,1,0:T(8,128)(2,1)S(1)} %collective-permute-done.12.refs_2_, bf16[4,32,512]{2,1,0:T(8,128)(2,1)S(1)} %collective-permute-done.13.refs_3_), custom_call_target="tpu_custom_call" | custom-call | tf_op jit(solution)/shard_map/join_levels/pallas_call | solution.py:343
Async XLA Ops:
  1.1 18.3 %collective-permute-start = (bf16[27,32,128]{2,1,0:T(8,128)(2,1)S(1)}, bf16[27,32,128]{2,1,0:T(8,128)(2,1)S(1)}, u32[]{:S(2)}, u32[]{:S(2)}) collective-permute-start(bf16[27,32,128]{2,1,0:T(8,128)(2,1)S(1)} %broadcast_select_fusion), channel_id=1, source_target_pairs={{0,2},{1,3},{2,0},{3,1},{4,6},{5,7},{6,4},{7,5},{8,10},{9,11},{10,... | collective-permute-start | bytes 663560 | tf_op jit(solution)/shard_map/ppermute | solution.py:355
  3.9 1.0 %copy-start = (bf16[4,4,32,512]{3,2,1,0:T(8,128)(2,1)S(1)}, bf16[4,4,32,512]{3,2,1,0:T(8,128)(2,1)}, u32[]{:S(2)}) copy-start(bf16[4,4,32,512]{3,2,1,0:T(8,128)(2,1)} %feat.1) | copy-start | bytes 1572868
  4.9 0.7 %copy-start.3 = (s32[4,27]{1,0:T(4,128)S(1)}, s32[4,27]{1,0:T(4,128)}, u32[]{:S(2)}) copy-start(s32[4,27]{1,0:T(4,128)} %near.1) | copy-start | bytes 1300
  5.6 0.7 %copy-start.4 = (f32[4,32]{1,0:T(4,128)S(1)}, f32[4,32]{1,0:T(4,128)}, u32[]{:S(2)}) copy-start(f32[4,32]{1,0:T(4,128)} %lev.1) | copy-start | bytes 1540
  6.3 0.7 %copy-start.5 = (s32[1,2,2]{2,1,0:T(2,128)S(1)}, s32[1,2,2]{2,1,0:T(2,128)}, u32[]{:S(2)}) copy-start(s32[1,2,2]{2,1,0:T(2,128)} %lists.1) | copy-start | bytes 52
  7.0 0.7 %copy-start.6 = (f32[32]{0:T(128)S(1)}, f32[32]{0:T(128)}, u32[]{:S(2)}) copy-start(f32[32]{0:T(128)} %param.12) | copy-start | bytes 388
  7.6 0.7 %copy-start.7 = (f32[32]{0:T(128)S(1)}, f32[32]{0:T(128)}, u32[]{:S(2)}) copy-start(f32[32]{0:T(128)} %param.14) | copy-start | bytes 388
  8.4 4.4 %collective-permute-start.1 = (bf16[17,32,128]{2,1,0:T(8,128)(2,1)S(1)}, bf16[17,32,128]{2,1,0:T(8,128)(2,1)S(1)}, u32[]{:S(2)}, u32[]{:S(2)}) collective-permute-start(bf16[17,32,128]{2,1,0:T(8,128)(2,1)S(1)} %get-tuple-element.24), channel_id=1, source_target_pairs={{0,1},{1,0},{2,3},{3,2},{4,5},{5,4},{6,7},{7,6},{8,9},{9,8},{10,11... | collective-permute-start | bytes 417800 | tf_op jit(solution)/shard_map/ppermute | solution.py:355
  9.4 6.7 %collective-permute-start.2 = (bf16[17,32,128]{2,1,0:T(8,128)(2,1)S(1)}, bf16[17,32,128]{2,1,0:T(8,128)(2,1)S(1)}, u32[]{:S(2)}, u32[]{:S(2)}) collective-permute-start(bf16[17,32,128]{2,1,0:T(8,128)(2,1)S(1)} %get-tuple-element.25), channel_id=1, source_target_pairs={{0,2},{1,3},{2,0},{3,1},{4,6},{5,7},{6,4},{7,5},{8,10},{9,11},{10,... | collective-permute-start | bytes 417800 | tf_op jit(solution)/shard_map/ppermute | solution.py:355
  9.7 9.7 %collective-permute-start.3 = (bf16[17,32,128]{2,1,0:T(8,128)(2,1)S(1)}, bf16[17,32,128]{2,1,0:T(8,128)(2,1)S(1)}, u32[]{:S(2)}, u32[]{:S(2)}) collective-permute-start(bf16[17,32,128]{2,1,0:T(8,128)(2,1)S(1)} %get-tuple-element.26), channel_id=1, source_target_pairs={{0,3},{1,2},{2,1},{3,0},{4,7},{5,6},{6,5},{7,4},{8,11},{9,10},{10,... | collective-permute-start | bytes 417800 | tf_op jit(solution)/shard_map/ppermute | solution.py:355
  12.7 10.6 %collective-permute-start.6 = (bf16[27,32,128]{2,1,0:T(8,128)(2,1)}, bf16[27,32,128]{2,1,0:T(8,128)(2,1)S(1)}, u32[]{:S(2)}, u32[]{:S(2)}) collective-permute-start(bf16[27,32,128]{2,1,0:T(8,128)(2,1)} %bitcast.6), channel_id=1, source_target_pairs={{0,1},{1,0},{2,3},{3,2},{4,5},{5,4},{6,7},{7,6},{8,9},{9,8},{10,11... | collective-permute-start | bytes 663560 | tf_op jit(solution)/shard_map/ppermute | solution.py:355
  19.3 12.5 %collective-permute-start.7 = (bf16[27,32,128]{2,1,0:T(8,128)(2,1)S(1)}, bf16[27,32,128]{2,1,0:T(8,128)(2,1)S(1)}, u32[]{:S(2)}, u32[]{:S(2)}) collective-permute-start(bf16[27,32,128]{2,1,0:T(8,128)(2,1)S(1)} %collective-permute-done.refs_8_.refs_2_), channel_id=1, source_target_pairs={{0,1},{1,0},{2,3},{3,2},{4,5},{5,4},{6,7},{7,6},{8,9},{9,8},{10,11... | collective-permute-start | bytes 663560 | tf_op jit(solution)/shard_map/ppermute | solution.py:355
  19.6 12.3 %collective-permute-start.8 = (bf16[27,32,128]{2,1,0:T(8,128)(2,1)S(1)}, bf16[27,32,128]{2,1,0:T(8,128)(2,1)S(1)}, u32[]{:S(2)}, u32[]{:S(2)}) collective-permute-start(bf16[27,32,128]{2,1,0:T(8,128)(2,1)S(1)} %collective-permute-done.refs_8_.refs_2_), channel_id=1, source_target_pairs={{0,4},{1,5},{2,6},{3,7},{4,0},{5,1},{6,2},{7,3},{8,12},{9,13},{10,... | collective-permute-start | bytes 663560 | tf_op jit(solution)/shard_map/ppermute | solution.py:361
  21.2 10.7 %collective-permute-start.9 = (bf16[27,32,128]{2,1,0:T(8,128)(2,1)S(1)}, bf16[27,32,128]{2,1,0:T(8,128)(2,1)S(1)}, u32[]{:S(2)}, u32[]{:S(2)}) collective-permute-start(bf16[27,32,128]{2,1,0:T(8,128)(2,1)S(1)} %collective-permute-done.refs_8_.refs_2_), channel_id=1, source_target_pairs={{0,33},{1,32},{2,35},{3,34},{4,37},{5,36},{6,39},{7,38},{8,41},{9,... | collective-permute-start | bytes 663560 | tf_op jit(solution)/shard_map/ppermute | solution.py:361
  23.1 6.3 %collective-permute-start.4 = (bf16[9,32,128]{2,1,0:T(8,128)(2,1)S(1)}, bf16[9,32,128]{2,1,0:T(8,128)(2,1)S(1)}, u32[]{:S(2)}, u32[]{:S(2)}) collective-permute-start(bf16[9,32,128]{2,1,0:T(8,128)(2,1)S(1)} %get-tuple-element.30), channel_id=1, source_target_pairs={{0,4},{4,0},{8,12},{12,8},{16,20},{20,16},{24,28},{28,24},{32,36},... | collective-permute-start | bytes 221192 | tf_op jit(solution)/shard_map/ppermute | solution.py:367
  23.2 8.6 %collective-permute-start.5 = (bf16[9,32,128]{2,1,0:T(8,128)(2,1)S(1)}, bf16[9,32,128]{2,1,0:T(8,128)(2,1)S(1)}, u32[]{:S(2)}, u32[]{:S(2)}) collective-permute-start(bf16[9,32,128]{2,1,0:T(8,128)(2,1)S(1)} %get-tuple-element.31), channel_id=1, source_target_pairs={{0,0},{4,8},{8,4},{12,16},{16,12},{20,24},{24,20},{28,32},{32,28},... | collective-permute-start | bytes 221192 | tf_op jit(solution)/shard_map/ppermute | solution.py:367
  29.5 10.6 %collective-permute-start.10 = (bf16[27,32,128]{2,1,0:T(8,128)(2,1)}, bf16[27,32,128]{2,1,0:T(8,128)(2,1)S(1)}, u32[]{:S(2)}, u32[]{:S(2)}) collective-permute-start(bf16[27,32,128]{2,1,0:T(8,128)(2,1)} %bitcast.8), channel_id=1, source_target_pairs={{0,1},{1,0},{2,3},{3,2},{4,5},{5,4},{6,7},{7,6},{8,9},{9,8},{10,11... | collective-permute-start | bytes 663560 | tf_op jit(solution)/shard_map/ppermute | solution.py:355
  31.9 0.9 %copy-start.1 = (bf16[27,128,32]{1,2,0:T(8,128)(2,1)S(1)}, bf16[27,128,32]{1,2,0:T(8,128)(2,1)}, u32[]{:S(2)}) copy-start(bf16[27,128,32]{1,2,0:T(8,128)(2,1)} %param.11) | copy-start | bytes 663556
  32.8 7.2 %copy-start.2 = (bf16[27,128,32]{1,2,0:T(8,128)(2,1)S(1)}, bf16[27,128,32]{1,2,0:T(8,128)(2,1)}, u32[]{:S(2)}) copy-start(bf16[27,128,32]{1,2,0:T(8,128)(2,1)} %param.13) | copy-start | bytes 663556
  43.8 4.4 %collective-permute-start.11 = (bf16[4,32,512]{2,1,0:T(8,128)(2,1)S(1)}, bf16[4,32,512]{2,1,0:T(8,128)(2,1)S(1)}, u32[]{:S(2)}, u32[]{:S(2)}) collective-permute-start(bf16[4,32,512]{2,1,0:T(8,128)(2,1)S(1)} %get-tuple-element.36), channel_id=1, source_target_pairs={{0,1},{1,0},{2,3},{3,2},{4,5},{5,4},{6,7},{7,6},{8,9},{9,8},{10,11... | collective-permute-start | bytes 393224 | tf_op jit(solution)/shard_map/ppermute | solution.py:355
  44.9 6.6 %collective-permute-start.12 = (bf16[4,32,512]{2,1,0:T(8,128)(2,1)S(1)}, bf16[4,32,512]{2,1,0:T(8,128)(2,1)S(1)}, u32[]{:S(2)}, u32[]{:S(2)}) collective-permute-start(bf16[4,32,512]{2,1,0:T(8,128)(2,1)S(1)} %get-tuple-element.37), channel_id=1, source_target_pairs={{0,2},{1,3},{2,0},{3,1},{4,6},{5,7},{6,4},{7,5},{8,10},{9,11},{10,... | collective-permute-start | bytes 393224 | tf_op jit(solution)/shard_map/ppermute | solution.py:355
  46.4 8.1 %collective-permute-start.13 = (bf16[4,32,512]{2,1,0:T(8,128)(2,1)S(1)}, bf16[4,32,512]{2,1,0:T(8,128)(2,1)S(1)}, u32[]{:S(2)}, u32[]{:S(2)}) collective-permute-start(bf16[4,32,512]{2,1,0:T(8,128)(2,1)S(1)} %get-tuple-element.38), channel_id=1, source_target_pairs={{0,3},{1,2},{2,1},{3,0},{4,7},{5,6},{6,5},{7,4},{8,11},{9,10},{10,... | collective-permute-start | bytes 393224 | tf_op jit(solution)/shard_map/ppermute | solution.py:355

commit v11 on v8

--- a/solution.py
+++ b/solution.py
@@ -20,10 +20,10 @@
 PIECE = 17
 
 
-def split_kernel(feat, near, lists, b1, b2, lev, *refs):
+def split_kernel(feat, small, *refs):
     pieces, tables = refs[:4], refs[4]
     me = lax.axis_index("chan")
-    values = jnp.concatenate([b1[...], b2[...], lev[...], jnp.zeros((2, 32), F32)], axis=0)
+    values = small[pl.ds(0, 8), pl.ds(0, 32)]
     values = jnp.concatenate([values] * 4, axis=1)
     lane = lax.broadcasted_iota(jnp.int32, (8, 128), 1)
     values = jnp.where(lane // 32 == me, values, 0.0)
@@ -34,24 +34,30 @@
             for v in range(4):
                 pieces[m][4 * v + b] = feat[me ^ m, b, :, 128 * v : 128 * v + 128]
         pieces[m][16] = values
-    tables[...] = jnp.zeros((8, 128), jnp.int32)
-    tables[pl.ds(0, 4), pl.ds(0, 27)] = near[...]
-    tables[pl.ds(4, 2), pl.ds(0, 2)] = lists[0]
-    sent = tables[...].astype(F32)
+    sent = small[pl.ds(8, 8), :]
+    tables[...] = sent.astype(jnp.int32)
     pieces[0][17] = jnp.concatenate([sent, jnp.zeros((24, 128), F32)], axis=0).astype(BF16)
 
 
+def in_rows(array, first, count):
+    array = array.reshape(-1, array.shape[-1]).astype(F32)
+    rows, lanes = array.shape
+    return jnp.pad(array, ((first, count - first - rows), (0, 128 - lanes)))
+
+
 def split(features, neighbours, face_lists, b1, b2, lev):
+    small = [(b1, 0), (b2, 1), (lev, 2), (neighbours, 8), (face_lists, 12)]
+    small = sum(in_rows(array, first, 16) for array, first in small)
     piece = jax.ShapeDtypeStruct((PIECE, 32, 128), BF16)
     kept = jax.ShapeDtypeStruct((PIECE + 1, 32, 128), BF16)
     return pl.pallas_call(
         split_kernel,
         out_shape=[kept, piece, piece, piece, jax.ShapeDtypeStruct((8, 128), jnp.int32)],
-        in_specs=[VMEM] * 6,
+        in_specs=[VMEM] * 2,
         out_specs=[VMEM] * 5,
         compiler_params=pltpu.CompilerParams(vmem_limit_bytes=8 << 20),
         name="split_features",
-    )(features, neighbours, face_lists, b1.reshape(1, 32), b2.reshape(1, 32), lev)
+    )(features, small)
 
 
 def faces_kernel(tables, *refs):

time: 54.7 us -> 53.4 us (0.976)
  local copies, waits for them, and re-layouts: 5.33 us -> 1.98 us
  other arithmetic: 0 us -> 2.07 us
    unnamed x16 -> x6, local copies, waits for them, and re-layouts: 5.33 us -> 1.98 us
    convert_element_type x0 -> x2, other arithmetic: none -> 1.36 us  [in_rows(): array = array.reshape(-1, array.shape[-1]).astype(F32)]
    add x0 -> x1, other arithmetic: none -> 0.71 us  [split(): small = sum((in_rows(array, first, 16) for array, first in small))]
  transfers between devices with their start and end apart: 14 -> 14, of which waited for: 5 -> 5; matrix products, arithmetic and copies ran while one was open for 0% -> 4% of each run, Pallas kernels for 15% -> 16%
where the time goes in v11:
time: 53.4 us; the launch traced here: 53.1 us
  starting transfers between devices  21.1 us (40%)
  waiting for transfers between devices  15.2 us (28%)
  Pallas kernels  12.8 us (24%)
  other arithmetic  2.07 us (4%)
  local copies, waits for them, and re-layouts  1.98 us (4%)
    ppermute x12, waiting for transfers between devices, swap(): return lax.ppermute(value, 'chan', [(i, i ^ m) for i in range(4)])  15.1 us
    ppermute x12, starting transfers between devices, swap(): return lax.ppermute(value, 'chan', [(i, i ^ m) for i in range(4)])  15 us
    pallas_call x1, Pallas kernels, convolve_first(): pl.pallas_call(first_kernel, out_shape=[jax.ShapeDtypeStruct((2, 10, 10,...  7.16 us
    ppermute x2, starting transfers between devices, swap_faces(): lax.ppermute(value, 'slab', [(s, p if 0 <= p < count else s) for s, p in...  6.06 us
    pallas_call x1, Pallas kernels, convolve_second(): pl.pallas_call(second_kernel, out_shape=[piece] * 4, in_specs=[SMEM, VMEM...  3.69 us
    unnamed x6, local copies, waits for them, and re-layouts  1.98 us
    convert_element_type x2, other arithmetic, in_rows(): array = array.reshape(-1, array.shape[-1]).astype(F32)  1.36 us
  transfers between devices with their start and end apart: 14, of which 5 were waited for; matrix products, arithmetic and copies ran while one was open for 4% of the time, Pallas kernels for 16%

profile of v11, /device:TPU:25, one launch (start us, length us, event | category | flops | bytes accessed | tf_op | source)
XLA Modules:
  0.0 53.1 jit_solution(5161247106420046700)
XLA Ops:
  0.0 2.7 %collective-permute-start = (bf16[27,32,128]{2,1,0:T(8,128)(2,1)}, bf16[27,32,128]{2,1,0:T(8,128)(2,1)S(1)}, u32[]{:S(2)}, u32[]{:S(2)}) collective-permute-start(bf16[27,32,128]{2,1,0:T(8,128)(2,1)} %bitcast.6), channel_id=1, source_target_pairs={{0,2},{1,3},{2,0},{3,1},{4,6},{5,7},{6,4},{7,5},{8,10},{9,11},{10,... | collective-permute-start | bytes 663560 | tf_op jit(solution)/shard_map/ppermute | solution.py:348
  2.7 0.7 %convert_element_type.19 = f32[4,27]{1,0:T(4,128)S(1)} convert(s32[4,27]{1,0:T(4,128)} %param.9) | non-fusion elementwise | flops 108 | bytes 864 | tf_op jit(solution)/shard_map/convert_element_type | solution.py:43
  3.4 0.7 %convert_bitcast_fusion = f32[2,2]{1,0:T(2,128)S(1)} fusion(s32[1,2,2]{2,1,0:T(2,128)} %param.10), kind=kLoop, calls=%fused_computation.1 | loop fusion | flops 4 | bytes 32 | tf_op jit(solution)/shard_map/convert_element_type | solution.py:43
  4.1 0.7 %pad_add_fusion.small = f32[16,128]{1,0:T(8,128)S(1)} fusion(f32[2,2]{1,0:T(2,128)S(1)} %convert_bitcast_fusion, f32[4,27]{1,0:T(4,128)S(1)} %convert_element_type.19, f32[4,32]{1,0:T(4,128)} %param.15, f32[1,32]{1,0:T(1,128)} %bitcast.13, f32[1,32]{1,0:T(1,128)} %bitcast.14), kind=kLoop, calls=%fused_computation | loop fusion | flops 8192 | bytes 9408 | tf_op jit(solution)/shard_map/add | solution.py:50
  4.8 0.0 copy-start
  4.8 1.0 %copy-done = bf16[4,4,32,512]{3,2,1,0:T(8,128)(2,1)S(1)} copy-done((bf16[4,4,32,512]{3,2,1,0:T(8,128)(2,1)S(1)}, bf16[4,4,32,512]{3,2,1,0:T(8,128)(2,1)}, u32[]{:S(2)}) %copy-start) | copy-done | bytes 524312
  5.9 0.1 split_features.1
  6.0 1.0 %collective-permute-start.1 = (bf16[17,32,128]{2,1,0:T(8,128)(2,1)S(1)}, bf16[17,32,128]{2,1,0:T(8,128)(2,1)S(1)}, u32[]{:S(2)}, u32[]{:S(2)}) collective-permute-start(bf16[17,32,128]{2,1,0:T(8,128)(2,1)S(1)} %get-tuple-element.25), channel_id=1, source_target_pairs={{0,1},{1,0},{2,3},{3,2},{4,5},{5,4},{6,7},{7,6},{8,9},{9,8},{10,11... | collective-permute-start | bytes 417800 | tf_op jit(solution)/shard_map/ppermute | solution.py:348
  7.0 0.2 collective-permute-start.2
  7.2 3.0 %collective-permute-start.3 = (bf16[17,32,128]{2,1,0:T(8,128)(2,1)S(1)}, bf16[17,32,128]{2,1,0:T(8,128)(2,1)S(1)}, u32[]{:S(2)}, u32[]{:S(2)}) collective-permute-start(bf16[17,32,128]{2,1,0:T(8,128)(2,1)S(1)} %get-tuple-element.27), channel_id=1, source_target_pairs={{0,3},{1,2},{2,1},{3,0},{4,7},{5,6},{6,5},{7,4},{8,11},{9,10},{10,... | collective-permute-start | bytes 417800 | tf_op jit(solution)/shard_map/ppermute | solution.py:348
  10.2 0.2 collective-permute-start.6
  10.4 0.0 collective-permute-done.1.refs_1_
  10.4 3.4 %collective-permute-done.2.refs_2_ = bf16[17,32,128]{2,1,0:T(8,128)(2,1)S(1)} collective-permute-done((bf16[17,32,128]{2,1,0:T(8,128)(2,1)S(1)}, bf16[17,32,128]{2,1,0:T(8,128)(2,1)S(1)}, u32[]{:S(2)}, u32[]{:S(2)}) %collective-permute-start.2) | collective-permute-done | bytes 139296 | tf_op jit(solution)/shard_map/ppermute | solution.py:348
  13.7 3.2 %collective-permute-done.3.refs_3_ = bf16[17,32,128]{2,1,0:T(8,128)(2,1)S(1)} collective-permute-done((bf16[17,32,128]{2,1,0:T(8,128)(2,1)S(1)}, bf16[17,32,128]{2,1,0:T(8,128)(2,1)S(1)}, u32[]{:S(2)}, u32[]{:S(2)}) %collective-permute-start.3) | collective-permute-done | bytes 139296 | tf_op jit(solution)/shard_map/ppermute | solution.py:348
  16.9 0.0 collective-permute-done.refs_8_
  16.9 0.2 collective-permute-start.7
  17.1 0.0 copy-start.2
  17.1 1.0 %pick_faces.1 = (bf16[9,32,128]{2,1,0:T(8,128)(2,1)S(1)}, bf16[9,32,128]{2,1,0:T(8,128)(2,1)S(1)}) custom-call(s32[8,128]{1,0:T(8,128)S(1)} %get-tuple-element.23.tables.tab, bf16[18,32,128]{2,1,0:T(8,128)(2,1)S(1)} %get-tuple-element.24.refs_0_, bf16[17,32,128]{2,1,0:T(8,128)(2,1)S(1)} %collective-permute-done.1.refs_1_, ...), custom_call_target="tpu_custom_call" | custom-call | tf_op jit(solution)/shard_map/pick_faces/pallas_call | solution.py:83
  18.1 1.7 %collective-permute-start.4 = (bf16[9,32,128]{2,1,0:T(8,128)(2,1)S(1)}, bf16[9,32,128]{2,1,0:T(8,128)(2,1)S(1)}, u32[]{:S(2)}, u32[]{:S(2)}) collective-permute-start(bf16[9,32,128]{2,1,0:T(8,128)(2,1)S(1)} %get-tuple-element.31), channel_id=1, source_target_pairs={{0,4},{4,0},{8,12},{12,8},{16,20},{20,16},{24,28},{28,24},{32,36},... | collective-permute-start | bytes 221192 | tf_op jit(solution)/shard_map/ppermute | solution.py:354
  19.9 4.3 %collective-permute-start.5 = (bf16[9,32,128]{2,1,0:T(8,128)(2,1)S(1)}, bf16[9,32,128]{2,1,0:T(8,128)(2,1)S(1)}, u32[]{:S(2)}, u32[]{:S(2)}) collective-permute-start(bf16[9,32,128]{2,1,0:T(8,128)(2,1)S(1)} %get-tuple-element.32), channel_id=1, source_target_pairs={{0,0},{4,8},{8,4},{12,16},{16,12},{20,24},{24,20},{28,32},{32,28},... | collective-permute-start | bytes 221192 | tf_op jit(solution)/shard_map/ppermute | solution.py:354
  24.2 2.6 %collective-permute-start.10 = (bf16[27,32,128]{2,1,0:T(8,128)(2,1)}, bf16[27,32,128]{2,1,0:T(8,128)(2,1)S(1)}, u32[]{:S(2)}, u32[]{:S(2)}) collective-permute-start(bf16[27,32,128]{2,1,0:T(8,128)(2,1)} %bitcast.9), channel_id=1, source_target_pairs={{0,3},{1,2},{2,1},{3,0},{4,7},{5,6},{6,5},{7,4},{8,11},{9,10},{10,... | collective-permute-start | bytes 663560 | tf_op jit(solution)/shard_map/ppermute | solution.py:348
  26.8 0.0 collective-permute-done.6.refs_7_
  26.8 0.0 collective-permute-start.8
  26.8 0.0 collective-permute-done.4.refs_4_
  26.8 1.3 %collective-permute-start.9 = (bf16[27,32,128]{2,1,0:T(8,128)(2,1)}, bf16[27,32,128]{2,1,0:T(8,128)(2,1)S(1)}, u32[]{:S(2)}, u32[]{:S(2)}) collective-permute-start(bf16[27,32,128]{2,1,0:T(8,128)(2,1)} %bitcast.11), channel_id=1, source_target_pairs={{0,2},{1,3},{2,0},{3,1},{4,6},{5,7},{6,4},{7,5},{8,10},{9,11},{10,... | collective-permute-start | bytes 663560 | tf_op jit(solution)/shard_map/ppermute | solution.py:348
  28.1 0.0 collective-permute-done.5.refs_5_
  28.1 0.0 collective-permute-done.7.refs_9_
  28.1 0.0 copy-start.1
  28.1 0.9 %copy-done.1 = bf16[27,128,32]{1,2,0:T(8,128)(2,1)S(1)} copy-done((bf16[27,128,32]{1,2,0:T(8,128)(2,1)S(1)}, bf16[27,128,32]{1,2,0:T(8,128)(2,1)}, u32[]{:S(2)}) %copy-start.1) | copy-done | bytes 221208
  29.1 7.2 %convolve_first.1 = (bf16[2,10,10,16,384]{4,3,2,1,0:T(8,128)(2,1)S(1)}, f32[8,128]{1,0:T(8,128)S(1)}) custom-call(s32[8,128]{1,0:T(8,128)S(1)} %get-tuple-element.23.tables.tab, bf16[18,32,128]{2,1,0:T(8,128)(2,1)S(1)} %get-tuple-element.24.refs_0_, bf16[17,32,128]{2,1,0:T(8,128)(2,1)S(1)} %collective-permute-done.1.refs_1_, ...), custom_call_target="tpu_custom_call" | custom-call | flops 5000000000 | bytes 4000000 | tf_op jit(solution)/shard_map/convolve_first/pallas_call | solution.py:260
  36.2 0.0 collective-permute-done.10.refs_3_
  36.2 0.0 collective-permute-done.8.refs_1_
  36.2 2.4 %collective-permute-done.9.refs_2_ = bf16[27,32,128]{2,1,0:T(8,128)(2,1)S(1)} collective-permute-done((bf16[27,32,128]{2,1,0:T(8,128)(2,1)}, bf16[27,32,128]{2,1,0:T(8,128)(2,1)S(1)}, u32[]{:S(2)}, u32[]{:S(2)}) %collective-permute-start.9) | collective-permute-done | bytes 221216 | tf_op jit(solution)/shard_map/ppermute | solution.py:348
  38.6 0.0 copy-done.2
  38.6 3.7 %convolve_second.1 = (bf16[4,32,512]{2,1,0:T(8,128)(2,1)S(1)}, bf16[4,32,512]{2,1,0:T(8,128)(2,1)S(1)}, bf16[4,32,512]{2,1,0:T(8,128)(2,1)S(1)}, bf16[4,32,512]{2,1,0:T(8,128)(2,1)S(1)}) custom-call(s32[8,128]{1,0:T(8,128)S(1)} %get-tuple-element.23.tables.tab, bf16[2,10,10,16,384]{4,3,2,1,0:T(8,128)(2,1)S(1)} %get-tuple-element.34.pad, ...), custom_call_target="tpu_custom_call" | custom-call | flops 4000000000 | bytes 4000000 | tf_op jit(solution)/shard_map/convolve_second/pallas_call | solution.py:307
  42.3 0.5 collective-permute-start.11
  42.8 1.7 %collective-permute-start.12 = (bf16[4,32,512]{2,1,0:T(8,128)(2,1)S(1)}, bf16[4,32,512]{2,1,0:T(8,128)(2,1)S(1)}, u32[]{:S(2)}, u32[]{:S(2)}) collective-permute-start(bf16[4,32,512]{2,1,0:T(8,128)(2,1)S(1)} %get-tuple-element.39), channel_id=1, source_target_pairs={{0,2},{1,3},{2,0},{3,1},{4,6},{5,7},{6,4},{7,5},{8,10},{9,11},{10,... | collective-permute-start | bytes 393224 | tf_op jit(solution)/shard_map/ppermute | solution.py:348
  44.5 1.6 %collective-permute-start.13 = (bf16[4,32,512]{2,1,0:T(8,128)(2,1)S(1)}, bf16[4,32,512]{2,1,0:T(8,128)(2,1)S(1)}, u32[]{:S(2)}, u32[]{:S(2)}) collective-permute-start(bf16[4,32,512]{2,1,0:T(8,128)(2,1)S(1)} %get-tuple-element.40), channel_id=1, source_target_pairs={{0,3},{1,2},{2,1},{3,0},{4,7},{5,6},{6,5},{7,4},{8,11},{9,10},{10,... | collective-permute-start | bytes 393224 | tf_op jit(solution)/shard_map/ppermute | solution.py:348
  46.1 0.0 collective-permute-done.11.refs_1_
  46.1 3.2 %collective-permute-done.12.refs_2_ = bf16[4,32,512]{2,1,0:T(8,128)(2,1)S(1)} collective-permute-done((bf16[4,32,512]{2,1,0:T(8,128)(2,1)S(1)}, bf16[4,32,512]{2,1,0:T(8,128)(2,1)S(1)}, u32[]{:S(2)}, u32[]{:S(2)}) %collective-permute-start.12) | collective-permute-done | bytes 131104 | tf_op jit(solution)/shard_map/ppermute | solution.py:348
  49.3 3.1 %collective-permute-done.13.refs_3_ = bf16[4,32,512]{2,1,0:T(8,128)(2,1)S(1)} collective-permute-done((bf16[4,32,512]{2,1,0:T(8,128)(2,1)S(1)}, bf16[4,32,512]{2,1,0:T(8,128)(2,1)S(1)}, u32[]{:S(2)}, u32[]{:S(2)}) %collective-permute-start.13) | collective-permute-done | bytes 131104 | tf_op jit(solution)/shard_map/ppermute | solution.py:348
  52.3 0.8 %join_levels.1 = bf16[4,4,32,512]{3,2,1,0:T(8,128)(2,1)} custom-call(bf16[4,32,512]{2,1,0:T(8,128)(2,1)S(1)} %get-tuple-element.37.refs_0_, bf16[4,32,512]{2,1,0:T(8,128)(2,1)S(1)} %collective-permute-done.11.refs_1_, bf16[4,32,512]{2,1,0:T(8,128)(2,1)S(1)} %collective-permute-done.12.refs_2_, bf16[4,32,512]{2,1,0:T(8,128)(2,1)S(1)} %collective-permute-done.13.refs_3_), custom_call_target="tpu_custom_call" | custom-call | tf_op jit(solution)/shard_map/join_levels/pallas_call | solution.py:336
Async XLA Ops:
  0.0 16.9 %collective-permute-start = (bf16[27,32,128]{2,1,0:T(8,128)(2,1)}, bf16[27,32,128]{2,1,0:T(8,128)(2,1)S(1)}, u32[]{:S(2)}, u32[]{:S(2)}) collective-permute-start(bf16[27,32,128]{2,1,0:T(8,128)(2,1)} %bitcast.6), channel_id=1, source_target_pairs={{0,2},{1,3},{2,0},{3,1},{4,6},{5,7},{6,4},{7,5},{8,10},{9,11},{10,... | collective-permute-start | bytes 663560 | tf_op jit(solution)/shard_map/ppermute | solution.py:348
  4.8 1.0 %copy-start = (bf16[4,4,32,512]{3,2,1,0:T(8,128)(2,1)S(1)}, bf16[4,4,32,512]{3,2,1,0:T(8,128)(2,1)}, u32[]{:S(2)}) copy-start(bf16[4,4,32,512]{3,2,1,0:T(8,128)(2,1)} %feat.1) | copy-start | bytes 1572868
  6.0 4.4 %collective-permute-start.1 = (bf16[17,32,128]{2,1,0:T(8,128)(2,1)S(1)}, bf16[17,32,128]{2,1,0:T(8,128)(2,1)S(1)}, u32[]{:S(2)}, u32[]{:S(2)}) collective-permute-start(bf16[17,32,128]{2,1,0:T(8,128)(2,1)S(1)} %get-tuple-element.25), channel_id=1, source_target_pairs={{0,1},{1,0},{2,3},{3,2},{4,5},{5,4},{6,7},{7,6},{8,9},{9,8},{10,11... | collective-permute-start | bytes 417800 | tf_op jit(solution)/shard_map/ppermute | solution.py:348
  7.0 6.7 %collective-permute-start.2 = (bf16[17,32,128]{2,1,0:T(8,128)(2,1)S(1)}, bf16[17,32,128]{2,1,0:T(8,128)(2,1)S(1)}, u32[]{:S(2)}, u32[]{:S(2)}) collective-permute-start(bf16[17,32,128]{2,1,0:T(8,128)(2,1)S(1)} %get-tuple-element.26), channel_id=1, source_target_pairs={{0,2},{1,3},{2,0},{3,1},{4,6},{5,7},{6,4},{7,5},{8,10},{9,11},{10,... | collective-permute-start | bytes 417800 | tf_op jit(solution)/shard_map/ppermute | solution.py:348
  7.2 9.7 %collective-permute-start.3 = (bf16[17,32,128]{2,1,0:T(8,128)(2,1)S(1)}, bf16[17,32,128]{2,1,0:T(8,128)(2,1)S(1)}, u32[]{:S(2)}, u32[]{:S(2)}) collective-permute-start(bf16[17,32,128]{2,1,0:T(8,128)(2,1)S(1)} %get-tuple-element.27), channel_id=1, source_target_pairs={{0,3},{1,2},{2,1},{3,0},{4,7},{5,6},{6,5},{7,4},{8,11},{9,10},{10,... | collective-permute-start | bytes 417800 | tf_op jit(solution)/shard_map/ppermute | solution.py:348
  10.2 16.5 %collective-permute-start.6 = (bf16[27,32,128]{2,1,0:T(8,128)(2,1)}, bf16[27,32,128]{2,1,0:T(8,128)(2,1)S(1)}, u32[]{:S(2)}, u32[]{:S(2)}) collective-permute-start(bf16[27,32,128]{2,1,0:T(8,128)(2,1)} %bitcast.7), channel_id=1, source_target_pairs={{0,1},{1,0},{2,3},{3,2},{4,5},{5,4},{6,7},{7,6},{8,9},{9,8},{10,11... | collective-permute-start | bytes 663560 | tf_op jit(solution)/shard_map/ppermute | solution.py:348
  16.9 11.2 %collective-permute-start.7 = (bf16[27,32,128]{2,1,0:T(8,128)(2,1)S(1)}, bf16[27,32,128]{2,1,0:T(8,128)(2,1)S(1)}, u32[]{:S(2)}, u32[]{:S(2)}) collective-permute-start(bf16[27,32,128]{2,1,0:T(8,128)(2,1)S(1)} %collective-permute-done.refs_8_), channel_id=1, source_target_pairs={{0,1},{1,0},{2,3},{3,2},{4,5},{5,4},{6,7},{7,6},{8,9},{9,8},{10,11... | collective-permute-start | bytes 663560 | tf_op jit(solution)/shard_map/ppermute | solution.py:348
  17.1 21.5 %copy-start.2 = (bf16[27,128,32]{1,2,0:T(8,128)(2,1)S(1)}, bf16[27,128,32]{1,2,0:T(8,128)(2,1)}, u32[]{:S(2)}) copy-start(bf16[27,128,32]{1,2,0:T(8,128)(2,1)} %param.13) | copy-start | bytes 663556
  18.1 8.6 %collective-permute-start.4 = (bf16[9,32,128]{2,1,0:T(8,128)(2,1)S(1)}, bf16[9,32,128]{2,1,0:T(8,128)(2,1)S(1)}, u32[]{:S(2)}, u32[]{:S(2)}) collective-permute-start(bf16[9,32,128]{2,1,0:T(8,128)(2,1)S(1)} %get-tuple-element.31), channel_id=1, source_target_pairs={{0,4},{4,0},{8,12},{12,8},{16,20},{20,16},{24,28},{28,24},{32,36},... | collective-permute-start | bytes 221192 | tf_op jit(solution)/shard_map/ppermute | solution.py:354
  19.9 8.2 %collective-permute-start.5 = (bf16[9,32,128]{2,1,0:T(8,128)(2,1)S(1)}, bf16[9,32,128]{2,1,0:T(8,128)(2,1)S(1)}, u32[]{:S(2)}, u32[]{:S(2)}) collective-permute-start(bf16[9,32,128]{2,1,0:T(8,128)(2,1)S(1)} %get-tuple-element.32), channel_id=1, source_target_pairs={{0,0},{4,8},{8,4},{12,16},{16,12},{20,24},{24,20},{28,32},{32,28},... | collective-permute-start | bytes 221192 | tf_op jit(solution)/shard_map/ppermute | solution.py:354
  24.2 12.0 %collective-permute-start.10 = (bf16[27,32,128]{2,1,0:T(8,128)(2,1)}, bf16[27,32,128]{2,1,0:T(8,128)(2,1)S(1)}, u32[]{:S(2)}, u32[]{:S(2)}) collective-permute-start(bf16[27,32,128]{2,1,0:T(8,128)(2,1)} %bitcast.9), channel_id=1, source_target_pairs={{0,3},{1,2},{2,1},{3,0},{4,7},{5,6},{6,5},{7,4},{8,11},{9,10},{10,... | collective-permute-start | bytes 663560 | tf_op jit(solution)/shard_map/ppermute | solution.py:348
  26.8 9.5 %collective-permute-start.8 = (bf16[27,32,128]{2,1,0:T(8,128)(2,1)}, bf16[27,32,128]{2,1,0:T(8,128)(2,1)S(1)}, u32[]{:S(2)}, u32[]{:S(2)}) collective-permute-start(bf16[27,32,128]{2,1,0:T(8,128)(2,1)} %bitcast.10), channel_id=1, source_target_pairs={{0,1},{1,0},{2,3},{3,2},{4,5},{5,4},{6,7},{7,6},{8,9},{9,8},{10,11... | collective-permute-start | bytes 663560 | tf_op jit(solution)/shard_map/ppermute | solution.py:348
  26.8 11.8 %collective-permute-start.9 = (bf16[27,32,128]{2,1,0:T(8,128)(2,1)}, bf16[27,32,128]{2,1,0:T(8,128)(2,1)S(1)}, u32[]{:S(2)}, u32[]{:S(2)}) collective-permute-start(bf16[27,32,128]{2,1,0:T(8,128)(2,1)} %bitcast.11), channel_id=1, source_target_pairs={{0,2},{1,3},{2,0},{3,1},{4,6},{5,7},{6,4},{7,5},{8,10},{9,11},{10,... | collective-permute-start | bytes 663560 | tf_op jit(solution)/shard_map/ppermute | solution.py:348
  28.1 0.9 %copy-start.1 = (bf16[27,128,32]{1,2,0:T(8,128)(2,1)S(1)}, bf16[27,128,32]{1,2,0:T(8,128)(2,1)}, u32[]{:S(2)}) copy-start(bf16[27,128,32]{1,2,0:T(8,128)(2,1)} %param.11) | copy-start | bytes 663556
  42.3 3.8 %collective-permute-start.11 = (bf16[4,32,512]{2,1,0:T(8,128)(2,1)S(1)}, bf16[4,32,512]{2,1,0:T(8,128)(2,1)S(1)}, u32[]{:S(2)}, u32[]{:S(2)}) collective-permute-start(bf16[4,32,512]{2,1,0:T(8,128)(2,1)S(1)} %get-tuple-element.38), channel_id=1, source_target_pairs={{0,1},{1,0},{2,3},{3,2},{4,5},{5,4},{6,7},{7,6},{8,9},{9,8},{10,11... | collective-permute-start | bytes 393224 | tf_op jit(solution)/shard_map/ppermute | solution.py:348
  42.8 6.5 %collective-permute-start.12 = (bf16[4,32,512]{2,1,0:T(8,128)(2,1)S(1)}, bf16[4,32,512]{2,1,0:T(8,128)(2,1)S(1)}, u32[]{:S(2)}, u32[]{:S(2)}) collective-permute-start(bf16[4,32,512]{2,1,0:T(8,128)(2,1)S(1)} %get-tuple-element.39), channel_id=1, source_target_pairs={{0,2},{1,3},{2,0},{3,1},{4,6},{5,7},{6,4},{7,5},{8,10},{9,11},{10,... | collective-permute-start | bytes 393224 | tf_op jit(solution)/shard_map/ppermute | solution.py:348
  44.5 7.8 %collective-permute-start.13 = (bf16[4,32,512]{2,1,0:T(8,128)(2,1)S(1)}, bf16[4,32,512]{2,1,0:T(8,128)(2,1)S(1)}, u32[]{:S(2)}, u32[]{:S(2)}) collective-permute-start(bf16[4,32,512]{2,1,0:T(8,128)(2,1)S(1)} %get-tuple-element.40), channel_id=1, source_target_pairs={{0,3},{1,2},{2,1},{3,0},{4,7},{5,6},{6,5},{7,4},{8,11},{9,10},{10,... | collective-permute-start | bytes 393224 | tf_op jit(solution)/shard_map/ppermute | solution.py:348

commit v12 on v11

--- a/solution.py
+++ b/solution.py
@@ -61,21 +61,15 @@
 
 
 def faces_kernel(tables, *refs):
-    pieces, sides, sem = refs[:4], refs[4:6], refs[6]
+    pieces, sides = refs[:4], refs[4:6]
     odd = lax.axis_index("slab") % 2
-    copies = []
     for i, out in enumerate(sides):
         tier = (odd + 1 + i) % 2
         for c in range(2):
             b = jnp.maximum(tables[4 + tier, c], 0)
             for m in range(4):
-                source = pieces[m].at[12 * tier + b]
-                copies.append(pltpu.make_async_copy(source, out.at[4 * c + m], sem.at[8 * i + 4 * c + m]))
-        copies.append(pltpu.make_async_copy(pieces[0].at[17], out.at[8], sem.at[16 + i]))
-    for copy in copies:
-        copy.start()
-    for copy in copies:
-        copy.wait()
+                out[4 * c + m] = pieces[m][12 * tier + b]
+        out[8] = pieces[0][17]
 
 
 def faces(tables, pieces):
@@ -83,9 +77,8 @@
     return pl.pallas_call(
         faces_kernel,
         out_shape=[side] * 2,
-        in_specs=[SMEM] + [HBM] * 4,
+        in_specs=[SMEM] + [VMEM] * 4,
         out_specs=[VMEM] * 2,
-        scratch_shapes=[pltpu.SemaphoreType.DMA((18,))],
         compiler_params=pltpu.CompilerParams(vmem_limit_bytes=4 << 20),
         name="pick_faces",
     )(tables, *pieces)
@@ -174,7 +167,7 @@
 def first_kernel(tab, *refs):
     feat, sides, shards = refs[0:4], refs[4:6], refs[6:10]
     pad_out, shift = refs[10:12]
-    fs, hs, w1, bias, sent, sent_int, tables, slots, pad, pad_face, acc, sem = refs[12:]
+    hs, w1, sent, sent_int, tables, slots, pad, pad_face, acc, sem = refs[12:]
     me = lax.axis_index("chan")
 
     f_copies, t_copies = [], []
@@ -182,9 +175,6 @@
         side = (lax.axis_index("slab") + 1 + i) % 2
         t_copies.append(pltpu.make_async_copy(sides[i].at[8, pl.ds(0, 16)], sent.at[side], sem.at[i]))
         f_copies.append(pltpu.make_async_copy(sides[i].at[pl.ds(0, 8)], hs.at[side], sem.at[2 + i]))
-    for m in range(4):
-        f_copies.append(pltpu.make_async_copy(feat[m].at[pl.ds(0, 16)], fs.at[m], sem.at[4 + m]))
-        f_copies.append(pltpu.make_async_copy(feat[m].at[16, pl.ds(0, 16)], bias.at[m], sem.at[8 + m]))
     w_copies = [
         pltpu.make_async_copy(shards[m], w1.at[:, pl.ds(32 * m, 32), :], sem.at[12 + m]) for m in range(4)
     ]
@@ -201,7 +191,7 @@
     slots[NONE] = jnp.zeros((8, 8, 8, 128), F32)
     for b in range(4):
         for v in range(4):
-            brick = jnp.concatenate([fs[m, 4 * v + b] for m in range(4)], axis=0)
+            brick = jnp.concatenate([feat[m][4 * v + b] for m in range(4)], axis=0)
             slots[b, 2 * v : 2 * v + 2] = brick.T.astype(F32).reshape(2, 8, 8, 128)
     for side in range(2):
         for c in range(2):
@@ -239,7 +229,7 @@
     for pair in range(2):
         gather_padded(slots, pad, pair, own(pair), OWN_PLANES)
 
-    values = sum(bias[m].astype(F32) for m in range(4))
+    values = sum(feat[m][16, pl.ds(0, 16), :].astype(F32) for m in range(4))
     shift[...] = values[0:8] + values[8:16]
     moved = shift[0:1, :] + shift[pl.ds(2 + me, 1), :]
     for copy in w_copies:
@@ -260,13 +250,11 @@
     return pl.pallas_call(
         first_kernel,
         out_shape=[jax.ShapeDtypeStruct((2, 10, 10, 16, 384), BF16), jax.ShapeDtypeStruct((8, 128), F32)],
-        in_specs=[SMEM] + [HBM] * 10,
+        in_specs=[SMEM] + [VMEM] * 4 + [HBM] * 6,
         out_specs=[VMEM] * 2,
         scratch_shapes=[
-            pltpu.VMEM((4, 16, 32, 128), BF16),
             pltpu.VMEM((2, 8, 32, 128), BF16),
             pltpu.VMEM((27, 128, 128), BF16),
-            pltpu.VMEM((4, 16, 128), BF16),
             pltpu.VMEM((2, 16, 128), BF16),
             pltpu.VMEM((32, 128), jnp.int32),
             pltpu.SMEM((32, 128), jnp.int32),

time: 53.4 us -> 53 us (level)
  Pallas kernels: 12.8 us -> 11.7 us
  waiting for transfers between devices: 15.2 us -> 15.9 us
    ppermute x12, waiting for transfers between devices: 15.1 us -> 15.9 us  [swap(): return lax.ppermute(value, 'chan', [(i, i ^ m) for i in range(4)])]
    pallas_call x1, Pallas kernels: 7.16 us -> 6.47 us  [convolve_first(): pl.pallas_call(first_kernel, out_shape=[jax.ShapeDtypeStruct((2, 10, 10,...]
  transfers between devices with their start and end apart: 14 -> 14, of which waited for: 5 -> 5; matrix products, arithmetic and copies ran while one was open for 4% -> 4% of each run, Pallas kernels for 16% -> 14%
where the time goes in v12:
time: 53 us; the launch traced here: 52.8 us
  starting transfers between devices  21 us (40%)
  waiting for transfers between devices  15.9 us (30%)
  Pallas kernels  11.7 us (22%)
  other arithmetic  2.07 us (4%)
  local copies, waits for them, and re-layouts  1.98 us (4%)
    ppermute x12, waiting for transfers between devices, swap(): return lax.ppermute(value, 'chan', [(i, i ^ m) for i in range(4)])  15.9 us
    ppermute x12, starting transfers between devices, swap(): return lax.ppermute(value, 'chan', [(i, i ^ m) for i in range(4)])  15 us
    pallas_call x1, Pallas kernels, convolve_first(): pl.pallas_call(first_kernel, out_shape=[jax.ShapeDtypeStruct((2, 10, 10,...  6.47 us
    ppermute x2, starting transfers between devices, swap_faces(): lax.ppermute(value, 'slab', [(s, p if 0 <= p < count else s) for s, p in...  6.06 us
    pallas_call x1, Pallas kernels, convolve_second(): pl.pallas_call(second_kernel, out_shape=[piece] * 4, in_specs=[SMEM, VMEM...  3.69 us
    unnamed x6, local copies, waits for them, and re-layouts  1.98 us
    convert_element_type x2, other arithmetic, in_rows(): array = array.reshape(-1, array.shape[-1]).astype(F32)  1.36 us
  transfers between devices with their start and end apart: 14, of which 5 were waited for; matrix products, arithmetic and copies ran while one was open for 4% of the time, Pallas kernels for 14%

profile of v12, /device:TPU:25, one launch (start us, length us, event | category | flops | bytes accessed | tf_op | source)
XLA Modules:
  0.0 52.8 jit_solution(6359536667956232273)
XLA Ops:
  0.0 2.7 %collective-permute-start = (bf16[27,32,128]{2,1,0:T(8,128)(2,1)}, bf16[27,32,128]{2,1,0:T(8,128)(2,1)S(1)}, u32[]{:S(2)}, u32[]{:S(2)}) collective-permute-start(bf16[27,32,128]{2,1,0:T(8,128)(2,1)} %bitcast.6), channel_id=1, source_target_pairs={{0,2},{1,3},{2,0},{3,1},{4,6},{5,7},{6,4},{7,5},{8,10},{9,11},{10,... | collective-permute-start | bytes 663560 | tf_op jit(solution)/shard_map/ppermute | solution.py:336
  2.7 0.7 %convert_element_type.19 = f32[4,27]{1,0:T(4,128)S(1)} convert(s32[4,27]{1,0:T(4,128)} %param.9) | non-fusion elementwise | flops 108 | bytes 864 | tf_op jit(solution)/shard_map/convert_element_type | solution.py:43
  3.4 0.7 %convert_bitcast_fusion = f32[2,2]{1,0:T(2,128)S(1)} fusion(s32[1,2,2]{2,1,0:T(2,128)} %param.10), kind=kLoop, calls=%fused_computation.1 | loop fusion | flops 4 | bytes 32 | tf_op jit(solution)/shard_map/convert_element_type | solution.py:43
  4.1 0.7 %pad_add_fusion.small = f32[16,128]{1,0:T(8,128)S(1)} fusion(f32[2,2]{1,0:T(2,128)S(1)} %convert_bitcast_fusion, f32[4,27]{1,0:T(4,128)S(1)} %convert_element_type.19, f32[4,32]{1,0:T(4,128)} %param.15, f32[1,32]{1,0:T(1,128)} %bitcast.13, f32[1,32]{1,0:T(1,128)} %bitcast.14), kind=kLoop, calls=%fused_computation | loop fusion | flops 8192 | bytes 9408 | tf_op jit(solution)/shard_map/add | solution.py:50
  4.8 0.0 copy-start
  4.8 1.0 %copy-done = bf16[4,4,32,512]{3,2,1,0:T(8,128)(2,1)S(1)} copy-done((bf16[4,4,32,512]{3,2,1,0:T(8,128)(2,1)S(1)}, bf16[4,4,32,512]{3,2,1,0:T(8,128)(2,1)}, u32[]{:S(2)}) %copy-start) | copy-done | bytes 524312
  5.9 0.1 split_features.1
  6.0 1.0 %collective-permute-start.1 = (bf16[17,32,128]{2,1,0:T(8,128)(2,1)S(1)}, bf16[17,32,128]{2,1,0:T(8,128)(2,1)S(1)}, u32[]{:S(2)}, u32[]{:S(2)}) collective-permute-start(bf16[17,32,128]{2,1,0:T(8,128)(2,1)S(1)} %get-tuple-element.25), channel_id=1, source_target_pairs={{0,1},{1,0},{2,3},{3,2},{4,5},{5,4},{6,7},{7,6},{8,9},{9,8},{10,11... | collective-permute-start | bytes 417800 | tf_op jit(solution)/shard_map/ppermute | solution.py:336
  7.0 0.2 collective-permute-start.2
  7.2 3.0 %collective-permute-start.3 = (bf16[17,32,128]{2,1,0:T(8,128)(2,1)S(1)}, bf16[17,32,128]{2,1,0:T(8,128)(2,1)S(1)}, u32[]{:S(2)}, u32[]{:S(2)}) collective-permute-start(bf16[17,32,128]{2,1,0:T(8,128)(2,1)S(1)} %get-tuple-element.27), channel_id=1, source_target_pairs={{0,3},{1,2},{2,1},{3,0},{4,7},{5,6},{6,5},{7,4},{8,11},{9,10},{10,... | collective-permute-start | bytes 417800 | tf_op jit(solution)/shard_map/ppermute | solution.py:336
  10.2 0.2 collective-permute-start.6
  10.4 0.0 collective-permute-done.1.refs_1_
  10.4 3.4 %collective-permute-done.2.refs_2_ = bf16[17,32,128]{2,1,0:T(8,128)(2,1)S(1)} collective-permute-done((bf16[17,32,128]{2,1,0:T(8,128)(2,1)S(1)}, bf16[17,32,128]{2,1,0:T(8,128)(2,1)S(1)}, u32[]{:S(2)}, u32[]{:S(2)}) %collective-permute-start.2) | collective-permute-done | bytes 139296 | tf_op jit(solution)/shard_map/ppermute | solution.py:336
  13.7 3.2 %collective-permute-done.3.refs_3_ = bf16[17,32,128]{2,1,0:T(8,128)(2,1)S(1)} collective-permute-done((bf16[17,32,128]{2,1,0:T(8,128)(2,1)S(1)}, bf16[17,32,128]{2,1,0:T(8,128)(2,1)S(1)}, u32[]{:S(2)}, u32[]{:S(2)}) %collective-permute-start.3) | collective-permute-done | bytes 139296 | tf_op jit(solution)/shard_map/ppermute | solution.py:336
  16.9 0.0 collective-permute-done.refs_8_
  16.9 0.2 collective-permute-start.7
  17.1 0.0 copy-start.2
  17.1 0.6 %pick_faces.1 = (bf16[9,32,128]{2,1,0:T(8,128)(2,1)S(1)}, bf16[9,32,128]{2,1,0:T(8,128)(2,1)S(1)}) custom-call(s32[8,128]{1,0:T(8,128)S(1)} %get-tuple-element.23.tables.tab, bf16[18,32,128]{2,1,0:T(8,128)(2,1)S(1)} %get-tuple-element.24.refs_0_, bf16[17,32,128]{2,1,0:T(8,128)(2,1)S(1)} %collective-permute-done.1.refs_1_, ...), custom_call_target="tpu_custom_call" | custom-call | tf_op jit(solution)/shard_map/pick_faces/pallas_call | solution.py:77
  17.8 1.7 %collective-permute-start.4 = (bf16[9,32,128]{2,1,0:T(8,128)(2,1)S(1)}, bf16[9,32,128]{2,1,0:T(8,128)(2,1)S(1)}, u32[]{:S(2)}, u32[]{:S(2)}) collective-permute-start(bf16[9,32,128]{2,1,0:T(8,128)(2,1)S(1)} %get-tuple-element.31), channel_id=1, source_target_pairs={{0,4},{4,0},{8,12},{12,8},{16,20},{20,16},{24,28},{28,24},{32,36},... | collective-permute-start | bytes 221192 | tf_op jit(solution)/shard_map/ppermute | solution.py:342
  19.5 4.3 %collective-permute-start.5 = (bf16[9,32,128]{2,1,0:T(8,128)(2,1)S(1)}, bf16[9,32,128]{2,1,0:T(8,128)(2,1)S(1)}, u32[]{:S(2)}, u32[]{:S(2)}) collective-permute-start(bf16[9,32,128]{2,1,0:T(8,128)(2,1)S(1)} %get-tuple-element.32), channel_id=1, source_target_pairs={{0,0},{4,8},{8,4},{12,16},{16,12},{20,24},{24,20},{28,32},{32,28},... | collective-permute-start | bytes 221192 | tf_op jit(solution)/shard_map/ppermute | solution.py:342
  23.8 2.6 %collective-permute-start.10 = (bf16[27,32,128]{2,1,0:T(8,128)(2,1)}, bf16[27,32,128]{2,1,0:T(8,128)(2,1)S(1)}, u32[]{:S(2)}, u32[]{:S(2)}) collective-permute-start(bf16[27,32,128]{2,1,0:T(8,128)(2,1)} %bitcast.9), channel_id=1, source_target_pairs={{0,3},{1,2},{2,1},{3,0},{4,7},{5,6},{6,5},{7,4},{8,11},{9,10},{10,... | collective-permute-start | bytes 663560 | tf_op jit(solution)/shard_map/ppermute | solution.py:336
  26.4 0.0 collective-permute-done.6.refs_7_
  26.4 0.0 collective-permute-start.8
  26.4 0.0 collective-permute-done.4.refs_4_
  26.4 1.3 %collective-permute-start.9 = (bf16[27,32,128]{2,1,0:T(8,128)(2,1)}, bf16[27,32,128]{2,1,0:T(8,128)(2,1)S(1)}, u32[]{:S(2)}, u32[]{:S(2)}) collective-permute-start(bf16[27,32,128]{2,1,0:T(8,128)(2,1)} %bitcast.11), channel_id=1, source_target_pairs={{0,2},{1,3},{2,0},{3,1},{4,6},{5,7},{6,4},{7,5},{8,10},{9,11},{10,... | collective-permute-start | bytes 663560 | tf_op jit(solution)/shard_map/ppermute | solution.py:336
  27.7 0.0 collective-permute-done.5.refs_5_
  27.7 0.0 collective-permute-done.7.refs_9_
  27.7 0.0 copy-start.1
  27.7 0.9 %copy-done.1 = bf16[27,128,32]{1,2,0:T(8,128)(2,1)S(1)} copy-done((bf16[27,128,32]{1,2,0:T(8,128)(2,1)S(1)}, bf16[27,128,32]{1,2,0:T(8,128)(2,1)}, u32[]{:S(2)}) %copy-start.1) | copy-done | bytes 221208
  28.7 6.5 %convolve_first.1 = (bf16[2,10,10,16,384]{4,3,2,1,0:T(8,128)(2,1)S(1)}, f32[8,128]{1,0:T(8,128)S(1)}) custom-call(s32[8,128]{1,0:T(8,128)S(1)} %get-tuple-element.23.tables.tab, bf16[18,32,128]{2,1,0:T(8,128)(2,1)S(1)} %get-tuple-element.24.refs_0_, bf16[17,32,128]{2,1,0:T(8,128)(2,1)S(1)} %collective-permute-done.1.refs_1_, ...), custom_call_target="tpu_custom_call" | custom-call | flops 5000000000 | bytes 4000000 | tf_op jit(solution)/shard_map/convolve_first/pallas_call | solution.py:250
  35.1 0.0 collective-permute-done.10.refs_3_
  35.2 0.0 collective-permute-done.8.refs_1_
  35.2 3.1 %collective-permute-done.9.refs_2_ = bf16[27,32,128]{2,1,0:T(8,128)(2,1)S(1)} collective-permute-done((bf16[27,32,128]{2,1,0:T(8,128)(2,1)}, bf16[27,32,128]{2,1,0:T(8,128)(2,1)S(1)}, u32[]{:S(2)}, u32[]{:S(2)}) %collective-permute-start.9) | collective-permute-done | bytes 221216 | tf_op jit(solution)/shard_map/ppermute | solution.py:336
  38.2 0.0 copy-done.2
  38.2 3.7 %convolve_second.1 = (bf16[4,32,512]{2,1,0:T(8,128)(2,1)S(1)}, bf16[4,32,512]{2,1,0:T(8,128)(2,1)S(1)}, bf16[4,32,512]{2,1,0:T(8,128)(2,1)S(1)}, bf16[4,32,512]{2,1,0:T(8,128)(2,1)S(1)}) custom-call(s32[8,128]{1,0:T(8,128)S(1)} %get-tuple-element.23.tables.tab, bf16[2,10,10,16,384]{4,3,2,1,0:T(8,128)(2,1)S(1)} %get-tuple-element.34.pad, ...), custom_call_target="tpu_custom_call" | custom-call | flops 4000000000 | bytes 4000000 | tf_op jit(solution)/shard_map/convolve_second/pallas_call | solution.py:295
  41.9 0.5 collective-permute-start.11
  42.4 1.7 %collective-permute-start.12 = (bf16[4,32,512]{2,1,0:T(8,128)(2,1)S(1)}, bf16[4,32,512]{2,1,0:T(8,128)(2,1)S(1)}, u32[]{:S(2)}, u32[]{:S(2)}) collective-permute-start(bf16[4,32,512]{2,1,0:T(8,128)(2,1)S(1)} %get-tuple-element.39), channel_id=1, source_target_pairs={{0,2},{1,3},{2,0},{3,1},{4,6},{5,7},{6,4},{7,5},{8,10},{9,11},{10,... | collective-permute-start | bytes 393224 | tf_op jit(solution)/shard_map/ppermute | solution.py:336
  44.1 1.5 %collective-permute-start.13 = (bf16[4,32,512]{2,1,0:T(8,128)(2,1)S(1)}, bf16[4,32,512]{2,1,0:T(8,128)(2,1)S(1)}, u32[]{:S(2)}, u32[]{:S(2)}) collective-permute-start(bf16[4,32,512]{2,1,0:T(8,128)(2,1)S(1)} %get-tuple-element.40), channel_id=1, source_target_pairs={{0,3},{1,2},{2,1},{3,0},{4,7},{5,6},{6,5},{7,4},{8,11},{9,10},{10,... | collective-permute-start | bytes 393224 | tf_op jit(solution)/shard_map/ppermute | solution.py:336
  45.7 0.0 collective-permute-done.11.refs_1_
  45.7 3.3 %collective-permute-done.12.refs_2_ = bf16[4,32,512]{2,1,0:T(8,128)(2,1)S(1)} collective-permute-done((bf16[4,32,512]{2,1,0:T(8,128)(2,1)S(1)}, bf16[4,32,512]{2,1,0:T(8,128)(2,1)S(1)}, u32[]{:S(2)}, u32[]{:S(2)}) %collective-permute-start.12) | collective-permute-done | bytes 131104 | tf_op jit(solution)/shard_map/ppermute | solution.py:336
  49.0 3.0 %collective-permute-done.13.refs_3_ = bf16[4,32,512]{2,1,0:T(8,128)(2,1)S(1)} collective-permute-done((bf16[4,32,512]{2,1,0:T(8,128)(2,1)S(1)}, bf16[4,32,512]{2,1,0:T(8,128)(2,1)S(1)}, u32[]{:S(2)}, u32[]{:S(2)}) %collective-permute-start.13) | collective-permute-done | bytes 131104 | tf_op jit(solution)/shard_map/ppermute | solution.py:336
  52.0 0.8 %join_levels.1 = bf16[4,4,32,512]{3,2,1,0:T(8,128)(2,1)} custom-call(bf16[4,32,512]{2,1,0:T(8,128)(2,1)S(1)} %get-tuple-element.37.refs_0_, bf16[4,32,512]{2,1,0:T(8,128)(2,1)S(1)} %collective-permute-done.11.refs_1_, bf16[4,32,512]{2,1,0:T(8,128)(2,1)S(1)} %collective-permute-done.12.refs_2_, bf16[4,32,512]{2,1,0:T(8,128)(2,1)S(1)} %collective-permute-done.13.refs_3_), custom_call_target="tpu_custom_call" | custom-call | tf_op jit(solution)/shard_map/join_levels/pallas_call | solution.py:324
Async XLA Ops:
  0.0 16.9 %collective-permute-start = (bf16[27,32,128]{2,1,0:T(8,128)(2,1)}, bf16[27,32,128]{2,1,0:T(8,128)(2,1)S(1)}, u32[]{:S(2)}, u32[]{:S(2)}) collective-permute-start(bf16[27,32,128]{2,1,0:T(8,128)(2,1)} %bitcast.6), channel_id=1, source_target_pairs={{0,2},{1,3},{2,0},{3,1},{4,6},{5,7},{6,4},{7,5},{8,10},{9,11},{10,... | collective-permute-start | bytes 663560 | tf_op jit(solution)/shard_map/ppermute | solution.py:336
  4.8 1.0 %copy-start = (bf16[4,4,32,512]{3,2,1,0:T(8,128)(2,1)S(1)}, bf16[4,4,32,512]{3,2,1,0:T(8,128)(2,1)}, u32[]{:S(2)}) copy-start(bf16[4,4,32,512]{3,2,1,0:T(8,128)(2,1)} %feat.1) | copy-start | bytes 1572868
  6.0 4.4 %collective-permute-start.1 = (bf16[17,32,128]{2,1,0:T(8,128)(2,1)S(1)}, bf16[17,32,128]{2,1,0:T(8,128)(2,1)S(1)}, u32[]{:S(2)}, u32[]{:S(2)}) collective-permute-start(bf16[17,32,128]{2,1,0:T(8,128)(2,1)S(1)} %get-tuple-element.25), channel_id=1, source_target_pairs={{0,1},{1,0},{2,3},{3,2},{4,5},{5,4},{6,7},{7,6},{8,9},{9,8},{10,11... | collective-permute-start | bytes 417800 | tf_op jit(solution)/shard_map/ppermute | solution.py:336
  7.0 6.7 %collective-permute-start.2 = (bf16[17,32,128]{2,1,0:T(8,128)(2,1)S(1)}, bf16[17,32,128]{2,1,0:T(8,128)(2,1)S(1)}, u32[]{:S(2)}, u32[]{:S(2)}) collective-permute-start(bf16[17,32,128]{2,1,0:T(8,128)(2,1)S(1)} %get-tuple-element.26), channel_id=1, source_target_pairs={{0,2},{1,3},{2,0},{3,1},{4,6},{5,7},{6,4},{7,5},{8,10},{9,11},{10,... | collective-permute-start | bytes 417800 | tf_op jit(solution)/shard_map/ppermute | solution.py:336
  7.2 9.7 %collective-permute-start.3 = (bf16[17,32,128]{2,1,0:T(8,128)(2,1)S(1)}, bf16[17,32,128]{2,1,0:T(8,128)(2,1)S(1)}, u32[]{:S(2)}, u32[]{:S(2)}) collective-permute-start(bf16[17,32,128]{2,1,0:T(8,128)(2,1)S(1)} %get-tuple-element.27), channel_id=1, source_target_pairs={{0,3},{1,2},{2,1},{3,0},{4,7},{5,6},{6,5},{7,4},{8,11},{9,10},{10,... | collective-permute-start | bytes 417800 | tf_op jit(solution)/shard_map/ppermute | solution.py:336
  10.2 16.2 %collective-permute-start.6 = (bf16[27,32,128]{2,1,0:T(8,128)(2,1)}, bf16[27,32,128]{2,1,0:T(8,128)(2,1)S(1)}, u32[]{:S(2)}, u32[]{:S(2)}) collective-permute-start(bf16[27,32,128]{2,1,0:T(8,128)(2,1)} %bitcast.7), channel_id=1, source_target_pairs={{0,1},{1,0},{2,3},{3,2},{4,5},{5,4},{6,7},{7,6},{8,9},{9,8},{10,11... | collective-permute-start | bytes 663560 | tf_op jit(solution)/shard_map/ppermute | solution.py:336
  16.9 10.8 %collective-permute-start.7 = (bf16[27,32,128]{2,1,0:T(8,128)(2,1)S(1)}, bf16[27,32,128]{2,1,0:T(8,128)(2,1)S(1)}, u32[]{:S(2)}, u32[]{:S(2)}) collective-permute-start(bf16[27,32,128]{2,1,0:T(8,128)(2,1)S(1)} %collective-permute-done.refs_8_), channel_id=1, source_target_pairs={{0,1},{1,0},{2,3},{3,2},{4,5},{5,4},{6,7},{7,6},{8,9},{9,8},{10,11... | collective-permute-start | bytes 663560 | tf_op jit(solution)/shard_map/ppermute | solution.py:336
  17.1 21.1 %copy-start.2 = (bf16[27,128,32]{1,2,0:T(8,128)(2,1)S(1)}, bf16[27,128,32]{1,2,0:T(8,128)(2,1)}, u32[]{:S(2)}) copy-start(bf16[27,128,32]{1,2,0:T(8,128)(2,1)} %param.13) | copy-start | bytes 663556
  17.8 8.6 %collective-permute-start.4 = (bf16[9,32,128]{2,1,0:T(8,128)(2,1)S(1)}, bf16[9,32,128]{2,1,0:T(8,128)(2,1)S(1)}, u32[]{:S(2)}, u32[]{:S(2)}) collective-permute-start(bf16[9,32,128]{2,1,0:T(8,128)(2,1)S(1)} %get-tuple-element.31), channel_id=1, source_target_pairs={{0,4},{4,0},{8,12},{12,8},{16,20},{20,16},{24,28},{28,24},{32,36},... | collective-permute-start | bytes 221192 | tf_op jit(solution)/shard_map/ppermute | solution.py:342
  19.5 8.2 %collective-permute-start.5 = (bf16[9,32,128]{2,1,0:T(8,128)(2,1)S(1)}, bf16[9,32,128]{2,1,0:T(8,128)(2,1)S(1)}, u32[]{:S(2)}, u32[]{:S(2)}) collective-permute-start(bf16[9,32,128]{2,1,0:T(8,128)(2,1)S(1)} %get-tuple-element.32), channel_id=1, source_target_pairs={{0,0},{4,8},{8,4},{12,16},{16,12},{20,24},{24,20},{28,32},{32,28},... | collective-permute-start | bytes 221192 | tf_op jit(solution)/shard_map/ppermute | solution.py:342
  23.8 11.3 %collective-permute-start.10 = (bf16[27,32,128]{2,1,0:T(8,128)(2,1)}, bf16[27,32,128]{2,1,0:T(8,128)(2,1)S(1)}, u32[]{:S(2)}, u32[]{:S(2)}) collective-permute-start(bf16[27,32,128]{2,1,0:T(8,128)(2,1)} %bitcast.9), channel_id=1, source_target_pairs={{0,3},{1,2},{2,1},{3,0},{4,7},{5,6},{6,5},{7,4},{8,11},{9,10},{10,... | collective-permute-start | bytes 663560 | tf_op jit(solution)/shard_map/ppermute | solution.py:336
  26.4 8.8 %collective-permute-start.8 = (bf16[27,32,128]{2,1,0:T(8,128)(2,1)}, bf16[27,32,128]{2,1,0:T(8,128)(2,1)S(1)}, u32[]{:S(2)}, u32[]{:S(2)}) collective-permute-start(bf16[27,32,128]{2,1,0:T(8,128)(2,1)} %bitcast.10), channel_id=1, source_target_pairs={{0,1},{1,0},{2,3},{3,2},{4,5},{5,4},{6,7},{7,6},{8,9},{9,8},{10,11... | collective-permute-start | bytes 663560 | tf_op jit(solution)/shard_map/ppermute | solution.py:336
  26.4 11.8 %collective-permute-start.9 = (bf16[27,32,128]{2,1,0:T(8,128)(2,1)}, bf16[27,32,128]{2,1,0:T(8,128)(2,1)S(1)}, u32[]{:S(2)}, u32[]{:S(2)}) collective-permute-start(bf16[27,32,128]{2,1,0:T(8,128)(2,1)} %bitcast.11), channel_id=1, source_target_pairs={{0,2},{1,3},{2,0},{3,1},{4,6},{5,7},{6,4},{7,5},{8,10},{9,11},{10,... | collective-permute-start | bytes 663560 | tf_op jit(solution)/shard_map/ppermute | solution.py:336
  27.7 0.9 %copy-start.1 = (bf16[27,128,32]{1,2,0:T(8,128)(2,1)S(1)}, bf16[27,128,32]{1,2,0:T(8,128)(2,1)}, u32[]{:S(2)}) copy-start(bf16[27,128,32]{1,2,0:T(8,128)(2,1)} %param.11) | copy-start | bytes 663556
  41.9 3.7 %collective-permute-start.11 = (bf16[4,32,512]{2,1,0:T(8,128)(2,1)S(1)}, bf16[4,32,512]{2,1,0:T(8,128)(2,1)S(1)}, u32[]{:S(2)}, u32[]{:S(2)}) collective-permute-start(bf16[4,32,512]{2,1,0:T(8,128)(2,1)S(1)} %get-tuple-element.38), channel_id=1, source_target_pairs={{0,1},{1,0},{2,3},{3,2},{4,5},{5,4},{6,7},{7,6},{8,9},{9,8},{10,11... | collective-permute-start | bytes 393224 | tf_op jit(solution)/shard_map/ppermute | solution.py:336
  42.4 6.6 %collective-permute-start.12 = (bf16[4,32,512]{2,1,0:T(8,128)(2,1)S(1)}, bf16[4,32,512]{2,1,0:T(8,128)(2,1)S(1)}, u32[]{:S(2)}, u32[]{:S(2)}) collective-permute-start(bf16[4,32,512]{2,1,0:T(8,128)(2,1)S(1)} %get-tuple-element.39), channel_id=1, source_target_pairs={{0,2},{1,3},{2,0},{3,1},{4,6},{5,7},{6,4},{7,5},{8,10},{9,11},{10,... | collective-permute-start | bytes 393224 | tf_op jit(solution)/shard_map/ppermute | solution.py:336
  44.1 7.8 %collective-permute-start.13 = (bf16[4,32,512]{2,1,0:T(8,128)(2,1)S(1)}, bf16[4,32,512]{2,1,0:T(8,128)(2,1)S(1)}, u32[]{:S(2)}, u32[]{:S(2)}) collective-permute-start(bf16[4,32,512]{2,1,0:T(8,128)(2,1)S(1)} %get-tuple-element.40), channel_id=1, source_target_pairs={{0,3},{1,2},{2,1},{3,0},{4,7},{5,6},{6,5},{7,4},{8,11},{9,10},{10,... | collective-permute-start | bytes 393224 | tf_op jit(solution)/shard_map/ppermute | solution.py:336

commit v13 on v12

--- a/solution.py
+++ b/solution.py
@@ -355,8 +355,10 @@
     first = [w1, swap(w1, 1), far, swap(far, 1)]
     sides = faces(tables, pieces)
     sides = [swap_faces(sides[i], i) for i in range(2)]
-    second = [w2] + [swap(later, m) for m in (1, 2, 3)]
+    second = [w2, swap(later, 1), swap(later, 2)]
     pad, shift = convolve_first(tables, pieces, sides, first)
+    passed, shift = lax.optimization_barrier((second[2], shift))
+    second = [w2, second[1], passed, swap(passed, 1)]
     outs = convolve_second(tables, pad, shift, second)
     return join([outs[0]] + [swap(outs[m], m) for m in (1, 2, 3)])
 

time: 53 us -> 53.5 us (level)
  starting transfers between devices: 21 us -> 22.7 us
  waiting for transfers between devices: 15.9 us -> 14.6 us
    ppermute x12, waiting for transfers between devices: 15.9 us -> 13.9 us  [swap(): return lax.ppermute(value, 'chan', [(i, i ^ m) for i in range(4)])]
    ppermute x12, starting transfers between devices: 15 us -> 16.7 us  [swap(): return lax.ppermute(value, 'chan', [(i, i ^ m) for i in range(4)])]
    ppermute x2, waiting for transfers between devices: 0.01 us -> 0.78 us  [swap_faces(): lax.ppermute(value, 'slab', [(s, p if 0 <= p < count else s) for s, p in...]
  transfers between devices with their start and end apart: 14 -> 14, of which waited for: 5 -> 6; matrix products, arithmetic and copies ran while one was open for 4% -> 4% of each run, Pallas kernels for 14% -> 14%
where the time goes in v13:
time: 53.5 us; the launch traced here: 53.2 us
  starting transfers between devices  22.7 us (42%)
  waiting for transfers between devices  14.6 us (27%)
  Pallas kernels  11.7 us (22%)
  other arithmetic  2.07 us (4%)
  local copies, waits for them, and re-layouts  1.98 us (4%)
    ppermute x12, starting transfers between devices, swap(): return lax.ppermute(value, 'chan', [(i, i ^ m) for i in range(4)])  16.7 us
    ppermute x12, waiting for transfers between devices, swap(): return lax.ppermute(value, 'chan', [(i, i ^ m) for i in range(4)])  13.9 us
    pallas_call x1, Pallas kernels, convolve_first(): pl.pallas_call(first_kernel, out_shape=[jax.ShapeDtypeStruct((2, 10, 10,...  6.47 us
    ppermute x2, starting transfers between devices, swap_faces(): lax.ppermute(value, 'slab', [(s, p if 0 <= p < count else s) for s, p in...  6.06 us
    pallas_call x1, Pallas kernels, convolve_second(): pl.pallas_call(second_kernel, out_shape=[piece] * 4, in_specs=[SMEM, VMEM...  3.69 us
    unnamed x6, local copies, waits for them, and re-layouts  1.98 us
    convert_element_type x2, other arithmetic, in_rows(): array = array.reshape(-1, array.shape[-1]).astype(F32)  1.36 us
  transfers between devices with their start and end apart: 14, of which 6 were waited for; matrix products, arithmetic and copies ran while one was open for 4% of the time, Pallas kernels for 14%

profile of v13, /device:TPU:25, one launch (start us, length us, event | category | flops | bytes accessed | tf_op | source)
XLA Modules:
  0.0 53.2 jit_solution(14784009504932045527)
XLA Ops:
  0.0 2.7 %collective-permute-start = (bf16[27,32,128]{2,1,0:T(8,128)(2,1)}, bf16[27,32,128]{2,1,0:T(8,128)(2,1)S(1)}, u32[]{:S(2)}, u32[]{:S(2)}) collective-permute-start(bf16[27,32,128]{2,1,0:T(8,128)(2,1)} %bitcast.6), channel_id=1, source_target_pairs={{0,2},{1,3},{2,0},{3,1},{4,6},{5,7},{6,4},{7,5},{8,10},{9,11},{10,... | collective-permute-start | bytes 663560 | tf_op jit(solution)/shard_map/ppermute | solution.py:336
  2.7 0.7 %convert_element_type.19 = f32[4,27]{1,0:T(4,128)S(1)} convert(s32[4,27]{1,0:T(4,128)} %param.9) | non-fusion elementwise | flops 108 | bytes 864 | tf_op jit(solution)/shard_map/convert_element_type | solution.py:43
  3.4 0.7 %convert_bitcast_fusion = f32[2,2]{1,0:T(2,128)S(1)} fusion(s32[1,2,2]{2,1,0:T(2,128)} %param.10), kind=kLoop, calls=%fused_computation.1 | loop fusion | flops 4 | bytes 32 | tf_op jit(solution)/shard_map/convert_element_type | solution.py:43
  4.1 0.7 %pad_add_fusion.small = f32[16,128]{1,0:T(8,128)S(1)} fusion(f32[2,2]{1,0:T(2,128)S(1)} %convert_bitcast_fusion, f32[4,27]{1,0:T(4,128)S(1)} %convert_element_type.19, f32[4,32]{1,0:T(4,128)} %param.15, f32[1,32]{1,0:T(1,128)} %bitcast.12, f32[1,32]{1,0:T(1,128)} %bitcast.13), kind=kLoop, calls=%fused_computation | loop fusion | flops 8192 | bytes 9408 | tf_op jit(solution)/shard_map/add | solution.py:50
  4.8 0.0 copy-start
  4.8 1.0 %copy-done = bf16[4,4,32,512]{3,2,1,0:T(8,128)(2,1)S(1)} copy-done((bf16[4,4,32,512]{3,2,1,0:T(8,128)(2,1)S(1)}, bf16[4,4,32,512]{3,2,1,0:T(8,128)(2,1)}, u32[]{:S(2)}) %copy-start) | copy-done | bytes 524312
  5.9 0.1 split_features.1
  6.0 1.0 %collective-permute-start.1 = (bf16[17,32,128]{2,1,0:T(8,128)(2,1)S(1)}, bf16[17,32,128]{2,1,0:T(8,128)(2,1)S(1)}, u32[]{:S(2)}, u32[]{:S(2)}) collective-permute-start(bf16[17,32,128]{2,1,0:T(8,128)(2,1)S(1)} %get-tuple-element.27), channel_id=1, source_target_pairs={{0,1},{1,0},{2,3},{3,2},{4,5},{5,4},{6,7},{7,6},{8,9},{9,8},{10,11... | collective-permute-start | bytes 417800 | tf_op jit(solution)/shard_map/ppermute | solution.py:336
  7.0 0.2 collective-permute-start.2
  7.2 3.0 %collective-permute-start.3 = (bf16[17,32,128]{2,1,0:T(8,128)(2,1)S(1)}, bf16[17,32,128]{2,1,0:T(8,128)(2,1)S(1)}, u32[]{:S(2)}, u32[]{:S(2)}) collective-permute-start(bf16[17,32,128]{2,1,0:T(8,128)(2,1)S(1)} %get-tuple-element.29), channel_id=1, source_target_pairs={{0,3},{1,2},{2,1},{3,0},{4,7},{5,6},{6,5},{7,4},{8,11},{9,10},{10,... | collective-permute-start | bytes 417800 | tf_op jit(solution)/shard_map/ppermute | solution.py:336
  10.2 0.2 collective-permute-start.6
  10.4 0.0 collective-permute-done.1.refs_1_
  10.4 3.4 %collective-permute-done.2.refs_2_ = bf16[17,32,128]{2,1,0:T(8,128)(2,1)S(1)} collective-permute-done((bf16[17,32,128]{2,1,0:T(8,128)(2,1)S(1)}, bf16[17,32,128]{2,1,0:T(8,128)(2,1)S(1)}, u32[]{:S(2)}, u32[]{:S(2)}) %collective-permute-start.2) | collective-permute-done | bytes 139296 | tf_op jit(solution)/shard_map/ppermute | solution.py:336
  13.7 3.2 %collective-permute-done.3.refs_3_ = bf16[17,32,128]{2,1,0:T(8,128)(2,1)S(1)} collective-permute-done((bf16[17,32,128]{2,1,0:T(8,128)(2,1)S(1)}, bf16[17,32,128]{2,1,0:T(8,128)(2,1)S(1)}, u32[]{:S(2)}, u32[]{:S(2)}) %collective-permute-start.3) | collective-permute-done | bytes 139296 | tf_op jit(solution)/shard_map/ppermute | solution.py:336
  16.9 0.0 collective-permute-done.refs_8_
  16.9 0.2 collective-permute-start.7
  17.1 0.0 copy-start.2
  17.1 0.6 %pick_faces.1 = (bf16[9,32,128]{2,1,0:T(8,128)(2,1)S(1)}, bf16[9,32,128]{2,1,0:T(8,128)(2,1)S(1)}) custom-call(s32[8,128]{1,0:T(8,128)S(1)} %get-tuple-element.25.tables.tab, bf16[18,32,128]{2,1,0:T(8,128)(2,1)S(1)} %get-tuple-element.26.refs_0_, bf16[17,32,128]{2,1,0:T(8,128)(2,1)S(1)} %collective-permute-done.1.refs_1_, ...), custom_call_target="tpu_custom_call" | custom-call | tf_op jit(solution)/shard_map/pick_faces/pallas_call | solution.py:77
  17.8 1.7 %collective-permute-start.4 = (bf16[9,32,128]{2,1,0:T(8,128)(2,1)S(1)}, bf16[9,32,128]{2,1,0:T(8,128)(2,1)S(1)}, u32[]{:S(2)}, u32[]{:S(2)}) collective-permute-start(bf16[9,32,128]{2,1,0:T(8,128)(2,1)S(1)} %get-tuple-element.33), channel_id=1, source_target_pairs={{0,4},{4,0},{8,12},{12,8},{16,20},{20,16},{24,28},{28,24},{32,36},... | collective-permute-start | bytes 221192 | tf_op jit(solution)/shard_map/ppermute | solution.py:342
  19.5 4.3 %collective-permute-start.5 = (bf16[9,32,128]{2,1,0:T(8,128)(2,1)S(1)}, bf16[9,32,128]{2,1,0:T(8,128)(2,1)S(1)}, u32[]{:S(2)}, u32[]{:S(2)}) collective-permute-start(bf16[9,32,128]{2,1,0:T(8,128)(2,1)S(1)} %get-tuple-element.34), channel_id=1, source_target_pairs={{0,0},{4,8},{8,4},{12,16},{16,12},{20,24},{24,20},{28,32},{32,28},... | collective-permute-start | bytes 221192 | tf_op jit(solution)/shard_map/ppermute | solution.py:342
  23.8 1.8 %collective-permute-start.8 = (bf16[27,32,128]{2,1,0:T(8,128)(2,1)}, bf16[27,32,128]{2,1,0:T(8,128)(2,1)S(1)}, u32[]{:S(2)}, u32[]{:S(2)}) collective-permute-start(bf16[27,32,128]{2,1,0:T(8,128)(2,1)} %bitcast.9), channel_id=1, source_target_pairs={{0,2},{1,3},{2,0},{3,1},{4,6},{5,7},{6,4},{7,5},{8,10},{9,11},{10,... | collective-permute-start | bytes 663560 | tf_op jit(solution)/shard_map/ppermute | solution.py:336
  25.7 0.0 collective-permute-done.6.refs_7_
  25.7 1.1 %collective-permute-start.9 = (bf16[27,32,128]{2,1,0:T(8,128)(2,1)}, bf16[27,32,128]{2,1,0:T(8,128)(2,1)S(1)}, u32[]{:S(2)}, u32[]{:S(2)}) collective-permute-start(bf16[27,32,128]{2,1,0:T(8,128)(2,1)} %bitcast.10), channel_id=1, source_target_pairs={{0,1},{1,0},{2,3},{3,2},{4,5},{5,4},{6,7},{7,6},{8,9},{9,8},{10,11... | collective-permute-start | bytes 663560 | tf_op jit(solution)/shard_map/ppermute | solution.py:336
  26.8 0.0 collective-permute-done.4.refs_4_
  26.8 0.8 %collective-permute-done.5.refs_5_ = bf16[9,32,128]{2,1,0:T(8,128)(2,1)S(1)} collective-permute-done((bf16[9,32,128]{2,1,0:T(8,128)(2,1)S(1)}, bf16[9,32,128]{2,1,0:T(8,128)(2,1)S(1)}, u32[]{:S(2)}, u32[]{:S(2)}) %collective-permute-start.5) | collective-permute-done | bytes 73760 | tf_op jit(solution)/shard_map/ppermute | solution.py:342
  27.6 0.0 collective-permute-done.7.refs_9_
  27.6 0.0 copy-start.1
  27.6 0.9 %copy-done.1 = bf16[27,128,32]{1,2,0:T(8,128)(2,1)S(1)} copy-done((bf16[27,128,32]{1,2,0:T(8,128)(2,1)S(1)}, bf16[27,128,32]{1,2,0:T(8,128)(2,1)}, u32[]{:S(2)}) %copy-start.1) | copy-done | bytes 221208
  28.5 6.5 %convolve_first.1 = (bf16[2,10,10,16,384]{4,3,2,1,0:T(8,128)(2,1)S(1)}, f32[8,128]{1,0:T(8,128)S(1)}) custom-call(s32[8,128]{1,0:T(8,128)S(1)} %get-tuple-element.25.tables.tab, bf16[18,32,128]{2,1,0:T(8,128)(2,1)S(1)} %get-tuple-element.26.refs_0_, bf16[17,32,128]{2,1,0:T(8,128)(2,1)S(1)} %collective-permute-done.1.refs_1_, ...), custom_call_target="tpu_custom_call" | custom-call | flops 5000000000 | bytes 4000000 | tf_op jit(solution)/shard_map/convolve_first/pallas_call | solution.py:250
  35.0 0.0 collective-permute-done.8.refs_2_
  35.0 2.6 %collective-permute-start.10 = (bf16[27,32,128]{2,1,0:T(8,128)(2,1)S(1)}, bf16[27,32,128]{2,1,0:T(8,128)(2,1)S(1)}, u32[]{:S(2)}, u32[]{:S(2)}) collective-permute-start(bf16[27,32,128]{2,1,0:T(8,128)(2,1)S(1)} %collective-permute-done.8.refs_2_), channel_id=1, source_target_pairs={{0,1},{1,0},{2,3},{3,2},{4,5},{5,4},{6,7},{7,6},{8,9},{9,8},{10,11... | collective-permute-start | bytes 663560 | tf_op jit(solution)/shard_map/ppermute | solution.py:336
  37.6 0.0 collective-permute-done.9.refs_1_
  37.6 1.1 %collective-permute-done.10.refs_3_ = bf16[27,32,128]{2,1,0:T(8,128)(2,1)S(1)} collective-permute-done((bf16[27,32,128]{2,1,0:T(8,128)(2,1)S(1)}, bf16[27,32,128]{2,1,0:T(8,128)(2,1)S(1)}, u32[]{:S(2)}, u32[]{:S(2)}) %collective-permute-start.10) | collective-permute-done | bytes 221216 | tf_op jit(solution)/shard_map/ppermute | solution.py:336
  38.7 0.0 copy-done.2
  38.7 3.7 %convolve_second.1 = (bf16[4,32,512]{2,1,0:T(8,128)(2,1)S(1)}, bf16[4,32,512]{2,1,0:T(8,128)(2,1)S(1)}, bf16[4,32,512]{2,1,0:T(8,128)(2,1)S(1)}, bf16[4,32,512]{2,1,0:T(8,128)(2,1)S(1)}) custom-call(s32[8,128]{1,0:T(8,128)S(1)} %get-tuple-element.25.tables.tab, bf16[2,10,10,16,384]{4,3,2,1,0:T(8,128)(2,1)S(1)} %get-tuple-element.36.pad, ...), custom_call_target="tpu_custom_call" | custom-call | flops 4000000000 | bytes 4000000 | tf_op jit(solution)/shard_map/convolve_second/pallas_call | solution.py:295
  42.4 0.5 collective-permute-start.11
  42.9 0.0 collective-permute-start.12
  42.9 3.3 %collective-permute-start.13 = (bf16[4,32,512]{2,1,0:T(8,128)(2,1)S(1)}, bf16[4,32,512]{2,1,0:T(8,128)(2,1)S(1)}, u32[]{:S(2)}, u32[]{:S(2)}) collective-permute-start(bf16[4,32,512]{2,1,0:T(8,128)(2,1)S(1)} %get-tuple-element.44), channel_id=1, source_target_pairs={{0,3},{1,2},{2,1},{3,0},{4,7},{5,6},{6,5},{7,4},{8,11},{9,10},{10,... | collective-permute-start | bytes 393224 | tf_op jit(solution)/shard_map/ppermute | solution.py:336
  46.2 0.0 collective-permute-done.11.refs_1_
  46.2 3.1 %collective-permute-done.12.refs_2_ = bf16[4,32,512]{2,1,0:T(8,128)(2,1)S(1)} collective-permute-done((bf16[4,32,512]{2,1,0:T(8,128)(2,1)S(1)}, bf16[4,32,512]{2,1,0:T(8,128)(2,1)S(1)}, u32[]{:S(2)}, u32[]{:S(2)}) %collective-permute-start.12) | collective-permute-done | bytes 131104 | tf_op jit(solution)/shard_map/ppermute | solution.py:336
  49.3 3.1 %collective-permute-done.13.refs_3_ = bf16[4,32,512]{2,1,0:T(8,128)(2,1)S(1)} collective-permute-done((bf16[4,32,512]{2,1,0:T(8,128)(2,1)S(1)}, bf16[4,32,512]{2,1,0:T(8,128)(2,1)S(1)}, u32[]{:S(2)}, u32[]{:S(2)}) %collective-permute-start.13) | collective-permute-done | bytes 131104 | tf_op jit(solution)/shard_map/ppermute | solution.py:336
  52.4 0.8 %join_levels.1 = bf16[4,4,32,512]{3,2,1,0:T(8,128)(2,1)} custom-call(bf16[4,32,512]{2,1,0:T(8,128)(2,1)S(1)} %get-tuple-element.41.refs_0_, bf16[4,32,512]{2,1,0:T(8,128)(2,1)S(1)} %collective-permute-done.11.refs_1_, bf16[4,32,512]{2,1,0:T(8,128)(2,1)S(1)} %collective-permute-done.12.refs_2_, bf16[4,32,512]{2,1,0:T(8,128)(2,1)S(1)} %collective-permute-done.13.refs_3_), custom_call_target="tpu_custom_call" | custom-call | tf_op jit(solution)/shard_map/join_levels/pallas_call | solution.py:324
Async XLA Ops:
  0.0 16.9 %collective-permute-start = (bf16[27,32,128]{2,1,0:T(8,128)(2,1)}, bf16[27,32,128]{2,1,0:T(8,128)(2,1)S(1)}, u32[]{:S(2)}, u32[]{:S(2)}) collective-permute-start(bf16[27,32,128]{2,1,0:T(8,128)(2,1)} %bitcast.6), channel_id=1, source_target_pairs={{0,2},{1,3},{2,0},{3,1},{4,6},{5,7},{6,4},{7,5},{8,10},{9,11},{10,... | collective-permute-start | bytes 663560 | tf_op jit(solution)/shard_map/ppermute | solution.py:336
  4.8 1.0 %copy-start = (bf16[4,4,32,512]{3,2,1,0:T(8,128)(2,1)S(1)}, bf16[4,4,32,512]{3,2,1,0:T(8,128)(2,1)}, u32[]{:S(2)}) copy-start(bf16[4,4,32,512]{3,2,1,0:T(8,128)(2,1)} %feat.1) | copy-start | bytes 1572868
  6.0 4.4 %collective-permute-start.1 = (bf16[17,32,128]{2,1,0:T(8,128)(2,1)S(1)}, bf16[17,32,128]{2,1,0:T(8,128)(2,1)S(1)}, u32[]{:S(2)}, u32[]{:S(2)}) collective-permute-start(bf16[17,32,128]{2,1,0:T(8,128)(2,1)S(1)} %get-tuple-element.27), channel_id=1, source_target_pairs={{0,1},{1,0},{2,3},{3,2},{4,5},{5,4},{6,7},{7,6},{8,9},{9,8},{10,11... | collective-permute-start | bytes 417800 | tf_op jit(solution)/shard_map/ppermute | solution.py:336
  7.0 6.7 %collective-permute-start.2 = (bf16[17,32,128]{2,1,0:T(8,128)(2,1)S(1)}, bf16[17,32,128]{2,1,0:T(8,128)(2,1)S(1)}, u32[]{:S(2)}, u32[]{:S(2)}) collective-permute-start(bf16[17,32,128]{2,1,0:T(8,128)(2,1)S(1)} %get-tuple-element.28), channel_id=1, source_target_pairs={{0,2},{1,3},{2,0},{3,1},{4,6},{5,7},{6,4},{7,5},{8,10},{9,11},{10,... | collective-permute-start | bytes 417800 | tf_op jit(solution)/shard_map/ppermute | solution.py:336
  7.2 9.7 %collective-permute-start.3 = (bf16[17,32,128]{2,1,0:T(8,128)(2,1)S(1)}, bf16[17,32,128]{2,1,0:T(8,128)(2,1)S(1)}, u32[]{:S(2)}, u32[]{:S(2)}) collective-permute-start(bf16[17,32,128]{2,1,0:T(8,128)(2,1)S(1)} %get-tuple-element.29), channel_id=1, source_target_pairs={{0,3},{1,2},{2,1},{3,0},{4,7},{5,6},{6,5},{7,4},{8,11},{9,10},{10,... | collective-permute-start | bytes 417800 | tf_op jit(solution)/shard_map/ppermute | solution.py:336
  10.2 15.4 %collective-permute-start.6 = (bf16[27,32,128]{2,1,0:T(8,128)(2,1)}, bf16[27,32,128]{2,1,0:T(8,128)(2,1)S(1)}, u32[]{:S(2)}, u32[]{:S(2)}) collective-permute-start(bf16[27,32,128]{2,1,0:T(8,128)(2,1)} %bitcast.7), channel_id=1, source_target_pairs={{0,1},{1,0},{2,3},{3,2},{4,5},{5,4},{6,7},{7,6},{8,9},{9,8},{10,11... | collective-permute-start | bytes 663560 | tf_op jit(solution)/shard_map/ppermute | solution.py:336
  16.9 10.7 %collective-permute-start.7 = (bf16[27,32,128]{2,1,0:T(8,128)(2,1)S(1)}, bf16[27,32,128]{2,1,0:T(8,128)(2,1)S(1)}, u32[]{:S(2)}, u32[]{:S(2)}) collective-permute-start(bf16[27,32,128]{2,1,0:T(8,128)(2,1)S(1)} %collective-permute-done.refs_8_), channel_id=1, source_target_pairs={{0,1},{1,0},{2,3},{3,2},{4,5},{5,4},{6,7},{7,6},{8,9},{9,8},{10,11... | collective-permute-start | bytes 663560 | tf_op jit(solution)/shard_map/ppermute | solution.py:336
  17.1 21.6 %copy-start.2 = (bf16[27,128,32]{1,2,0:T(8,128)(2,1)S(1)}, bf16[27,128,32]{1,2,0:T(8,128)(2,1)}, u32[]{:S(2)}) copy-start(bf16[27,128,32]{1,2,0:T(8,128)(2,1)} %param.13) | copy-start | bytes 663556
  17.8 9.0 %collective-permute-start.4 = (bf16[9,32,128]{2,1,0:T(8,128)(2,1)S(1)}, bf16[9,32,128]{2,1,0:T(8,128)(2,1)S(1)}, u32[]{:S(2)}, u32[]{:S(2)}) collective-permute-start(bf16[9,32,128]{2,1,0:T(8,128)(2,1)S(1)} %get-tuple-element.33), channel_id=1, source_target_pairs={{0,4},{4,0},{8,12},{12,8},{16,20},{20,16},{24,28},{28,24},{32,36},... | collective-permute-start | bytes 221192 | tf_op jit(solution)/shard_map/ppermute | solution.py:342
  19.5 8.1 %collective-permute-start.5 = (bf16[9,32,128]{2,1,0:T(8,128)(2,1)S(1)}, bf16[9,32,128]{2,1,0:T(8,128)(2,1)S(1)}, u32[]{:S(2)}, u32[]{:S(2)}) collective-permute-start(bf16[9,32,128]{2,1,0:T(8,128)(2,1)S(1)} %get-tuple-element.34), channel_id=1, source_target_pairs={{0,0},{4,8},{8,4},{12,16},{16,12},{20,24},{24,20},{28,32},{32,28},... | collective-permute-start | bytes 221192 | tf_op jit(solution)/shard_map/ppermute | solution.py:342
  23.8 11.2 %collective-permute-start.8 = (bf16[27,32,128]{2,1,0:T(8,128)(2,1)}, bf16[27,32,128]{2,1,0:T(8,128)(2,1)S(1)}, u32[]{:S(2)}, u32[]{:S(2)}) collective-permute-start(bf16[27,32,128]{2,1,0:T(8,128)(2,1)} %bitcast.9), channel_id=1, source_target_pairs={{0,2},{1,3},{2,0},{3,1},{4,6},{5,7},{6,4},{7,5},{8,10},{9,11},{10,... | collective-permute-start | bytes 663560 | tf_op jit(solution)/shard_map/ppermute | solution.py:336
  25.7 12.0 %collective-permute-start.9 = (bf16[27,32,128]{2,1,0:T(8,128)(2,1)}, bf16[27,32,128]{2,1,0:T(8,128)(2,1)S(1)}, u32[]{:S(2)}, u32[]{:S(2)}) collective-permute-start(bf16[27,32,128]{2,1,0:T(8,128)(2,1)} %bitcast.10), channel_id=1, source_target_pairs={{0,1},{1,0},{2,3},{3,2},{4,5},{5,4},{6,7},{7,6},{8,9},{9,8},{10,11... | collective-permute-start | bytes 663560 | tf_op jit(solution)/shard_map/ppermute | solution.py:336
  27.6 0.9 %copy-start.1 = (bf16[27,128,32]{1,2,0:T(8,128)(2,1)S(1)}, bf16[27,128,32]{1,2,0:T(8,128)(2,1)}, u32[]{:S(2)}) copy-start(bf16[27,128,32]{1,2,0:T(8,128)(2,1)} %param.11) | copy-start | bytes 663556
  35.0 3.7 %collective-permute-start.10 = (bf16[27,32,128]{2,1,0:T(8,128)(2,1)S(1)}, bf16[27,32,128]{2,1,0:T(8,128)(2,1)S(1)}, u32[]{:S(2)}, u32[]{:S(2)}) collective-permute-start(bf16[27,32,128]{2,1,0:T(8,128)(2,1)S(1)} %collective-permute-done.8.refs_2_), channel_id=1, source_target_pairs={{0,1},{1,0},{2,3},{3,2},{4,5},{5,4},{6,7},{7,6},{8,9},{9,8},{10,11... | collective-permute-start | bytes 663560 | tf_op jit(solution)/shard_map/ppermute | solution.py:336
  42.4 3.8 %collective-permute-start.11 = (bf16[4,32,512]{2,1,0:T(8,128)(2,1)S(1)}, bf16[4,32,512]{2,1,0:T(8,128)(2,1)S(1)}, u32[]{:S(2)}, u32[]{:S(2)}) collective-permute-start(bf16[4,32,512]{2,1,0:T(8,128)(2,1)S(1)} %get-tuple-element.42), channel_id=1, source_target_pairs={{0,1},{1,0},{2,3},{3,2},{4,5},{5,4},{6,7},{7,6},{8,9},{9,8},{10,11... | collective-permute-start | bytes 393224 | tf_op jit(solution)/shard_map/ppermute | solution.py:336
  42.9 6.4 %collective-permute-start.12 = (bf16[4,32,512]{2,1,0:T(8,128)(2,1)S(1)}, bf16[4,32,512]{2,1,0:T(8,128)(2,1)S(1)}, u32[]{:S(2)}, u32[]{:S(2)}) collective-permute-start(bf16[4,32,512]{2,1,0:T(8,128)(2,1)S(1)} %get-tuple-element.43), channel_id=1, source_target_pairs={{0,2},{1,3},{2,0},{3,1},{4,6},{5,7},{6,4},{7,5},{8,10},{9,11},{10,... | collective-permute-start | bytes 393224 | tf_op jit(solution)/shard_map/ppermute | solution.py:336
  42.9 9.5 %collective-permute-start.13 = (bf16[4,32,512]{2,1,0:T(8,128)(2,1)S(1)}, bf16[4,32,512]{2,1,0:T(8,128)(2,1)S(1)}, u32[]{:S(2)}, u32[]{:S(2)}) collective-permute-start(bf16[4,32,512]{2,1,0:T(8,128)(2,1)S(1)} %get-tuple-element.44), channel_id=1, source_target_pairs={{0,3},{1,2},{2,1},{3,0},{4,7},{5,6},{6,5},{7,4},{8,11},{9,10},{10,... | collective-permute-start | bytes 393224 | tf_op jit(solution)/shard_map/ppermute | solution.py:336
